TPU v7x, 128 devices: a whole 4x4x4 slice. The times are simulated.
128 devices in a mesh: layer: 8 (over x, core), row: 4 (over z), col: 4 (over y).
Axes of the slice: x: 4, y: 4, z: 4, core: 2. Of those that a mesh axis runs over, the one named last changes fastest.
Arguments:
- grad_tiles: bfloat16 [1792, 128, 1152], P(('layer', 'row', 'col')), parts along dimension 0, may hold values from -6 to 6
- tile_ids: int32 [1792], P(('layer', 'row', 'col')), parts along dimension 0, may hold values from 0 to 223, as said below
- momentum: float32 [28672, 9216], P(('layer', 'row'), 'col'), parts along dimension 0, may hold values from -60 to 60
Outputs:
- new_momentum: float32 [28672, 9216], P(('layer', 'row'), 'col'), parts along dimension 0
- update: bfloat16 [28672, 9216], P(('layer', 'row'), 'col'), parts along dimension 0
There are 8 independent parts, one for each index of `layer`. A program takes and returns all parts, laid end to end along the dimension named above; each array names one. Nothing has to cross between parts.
Inputs may be any that keep to these rules, and one draw needn't show every extreme that they name: tile_ids is a permutation of 0 to 223. The owner of a tile is the device whose block of the 3584 x 9216 matrix (rows split over row, columns over col) contains it; the 14 tiles of one device belong to 14 different owners.
All inputs are finite; a program needn't handle non-finite values.
Results may differ from a plain program's by a relative error of at most 0.0058.
Values may be sent and summed in bfloat16 or wider, within the bound.
No kernel may reach another device: no remote copies, remote signals or barrier semaphores. Data moves between devices by JAX's collectives and lax.ppermute only.
A program may use at most 192 MiB of HBM per device.

v0:
```python
import math

import jax
import jax.numpy as jnp
from jax import lax
from jax.sharding import PartitionSpec as P

ROWS = 3584
COLS = 9216


MOMENTUM_RATE = 0.95
COEF_LINEAR = 3.4445
COEF_CUBIC = -4.775
COEF_QUINTIC = 2.0315
EPSILON = 1e-06


def pair_block(row_pos, col_pos, diagonal, adjacent, opposite, height):
    offset = (col_pos - row_pos) % 4
    if offset == 0:
        return diagonal[row_pos * height : (row_pos + 1) * height]
    if offset == 1:
        return adjacent[row_pos * height : (row_pos + 1) * height]
    if offset == 3:
        return adjacent[col_pos * height : (col_pos + 1) * height].T
    lower_index = min(row_pos, col_pos)
    half_rows = height // 2
    upper_part = opposite[lower_index * half_rows : (lower_index + 1) * half_rows]
    bottom = opposite[(lower_index + 2) * half_rows : (lower_index + 3) * half_rows]
    joined = jnp.concatenate([upper_part, bottom], axis=0)
    if row_pos < col_pos:
        return joined
    return joined.T


def make_factor(total):
    return math.sqrt(ROWS) / (2.0 * (jnp.sqrt(total) + EPSILON))


def on_device(grad_tiles, tile_ids, momentum):
    grid_rows = lax.axis_size("row")
    grid_cols = lax.axis_size("col")
    groups = grid_rows * grid_cols
    tile_count = grad_tiles.shape[0]
    tile_rows = grad_tiles.shape[1]
    tile_width = grad_tiles.shape[2]
    height, width = momentum.shape
    owner_blocks = height // tile_rows
    tile_row = tile_ids // (2 * grid_cols)
    tile_half = tile_ids % (2 * grid_cols)
    owners = tile_row // owner_blocks * grid_cols + tile_half // 2
    places = tile_row % owner_blocks * 2 + tile_half % 2
    matches = owners[:, None] == jnp.arange(groups, dtype=jnp.int32)[None, :]
    slot_of = jnp.sum(
        jnp.where(matches, jnp.arange(tile_count, dtype=jnp.int32)[:, None], 0), axis=0
    )
    filled = jnp.any(matches, axis=0)
    picked = jnp.take(grad_tiles, slot_of, axis=0)
    outgoing = jnp.where(filled[:, None, None], picked, jnp.zeros((), grad_tiles.dtype))
    labels = jnp.where(filled, jnp.sum(jnp.where(matches, places[:, None], 0), axis=0), -1)
    arrived, arrived_labels = (
        lax.all_to_all(outgoing, ("row", "col"), split_axis=0, concat_axis=0, tiled=True),
        lax.all_to_all(labels, ("row", "col"), split_axis=0, concat_axis=0, tiled=True),
    )
    found = arrived_labels[None, :] == jnp.arange(tile_count, dtype=jnp.int32)[:, None]
    source_of = jnp.sum(jnp.where(found, jnp.arange(groups, dtype=jnp.int32)[None, :], 0), axis=1)
    local_tiles = jnp.take(arrived, source_of, axis=0)
    gradient = (
        local_tiles.reshape(owner_blocks, 2, tile_rows, tile_width)
        .transpose(0, 2, 1, 3)
        .reshape(height, width)
    )
    gradient = gradient.astype(jnp.float32)
    new_momentum = MOMENTUM_RATE * momentum + gradient
    direction = gradient + MOMENTUM_RATE * new_momentum
    rounded = direction.astype(jnp.bfloat16)
    panel = lax.all_gather(rounded, "row", axis=0, tiled=True)
    grid_row = lax.axis_index("row")
    grid_col = lax.axis_index("col")
    half_rows = height // 2
    pair_low = grid_row % 2
    pair_half = grid_row // 2
    neighbour = lax.dynamic_slice_in_dim(panel, (grid_row + 1) % 4 * height, height, 0)
    upper_rows = lax.dynamic_slice_in_dim(
        panel, pair_low * height + pair_half * half_rows, half_rows, 0
    )
    partner = lax.dynamic_slice_in_dim(panel, (pair_low + 2) * height, height, 0)
    term_diag = jnp.einsum("ik,jk->ij", rounded, rounded, preferred_element_type=jnp.float32)
    term_next = jnp.einsum("ik,jk->ij", rounded, neighbour, preferred_element_type=jnp.float32)
    term_pair = jnp.einsum("ik,jk->ij", upper_rows, partner, preferred_element_type=jnp.float32)
    panel_squares = jnp.sum(jnp.square(panel.astype(jnp.float32)))
    sum_diag, sum_next, sum_pair, total = lax.psum(
        (term_diag, term_next, term_pair, panel_squares), "col"
    )
    factor = make_factor(total)
    factor_sq = factor * factor
    scaled_diag = (factor_sq * sum_diag).astype(jnp.bfloat16)
    scaled_next = (factor_sq * sum_next).astype(jnp.bfloat16)
    scaled_pair = (factor_sq * sum_pair).astype(jnp.bfloat16)
    all_diag, all_next, all_pair = (
        lax.all_gather(scaled_diag, "row", axis=0, tiled=True),
        lax.all_gather(scaled_next, "row", axis=0, tiled=True),
        lax.all_gather(scaled_pair, "row", axis=0, tiled=True),
    )
    block_rows = []
    for row_pos in range(4):
        block_rows.append(
            [
                pair_block(row_pos, col_pos, all_diag, all_next, all_pair, height)
                for col_pos in range(4)
            ]
        )
    full_gram = jnp.block(block_rows)
    row_panel = lax.dynamic_slice_in_dim(full_gram, grid_row * height, height, 0)
    col_panel = lax.dynamic_slice_in_dim(full_gram, grid_col * height, height, 1)
    corner = lax.dynamic_slice_in_dim(row_panel, grid_col * height, height, 1)
    square = jnp.dot(row_panel, col_panel, preferred_element_type=jnp.float32)
    poly_block = (COEF_CUBIC * corner.astype(jnp.float32) + COEF_QUINTIC * square).astype(
        jnp.bfloat16
    )
    piece = lax.all_gather(poly_block, "col", axis=1, tiled=True)
    matching = lax.slice_in_dim(panel, 0, piece.shape[1], axis=0)
    product = jnp.zeros((height, width), jnp.float32) + jnp.dot(
        piece, matching, preferred_element_type=jnp.float32
    )
    update = (
        math.sqrt(COLS) * factor * (COEF_LINEAR * rounded.astype(jnp.float32) + product)
    ).astype(jnp.bfloat16)
    return (new_momentum, update)


def solution(mesh):
    in_specs = (
        P(("layer", "row", "col"), None, None),
        P(("layer", "row", "col")),
        P(("layer", "row"), "col"),
    )
    out_specs = (P(("layer", "row"), "col"), P(("layer", "row"), "col"))
    return jax.shard_map(
        on_device, mesh=mesh, in_specs=in_specs, out_specs=out_specs, check_vma=False
    )
```

profile of v0, /device:TPU:1, one launch (start us, length us, event | category | flops | bytes accessed | tf_op | source)
XLA Modules:
  0.0 838.3 jit_solution(1370253498416310893)
XLA Ops:
  8.7 8.6 %all-to-all-start = ((s32[16,1,1]{2,1,0:T(1,128)}), s32[16,1,1]{2,1,0:T(1,128)S(1)}, u32[]{:S(2)}, u32[]{:S(2)}) async-start(s32[16,1,1]{2,1,0:T(1,128)} %copy.39), calls=%async_computation | async-start | bytes 16384 | tf_op jit(solution)/shard_map/all_to_all | solution.py:64
  17.4 5.4 gather_fusion
  22.8 5.2 select_select_fusion
  28.0 6.7 all-to-all-start.1
  35.4 67.9 %all-to-all-done.1 = bf16[16,128,1152]{2,1,0:T(8,128)(2,1)} async-done(((bf16[16,128,1152]{2,1,0:T(8,128)(2,1)}), bf16[16,128,1152]{2,1,0:T(8,128)(2,1)}, u32[]{:S(2)}, u32[]{:S(2)}) %all-to-all-start.1) | async-done | bytes 4718624 | tf_op jit(solution)/shard_map/all_to_all | solution.py:63
  103.3 5.5 gather_fusion.1
  108.8 10.2 %fusion.3 = f32[7,2,128,1152]{3,1,2,0:T(2,128)} fusion(pred[7,2]{1,0:T(8,128)(4,1)S(1)} %compare_and_fusion, bf16[7,2,128,1152]{3,2,1,0:T(8,128)(2,1)} %bitcast.33), kind=kLoop, calls=%fused_computation.12 | loop fusion | flops 4128768 | bytes 12386318 | tf_op jit(solution)/shard_map/convert_element_type | solution.py:74
  119.0 3.9 copy.49
  122.9 7.5 add_convert_fusion
  130.6 9.6 %fusion.24 = f32[896,896]{1,0:T(8,128)} fusion(bf16[896,2304]{1,0:T(8,128)(2,1)} %get-tuple-element.7), kind=kOutput, calls=%fused_computation.65 | convolution fusion | flops 3699376128 | bytes 7340032 | tf_op jit(solution)/shard_map/ik,jk->ij/dot_general | solution.py:89
  140.3 143.0 %all-gather.6.cloned.1.call-done = bf16[3584,2304]{1,0:T(8,128)(2,1)} async-done(((bf16[896,2304]{1,0:T(8,128)(2,1)}), bf16[3584,2304]{1,0:T(8,128)(2,1)}) %all-gather.6.cloned.1.call-update) | async-done | bytes 16515088 | tf_op jit(solution)/shard_map/all_gather | solution.py:78
  283.3 9.6 %fusion.6 = f32[896,896]{1,0:T(8,128)} fusion(bf16[896,2304]{1,0:T(8,128)(2,1)} %get-tuple-element.7, bf16[3584,2304]{1,0:T(8,128)(2,1)} %all-gather.6.cloned.1.call-done, s32[]{:T(128)S(6)} %select_n.149), kind=kOutput, calls=%fused_computation.15 | convolution fusion | flops 3699376128 | bytes 11468804 | tf_op jit(solution)/shard_map/ik,jk->ij/dot_general | solution.py:90
  292.9 6.3 fusion.4
  299.2 10.7 %multiply_reduce_fusion = f32[]{:T(128)} fusion(bf16[3584,2304]{1,0:T(8,128)(2,1)} %all-gather.6.cloned.1.call-done), kind=kLoop, calls=%fused_computation.2 | loop fusion | flops 24772608 | bytes 16515076 | tf_op jit(solution)/shard_map/reduce_sum | solution.py:92
  310.0 10.0 %psum.28 = f32[]{:T(128)} all-reduce(f32[]{:T(128)} %multiply_reduce_fusion), channel_id=1, replica_groups=mesh['layer'=8,'row'=4,'col'=4] {'col'}, use_global_device_ids=true, to_apply=%region_5.6 | all-reduce | flops 1 | bytes 8 | tf_op jit(solution)/shard_map/psum | solution.py:93
  320.7 135.0 %all-reduce.3.cloned.1.call-done = (f32[896,896]{1,0:T(8,128)}, f32[896,896]{1,0:T(8,128)}, f32[448,896]{1,0:T(8,128)}) async-done(((f32[896,896]{1,0:T(8,128)}, f32[896,896]{1,0:T(8,128)}, f32[448,896]{1,0:T(8,128)}), (f32[896,896]{1,0:T(8,128)}, f32[896,896]{1,0:T(8,128)}, f32[448,896]{1,0:T(8,128)})) %all-reduce.3.cloned.1.call-update) | async-done | bytes 8028176 | tf_op jit(solution)/shard_map/psum | solution.py:93
  455.6 2.4 multiply_convert_fusion.3
  458.1 3.5 multiply_convert_fusion.1
  463.2 35.2 %all-gather.12.cloned.1.call-done = bf16[1792,896]{1,0:T(8,128)(2,1)} async-done(((bf16[448,896]{1,0:T(8,128)(2,1)}), bf16[1792,896]{1,0:T(8,128)(2,1)}) %all-gather.12.cloned.1.call-update) | async-done | bytes 3211280 | tf_op jit(solution)/shard_map/all_gather | solution.py:104
  502.9 3.6 copy.46
  506.5 2.3 copy.43
  508.8 58.2 %all-gather.10.cloned.1.call-done = bf16[3584,896]{1,0:T(8,128)(2,1)} async-done(((bf16[896,896]{1,0:T(8,128)(2,1)}), bf16[3584,896]{1,0:T(8,128)(2,1)}) %all-gather.10.cloned.1.call-update) | async-done | bytes 6422544 | tf_op jit(solution)/shard_map/all_gather | solution.py:103
  567.0 5.7 fusion.22
  572.6 3.6 copy.47
  576.2 3.6 copy.44
  579.8 3.7 copy.42
  585.7 50.3 %all-gather.8.cloned.1.call-done = bf16[3584,896]{1,0:T(8,128)(2,1)} async-done(((bf16[896,896]{1,0:T(8,128)(2,1)}), bf16[3584,896]{1,0:T(8,128)(2,1)}) %all-gather.8.cloned.1.call-update) | async-done | bytes 6422544 | tf_op jit(solution)/shard_map/all_gather | solution.py:102
  636.1 6.0 fusion.21
  642.4 87.9 %maximum_maximum_fusion = bf16[3584,3584]{1,0:T(8,128)(2,1)} fusion(bf16[896,896]{1,0:T(8,128)(2,1)} %get-tuple-element.14, bf16[896,896]{1,0:T(8,128)(2,1)} %copy.47, bf16[896,896]{1,0:T(8,128)(2,1)} %copy.46, bf16[896,896]{1,0:T(8,128)(2,1)S(1)} %get-tuple-element.23, bf16[896,896]{1,0:T(8,128)(2,1)S(1)} %copy-done.5, ...), kind=kLoop, calls=%fused_computation.3 | loop fusion | flops 462422016 | bytes 51380224 | tf_op jit(solution)/shard_map/jit(block)/concatenate | solution.py:114
  730.3 12.0 %add_convert_fusion.1 = bf16[896,896]{1,0:T(8,128)(2,1)} fusion(bf16[3584,3584]{1,0:T(8,128)(2,1)} %maximum_maximum_fusion, s32[]{:T(128)S(6)} %select_n.155, s32[]{:T(128)S(6)} %select_n.157, s32[]{:T(128)S(6)} %select_n.156, s32[]{:T(128)S(6)} %select_n.154), kind=kOutput, calls=%fused_computation.17 | convolution fusion | flops 5758599168 | bytes 16056336 | tf_op jit(solution)/shard_map/dot_general | solution.py:118
  742.4 67.7 %all-gather.14.cloned.1.call-done = bf16[896,3584]{1,0:T(8,128)(2,1)} async-done(((bf16[896,896]{1,0:T(8,128)(2,1)}), bf16[896,3584]{1,0:T(8,128)(2,1)}) %all-gather.14.cloned.1.call-update) | async-done | bytes 6422544 | tf_op jit(solution)/shard_map/all_gather | solution.py:122
  810.0 21.4 %multiply_convert_fusion = bf16[896,2304]{1,0:T(8,128)(2,1)} fusion(bf16[896,2304]{1,0:T(8,128)(2,1)} %get-tuple-element.7, bf16[896,3584]{1,0:T(8,128)(2,1)} %all-gather.14.cloned.1.call-done, bf16[3584,2304]{1,0:T(8,128)(2,1)} %all-gather.6.cloned.1.call-done, f32[]{:T(128)S(6)} %mul_shard_map.7), kind=kOutput, calls=%fused_computation.4 | convolution fusion | flops 14807826432 | bytes 31195140 | tf_op jit(solution)/shard_map/dot_general | solution.py:124
  (48 shorter events, 11.2 us)
Async XLA Ops:
  8.7 19.3 %all-to-all-start = ((s32[16,1,1]{2,1,0:T(1,128)}), s32[16,1,1]{2,1,0:T(1,128)S(1)}, u32[]{:S(2)}, u32[]{:S(2)}) async-start(s32[16,1,1]{2,1,0:T(1,128)} %copy.39), calls=%async_computation | async-start | bytes 16384 | tf_op jit(solution)/shard_map/all_to_all | solution.py:64
  28.0 75.3 %all-to-all-start.1 = ((bf16[16,128,1152]{2,1,0:T(8,128)(2,1)}), bf16[16,128,1152]{2,1,0:T(8,128)(2,1)}, u32[]{:S(2)}, u32[]{:S(2)}) async-start(bf16[16,128,1152]{2,1,0:T(8,128)(2,1)} %select_select_fusion), calls=%async_computation.1 | async-start | bytes 9437184 | tf_op jit(solution)/shard_map/all_to_all | solution.py:63
  34.7 248.6 %all-gather.6.cloned.1.call-start = ((), (), s32[]{:S(2)}) async-start(), calls=%async_computation.2 | async-start | bytes 20643840 | tf_op jit(solution)/shard_map/all_gather | solution.py:78
  130.4 325.3 %all-reduce.3.cloned.1.call-start = ((), (), s32[]{:S(2)}) async-start(), calls=%async_computation.7 | async-start | bytes 16056320 | tf_op jit(solution)/shard_map/psum | solution.py:93
  299.2 199.2 %all-gather.12.cloned.1.call-start = ((), (), s32[]{:S(2)}) async-start(), calls=%async_computation.5 | async-start | bytes 4014080 | tf_op jit(solution)/shard_map/all_gather | solution.py:104
  458.1 3.6 copy-start.7
  458.1 108.9 %all-gather.10.cloned.1.call-start = ((), (), s32[]{:S(2)}) async-start(), calls=%async_computation.4 | async-start | bytes 8028160 | tf_op jit(solution)/shard_map/all_gather | solution.py:103
  461.6 174.4 %all-gather.8.cloned.1.call-start = ((), (), s32[]{:S(2)}) async-start(), calls=%async_computation.3 | async-start | bytes 8028160 | tf_op jit(solution)/shard_map/all_gather | solution.py:102
  463.1 346.9 %all-gather.14.cloned.1.call-start = ((), (), s32[]{:S(2)}) async-start(), calls=%async_computation.6 | async-start | bytes 8028160 | tf_op jit(solution)/shard_map/all_gather | solution.py:122
  500.5 0.9 copy-start
  500.6 2.3 copy-start.2
  636.0 6.0 copy-start.1
  636.1 6.0 copy-start.3
  636.1 6.0 copy-start.4
  636.1 6.0 copy-start.5
  636.1 6.4 copy-start.6
Sparse Core Ops, SparseCore 0:
  130.5 152.7 all-gather.5
  299.3 156.2 all-reduce.2
  458.2 40.1 all-gather.11
  499.9 66.9 all-gather.9
  568.5 67.5 all-gather.7
  742.5 67.4 all-gather.13
where the time goes:
time: 839 us; the launch traced here: 838 us
  waiting for transfers between devices  557 us (66%)
  other arithmetic  132 us (16%)
  matrix products  58.9 us (7%)
  local copies, waits for them, and re-layouts  49.6 us (6%)
  starting transfers between devices  15.7 us (2%)
  between operations  15 us (2%)
  blocking collectives  9.98 us (1%)
    all_gather x1, waiting for transfers between devices, on_device(): panel = lax.all_gather(rounded, 'row', axis=0, tiled=True)  143 us
    psum x1, waiting for transfers between devices, on_device(): lax.psum((term_diag, term_next, term_pair, panel_squares), 'col')  135 us
    concatenate x1, other arithmetic, on_device(): full_gram = jnp.block(block_rows)  87.9 us
    all_to_all x1, waiting for transfers between devices, on_device(): lax.all_to_all(outgoing, ('row', 'col'), split_axis=0, concat_axis=0, til...  67.9 us
    all_gather x1, waiting for transfers between devices, on_device(): piece = lax.all_gather(poly_block, 'col', axis=1, tiled=True)  67.7 us
    all_gather x1, waiting for transfers between devices, on_device(): lax.all_gather(scaled_next, 'row', axis=0, tiled=True)  58.2 us
    all_gather x1, waiting for transfers between devices, on_device(): lax.all_gather(scaled_diag, 'row', axis=0, tiled=True)  50.3 us
    all_gather x1, waiting for transfers between devices, on_device(): lax.all_gather(scaled_pair, 'row', axis=0, tiled=True)  35.2 us
  transfers between devices with their start and end apart: 8, of which 7 were waited for; matrix products, arithmetic and copies ran while one was open for 8% of the time, Pallas kernels for 0%

commit v1 on v0

v1 whole, which is shorter than its diff:
```python
import math

import jax
import jax.numpy as jnp
from jax import lax
from jax.experimental import pallas as pl
from jax.experimental.pallas import tpu as pltpu
from jax.sharding import Mesh
from jax.sharding import PartitionSpec as P

ROWS = 3584
COLS = 9216
MOMENTUM_RATE = 0.95
COEF_LINEAR = 3.4445
COEF_CUBIC = -4.775
COEF_QUINTIC = 2.0315
EPSILON = 1e-06

HEIGHT = 896
HALF = 1152
TILE = 128
SLOT = 1168
SIDE = 256
BLOCKS = ROWS // SIDE
HALF_BLOCKS = BLOCKS // 2
CHUNK = HALF_BLOCKS * SIDE
PARTS = ((0, 608), (608, 592), (1200, 592))
WIDE = 640
AROUND = ROWS + CHUNK
BACK_ROWS = 4032

AXES = ("x", "core", "zm", "zl", "y")
PLANE = ("zm", "zl", "y")
BF16 = jnp.bfloat16
F32 = jnp.float32
MIB = 1 << 20
ANY = pl.BlockSpec(memory_space=pl.ANY)
VMEM = pl.BlockSpec(memory_space=pltpu.VMEM)
SMEM = pl.BlockSpec(memory_space=pltpu.SMEM)


def cost(flops, size):
    return pl.CostEstimate(flops=int(flops), bytes_accessed=int(size), transcendentals=0)


def move(x, route):
    pairs = []
    for c in range(2):
        for m in range(2):
            for a in range(2):
                for y in range(4):
                    c2, m2, a2, y2 = route(c, m, a, y)
                    pairs.append((((c * 2 + m) * 2 + a) * 4 + y, ((c2 * 2 + m2) * 2 + a2) * 4 + y2 % 4))
    return lax.ppermute(x, AXES[1:], pairs)


def up(x):
    return move(x, lambda c, m, a, y: (c, m, a, y + 1))


def down(x):
    return move(x, lambda c, m, a, y: (c, m, a, y + 3))


def across(x):
    return move(x, lambda c, m, a, y: (c, m, 1 - a, y))


def swap(x):
    return move(x, lambda c, m, a, y: (1 - c, m, a, y))


def pack_kernel(details, tiles, out):
    @pl.loop(0, out.shape[0])
    def _(o):
        slot = details[o]
        for j in range(HALF // TILE):
            out[o, j * TILE : (j + 1) * TILE, :] = tiles[slot, :, j * TILE : (j + 1) * TILE]
        place = jnp.full((SLOT - HALF, TILE), details[16 + o], jnp.int32)
        out[o, HALF:, :] = place.astype(F32).astype(BF16)


def pack(details, tiles):
    n = details.shape[0] // 2
    return pl.pallas_call(
        pack_kernel,
        in_specs=[SMEM, VMEM],
        out_specs=VMEM,
        out_shape=jax.ShapeDtypeStruct((n, SLOT, TILE), BF16),
        compiler_params=pltpu.CompilerParams(vmem_limit_bytes=32 * MIB),
        cost_estimate=cost(0, 2 * n * SLOT * TILE * 2),
    )(details, tiles)


def momentum_kernel(info, tile, old, *refs):
    new, out = refs[-2:]
    for j in range(HALF // TILE):
        columns = slice(j * TILE, (j + 1) * TILE)
        g = tile[0, columns, :].astype(F32)
        fresh = MOMENTUM_RATE * old[:, columns] + g
        new[:, columns] = fresh
        out[:, columns] = (g + MOMENTUM_RATE * fresh).astype(BF16)


def update_momentum(info, arrived, momentum, turn, so_far):
    def half(s):
        return (turn + s[14]) % 2

    more = () if so_far is None else (so_far,)
    return pl.pallas_call(
        momentum_kernel,
        grid_spec=pltpu.PrefetchScalarGridSpec(
            num_scalar_prefetch=1,
            grid=(HEIGHT // TILE,),
            in_specs=[
                pl.BlockSpec((1, SLOT, TILE), lambda r, s: (s[2 * r + half(s)], 0, 0)),
                pl.BlockSpec((TILE, HALF), lambda r, s: (r, half(s))),
            ]
            + [ANY] * len(more),
            out_specs=[
                pl.BlockSpec((TILE, HALF), lambda r, s: (r, half(s))),
                pl.BlockSpec((TILE, HALF), lambda r, s: (r, 0)),
            ],
        ),
        out_shape=[
            jax.ShapeDtypeStruct(momentum.shape, F32),
            jax.ShapeDtypeStruct((HEIGHT, HALF), BF16),
        ],
        input_output_aliases={3: 0} if more else {},
        cost_estimate=cost(0, HEIGHT * HALF * 12),
    )(info, arrived, momentum, *more)


def panel_rows(info, which):
    c, a = info[0], info[2]
    other, t = divmod(which, 2)
    core = 1 - c if other else c
    return 2 * core + (a + t) % 2


def chip_at(info, flip, dy):
    a, y = info[2], info[3]
    return (1 - a if flip else a) * 4 + (y + dy) % 4


def load_all(copies, sems):
    copies = [pltpu.make_async_copy(src, dst, sems.at[i]) for i, (src, dst) in enumerate(copies)]
    for copy in copies:
        copy.start()
    for copy in copies:
        copy.wait()


def gram_kernel(dests, info, *refs):
    blocks, outs = refs[:4], refs[4:-2]
    panel, sems = refs[-2:]
    starts = [pl.multiple_of(panel_rows(info, i) * HEIGHT, HEIGHT) for i in range(4)]
    load_all([(blocks[i], panel.at[pl.ds(starts[i], HEIGHT)]) for i in range(4)], sems)

    def term(b, d):
        left = panel[pl.ds(pl.multiple_of(b * SIDE, SIDE), SIDE)]
        right = panel[pl.ds(pl.multiple_of((b + d) % BLOCKS * SIDE, SIDE), SIDE)]
        return lax.dot_general(left, right, (((1,), (1,)), ((), ())), preferred_element_type=F32)

    base = HALF_BLOCKS * info[0]
    if len(dests) == 1:
        d = chip_at(info, *dests[0])
        for b in range(HALF_BLOCKS):
            block = term(base + b, d).astype(BF16)
            for out, (row, size) in zip(outs, PARTS):
                low, high = max(row, b * SIDE), min(row + size, (b + 1) * SIDE)
                if low < high:
                    out[low - row : high - row] = block[low - b * SIDE : high - b * SIDE]
    else:

        @pl.loop(0, HALF_BLOCKS)
        def _(b):
            for dest, out in zip(dests, outs):
                block = term(base + b, chip_at(info, *dest))
                out[pl.ds(pl.multiple_of(b * SIDE, SIDE), SIDE)] = block.astype(out.dtype)


def gram_chunks(info, blocks, dests, shapes):
    return pl.pallas_call(
        lambda *refs: gram_kernel(dests, *refs),
        in_specs=[SMEM] + [ANY] * 4,
        out_specs=[VMEM] * len(shapes),
        out_shape=shapes,
        scratch_shapes=[pltpu.VMEM((ROWS, HALF), BF16), pltpu.SemaphoreType.DMA((4,))],
        compiler_params=pltpu.CompilerParams(vmem_limit_bytes=48 * MIB),
        cost_estimate=cost(len(dests) * 2 * CHUNK * SIDE * HALF, 8.3e6 + len(dests) * CHUNK * SIDE * 4),
    )(info, *blocks)


def chunk(dtype=BF16, rows=CHUNK):
    return jax.ShapeDtypeStruct((rows, SIDE), dtype)


def second_sums_kernel(p1, p2, p3, r1, r2, r3, q1, q2, q3):
    for own, got, out, (row, size) in zip((p1, p2, p3), (r1, r2, r3), (q1, q2, q3), PARTS):
        if row:
            out[:row] = own[:row].astype(BF16)
        out[row : row + size] = (own[row : row + size] + got[...].astype(F32)).astype(BF16)
        if row + size < CHUNK:
            out[row + size :] = own[row + size :].astype(BF16)


def third_sums_kernel(p1, p2, g1, g2, g3, v1, v2):
    v1[...] = (p1[...] + (g1[...].astype(F32) + g3[...].astype(F32))).astype(BF16)
    v2[...] = (p2[...] + g2[...].astype(F32)).astype(BF16)


def last_sums_kernel(p, v1, v2, v3, out):
    total = p[...] + (v1[...].astype(F32) + v2[...].astype(F32) + v3[...].astype(F32))
    out[...] = total.astype(BF16)


def in_vmem(kernel, shapes, *args):
    size = sum(x.size * x.dtype.itemsize for x in args)
    return pl.pallas_call(
        kernel,
        in_specs=[VMEM] * len(args),
        out_specs=[VMEM] * len(shapes),
        out_shape=shapes,
        compiler_params=pltpu.CompilerParams(vmem_limit_bytes=32 * MIB),
        cost_estimate=cost(0, size),
    )(*args)


def turn_kernel(info, *refs):
    blocks, out, held, sems = refs[:4], refs[4], refs[5], refs[6]
    shift = pl.multiple_of(512 * info[0], TILE)
    load_all([(blocks[i].at[:, pl.ds(shift, WIDE)], held.at[i]) for i in range(4)], sems)
    for i in range(4):
        start = pl.multiple_of(panel_rows(info, i) * HEIGHT, TILE)
        for r in range(HEIGHT // TILE):
            piece = held[i, r * TILE : (r + 1) * TILE, :].T
            out[:, pl.ds(pl.multiple_of(start + r * TILE, TILE), TILE)] = piece
    out[:, ROWS:] = out[:, :CHUNK]


def turned_panel(info, blocks):
    return pl.pallas_call(
        turn_kernel,
        in_specs=[SMEM] + [ANY] * 4,
        out_specs=VMEM,
        out_shape=jax.ShapeDtypeStruct((WIDE, AROUND), BF16),
        scratch_shapes=[pltpu.VMEM((4, HEIGHT, WIDE), BF16), pltpu.SemaphoreType.DMA((4,))],
        compiler_params=pltpu.CompilerParams(vmem_limit_bytes=32 * MIB),
        cost_estimate=cost(0, 1.2e7),
    )(info, *blocks)


SOURCES = ((0, 0), (0, 3), (0, 1), (1, 0), (1, 1), (1, 3), (0, 2), (1, 2))


def apply_kernel(info, *refs):
    own, ends, swapped = refs[:7], refs[7:10], refs[10:14]
    turned = refs[14]
    outs = refs[15:19]
    direct, flipped, panel, mixed, stage, sems, panel_sem, out_sems = refs[19:]
    c, a = info[0], info[2]
    panel_copy = pltpu.make_async_copy(turned, panel, panel_sem)
    panel_copy.start()
    pieces = [(c, ref, 0, rel) for ref, rel in zip(own, SOURCES)]
    pieces += [(1 - c, swapped[0], 0, SOURCES[0]), (1 - c, swapped[3], 0, SOURCES[7])]
    pieces += [(1 - c, swapped[1 + n // 3], n % 3 * CHUNK, SOURCES[1 + n]) for n in range(6)]
    for n, (core, ref, row, rel) in enumerate(pieces):
        d = chip_at(info, *rel)

        @pl.loop(0, HALF_BLOCKS)
        def _(b):
            i = (core * HALF_BLOCKS + b + d) % BLOCKS
            src = ref.at[pl.ds(pl.multiple_of(row + b * SIDE, SIDE), SIDE)]
            pltpu.make_async_copy(src, direct.at[i, pl.ds(pl.multiple_of((7 - d) * SIDE, SIDE), SIDE)], sems.at[n]).start()

    d = chip_at(info, *SOURCES[7])
    last = []
    for ref, (row, size) in zip(ends, PARTS):
        for b in range(HALF_BLOCKS):
            low, high = max(row, b * SIDE), min(row + size, (b + 1) * SIDE)
            if low < high:
                i = (c * HALF_BLOCKS + b + d) % BLOCKS
                start = pl.multiple_of((7 - d) * SIDE + low - b * SIDE, 16)
                src = ref.at[low - row : high - row]
                last.append(pltpu.make_async_copy(src, direct.at[i, pl.ds(start, high - low)], sems.at[15 + len(last)]))
    for copy in last:
        copy.start()
    for n in range(15):
        whole = direct.at[0:HALF_BLOCKS, 0:SIDE]
        pltpu.make_async_copy(whole, whole, sems.at[n]).wait()
    for copy in last:
        copy.wait()
    panel_copy.wait()

    total = jnp.zeros((), F32)
    on = lax.broadcasted_iota(jnp.int32, (SIDE, SIDE), 0) == lax.broadcasted_iota(jnp.int32, (SIDE, SIDE), 1)
    diagonal = jnp.zeros((SIDE, SIDE), F32)
    for i in range(BLOCKS):
        diagonal += direct[i, 7 * SIDE :, :].astype(F32)
    total = jnp.sum(jnp.where(on, diagonal, 0.0))
    total = jnp.full((1, SIDE), total, F32)
    factor = math.sqrt(ROWS) / (2.0 * (jnp.sqrt(total) + EPSILON))
    square = factor * factor

    def product(i, x):
        first = pl.ds(pl.multiple_of((i + 7) % BLOCKS * SIDE, SIDE), 8 * SIDE)
        rest = pl.ds(pl.multiple_of((i + 1) % BLOCKS * SIDE, SIDE), 6 * SIDE)
        result = jnp.dot(x[:, first], direct[i], preferred_element_type=F32)
        result += jnp.dot(x[:, rest], flipped[i], preferred_element_type=F32)
        return result * square

    @pl.loop(0, BLOCKS)
    def _(i):
        for e in range(1, 7):
            far = (i + e) % BLOCKS
            flipped[i, (e - 1) * SIDE : e * SIDE, :] = direct[far, (7 - e) * SIDE : (8 - e) * SIDE, :].T
        columns = pl.ds(pl.multiple_of(i * SIDE, SIDE), SIDE)
        mix = COEF_CUBIC * panel[:, columns].astype(F32) + COEF_QUINTIC * product(i, panel)
        mix = mix.astype(BF16)
        mixed[:, columns] = mix

        @pl.when(i < HALF_BLOCKS)
        def _():
            mixed[:, pl.ds(pl.multiple_of(i * SIDE + ROWS, SIDE), SIDE)] = mix

    scale = math.sqrt(COLS) * factor
    sends = []
    for turn in range(2):
        half = 1 - c if turn else c

        @pl.loop(0, HALF_BLOCKS)
        def _(b):
            i = half * HALF_BLOCKS + b
            columns = pl.ds(pl.multiple_of(i * SIDE, SIDE), SIDE)
            result = scale * (COEF_LINEAR * panel[:, columns].astype(F32) + product(i, mixed))
            stage[turn, pl.ds(pl.multiple_of(b * SIDE, SIDE), SIDE)] = result.astype(BF16).T

        for side in range(2):
            out = outs[2 * turn + side]
            owner = 1 - a if side else a
            start = pl.multiple_of(owner * HEIGHT, 128)
            for j in range(4):
                columns = pl.ds(pl.multiple_of((j + c) * TILE, TILE), TILE)
                sends.append((stage.at[turn, pl.ds(start, HEIGHT), columns], out.at[pl.ds(j * HEIGHT, HEIGHT)]))
            columns = pl.ds(pl.multiple_of(4 * (1 - c) * TILE, TILE), TILE)
            shared = pl.ds(pl.multiple_of(start + 448 * c, 64), 448)
            sends.append((stage.at[turn, shared, columns], out.at[pl.ds(4 * HEIGHT, 448)]))
            for k in range(len(sends) - 5, len(sends)):
                sends[k] = pltpu.make_async_copy(*sends[k], out_sems.at[k])
                sends[k].start()
    for copy in sends:
        copy.wait()


def apply_poly(info, own, ends, swapped, turned):
    return pl.pallas_call(
        apply_kernel,
        in_specs=[SMEM] + [ANY] * 15,
        out_specs=[ANY] * 4,
        out_shape=[jax.ShapeDtypeStruct((BACK_ROWS, TILE), BF16)] * 4,
        scratch_shapes=[
            pltpu.VMEM((BLOCKS, 8 * SIDE, SIDE), BF16),
            pltpu.VMEM((BLOCKS, 6 * SIDE, SIDE), BF16),
            pltpu.VMEM((WIDE, AROUND), BF16),
            pltpu.VMEM((WIDE, AROUND), BF16),
            pltpu.VMEM((2, CHUNK, WIDE), BF16),
            pltpu.SemaphoreType.DMA((32,)),
            pltpu.SemaphoreType.DMA,
            pltpu.SemaphoreType.DMA((20,)),
        ],
        compiler_params=pltpu.CompilerParams(vmem_limit_bytes=58 * MIB),
        cost_estimate=cost(4 * ROWS * ROWS * WIDE, 3e7),
    )(info, *own, *ends, *swapped, turned)


def unpack_kernel(info, r0, r1, r2, r3, update):
    m, a = info[1], info[2]
    for s, got in enumerate((r0, r1, r2, r3)):
        core = 1 - m if s >= 2 else m
        side = 1 - a if s % 2 else a
        for j in range(4):
            start = pl.multiple_of((9 * side + j + 5 * core) * TILE, TILE)
            update[:, pl.ds(start, TILE)] = got[j * HEIGHT : (j + 1) * HEIGHT]
        start = pl.multiple_of((9 * side + 4) * TILE, TILE)
        rows = pl.ds(pl.multiple_of(448 * core, 64), 448)
        update[rows, pl.ds(start, TILE)] = got[4 * HEIGHT :]


def unpack(info, parts):
    return pl.pallas_call(
        unpack_kernel,
        in_specs=[SMEM] + [VMEM] * 4,
        out_specs=VMEM,
        out_shape=jax.ShapeDtypeStruct((HEIGHT, 2304), BF16),
        compiler_params=pltpu.CompilerParams(vmem_limit_bytes=32 * MIB),
        cost_estimate=cost(0, 8.3e6),
    )(info, *parts)


def on_device(grad_tiles, tile_ids, momentum):
    core, zm, zl, y = (lax.axis_index(name) for name in AXES[1:])
    info = jnp.stack([core, zm, zl, y]).astype(jnp.int32)
    tile_count = grad_tiles.shape[0]

    owners = tile_ids // 8 // 7 * 4 + tile_ids % 8 // 2
    places = tile_ids // 8 % 7 * 2 + tile_ids % 2
    matches = owners[:, None] == jnp.arange(16, dtype=jnp.int32)[None, :]
    slots = jnp.sum(jnp.where(matches, jnp.arange(tile_count, dtype=jnp.int32)[:, None], 0), axis=0)
    labels = jnp.sum(jnp.where(matches, places[:, None] + 1, 0), axis=0) - 1
    packed = pack(jnp.concatenate([slots, labels]), grad_tiles)
    arrived = lax.all_to_all(packed, PLANE, split_axis=0, concat_axis=0, tiled=True)

    got_labels = arrived[:, HALF, 0].astype(jnp.int32)
    found = got_labels[None, :] == jnp.arange(tile_count, dtype=jnp.int32)[:, None]
    sources = jnp.sum(jnp.where(found, jnp.arange(16, dtype=jnp.int32)[None, :], 0), axis=1)
    details = jnp.concatenate([sources, zl[None].astype(jnp.int32)])
    new_momentum, half0 = update_momentum(details, arrived, momentum, 0, None)
    new_momentum, half1 = update_momentum(details, arrived, momentum, 1, new_momentum)

    got0 = move(half0, lambda c, m, a, y: (m, c, a, y))
    got1 = move(half1, lambda c, m, a, y: (m, c, 1 - a, y))
    blocks = (got0, got1, swap(got0), swap(got1))

    far = gram_chunks(info, blocks, ((1, 2),), [chunk(BF16, size) for _, size in PARTS])
    far0, far1, far2 = up(far[0]), down(far[1]), across(far[2])
    terms = gram_chunks(info, blocks, ((1, 1), (1, 3), (0, 2)), [chunk(F32)] * 3)
    q1, q2, q3 = in_vmem(second_sums_kernel, [chunk()] * 3, *terms, far0, far1, far2)
    g1, g2, g3 = across(q1), down(q2), up(q3)
    later, _ = lax.optimization_barrier((blocks, q1))
    nearest, beside, below, center = gram_chunks(
        info, later, ((0, 1), (1, 0), (0, 3), (0, 0)), [chunk(F32), chunk(F32), chunk(), chunk(F32)]
    )
    near = down(below)
    v1, v2 = in_vmem(third_sums_kernel, [chunk()] * 2, nearest, beside, g1, g2, g3)
    w1, w2 = up(v1), across(v2)
    later, _ = lax.optimization_barrier((blocks, v1))
    turned = turned_panel(info, later)
    (mine,) = in_vmem(last_sums_kernel, [chunk()], center, w1, w2, near)

    low, high, pair = up(mine), down(mine), across(mine)
    a1, a2, a3 = across(high), up(pair), down(high)
    ends = tuple(
        send(x[row : row + size]) for send, x, (row, size) in zip((down, up, across), (a1, a2, a3), PARTS)
    )
    swapped = (
        swap(mine),
        swap(jnp.concatenate([low, high, pair])),
        swap(jnp.concatenate([a1, a2, a3])),
        swap(jnp.concatenate(ends)),
    )
    sent = apply_poly(info, (mine, low, high, pair, a1, a2, a3), ends, swapped, turned)

    parts = (
        move(sent[0], lambda c, m, a, y: (m, c, a, y)),
        move(sent[1], lambda c, m, a, y: (m, c, 1 - a, y)),
        move(sent[2], lambda c, m, a, y: (m, 1 - c, a, y)),
        move(sent[3], lambda c, m, a, y: (m, 1 - c, 1 - a, y)),
    )
    return new_momentum, unpack(info, parts)


def solution(mesh):
    fine = Mesh(mesh.devices.reshape(4, 2, 2, 2, 4), AXES)
    tall = P(("x", "core", "zm", "zl"), "y")
    return jax.shard_map(
        on_device,
        mesh=fine,
        in_specs=(P(AXES, None, None), P(AXES), tall),
        out_specs=(tall, tall),
        check_vma=False,
    )
```

time: 839 us -> 398 us (0.47)
  waiting for transfers between devices: 557 us -> 230 us
  other arithmetic: 132 us -> 3.94 us
  Pallas kernels: 0 us -> 103 us
  matrix products: 58.9 us -> 0 us
  local copies, waits for them, and re-layouts: 49.6 us -> 10.1 us
  starting transfers between devices: 15.7 us -> 49 us
  between operations: 15 us -> 0.98 us
  blocking collectives: 9.98 us -> 0 us
    all_gather x5 -> x0, waiting for transfers between devices: 354 us -> none  [the longest x1 143 us: on_device(): panel = lax.all_gather(rounded, 'row', axis=0, tiled=True)]
    ppermute x0 -> x30, waiting for transfers between devices: none -> 159 us  [move(): return lax.ppermute(x, AXES[1:], pairs)]
    psum x1 -> x0, waiting for transfers between devices: 135 us -> none  [on_device(): lax.psum((term_diag, term_next, term_pair, panel_squares), 'col')]
    pallas_call x0 -> x12, Pallas kernels: none -> 103 us  [the longest x1 49.7 us: apply_poly(): pl.pallas_call(apply_kernel, in_specs=[SMEM] + [ANY] * 15, out_specs=[ANY...]
    concatenate x1 -> x5, other arithmetic: 87.9 us -> 1.16 us  [the longest x1 0.66 us: on_device(): details = jnp.concatenate([sources, zl[None].astype(jnp.int32)])]
    dot_general x5 -> x0, matrix products: 58.9 us -> none  [the longest x1 21.4 us: on_device(): jnp.dot(piece, matching, preferred_element_type=jnp.float32)]
    ppermute x0 -> x30, starting transfers between devices: none -> 40.3 us  [move(): return lax.ppermute(x, AXES[1:], pairs)]
    convert_element_type x5 -> x1, other arithmetic: 24.9 us -> 1.13 us  [on_device(): got_labels = arrived[:, HALF, 0].astype(jnp.int32)]
  transfers between devices with their start and end apart: 8 -> 31, of which waited for: 7 -> 16; matrix products, arithmetic and copies ran while one was open for 8% -> 0% of each run, Pallas kernels for 0% -> 6%
where the time goes in v1:
time: 398 us; the launch traced here: 396 us
  waiting for transfers between devices  230 us (58%)
  Pallas kernels  103 us (26%)
  starting transfers between devices  49 us (12%)
  local copies, waits for them, and re-layouts  10.1 us (3%)
    ppermute x30, waiting for transfers between devices, move(): return lax.ppermute(x, AXES[1:], pairs)  159 us
    all_to_all x1, waiting for transfers between devices, on_device(): lax.all_to_all(packed, PLANE, split_axis=0, concat_axis=0, tiled=True)  70.8 us
    pallas_call x1, Pallas kernels, apply_poly(): pl.pallas_call(apply_kernel, in_specs=[SMEM] + [ANY] * 15, out_specs=[ANY...  49.7 us
    ppermute x30, starting transfers between devices, move(): return lax.ppermute(x, AXES[1:], pairs)  40.3 us
    pallas_call x3, Pallas kernels, gram_chunks(): pl.pallas_call(lambda *refs: gram_kernel(dests, *refs), in_specs=[SMEM] +...  25.5 us
    pallas_call x2, Pallas kernels, update_momentum(): pl.pallas_call(momentum_kernel, grid_spec=pltpu.PrefetchScalarGridSpec(nu...  17.5 us
    unnamed x42, local copies, waits for them, and re-layouts  10.1 us
    all_to_all x1, starting transfers between devices, on_device(): lax.all_to_all(packed, PLANE, split_axis=0, concat_axis=0, tiled=True)  8.64 us
  transfers between devices with their start and end apart: 31, of which 16 were waited for; matrix products, arithmetic and copies ran while one was open for 0% of the time, Pallas kernels for 6%

profile of v1, /device:TPU:1, one launch (start us, length us, event | category | flops | bytes accessed | tf_op | source)
XLA Modules:
  0.0 396.1 jit_solution(3900620905301306404)
XLA Ops:
  2.2 2.2 copy-done.4
  5.8 2.2 copy-done
  8.0 8.6 %all-to-all-start = ((bf16[16,1168,128]{2,1,0:T(8,128)(2,1)}), bf16[16,1168,128]{2,1,0:T(8,128)(2,1)}, u32[]{:S(2)}, u32[]{:S(2)}) async-start(bf16[16,1168,128]{2,1,0:T(8,128)(2,1)} %copy-done), calls=%async_computation | async-start | bytes 9568256 | tf_op jit(solution)/shard_map/all_to_all | solution.py:412
  16.7 70.8 %all-to-all-done.tile = bf16[16,1168,128]{2,1,0:T(8,128)(2,1)} async-done(((bf16[16,1168,128]{2,1,0:T(8,128)(2,1)}), bf16[16,1168,128]{2,1,0:T(8,128)(2,1)}, u32[]{:S(2)}, u32[]{:S(2)}) %all-to-all-start) | async-done | bytes 4784160 | tf_op jit(solution)/shard_map/all_to_all | solution.py:412
  89.4 8.7 %shard_map.51 = (f32[896,2304]{1,0:T(8,128)}, bf16[896,1152]{1,0:T(8,128)(2,1)}) custom-call(s32[15]{0:T(128)} %pad_add_fusion.1.info, bf16[16,1168,128]{2,1,0:T(8,128)(2,1)} %all-to-all-done.tile, f32[896,2304]{1,0:T(8,128)} %old.3), custom_call_target="tpu_custom_call" | custom-call | bytes 12386304 | tf_op jit(solution)/shard_map/pallas_call | solution.py:110
  98.1 8.7 %shard_map.52 = (f32[896,2304]{1,0:T(8,128)}, bf16[896,1152]{1,0:T(8,128)(2,1)}) custom-call(s32[15]{0:T(128)} %pad_add_fusion.1.info, bf16[16,1168,128]{2,1,0:T(8,128)(2,1)} %all-to-all-done.tile, f32[896,2304]{1,0:T(8,128)} %old.3, f32[896,2304]{1,0:T(8,128)} %get-tuple-element.33.refs_0_), custom_call_target="tpu_custom_call", output_to_operand_aliasing={{0}: (3, {})} | custom-call | bytes 12386304 | tf_op jit(solution)/shard_map/pallas_call | solution.py:110
  106.8 3.5 collective-permute-start.1
  110.3 1.9 collective-permute-start
  112.2 43.8 %collective-permute-done.1.refs_2_.refs_1_ = bf16[896,1152]{1,0:T(8,128)(2,1)S(1)} collective-permute-done((bf16[896,1152]{1,0:T(8,128)(2,1)}, bf16[896,1152]{1,0:T(8,128)(2,1)S(1)}, u32[]{:S(2)}, u32[]{:S(2)}) %collective-permute-start.1) | collective-permute-done | bytes 2064416 | tf_op jit(solution)/shard_map/ppermute | solution.py:54
  156.6 5.7 %collective-permute-done.3.refs_4_.refs_3_ = bf16[896,1152]{1,0:T(8,128)(2,1)} collective-permute-done((bf16[896,1152]{1,0:T(8,128)(2,1)S(1)}, bf16[896,1152]{1,0:T(8,128)(2,1)}, u32[]{:S(2)}, u32[]{:S(2)}) %collective-permute-start.3) | collective-permute-done | bytes 2064416 | tf_op jit(solution)/shard_map/ppermute | solution.py:54
  163.4 4.9 %shard_map.54 = (bf16[608,256]{1,0:T(8,128)(2,1)S(1)}, bf16[592,256]{1,0:T(8,128)(2,1)S(1)}, bf16[592,256]{1,0:T(8,128)(2,1)S(1)}) custom-call(s32[4]{0:T(128)S(1)} %pad_add_fusion.2.refs_0_.info, bf16[896,1152]{1,0:T(8,128)(2,1)} %collective-permute-done.refs_1_.refs_0_, bf16[896,1152]{1,0:T(8,128)(2,1)S(1)} %collective-permute-done.1.refs_2_.refs_1_, ...), custom_call_target="tpu_custom_call" | custom-call | flops 1056964608 | bytes 10135008 | tf_op jit(solution)/shard_map/pallas_call | solution.py:184
  168.4 2.7 collective-permute-start.5
  171.1 9.1 %shard_map.53 = (f32[1792,256]{1,0:T(8,128)S(1)}, f32[1792,256]{1,0:T(8,128)S(1)}, f32[1792,256]{1,0:T(8,128)S(1)}) custom-call(s32[4]{0:T(128)S(1)} %pad_add_fusion.2.refs_0_.info, bf16[896,1152]{1,0:T(8,128)(2,1)} %collective-permute-done.refs_1_.refs_0_, bf16[896,1152]{1,0:T(8,128)(2,1)} %copy-done.1, ...), custom_call_target="tpu_custom_call" | custom-call | flops 3170893824 | bytes 13805024 | tf_op jit(solution)/shard_map/pallas_call | solution.py:184
  183.6 11.5 %shard_map.56 = (f32[1792,256]{1,0:T(8,128)S(1)}, f32[1792,256]{1,0:T(8,128)S(1)}, bf16[1792,256]{1,0:T(8,128)(2,1)S(1)}, f32[1792,256]{1,0:T(8,128)}) custom-call(s32[4]{0:T(128)S(1)} %pad_add_fusion.2.refs_0_.info, bf16[896,1152]{1,0:T(8,128)(2,1)} %collective-permute-done.refs_1_.refs_0_, bf16[896,1152]{1,0:T(8,128)(2,1)} %copy-done.1, ...), custom_call_target="tpu_custom_call" | custom-call | flops 4227858432 | bytes 15640032 | tf_op jit(solution)/shard_map/pallas_call | solution.py:184
  196.4 5.4 %collective-permute-done.8.g2 = bf16[1792,256]{1,0:T(8,128)(2,1)S(1)} collective-permute-done((bf16[1792,256]{1,0:T(8,128)(2,1)S(1)}, bf16[1792,256]{1,0:T(8,128)(2,1)S(1)}, u32[]{:S(2)}, u32[]{:S(2)}) %collective-permute-start.8) | collective-permute-done | bytes 917536 | tf_op jit(solution)/shard_map/ppermute | solution.py:54
  204.8 16.7 %collective-permute-done.12.v3 = bf16[1792,256]{1,0:T(8,128)(2,1)S(1)} collective-permute-done((bf16[1792,256]{1,0:T(8,128)(2,1)S(1)}, bf16[1792,256]{1,0:T(8,128)(2,1)S(1)}, u32[]{:S(2)}, u32[]{:S(2)}) %collective-permute-start.12) | collective-permute-done | bytes 917536 | tf_op jit(solution)/shard_map/ppermute | solution.py:54
  222.9 2.5 collective-permute-done.10.v1
  227.5 17.0 %collective-permute-done.15.refs_3_ = bf16[1792,256]{1,0:T(8,128)(2,1)S(1)} collective-permute-done((bf16[1792,256]{1,0:T(8,128)(2,1)S(1)}, bf16[1792,256]{1,0:T(8,128)(2,1)S(1)}, u32[]{:S(2)}, u32[]{:S(2)}) %collective-permute-start.15) | collective-permute-done | bytes 917536 | tf_op jit(solution)/shard_map/ppermute | solution.py:54
  244.5 2.7 collective-permute-start.18
  248.2 5.1 %collective-permute-start.23 = (bf16[5376,256]{1,0:T(8,128)(2,1)S(1)}, bf16[5376,256]{1,0:T(8,128)(2,1)S(1)}, u32[]{:S(2)}, u32[]{:S(2)}) collective-permute-start(bf16[5376,256]{1,0:T(8,128)(2,1)S(1)} %pad_maximum_fusion), channel_id=1, source_target_pairs={{0,16},{1,17},{2,18},{3,19},{4,20},{5,21},{6,22},{7,23},{8,24},{9,... | collective-permute-start | bytes 8257544 | tf_op jit(solution)/shard_map/ppermute | solution.py:54
  253.3 12.7 %collective-permute-done.17.refs_5_ = bf16[1792,256]{1,0:T(8,128)(2,1)S(1)} collective-permute-done((bf16[1792,256]{1,0:T(8,128)(2,1)S(1)}, bf16[1792,256]{1,0:T(8,128)(2,1)S(1)}, u32[]{:S(2)}, u32[]{:S(2)}) %collective-permute-start.17) | collective-permute-done | bytes 917536 | tf_op jit(solution)/shard_map/ppermute | solution.py:54
  266.2 4.0 %collective-permute-start.24 = (bf16[5376,256]{1,0:T(8,128)(2,1)S(1)}, bf16[5376,256]{1,0:T(8,128)(2,1)}, u32[]{:S(2)}, u32[]{:S(2)}) collective-permute-start(bf16[5376,256]{1,0:T(8,128)(2,1)S(1)} %pad_maximum_fusion.1), channel_id=1, source_target_pairs={{0,16},{1,17},{2,18},{3,19},{4,20},{5,21},{6,22},{7,23},{8,24},{9,... | collective-permute-start | bytes 8257544 | tf_op jit(solution)/shard_map/ppermute | solution.py:54
  273.3 7.4 %collective-permute-done.20.refs_8_ = bf16[592,256]{1,0:T(8,128)(2,1)S(1)} collective-permute-done((bf16[592,256]{1,0:T(8,128)(2,1)S(1)}, bf16[592,256]{1,0:T(8,128)(2,1)S(1)}, u32[]{:S(2)}, u32[]{:S(2)}) %collective-permute-start.20) | collective-permute-done | bytes 303136 | tf_op jit(solution)/shard_map/ppermute | solution.py:54
  280.7 1.9 collective-permute-start.22
  282.8 3.9 shard_map.59.refs_14_
  286.8 2.8 copy-done.3
  291.7 49.7 %shard_map.60 = (bf16[4032,128]{1,0:T(8,128)(2,1)}, bf16[4032,128]{1,0:T(8,128)(2,1)}, bf16[4032,128]{1,0:T(8,128)(2,1)}, bf16[4032,128]{1,0:T(8,128)(2,1)}) custom-call(s32[4]{0:T(128)} %copy-done.7, bf16[1792,256]{1,0:T(8,128)(2,1)} %copy-done.6, bf16[1792,256]{1,0:T(8,128)(2,1)} %copy-done.14, bf16[1792,256]{1,0:T(8,128)(2,1)} %copy-done.13, ...), custom_call_target="tpu_custom_call" | custom-call | flops 32883343360 | bytes 30000000 | tf_op jit(solution)/shard_map/pallas_call | solution.py:357
  341.4 3.3 collective-permute-start.26
  346.4 2.3 collective-permute-start.29
  348.6 21.7 %collective-permute-done.26.r0 = bf16[4032,128]{1,0:T(8,128)(2,1)S(1)} collective-permute-done((bf16[4032,128]{1,0:T(8,128)(2,1)}, bf16[4032,128]{1,0:T(8,128)(2,1)S(1)}, u32[]{:S(2)}, u32[]{:S(2)}) %collective-permute-start.26) | collective-permute-done | bytes 1032224 | tf_op jit(solution)/shard_map/ppermute | solution.py:54
  370.3 22.1 %collective-permute-done.27.r1 = bf16[4032,128]{1,0:T(8,128)(2,1)S(1)} collective-permute-done((bf16[4032,128]{1,0:T(8,128)(2,1)}, bf16[4032,128]{1,0:T(8,128)(2,1)S(1)}, u32[]{:S(2)}, u32[]{:S(2)}) %collective-permute-start.27) | collective-permute-done | bytes 1032224 | tf_op jit(solution)/shard_map/ppermute | solution.py:54
  392.9 3.2 shard_map.61
  (99 shorter events, 26.6 us)
Async XLA Ops:
  8.0 79.4 %all-to-all-start = ((bf16[16,1168,128]{2,1,0:T(8,128)(2,1)}), bf16[16,1168,128]{2,1,0:T(8,128)(2,1)}, u32[]{:S(2)}, u32[]{:S(2)}) async-start(bf16[16,1168,128]{2,1,0:T(8,128)(2,1)} %copy-done), calls=%async_computation | async-start | bytes 9568256 | tf_op jit(solution)/shard_map/all_to_all | solution.py:412
  106.8 49.2 %collective-permute-start.1 = (bf16[896,1152]{1,0:T(8,128)(2,1)}, bf16[896,1152]{1,0:T(8,128)(2,1)S(1)}, u32[]{:S(2)}, u32[]{:S(2)}) collective-permute-start(bf16[896,1152]{1,0:T(8,128)(2,1)} %get-tuple-element.36), channel_id=1, source_target_pairs={{0,4},{1,5},{2,6},{3,7},{4,0},{5,1},{6,2},{7,3},{8,20},{9,21},{10,... | collective-permute-start | bytes 6193160 | tf_op jit(solution)/shard_map/ppermute | solution.py:54
  110.3 45.7 %collective-permute-start = (bf16[896,1152]{1,0:T(8,128)(2,1)}, bf16[896,1152]{1,0:T(8,128)(2,1)}, u32[]{:S(2)}, u32[]{:S(2)}) collective-permute-start(bf16[896,1152]{1,0:T(8,128)(2,1)} %get-tuple-element.35), channel_id=1, source_target_pairs={{0,0},{1,1},{2,2},{3,3},{4,4},{5,5},{6,6},{7,7},{8,16},{9,17},{10,... | collective-permute-start | bytes 6193160 | tf_op jit(solution)/shard_map/ppermute | solution.py:54
  156.0 6.3 %collective-permute-start.3 = (bf16[896,1152]{1,0:T(8,128)(2,1)S(1)}, bf16[896,1152]{1,0:T(8,128)(2,1)}, u32[]{:S(2)}, u32[]{:S(2)}) collective-permute-start(bf16[896,1152]{1,0:T(8,128)(2,1)S(1)} %collective-permute-done.1.refs_2_.refs_1_), channel_id=1, source_target_pairs={{0,16},{1,17},{2,18},{3,19},{4,20},{5,21},{6,22},{7,23},{8,24},{9,... | collective-permute-start | bytes 6193160 | tf_op jit(solution)/shard_map/ppermute | solution.py:54
  156.0 7.4 %collective-permute-start.2 = (bf16[896,1152]{1,0:T(8,128)(2,1)}, bf16[896,1152]{1,0:T(8,128)(2,1)}, u32[]{:S(2)}, u32[]{:S(2)}) collective-permute-start(bf16[896,1152]{1,0:T(8,128)(2,1)} %collective-permute-done.refs_1_.refs_0_), channel_id=1, source_target_pairs={{0,16},{1,17},{2,18},{3,19},{4,20},{5,21},{6,22},{7,23},{8,24},{9,... | collective-permute-start | bytes 6193160 | tf_op jit(solution)/shard_map/ppermute | solution.py:54
  156.6 126.2 %copy-start.7 = (s32[4]{0:T(128)}, s32[4]{0:T(128)S(1)}, u32[]{:S(2)}) copy-start(s32[4]{0:T(128)S(1)} %pad_add_fusion.2.refs_0_.info) | copy-start | bytes 52
  168.4 11.9 %collective-permute-start.4 = (bf16[608,256]{1,0:T(8,128)(2,1)S(1)}, bf16[608,256]{1,0:T(8,128)(2,1)S(1)}, u32[]{:S(2)}, u32[]{:S(2)}) collective-permute-start(bf16[608,256]{1,0:T(8,128)(2,1)S(1)} %get-tuple-element.40), channel_id=1, source_target_pairs={{0,1},{1,2},{2,3},{3,0},{4,5},{5,6},{6,7},{7,4},{8,9},{9,10},{10,1... | collective-permute-start | bytes 933896 | tf_op jit(solution)/shard_map/ppermute | solution.py:54
  168.4 11.8 %collective-permute-start.5 = (bf16[592,256]{1,0:T(8,128)(2,1)S(1)}, bf16[592,256]{1,0:T(8,128)(2,1)S(1)}, u32[]{:S(2)}, u32[]{:S(2)}) collective-permute-start(bf16[592,256]{1,0:T(8,128)(2,1)S(1)} %get-tuple-element.41), channel_id=1, source_target_pairs={{0,3},{1,0},{2,1},{3,2},{4,7},{5,4},{6,5},{7,6},{8,11},{9,8},{10,9... | collective-permute-start | bytes 909320 | tf_op jit(solution)/shard_map/ppermute | solution.py:54
  171.1 9.1 %collective-permute-start.6 = (bf16[592,256]{1,0:T(8,128)(2,1)S(1)}, bf16[592,256]{1,0:T(8,128)(2,1)S(1)}, u32[]{:S(2)}, u32[]{:S(2)}) collective-permute-start(bf16[592,256]{1,0:T(8,128)(2,1)S(1)} %get-tuple-element.42), channel_id=1, source_target_pairs={{0,4},{1,5},{2,6},{3,7},{4,0},{5,1},{6,2},{7,3},{8,12},{9,13},{10,... | collective-permute-start | bytes 909320 | tf_op jit(solution)/shard_map/ppermute | solution.py:54
  180.6 21.2 %collective-permute-start.8 = (bf16[1792,256]{1,0:T(8,128)(2,1)S(1)}, bf16[1792,256]{1,0:T(8,128)(2,1)S(1)}, u32[]{:S(2)}, u32[]{:S(2)}) collective-permute-start(bf16[1792,256]{1,0:T(8,128)(2,1)S(1)} %get-tuple-element.51), channel_id=1, source_target_pairs={{0,3},{1,0},{2,1},{3,2},{4,7},{5,4},{6,5},{7,6},{8,11},{9,8},{10,9... | collective-permute-start | bytes 2752520 | tf_op jit(solution)/shard_map/ppermute | solution.py:54
  181.1 21.5 %collective-permute-start.9 = (bf16[1792,256]{1,0:T(8,128)(2,1)S(1)}, bf16[1792,256]{1,0:T(8,128)(2,1)S(1)}, u32[]{:S(2)}, u32[]{:S(2)}) collective-permute-start(bf16[1792,256]{1,0:T(8,128)(2,1)S(1)} %get-tuple-element.52), channel_id=1, source_target_pairs={{0,1},{1,2},{2,3},{3,0},{4,5},{5,6},{6,7},{7,4},{8,9},{9,10},{10,1... | collective-permute-start | bytes 2752520 | tf_op jit(solution)/shard_map/ppermute | solution.py:54
  182.1 20.6 %collective-permute-start.7 = (bf16[1792,256]{1,0:T(8,128)(2,1)S(1)}, bf16[1792,256]{1,0:T(8,128)(2,1)S(1)}, u32[]{:S(2)}, u32[]{:S(2)}) collective-permute-start(bf16[1792,256]{1,0:T(8,128)(2,1)S(1)} %get-tuple-element.43), channel_id=1, source_target_pairs={{0,4},{1,5},{2,6},{3,7},{4,0},{5,1},{6,2},{7,3},{8,12},{9,13},{10,... | collective-permute-start | bytes 2752520 | tf_op jit(solution)/shard_map/ppermute | solution.py:54
  195.1 26.4 %collective-permute-start.12 = (bf16[1792,256]{1,0:T(8,128)(2,1)S(1)}, bf16[1792,256]{1,0:T(8,128)(2,1)S(1)}, u32[]{:S(2)}, u32[]{:S(2)}) collective-permute-start(bf16[1792,256]{1,0:T(8,128)(2,1)S(1)} %get-tuple-element.55), channel_id=1, source_target_pairs={{0,3},{1,0},{2,1},{3,2},{4,7},{5,4},{6,5},{7,6},{8,11},{9,8},{10,9... | collective-permute-start | bytes 2752520 | tf_op jit(solution)/shard_map/ppermute | solution.py:54
  203.1 19.8 %collective-permute-start.11 = (bf16[1792,256]{1,0:T(8,128)(2,1)S(1)}, bf16[1792,256]{1,0:T(8,128)(2,1)S(1)}, u32[]{:S(2)}, u32[]{:S(2)}) collective-permute-start(bf16[1792,256]{1,0:T(8,128)(2,1)S(1)} %get-tuple-element.54), channel_id=1, source_target_pairs={{0,4},{1,5},{2,6},{3,7},{4,0},{5,1},{6,2},{7,3},{8,12},{9,13},{10,... | collective-permute-start | bytes 2752520 | tf_op jit(solution)/shard_map/ppermute | solution.py:54
  204.8 20.6 %collective-permute-start.10 = (bf16[1792,256]{1,0:T(8,128)(2,1)S(1)}, bf16[1792,256]{1,0:T(8,128)(2,1)S(1)}, u32[]{:S(2)}, u32[]{:S(2)}) collective-permute-start(bf16[1792,256]{1,0:T(8,128)(2,1)S(1)} %get-tuple-element.53), channel_id=1, source_target_pairs={{0,1},{1,2},{2,3},{3,0},{4,5},{5,6},{6,7},{7,4},{8,9},{9,10},{10,1... | collective-permute-start | bytes 2752520 | tf_op jit(solution)/shard_map/ppermute | solution.py:54
  225.9 18.6 %collective-permute-start.15 = (bf16[1792,256]{1,0:T(8,128)(2,1)S(1)}, bf16[1792,256]{1,0:T(8,128)(2,1)S(1)}, u32[]{:S(2)}, u32[]{:S(2)}) collective-permute-start(bf16[1792,256]{1,0:T(8,128)(2,1)S(1)} %shard_map.58.refs_0_), channel_id=1, source_target_pairs={{0,4},{1,5},{2,6},{3,7},{4,0},{5,1},{6,2},{7,3},{8,12},{9,13},{10,... | collective-permute-start | bytes 2752520 | tf_op jit(solution)/shard_map/ppermute | solution.py:54
  226.0 18.5 %collective-permute-start.14 = (bf16[1792,256]{1,0:T(8,128)(2,1)S(1)}, bf16[1792,256]{1,0:T(8,128)(2,1)S(1)}, u32[]{:S(2)}, u32[]{:S(2)}) collective-permute-start(bf16[1792,256]{1,0:T(8,128)(2,1)S(1)} %shard_map.58.refs_0_), channel_id=1, source_target_pairs={{0,3},{1,0},{2,1},{3,2},{4,7},{5,4},{6,5},{7,6},{8,11},{9,8},{10,9... | collective-permute-start | bytes 2752520 | tf_op jit(solution)/shard_map/ppermute | solution.py:54
  226.2 21.0 %collective-permute-start.13 = (bf16[1792,256]{1,0:T(8,128)(2,1)S(1)}, bf16[1792,256]{1,0:T(8,128)(2,1)S(1)}, u32[]{:S(2)}, u32[]{:S(2)}) collective-permute-start(bf16[1792,256]{1,0:T(8,128)(2,1)S(1)} %shard_map.58.refs_0_), channel_id=1, source_target_pairs={{0,1},{1,2},{2,3},{3,0},{4,5},{5,6},{6,7},{7,4},{8,9},{9,10},{10,1... | collective-permute-start | bytes 2752520 | tf_op jit(solution)/shard_map/ppermute | solution.py:54
  244.5 21.5 %collective-permute-start.17 = (bf16[1792,256]{1,0:T(8,128)(2,1)S(1)}, bf16[1792,256]{1,0:T(8,128)(2,1)S(1)}, u32[]{:S(2)}, u32[]{:S(2)}) collective-permute-start(bf16[1792,256]{1,0:T(8,128)(2,1)S(1)} %collective-permute-done.15.refs_3_), channel_id=1, source_target_pairs={{0,1},{1,2},{2,3},{3,0},{4,5},{5,6},{6,7},{7,4},{8,9},{9,10},{10,1... | collective-permute-start | bytes 2752520 | tf_op jit(solution)/shard_map/ppermute | solution.py:54
  244.5 21.5 %collective-permute-start.18 = (bf16[1792,256]{1,0:T(8,128)(2,1)S(1)}, bf16[1792,256]{1,0:T(8,128)(2,1)S(1)}, u32[]{:S(2)}, u32[]{:S(2)}) collective-permute-start(bf16[1792,256]{1,0:T(8,128)(2,1)S(1)} %collective-permute-done.14.refs_2_), channel_id=1, source_target_pairs={{0,3},{1,0},{2,1},{3,2},{4,7},{5,4},{6,5},{7,6},{8,11},{9,8},{10,9... | collective-permute-start | bytes 2752520 | tf_op jit(solution)/shard_map/ppermute | solution.py:54
  247.2 18.8 %collective-permute-start.16 = (bf16[1792,256]{1,0:T(8,128)(2,1)S(1)}, bf16[1792,256]{1,0:T(8,128)(2,1)S(1)}, u32[]{:S(2)}, u32[]{:S(2)}) collective-permute-start(bf16[1792,256]{1,0:T(8,128)(2,1)S(1)} %collective-permute-done.14.refs_2_), channel_id=1, source_target_pairs={{0,4},{1,5},{2,6},{3,7},{4,0},{5,1},{6,2},{7,3},{8,12},{9,13},{10,... | collective-permute-start | bytes 2752520 | tf_op jit(solution)/shard_map/ppermute | solution.py:54
  248.2 41.5 %collective-permute-start.23 = (bf16[5376,256]{1,0:T(8,128)(2,1)S(1)}, bf16[5376,256]{1,0:T(8,128)(2,1)S(1)}, u32[]{:S(2)}, u32[]{:S(2)}) collective-permute-start(bf16[5376,256]{1,0:T(8,128)(2,1)S(1)} %pad_maximum_fusion), channel_id=1, source_target_pairs={{0,16},{1,17},{2,18},{3,19},{4,20},{5,21},{6,22},{7,23},{8,24},{9,... | collective-permute-start | bytes 8257544 | tf_op jit(solution)/shard_map/ppermute | solution.py:54
  266.2 25.0 %collective-permute-start.24 = (bf16[5376,256]{1,0:T(8,128)(2,1)S(1)}, bf16[5376,256]{1,0:T(8,128)(2,1)}, u32[]{:S(2)}, u32[]{:S(2)}) collective-permute-start(bf16[5376,256]{1,0:T(8,128)(2,1)S(1)} %pad_maximum_fusion.1), channel_id=1, source_target_pairs={{0,16},{1,17},{2,18},{3,19},{4,20},{5,21},{6,22},{7,23},{8,24},{9,... | collective-permute-start | bytes 8257544 | tf_op jit(solution)/shard_map/ppermute | solution.py:54
  270.2 12.4 %collective-permute-start.19 = (bf16[608,256]{1,0:T(8,128)(2,1)S(1)}, bf16[608,256]{1,0:T(8,128)(2,1)S(1)}, u32[]{:S(2)}, u32[]{:S(2)}) collective-permute-start(bf16[608,256]{1,0:T(8,128)(2,1)S(1)} %slice.17), channel_id=1, source_target_pairs={{0,3},{1,0},{2,1},{3,2},{4,7},{5,4},{6,5},{7,6},{8,11},{9,8},{10,9... | collective-permute-start | bytes 933896 | tf_op jit(solution)/shard_map/ppermute | solution.py:54
  271.7 9.0 %collective-permute-start.20 = (bf16[592,256]{1,0:T(8,128)(2,1)S(1)}, bf16[592,256]{1,0:T(8,128)(2,1)S(1)}, u32[]{:S(2)}, u32[]{:S(2)}) collective-permute-start(bf16[592,256]{1,0:T(8,128)(2,1)S(1)} %slice.18), channel_id=1, source_target_pairs={{0,1},{1,2},{2,3},{3,0},{4,5},{5,6},{6,7},{7,4},{8,9},{9,10},{10,1... | collective-permute-start | bytes 909320 | tf_op jit(solution)/shard_map/ppermute | solution.py:54
  272.1 10.5 %collective-permute-start.21 = (bf16[592,256]{1,0:T(8,128)(2,1)S(1)}, bf16[592,256]{1,0:T(8,128)(2,1)S(1)}, u32[]{:S(2)}, u32[]{:S(2)}) collective-permute-start(bf16[592,256]{1,0:T(8,128)(2,1)S(1)} %slice.19), channel_id=1, source_target_pairs={{0,4},{1,5},{2,6},{3,7},{4,0},{5,1},{6,2},{7,3},{8,12},{9,13},{10,... | collective-permute-start | bytes 909320 | tf_op jit(solution)/shard_map/ppermute | solution.py:54
  280.7 8.9 %collective-permute-start.22 = (bf16[1792,256]{1,0:T(8,128)(2,1)S(1)}, bf16[1792,256]{1,0:T(8,128)(2,1)S(1)}, u32[]{:S(2)}, u32[]{:S(2)}) collective-permute-start(bf16[1792,256]{1,0:T(8,128)(2,1)S(1)} %shard_map.58.refs_0_), channel_id=1, source_target_pairs={{0,16},{1,17},{2,18},{3,19},{4,20},{5,21},{6,22},{7,23},{8,24},{9,... | collective-permute-start | bytes 2752520 | tf_op jit(solution)/shard_map/ppermute | solution.py:54
  282.7 6.9 %collective-permute-start.25 = (bf16[1792,256]{1,0:T(8,128)(2,1)S(1)}, bf16[1792,256]{1,0:T(8,128)(2,1)S(1)}, u32[]{:S(2)}, u32[]{:S(2)}) collective-permute-start(bf16[1792,256]{1,0:T(8,128)(2,1)S(1)} %pad_maximum_fusion.2), channel_id=1, source_target_pairs={{0,16},{1,17},{2,18},{3,19},{4,20},{5,21},{6,22},{7,23},{8,24},{9,... | collective-permute-start | bytes 2752520 | tf_op jit(solution)/shard_map/ppermute | solution.py:54
  341.4 28.9 %collective-permute-start.26 = (bf16[4032,128]{1,0:T(8,128)(2,1)}, bf16[4032,128]{1,0:T(8,128)(2,1)S(1)}, u32[]{:S(2)}, u32[]{:S(2)}) collective-permute-start(bf16[4032,128]{1,0:T(8,128)(2,1)} %get-tuple-element.60), channel_id=1, source_target_pairs={{0,0},{1,1},{2,2},{3,3},{4,4},{5,5},{6,6},{7,7},{8,16},{9,17},{10,... | collective-permute-start | bytes 3096584 | tf_op jit(solution)/shard_map/ppermute | solution.py:54
  344.7 47.7 %collective-permute-start.27 = (bf16[4032,128]{1,0:T(8,128)(2,1)}, bf16[4032,128]{1,0:T(8,128)(2,1)S(1)}, u32[]{:S(2)}, u32[]{:S(2)}) collective-permute-start(bf16[4032,128]{1,0:T(8,128)(2,1)} %get-tuple-element.61), channel_id=1, source_target_pairs={{0,4},{1,5},{2,6},{3,7},{4,0},{5,1},{6,2},{7,3},{8,20},{9,21},{10,... | collective-permute-start | bytes 3096584 | tf_op jit(solution)/shard_map/ppermute | solution.py:54
  346.4 46.1 %collective-permute-start.28 = (bf16[4032,128]{1,0:T(8,128)(2,1)}, bf16[4032,128]{1,0:T(8,128)(2,1)S(1)}, u32[]{:S(2)}, u32[]{:S(2)}) collective-permute-start(bf16[4032,128]{1,0:T(8,128)(2,1)} %get-tuple-element.62), channel_id=1, source_target_pairs={{0,8},{1,9},{2,10},{3,11},{4,12},{5,13},{6,14},{7,15},{8,24},{9,25... | collective-permute-start | bytes 3096584 | tf_op jit(solution)/shard_map/ppermute | solution.py:54
  346.4 46.5 %collective-permute-start.29 = (bf16[4032,128]{1,0:T(8,128)(2,1)}, bf16[4032,128]{1,0:T(8,128)(2,1)S(1)}, u32[]{:S(2)}, u32[]{:S(2)}) collective-permute-start(bf16[4032,128]{1,0:T(8,128)(2,1)} %get-tuple-element.63), channel_id=1, source_target_pairs={{0,12},{1,13},{2,14},{3,15},{4,8},{5,9},{6,10},{7,11},{8,28},{9,29... | collective-permute-start | bytes 3096584 | tf_op jit(solution)/shard_map/ppermute | solution.py:54
  (20 other events, 259.7 us)

commit v2 on v1

--- a/solution.py
+++ b/solution.py
@@ -19,7 +19,9 @@
 HEIGHT = 896
 HALF = 1152
 TILE = 128
-SLOT = 1168
+PART = 64
+SENT = HALF // TILE * PART
+LABEL = 16
 SIDE = 256
 BLOCKS = ROWS // SIDE
 HALF_BLOCKS = BLOCKS // 2
@@ -35,6 +37,7 @@
 F32 = jnp.float32
 MIB = 1 << 20
 ANY = pl.BlockSpec(memory_space=pl.ANY)
+HBM = pl.BlockSpec(memory_space=pltpu.HBM)
 VMEM = pl.BlockSpec(memory_space=pltpu.VMEM)
 SMEM = pl.BlockSpec(memory_space=pltpu.SMEM)
 
@@ -70,72 +73,142 @@
     return move(x, lambda c, m, a, y: (1 - c, m, a, y))
 
 
-def pack_kernel(details, tiles, out):
-    @pl.loop(0, out.shape[0])
+def pack_kernel(details, tiles, upper, lower, held, first, second, sems, out_sems):
+    load_all([(tiles.at[i], held.at[i]) for i in range(tiles.shape[0])], sems)
+
+    def copies(o):
+        return (
+            pltpu.make_async_copy(first.at[o], upper.at[o], out_sems.at[0, o]),
+            pltpu.make_async_copy(second.at[o], lower.at[o], out_sems.at[1, o]),
+        )
+
+    @pl.loop(0, upper.shape[0])
     def _(o):
         slot = details[o]
         for j in range(HALF // TILE):
-            out[o, j * TILE : (j + 1) * TILE, :] = tiles[slot, :, j * TILE : (j + 1) * TILE]
-        place = jnp.full((SLOT - HALF, TILE), details[16 + o], jnp.int32)
-        out[o, HALF:, :] = place.astype(F32).astype(BF16)
+            piece = held[slot, :, j * TILE : (j + 1) * TILE]
+            first[o, j * PART : (j + 1) * PART, :] = piece[:PART]
+            second[o, j * PART : (j + 1) * PART, :] = piece[PART:]
+        place = jnp.full((LABEL, TILE), details[16 + o], jnp.int32)
+        first[o, SENT:, :] = place.astype(F32).astype(BF16)
+        for copy in copies(o):
+            copy.start()
+
+    @pl.loop(0, upper.shape[0])
+    def _(o):
+        for copy in copies(o):
+            copy.wait()
 
 
 def pack(details, tiles):
     n = details.shape[0] // 2
+    shapes = [(n, SENT + LABEL, TILE), (n, SENT, TILE)]
     return pl.pallas_call(
         pack_kernel,
-        in_specs=[SMEM, VMEM],
-        out_specs=VMEM,
-        out_shape=jax.ShapeDtypeStruct((n, SLOT, TILE), BF16),
+        in_specs=[SMEM, HBM],
+        out_specs=[HBM] * 2,
+        out_shape=[jax.ShapeDtypeStruct(shape, BF16) for shape in shapes],
+        scratch_shapes=[pltpu.VMEM(tiles.shape, BF16)]
+        + [pltpu.VMEM(shape, BF16) for shape in shapes]
+        + [pltpu.SemaphoreType.DMA((tiles.shape[0],)), pltpu.SemaphoreType.DMA((2, n))],
         compiler_params=pltpu.CompilerParams(vmem_limit_bytes=32 * MIB),
-        cost_estimate=cost(0, 2 * n * SLOT * TILE * 2),
+        cost_estimate=cost(0, 4 * n * SENT * TILE * 2),
     )(details, tiles)
 
 
-def momentum_kernel(info, tile, old, *refs):
-    new, out = refs[-2:]
-    for j in range(HALF // TILE):
-        columns = slice(j * TILE, (j + 1) * TILE)
-        g = tile[0, columns, :].astype(F32)
-        fresh = MOMENTUM_RATE * old[:, columns] + g
-        new[:, columns] = fresh
-        out[:, columns] = (g + MOMENTUM_RATE * fresh).astype(BF16)
-
-
-def update_momentum(info, arrived, momentum, turn, so_far):
-    def half(s):
-        return (turn + s[14]) % 2
-
+def momentum_kernel(part, info, arrived, momentum, *refs):
+    new, half0, half1, tile, old, fresh, rounded, in_sems, out_sems = refs[-9:]
+    n = HEIGHT // TILE
+
+    def place(t, r):
+        half = (t + info[14]) % 2
+        columns = pl.ds(pl.multiple_of(half * HALF, TILE), HALF)
+        return pl.ds(pl.multiple_of(r * TILE + part * PART, PART), PART), columns
+
+    def reads(t, r):
+        source = info[2 * r + (t + info[14]) % 2]
+        i = t * n + r
+        return (
+            pltpu.make_async_copy(momentum.at[place(t, r)], old.at[i], in_sems.at[0, i]),
+            pltpu.make_async_copy(arrived.at[source, 0:SENT], tile.at[i], in_sems.at[1, i]),
+        )
+
+    def writes(t, r):
+        i = t * n + r
+        out = (half0, half1)[t].at[r]
+        return (
+            pltpu.make_async_copy(fresh.at[i], new.at[place(t, r)], out_sems.at[0, i]),
+            pltpu.make_async_copy(rounded.at[i], out, out_sems.at[1, i]),
+        )
+
+    for t in range(2):
+        for r in range(n):
+            for copy in reads(t, r):
+                copy.start()
+    for t in range(2):
+
+        @pl.loop(0, n)
+        def _(r):
+            i = t * n + r
+            for copy in reads(t, r):
+                copy.wait()
+            for j in range(HALF // TILE):
+                columns = slice(j * TILE, (j + 1) * TILE)
+                g = tile[i, j * PART : (j + 1) * PART, :].astype(F32)
+                later = MOMENTUM_RATE * old[i, :, columns] + g
+                fresh[i, :, columns] = later
+                rounded[i, :, columns] = (g + MOMENTUM_RATE * later).astype(BF16)
+            for copy in writes(t, r):
+                copy.start()
+
+    for t in range(2):
+
+        @pl.loop(0, n)
+        def _(r):
+            for copy in writes(t, r):
+                copy.wait()
+
+
+def update_momentum(info, arrived, momentum, part, so_far):
     more = () if so_far is None else (so_far,)
-    return pl.pallas_call(
-        momentum_kernel,
-        grid_spec=pltpu.PrefetchScalarGridSpec(
-            num_scalar_prefetch=1,
-            grid=(HEIGHT // TILE,),
-            in_specs=[
-                pl.BlockSpec((1, SLOT, TILE), lambda r, s: (s[2 * r + half(s)], 0, 0)),
-                pl.BlockSpec((TILE, HALF), lambda r, s: (r, half(s))),
-            ]
-            + [ANY] * len(more),
-            out_specs=[
-                pl.BlockSpec((TILE, HALF), lambda r, s: (r, half(s))),
-                pl.BlockSpec((TILE, HALF), lambda r, s: (r, 0)),
-            ],
-        ),
+    n = 2 * HEIGHT // TILE
+    return pl.pallas_call(
+        lambda *refs: momentum_kernel(part, *refs),
+        in_specs=[SMEM] + [HBM] * (2 + len(more)),
+        out_specs=[HBM] * 3,
         out_shape=[
             jax.ShapeDtypeStruct(momentum.shape, F32),
-            jax.ShapeDtypeStruct((HEIGHT, HALF), BF16),
+            jax.ShapeDtypeStruct((n // 2, PART, HALF), BF16),
+            jax.ShapeDtypeStruct((n // 2, PART, HALF), BF16),
+        ],
+        scratch_shapes=[
+            pltpu.VMEM((n, SENT, TILE), BF16),
+            pltpu.VMEM((n, PART, HALF), F32),
+            pltpu.VMEM((n, PART, HALF), F32),
+            pltpu.VMEM((n, PART, HALF), BF16),
+            pltpu.SemaphoreType.DMA((2, n)),
+            pltpu.SemaphoreType.DMA((2, n)),
         ],
         input_output_aliases={3: 0} if more else {},
+        compiler_params=pltpu.CompilerParams(vmem_limit_bytes=32 * MIB),
         cost_estimate=cost(0, HEIGHT * HALF * 12),
     )(info, arrived, momentum, *more)
 
 
-def panel_rows(info, which):
+def panel_copies(info, blocks, panel, columns=None):
     c, a = info[0], info[2]
-    other, t = divmod(which, 2)
-    core = 1 - c if other else c
-    return 2 * core + (a + t) % 2
+    copies = []
+    for i, block in enumerate(blocks):
+        other, t, part = i // 4, i // 2 % 2, i % 2
+        core = 1 - c if other else c
+        z = 2 * core + (a + t) % 2
+        src = block if columns is None else block.at[:, :, columns]
+        copies.append((src, panel.at[pl.ds(z * (HEIGHT // TILE), HEIGHT // TILE), part]))
+    return copies
+
+
+def panel_shape(width):
+    return pltpu.VMEM((ROWS // TILE, TILE // PART, PART, width), BF16)
 
 
 def chip_at(info, flip, dy):
@@ -152,14 +225,13 @@
 
 
 def gram_kernel(dests, info, *refs):
-    blocks, outs = refs[:4], refs[4:-2]
+    blocks, outs = refs[:8], refs[8:-2]
     panel, sems = refs[-2:]
-    starts = [pl.multiple_of(panel_rows(info, i) * HEIGHT, HEIGHT) for i in range(4)]
-    load_all([(blocks[i], panel.at[pl.ds(starts[i], HEIGHT)]) for i in range(4)], sems)
+    load_all(panel_copies(info, blocks, panel), sems)
 
     def term(b, d):
-        left = panel[pl.ds(pl.multiple_of(b * SIDE, SIDE), SIDE)]
-        right = panel[pl.ds(pl.multiple_of((b + d) % BLOCKS * SIDE, SIDE), SIDE)]
+        left = panel[pl.ds(2 * b, 2)].reshape(SIDE, HALF)
+        right = panel[pl.ds(2 * ((b + d) % BLOCKS), 2)].reshape(SIDE, HALF)
         return lax.dot_general(left, right, (((1,), (1,)), ((), ())), preferred_element_type=F32)
 
     base = HALF_BLOCKS * info[0]
@@ -183,11 +255,11 @@
 def gram_chunks(info, blocks, dests, shapes):
     return pl.pallas_call(
         lambda *refs: gram_kernel(dests, *refs),
-        in_specs=[SMEM] + [ANY] * 4,
+        in_specs=[SMEM] + [HBM] * 8,
         out_specs=[VMEM] * len(shapes),
         out_shape=shapes,
-        scratch_shapes=[pltpu.VMEM((ROWS, HALF), BF16), pltpu.SemaphoreType.DMA((4,))],
-        compiler_params=pltpu.CompilerParams(vmem_limit_bytes=48 * MIB),
+        scratch_shapes=[panel_shape(HALF), pltpu.SemaphoreType.DMA((8,))],
+        compiler_params=pltpu.CompilerParams(vmem_limit_bytes=24 * MIB),
         cost_estimate=cost(len(dests) * 2 * CHUNK * SIDE * HALF, 8.3e6 + len(dests) * CHUNK * SIDE * 4),
     )(info, *blocks)
 
@@ -210,43 +282,40 @@
     v2[...] = (p2[...] + g2[...].astype(F32)).astype(BF16)
 
 
-def last_sums_kernel(p, v1, v2, v3, out):
+def last_sums_kernel(p, v1, v2, v3, turned, out):
     total = p[...] + (v1[...].astype(F32) + v2[...].astype(F32) + v3[...].astype(F32))
     out[...] = total.astype(BF16)
 
 
-def in_vmem(kernel, shapes, *args):
+def in_vmem(kernel, shapes, *args, after=()):
     size = sum(x.size * x.dtype.itemsize for x in args)
     return pl.pallas_call(
         kernel,
-        in_specs=[VMEM] * len(args),
+        in_specs=[VMEM] * len(args) + [ANY] * len(after),
         out_specs=[VMEM] * len(shapes),
         out_shape=shapes,
-        compiler_params=pltpu.CompilerParams(vmem_limit_bytes=32 * MIB),
+        compiler_params=pltpu.CompilerParams(vmem_limit_bytes=16 * MIB),
         cost_estimate=cost(0, size),
-    )(*args)
+    )(*args, *after)
 
 
 def turn_kernel(info, *refs):
-    blocks, out, held, sems = refs[:4], refs[4], refs[5], refs[6]
+    blocks, out, held, sems = refs[:8], refs[8], refs[9], refs[10]
     shift = pl.multiple_of(512 * info[0], TILE)
-    load_all([(blocks[i].at[:, pl.ds(shift, WIDE)], held.at[i]) for i in range(4)], sems)
-    for i in range(4):
-        start = pl.multiple_of(panel_rows(info, i) * HEIGHT, TILE)
-        for r in range(HEIGHT // TILE):
-            piece = held[i, r * TILE : (r + 1) * TILE, :].T
-            out[:, pl.ds(pl.multiple_of(start + r * TILE, TILE), TILE)] = piece
+    load_all(panel_copies(info, blocks, held, pl.ds(shift, WIDE)), sems)
+    for r in range(ROWS // TILE):
+        out[:, r * TILE : (r + 1) * TILE] = held[r].reshape(TILE, WIDE).T
     out[:, ROWS:] = out[:, :CHUNK]
 
 
 def turned_panel(info, blocks):
     return pl.pallas_call(
         turn_kernel,
-        in_specs=[SMEM] + [ANY] * 4,
+        in_specs=[SMEM] + [HBM] * 8,
         out_specs=VMEM,
         out_shape=jax.ShapeDtypeStruct((WIDE, AROUND), BF16),
-        scratch_shapes=[pltpu.VMEM((4, HEIGHT, WIDE), BF16), pltpu.SemaphoreType.DMA((4,))],
-        compiler_params=pltpu.CompilerParams(vmem_limit_bytes=32 * MIB),
+        scratch_shapes=[panel_shape(WIDE), pltpu.SemaphoreType.DMA((8,))],
+        compiler_params=pltpu.CompilerParams(vmem_limit_bytes=24 * MIB),
         cost_estimate=cost(0, 1.2e7),
     )(info, *blocks)
 
@@ -257,9 +326,9 @@
 def apply_kernel(info, *refs):
     own, ends, swapped = refs[:7], refs[7:10], refs[10:14]
     turned = refs[14]
-    outs = refs[15:19]
-    direct, flipped, panel, mixed, stage, sems, panel_sem, out_sems = refs[19:]
-    c, a = info[0], info[2]
+    outs, rest_direct, rest_flipped, all_mixed, scales = refs[15:17], *refs[17:21]
+    direct, flipped, panel, mixed, stage, sems, panel_sem, out_sems, keep_sems = refs[21:]
+    c = info[0]
     panel_copy = pltpu.make_async_copy(turned, panel, panel_sem)
     panel_copy.start()
     pieces = [(c, ref, 0, rel) for ref, rel in zip(own, SOURCES)]
@@ -304,11 +373,7 @@
     square = factor * factor
 
     def product(i, x):
-        first = pl.ds(pl.multiple_of((i + 7) % BLOCKS * SIDE, SIDE), 8 * SIDE)
-        rest = pl.ds(pl.multiple_of((i + 1) % BLOCKS * SIDE, SIDE), 6 * SIDE)
-        result = jnp.dot(x[:, first], direct[i], preferred_element_type=F32)
-        result += jnp.dot(x[:, rest], flipped[i], preferred_element_type=F32)
-        return result * square
+        return gram_times(i, x, direct.at[i], flipped.at[i]) * square
 
     @pl.loop(0, BLOCKS)
     def _(i):
@@ -324,53 +389,115 @@
         def _():
             mixed[:, pl.ds(pl.multiple_of(i * SIDE + ROWS, SIDE), SIDE)] = mix
 
+    other = (1 - c) * HALF_BLOCKS
     scale = math.sqrt(COLS) * factor
+    scales[...] = jnp.concatenate([scale] * 4 + [square] * 4)
+    keeps = [
+        pltpu.make_async_copy(direct.at[pl.ds(other, HALF_BLOCKS)], rest_direct, keep_sems.at[0]),
+        pltpu.make_async_copy(flipped.at[pl.ds(other, HALF_BLOCKS)], rest_flipped, keep_sems.at[1]),
+        pltpu.make_async_copy(mixed, all_mixed, keep_sems.at[2]),
+    ]
+    for copy in keeps:
+        copy.start()
+
+    @pl.loop(0, HALF_BLOCKS)
+    def _(b):
+        i = c * HALF_BLOCKS + b
+        columns = pl.ds(pl.multiple_of(i * SIDE, SIDE), SIDE)
+        result = scale * (COEF_LINEAR * panel[:, columns].astype(F32) + product(i, mixed))
+        stage[pl.ds(pl.multiple_of(b * SIDE, SIDE), SIDE)] = result.astype(BF16).T
+
+    send_back(info, stage, outs, out_sems)
+    for copy in keeps:
+        copy.wait()
+
+
+def gram_times(i, x, direct, flipped):
+    first = pl.ds(pl.multiple_of((i + 7) % BLOCKS * SIDE, SIDE), 8 * SIDE)
+    rest = pl.ds(pl.multiple_of((i + 1) % BLOCKS * SIDE, SIDE), 6 * SIDE)
+    result = jnp.dot(x[:, first], direct[...], preferred_element_type=F32)
+    return result + jnp.dot(x[:, rest], flipped[...], preferred_element_type=F32)
+
+
+def send_back(info, stage, outs, sems):
+    c, a = info[0], info[2]
     sends = []
-    for turn in range(2):
-        half = 1 - c if turn else c
-
-        @pl.loop(0, HALF_BLOCKS)
-        def _(b):
-            i = half * HALF_BLOCKS + b
-            columns = pl.ds(pl.multiple_of(i * SIDE, SIDE), SIDE)
-            result = scale * (COEF_LINEAR * panel[:, columns].astype(F32) + product(i, mixed))
-            stage[turn, pl.ds(pl.multiple_of(b * SIDE, SIDE), SIDE)] = result.astype(BF16).T
-
-        for side in range(2):
-            out = outs[2 * turn + side]
-            owner = 1 - a if side else a
-            start = pl.multiple_of(owner * HEIGHT, 128)
-            for j in range(4):
-                columns = pl.ds(pl.multiple_of((j + c) * TILE, TILE), TILE)
-                sends.append((stage.at[turn, pl.ds(start, HEIGHT), columns], out.at[pl.ds(j * HEIGHT, HEIGHT)]))
-            columns = pl.ds(pl.multiple_of(4 * (1 - c) * TILE, TILE), TILE)
-            shared = pl.ds(pl.multiple_of(start + 448 * c, 64), 448)
-            sends.append((stage.at[turn, shared, columns], out.at[pl.ds(4 * HEIGHT, 448)]))
-            for k in range(len(sends) - 5, len(sends)):
-                sends[k] = pltpu.make_async_copy(*sends[k], out_sems.at[k])
-                sends[k].start()
-    for copy in sends:
-        copy.wait()
+    for side, out in enumerate(outs):
+        owner = 1 - a if side else a
+        start = pl.multiple_of(owner * HEIGHT, 128)
+        for j in range(4):
+            columns = pl.ds(pl.multiple_of((j + c) * TILE, TILE), TILE)
+            sends.append((stage.at[pl.ds(start, HEIGHT), columns], out.at[pl.ds(j * HEIGHT, HEIGHT)]))
+        columns = pl.ds(pl.multiple_of(4 * (1 - c) * TILE, TILE), TILE)
+        shared = pl.ds(pl.multiple_of(start + 448 * c, 64), 448)
+        sends.append((stage.at[shared, columns], out.at[pl.ds(4 * HEIGHT, 448)]))
+    load_all(sends, sems)
+
+
+def rest_kernel(info, direct, flipped, panel, all_mixed, scales, out0, out1, mixed, stage, sems):
+    b = pl.program_id(0)
+
+    @pl.when(b == 0)
+    def _():
+        load_all([(all_mixed, mixed)], sems)
+
+    i = (1 - info[0]) * HALF_BLOCKS + b
+    product = gram_times(i, mixed, direct.at[0], flipped.at[0]) * scales[4:5]
+    result = scales[0:1] * (COEF_LINEAR * panel[...].astype(F32) + product)
+    stage[pl.ds(pl.multiple_of(b * SIDE, SIDE), SIDE)] = result.astype(BF16).T
+
+    @pl.when(b == HALF_BLOCKS - 1)
+    def _():
+        send_back(info, stage, (out0, out1), sems)
+
+
+def apply_rest(info, direct, flipped, mixed, scales, turned):
+    return pl.pallas_call(
+        rest_kernel,
+        grid_spec=pltpu.PrefetchScalarGridSpec(
+            num_scalar_prefetch=1,
+            grid=(HALF_BLOCKS,),
+            in_specs=[
+                pl.BlockSpec((1, 8 * SIDE, SIDE), lambda b, s: (b, 0, 0)),
+                pl.BlockSpec((1, 6 * SIDE, SIDE), lambda b, s: (b, 0, 0)),
+                pl.BlockSpec((WIDE, SIDE), lambda b, s: (0, (1 - s[0]) * HALF_BLOCKS + b)),
+                HBM,
+                VMEM,
+            ],
+            out_specs=[HBM] * 2,
+            scratch_shapes=[pltpu.VMEM((WIDE, AROUND), BF16), pltpu.VMEM((CHUNK, WIDE), BF16), pltpu.SemaphoreType.DMA((10,))],
+        ),
+        out_shape=[jax.ShapeDtypeStruct((BACK_ROWS, TILE), BF16)] * 2,
+        compiler_params=pltpu.CompilerParams(vmem_limit_bytes=40 * MIB),
+        cost_estimate=cost(ROWS * ROWS * WIDE, 2e7),
+    )(info, direct, flipped, turned, mixed, scales)
 
 
 def apply_poly(info, own, ends, swapped, turned):
     return pl.pallas_call(
         apply_kernel,
-        in_specs=[SMEM] + [ANY] * 15,
-        out_specs=[ANY] * 4,
-        out_shape=[jax.ShapeDtypeStruct((BACK_ROWS, TILE), BF16)] * 4,
+        in_specs=[SMEM] + [HBM] * 15,
+        out_specs=[HBM] * 5 + [VMEM],
+        out_shape=[jax.ShapeDtypeStruct((BACK_ROWS, TILE), BF16)] * 2
+        + [
+            jax.ShapeDtypeStruct((HALF_BLOCKS, 8 * SIDE, SIDE), BF16),
+            jax.ShapeDtypeStruct((HALF_BLOCKS, 6 * SIDE, SIDE), BF16),
+            jax.ShapeDtypeStruct((WIDE, AROUND), BF16),
+            jax.ShapeDtypeStruct((8, SIDE), F32),
+        ],
         scratch_shapes=[
             pltpu.VMEM((BLOCKS, 8 * SIDE, SIDE), BF16),
             pltpu.VMEM((BLOCKS, 6 * SIDE, SIDE), BF16),
             pltpu.VMEM((WIDE, AROUND), BF16),
             pltpu.VMEM((WIDE, AROUND), BF16),
-            pltpu.VMEM((2, CHUNK, WIDE), BF16),
+            pltpu.VMEM((CHUNK, WIDE), BF16),
             pltpu.SemaphoreType.DMA((32,)),
             pltpu.SemaphoreType.DMA,
-            pltpu.SemaphoreType.DMA((20,)),
+            pltpu.SemaphoreType.DMA((10,)),
+            pltpu.SemaphoreType.DMA((3,)),
         ],
         compiler_params=pltpu.CompilerParams(vmem_limit_bytes=58 * MIB),
-        cost_estimate=cost(4 * ROWS * ROWS * WIDE, 3e7),
+        cost_estimate=cost(3 * ROWS * ROWS * WIDE, 4e7),
     )(info, *own, *ends, *swapped, turned)
 
 
@@ -408,19 +535,28 @@
     matches = owners[:, None] == jnp.arange(16, dtype=jnp.int32)[None, :]
     slots = jnp.sum(jnp.where(matches, jnp.arange(tile_count, dtype=jnp.int32)[:, None], 0), axis=0)
     labels = jnp.sum(jnp.where(matches, places[:, None] + 1, 0), axis=0) - 1
-    packed = pack(jnp.concatenate([slots, labels]), grad_tiles)
-    arrived = lax.all_to_all(packed, PLANE, split_axis=0, concat_axis=0, tiled=True)
-
-    got_labels = arrived[:, HALF, 0].astype(jnp.int32)
+    upper, lower = pack(jnp.concatenate([slots, labels]), grad_tiles)
+    upper = lax.all_to_all(upper, PLANE, split_axis=0, concat_axis=0, tiled=True)
+    lower, _ = lax.optimization_barrier((lower, upper))
+    lower = lax.all_to_all(lower, PLANE, split_axis=0, concat_axis=0, tiled=True)
+
+    got_labels = upper[:, SENT, 0].astype(jnp.int32)
     found = got_labels[None, :] == jnp.arange(tile_count, dtype=jnp.int32)[:, None]
     sources = jnp.sum(jnp.where(found, jnp.arange(16, dtype=jnp.int32)[None, :], 0), axis=1)
     details = jnp.concatenate([sources, zl[None].astype(jnp.int32)])
-    new_momentum, half0 = update_momentum(details, arrived, momentum, 0, None)
-    new_momentum, half1 = update_momentum(details, arrived, momentum, 1, new_momentum)
-
-    got0 = move(half0, lambda c, m, a, y: (m, c, a, y))
-    got1 = move(half1, lambda c, m, a, y: (m, c, 1 - a, y))
-    blocks = (got0, got1, swap(got0), swap(got1))
+    new_momentum, *halves0 = update_momentum(details, upper, momentum, 0, None)
+    new_momentum, *halves1 = update_momentum(details, lower, momentum, 1, new_momentum)
+
+    def to_panel(halves):
+        half0, half1 = halves
+        return (
+            move(half0, lambda c, m, a, y: (m, c, a, y)),
+            move(half1, lambda c, m, a, y: (m, c, 1 - a, y)),
+        )
+
+    got0, got1 = to_panel(halves0), to_panel(halves1)
+    blocks = (got0[0], got1[0], got0[1], got1[1])
+    blocks += tuple(swap(x) for x in blocks)
 
     far = gram_chunks(info, blocks, ((1, 2),), [chunk(BF16, size) for _, size in PARTS])
     far0, far1, far2 = up(far[0]), down(far[1]), across(far[2])
@@ -436,7 +572,7 @@
     w1, w2 = up(v1), across(v2)
     later, _ = lax.optimization_barrier((blocks, v1))
     turned = turned_panel(info, later)
-    (mine,) = in_vmem(last_sums_kernel, [chunk()], center, w1, w2, near)
+    (mine,) = in_vmem(last_sums_kernel, [chunk()], center, w1, w2, near, after=(turned,))
 
     low, high, pair = up(mine), down(mine), across(mine)
     a1, a2, a3 = across(high), up(pair), down(high)
@@ -449,7 +585,8 @@
         swap(jnp.concatenate([a1, a2, a3])),
         swap(jnp.concatenate(ends)),
     )
-    sent = apply_poly(info, (mine, low, high, pair, a1, a2, a3), ends, swapped, turned)
+    *sent, direct, flipped, mixed, scales = apply_poly(info, (mine, low, high, pair, a1, a2, a3), ends, swapped, turned)
+    sent += apply_rest(info, direct, flipped, mixed, scales, turned)
 
     parts = (
         move(sent[0], lambda c, m, a, y: (m, c, a, y)),

time: 398 us -> 357 us (0.90)
  waiting for transfers between devices: 230 us -> 131 us
  blocking collectives: 0 us -> 39.4 us
  local copies, waits for them, and re-layouts: 10.1 us -> 17.8 us
  Pallas kernels: 103 us -> 109 us
  starting transfers between devices: 49 us -> 54.9 us
    all_to_all x1, waiting for transfers between devices: 70.8 us -> 14.4 us  [on_device(): lax.all_to_all(lower, PLANE, split_axis=0, concat_axis=0, tiled=True)]
    ppermute x30 -> x34, waiting for transfers between devices: 159 us -> 117 us  [move(): return lax.ppermute(x, AXES[1:], pairs)]
    all_to_all x0 -> x1, blocking collectives: none -> 39.4 us  [on_device(): lax.all_to_all(upper, PLANE, split_axis=0, concat_axis=0, tiled=True)]
    ppermute x30 -> x34, starting transfers between devices: 40.3 us -> 50.4 us  [move(): return lax.ppermute(x, AXES[1:], pairs)]
    pallas_call x8 -> x9, Pallas kernels: 73.8 us -> 83 us  [the longest x1 40.3 us: apply_poly(): pl.pallas_call(apply_kernel, in_specs=[SMEM] + [HBM] * 15, out_specs=[HBM...]
    unnamed x42 -> x46, local copies, waits for them, and re-layouts: 10.1 us -> 17.8 us
    all_to_all x1, starting transfers between devices: 8.64 us -> 4.45 us  [on_device(): lax.all_to_all(lower, PLANE, split_axis=0, concat_axis=0, tiled=True)]
  transfers between devices with their start and end apart: 31 -> 35, of which waited for: 16 -> 19; matrix products, arithmetic and copies ran while one was open for 0% -> 0% of each run, Pallas kernels for 6% -> 14%
where the time goes in v2:
time: 357 us; the launch traced here: 356 us
  waiting for transfers between devices  131 us (37%)
  Pallas kernels  109 us (31%)
  starting transfers between devices  54.9 us (15%)
  blocking collectives  39.4 us (11%)
  local copies, waits for them, and re-layouts  17.8 us (5%)
    ppermute x34, waiting for transfers between devices, move(): return lax.ppermute(x, AXES[1:], pairs)  117 us
    ppermute x34, starting transfers between devices, move(): return lax.ppermute(x, AXES[1:], pairs)  50.4 us
    pallas_call x1, Pallas kernels, apply_poly(): pl.pallas_call(apply_kernel, in_specs=[SMEM] + [HBM] * 15, out_specs=[HBM...  40.3 us
    all_to_all x1, blocking collectives, on_device(): lax.all_to_all(upper, PLANE, split_axis=0, concat_axis=0, tiled=True)  39.4 us
    pallas_call x3, Pallas kernels, gram_chunks(): pl.pallas_call(lambda *refs: gram_kernel(dests, *refs), in_specs=[SMEM] +...  22.6 us
    unnamed x46, local copies, waits for them, and re-layouts  17.8 us
    pallas_call x1, Pallas kernels, apply_rest(): pl.pallas_call(rest_kernel, grid_spec=pltpu.PrefetchScalarGridSpec(num_sc...  15.4 us
    all_to_all x1, waiting for transfers between devices, on_device(): lax.all_to_all(lower, PLANE, split_axis=0, concat_axis=0, tiled=True)  14.4 us
  transfers between devices with their start and end apart: 35, of which 19 were waited for; matrix products, arithmetic and copies ran while one was open for 0% of the time, Pallas kernels for 14%

profile of v2, /device:TPU:1, one launch (start us, length us, event | category | flops | bytes accessed | tf_op | source)
XLA Modules:
  0.0 355.8 jit_solution(2147940493199321733)
XLA Ops:
  4.3 9.0 %shard_map.50 = (bf16[16,592,128]{2,1,0:T(8,128)(2,1)S(1)}, bf16[16,576,128]{2,1,0:T(8,128)(2,1)S(1)}) custom-call(s32[32]{0:T(128)S(1)} %pad_add_fusion.details, bf16[14,128,1152]{2,1,0:T(8,128)(2,1)S(1)} %copy-done.4), custom_call_target="tpu_custom_call" | custom-call | bytes 9437184 | tf_op jit(solution)/shard_map/pallas_call | solution.py:106
  13.4 39.4 %all_to_all.10.refs_1_ = bf16[16,592,128]{2,1,0:T(8,128)(2,1)S(1)} all-to-all(bf16[16,592,128]{2,1,0:T(8,128)(2,1)S(1)} %get-tuple-element.50), channel_id=1, replica_groups=mesh['x'=4,'core'=2,'zm'=2,'zl'=2,'y'=4] {'zm','zl','y'}, dimensions={0} | all-to-all | bytes 4849664 | tf_op jit(solution)/shard_map/all_to_all | solution.py:539
  52.8 4.5 %all-to-all-start.1 = ((bf16[16,576,128]{2,1,0:T(8,128)(2,1)}), bf16[16,576,128]{2,1,0:T(8,128)(2,1)}, u32[]{:S(2)}, u32[]{:S(2)}) async-start(bf16[16,576,128]{2,1,0:T(8,128)(2,1)} %copy-done.5), calls=%async_computation.1 | async-start | bytes 4718592 | tf_op jit(solution)/shard_map/all_to_all | solution.py:541
  57.8 3.4 copy-done
  61.2 6.8 %shard_map.51 = (f32[896,2304]{1,0:T(8,128)}, bf16[7,64,1152]{2,1,0:T(8,128)(2,1)}, bf16[7,64,1152]{2,1,0:T(8,128)(2,1)}) custom-call(s32[15]{0:T(128)S(1)} %pad_add_fusion.1.refs_0_, bf16[16,592,128]{2,1,0:T(8,128)(2,1)S(1)} %all_to_all.10.refs_1_, f32[896,2304]{1,0:T(8,128)S(1)} %copy-done), custom_call_target="tpu_custom_call" | custom-call | bytes 12386304 | tf_op jit(solution)/shard_map/pallas_call | solution.py:175
  68.0 6.6 %collective-permute-start = (bf16[7,64,1152]{2,1,0:T(8,128)(2,1)}, bf16[7,64,1152]{2,1,0:T(8,128)(2,1)S(1)}, u32[]{:S(2)}, u32[]{:S(2)}) collective-permute-start(bf16[7,64,1152]{2,1,0:T(8,128)(2,1)} %get-tuple-element.55), channel_id=1, source_target_pairs={{0,0},{1,1},{2,2},{3,3},{4,4},{5,5},{6,6},{7,7},{8,16},{9,17},{10,... | collective-permute-start | bytes 3096584 | tf_op jit(solution)/shard_map/ppermute | solution.py:57
  74.7 14.4 %all-to-all-done.1.refs_1_ = bf16[16,576,128]{2,1,0:T(8,128)(2,1)} async-done(((bf16[16,576,128]{2,1,0:T(8,128)(2,1)}), bf16[16,576,128]{2,1,0:T(8,128)(2,1)}, u32[]{:S(2)}, u32[]{:S(2)}) %all-to-all-start.1) | async-done | bytes 2359328 | tf_op jit(solution)/shard_map/all_to_all | solution.py:541
  89.1 3.3 copy-done.1
  92.5 6.4 %shard_map.52 = (f32[896,2304]{1,0:T(8,128)}, bf16[7,64,1152]{2,1,0:T(8,128)(2,1)S(1)}, bf16[7,64,1152]{2,1,0:T(8,128)(2,1)S(1)}) custom-call(s32[15]{0:T(128)S(1)} %pad_add_fusion.1.refs_0_, bf16[16,576,128]{2,1,0:T(8,128)(2,1)} %all-to-all-done.1.refs_1_, f32[896,2304]{1,0:T(8,128)S(1)} %copy-done.1, ...), custom_call_target="tpu_custom_call", output_to_operand_aliasing={{0}: (3, {})} | custom-call | bytes 12386304 | tf_op jit(solution)/shard_map/pallas_call | solution.py:175
  98.9 6.2 %collective-permute-start.1 = (bf16[7,64,1152]{2,1,0:T(8,128)(2,1)S(1)}, bf16[7,64,1152]{2,1,0:T(8,128)(2,1)S(1)}, u32[]{:S(2)}, u32[]{:S(2)}) collective-permute-start(bf16[7,64,1152]{2,1,0:T(8,128)(2,1)S(1)} %get-tuple-element.56), channel_id=1, source_target_pairs={{0,0},{1,1},{2,2},{3,3},{4,4},{5,5},{6,6},{7,7},{8,16},{9,17},{10,... | collective-permute-start | bytes 3096584 | tf_op jit(solution)/shard_map/ppermute | solution.py:57
  105.6 3.8 %collective-permute-done.refs_1_.refs_0_ = bf16[7,64,1152]{2,1,0:T(8,128)(2,1)S(1)} collective-permute-done((bf16[7,64,1152]{2,1,0:T(8,128)(2,1)}, bf16[7,64,1152]{2,1,0:T(8,128)(2,1)S(1)}, u32[]{:S(2)}, u32[]{:S(2)}) %collective-permute-start) | collective-permute-done | bytes 1032224 | tf_op jit(solution)/shard_map/ppermute | solution.py:57
  109.9 20.9 %collective-permute-done.1.refs_2_.refs_1_ = bf16[7,64,1152]{2,1,0:T(8,128)(2,1)S(1)} collective-permute-done((bf16[7,64,1152]{2,1,0:T(8,128)(2,1)S(1)}, bf16[7,64,1152]{2,1,0:T(8,128)(2,1)S(1)}, u32[]{:S(2)}, u32[]{:S(2)}) %collective-permute-start.1) | collective-permute-done | bytes 1032224 | tf_op jit(solution)/shard_map/ppermute | solution.py:57
  135.2 4.7 %shard_map.54 = (bf16[608,256]{1,0:T(8,128)(2,1)S(1)}, bf16[592,256]{1,0:T(8,128)(2,1)S(1)}, bf16[592,256]{1,0:T(8,128)(2,1)S(1)}) custom-call(s32[4]{0:T(128)S(1)} %pad_add_fusion.2.refs_0_.info, bf16[7,64,1152]{2,1,0:T(8,128)(2,1)S(1)} %collective-permute-done.refs_1_.refs_0_, bf16[7,64,1152]{2,1,0:T(8,128)(2,1)S(1)} %collective-permute-done.1.refs_2_.refs_1_, ...), custom_call_target="tpu_custom_call" | custom-call | flops 1056964608 | bytes 10135008 | tf_op jit(solution)/shard_map/pallas_call | solution.py:256
  143.3 8.3 %shard_map.53 = (f32[1792,256]{1,0:T(8,128)S(1)}, f32[1792,256]{1,0:T(8,128)S(1)}, f32[1792,256]{1,0:T(8,128)S(1)}) custom-call(s32[4]{0:T(128)S(1)} %pad_add_fusion.2.refs_0_.info, bf16[7,64,1152]{2,1,0:T(8,128)(2,1)S(1)} %collective-permute-done.refs_1_.refs_0_, bf16[7,64,1152]{2,1,0:T(8,128)(2,1)S(1)} %collective-permute-done.1.refs_2_.refs_1_, ...), custom_call_target="tpu_custom_call" | custom-call | flops 3170893824 | bytes 13805024 | tf_op jit(solution)/shard_map/pallas_call | solution.py:256
  154.6 9.5 %shard_map.56 = (f32[1792,256]{1,0:T(8,128)S(1)}, f32[1792,256]{1,0:T(8,128)S(1)}, bf16[1792,256]{1,0:T(8,128)(2,1)S(1)}, f32[1792,256]{1,0:T(8,128)S(1)}) custom-call(s32[4]{0:T(128)S(1)} %pad_add_fusion.2.refs_0_.info, bf16[7,64,1152]{2,1,0:T(8,128)(2,1)S(1)} %collective-permute-done.refs_1_.refs_0_, ...), custom_call_target="tpu_custom_call" | custom-call | flops 4227858432 | bytes 15640032 | tf_op jit(solution)/shard_map/pallas_call | solution.py:256
  164.2 2.7 collective-permute-start.16
  166.8 6.4 %collective-permute-done.12.g2 = bf16[1792,256]{1,0:T(8,128)(2,1)S(1)} collective-permute-done((bf16[1792,256]{1,0:T(8,128)(2,1)S(1)}, bf16[1792,256]{1,0:T(8,128)(2,1)S(1)}, u32[]{:S(2)}, u32[]{:S(2)}) %collective-permute-start.12) | collective-permute-done | bytes 917536 | tf_op jit(solution)/shard_map/ppermute | solution.py:57
  176.8 3.9 %shard_map.58.turned.refs_14_.panel = bf16[640,5376]{1,0:T(8,128)(2,1)S(1)} custom-call(s32[4]{0:T(128)S(1)} %pad_add_fusion.2.refs_0_.info, bf16[7,64,1152]{2,1,0:T(8,128)(2,1)S(1)} %collective-permute-done.refs_1_.refs_0_, bf16[7,64,1152]{2,1,0:T(8,128)(2,1)S(1)} %collective-permute-done.1.refs_2_.refs_1_, ...), custom_call_target="tpu_custom_call" | custom-call | bytes 12000000 | tf_op jit(solution)/shard_map/pallas_call | solution.py:312
  180.8 12.1 %collective-permute-done.16.v3 = bf16[1792,256]{1,0:T(8,128)(2,1)S(1)} collective-permute-done((bf16[1792,256]{1,0:T(8,128)(2,1)S(1)}, bf16[1792,256]{1,0:T(8,128)(2,1)S(1)}, u32[]{:S(2)}, u32[]{:S(2)}) %collective-permute-start.16) | collective-permute-done | bytes 917536 | tf_op jit(solution)/shard_map/ppermute | solution.py:57
  199.8 16.6 %collective-permute-done.19.refs_3_ = bf16[1792,256]{1,0:T(8,128)(2,1)S(1)} collective-permute-done((bf16[1792,256]{1,0:T(8,128)(2,1)S(1)}, bf16[1792,256]{1,0:T(8,128)(2,1)S(1)}, u32[]{:S(2)}, u32[]{:S(2)}) %collective-permute-start.19) | collective-permute-done | bytes 917536 | tf_op jit(solution)/shard_map/ppermute | solution.py:57
  220.5 5.2 %collective-permute-start.27 = (bf16[5376,256]{1,0:T(8,128)(2,1)S(1)}, bf16[5376,256]{1,0:T(8,128)(2,1)S(1)}, u32[]{:S(2)}, u32[]{:S(2)}) collective-permute-start(bf16[5376,256]{1,0:T(8,128)(2,1)S(1)} %pad_maximum_fusion), channel_id=1, source_target_pairs={{0,16},{1,17},{2,18},{3,19},{4,20},{5,21},{6,22},{7,23},{8,24},{9,... | collective-permute-start | bytes 8257544 | tf_op jit(solution)/shard_map/ppermute | solution.py:57
  225.6 12.8 %collective-permute-done.21.refs_5_ = bf16[1792,256]{1,0:T(8,128)(2,1)S(1)} collective-permute-done((bf16[1792,256]{1,0:T(8,128)(2,1)S(1)}, bf16[1792,256]{1,0:T(8,128)(2,1)S(1)}, u32[]{:S(2)}, u32[]{:S(2)}) %collective-permute-start.21) | collective-permute-done | bytes 917536 | tf_op jit(solution)/shard_map/ppermute | solution.py:57
  238.6 3.7 %collective-permute-start.28 = (bf16[5376,256]{1,0:T(8,128)(2,1)S(1)}, bf16[5376,256]{1,0:T(8,128)(2,1)}, u32[]{:S(2)}, u32[]{:S(2)}) collective-permute-start(bf16[5376,256]{1,0:T(8,128)(2,1)S(1)} %pad_maximum_fusion.1), channel_id=1, source_target_pairs={{0,16},{1,17},{2,18},{3,19},{4,20},{5,21},{6,22},{7,23},{8,24},{9,... | collective-permute-start | bytes 8257544 | tf_op jit(solution)/shard_map/ppermute | solution.py:57
  245.1 7.3 %collective-permute-done.24.refs_8_ = bf16[592,256]{1,0:T(8,128)(2,1)S(1)} collective-permute-done((bf16[592,256]{1,0:T(8,128)(2,1)S(1)}, bf16[592,256]{1,0:T(8,128)(2,1)S(1)}, u32[]{:S(2)}, u32[]{:S(2)}) %collective-permute-start.24) | collective-permute-done | bytes 303136 | tf_op jit(solution)/shard_map/ppermute | solution.py:57
  259.7 40.3 %shard_map.60 = (bf16[4032,128]{1,0:T(8,128)(2,1)}, bf16[4032,128]{1,0:T(8,128)(2,1)}, bf16[7,2048,256]{2,1,0:T(8,128)(2,1)}, bf16[7,1536,256]{2,1,0:T(8,128)(2,...) custom-call(s32[4]{0:T(128)} %copy-done.7, bf16[1792,256]{1,0:T(8,128)(2,1)} %copy-done.6, bf16[1792,256]{1,0:T(8,128)(2,1)} %copy-done.16, ...), custom_call_target="tpu_custom_call" | custom-call | flops 24662507520 | bytes 40000000 | tf_op jit(solution)/shard_map/pallas_call | solution.py:477
  299.9 4.3 %collective-permute-start.30 = (bf16[4032,128]{1,0:T(8,128)(2,1)}, bf16[4032,128]{1,0:T(8,128)(2,1)S(1)}, u32[]{:S(2)}, u32[]{:S(2)}) collective-permute-start(bf16[4032,128]{1,0:T(8,128)(2,1)} %get-tuple-element.90), channel_id=1, source_target_pairs={{0,0},{1,1},{2,2},{3,3},{4,4},{5,5},{6,6},{7,7},{8,16},{9,17},{10,... | collective-permute-start | bytes 3096584 | tf_op jit(solution)/shard_map/ppermute | solution.py:57
  305.0 3.0 copy-done.3
  308.0 2.6 copy-done.9
  311.2 15.4 %shard_map.61 = (bf16[4032,128]{1,0:T(8,128)(2,1)S(1)}, bf16[4032,128]{1,0:T(8,128)(2,1)S(1)}) custom-call(s32[4]{0:T(128)S(1)} %copy-done.8, bf16[7,2048,256]{2,1,0:T(8,128)(2,1)} %get-tuple-element.92.direct, bf16[7,1536,256]{2,1,0:T(8,128)(2,1)S(1)} %copy-done.9, bf16[640,5376]{1,0:T(8,128)(2,1)S(1)} %copy-done.3, ...), custom_call_target="tpu_custom_call" | custom-call | flops 8220835840 | bytes 20000000 | tf_op jit(solution)/shard_map/pallas_call | solution.py:455
  326.8 3.1 collective-permute-start.33
  329.9 22.0 %collective-permute-done.32.r2 = bf16[4032,128]{1,0:T(8,128)(2,1)S(1)} collective-permute-done((bf16[4032,128]{1,0:T(8,128)(2,1)S(1)}, bf16[4032,128]{1,0:T(8,128)(2,1)S(1)}, u32[]{:S(2)}, u32[]{:S(2)}) %collective-permute-start.32) | collective-permute-done | bytes 1032224 | tf_op jit(solution)/shard_map/ppermute | solution.py:57
  352.6 3.2 shard_map.62
  (113 shorter events, 43.2 us)
Async XLA Ops:
  52.8 36.3 %all-to-all-start.1 = ((bf16[16,576,128]{2,1,0:T(8,128)(2,1)}), bf16[16,576,128]{2,1,0:T(8,128)(2,1)}, u32[]{:S(2)}, u32[]{:S(2)}) async-start(bf16[16,576,128]{2,1,0:T(8,128)(2,1)} %copy-done.5), calls=%async_computation.1 | async-start | bytes 4718592 | tf_op jit(solution)/shard_map/all_to_all | solution.py:541
  68.0 41.4 %collective-permute-start = (bf16[7,64,1152]{2,1,0:T(8,128)(2,1)}, bf16[7,64,1152]{2,1,0:T(8,128)(2,1)S(1)}, u32[]{:S(2)}, u32[]{:S(2)}) collective-permute-start(bf16[7,64,1152]{2,1,0:T(8,128)(2,1)} %get-tuple-element.55), channel_id=1, source_target_pairs={{0,0},{1,1},{2,2},{3,3},{4,4},{5,5},{6,6},{7,7},{8,16},{9,17},{10,... | collective-permute-start | bytes 3096584 | tf_op jit(solution)/shard_map/ppermute | solution.py:57
  74.7 34.8 %collective-permute-start.2 = (bf16[7,64,1152]{2,1,0:T(8,128)(2,1)}, bf16[7,64,1152]{2,1,0:T(8,128)(2,1)S(1)}, u32[]{:S(2)}, u32[]{:S(2)}) collective-permute-start(bf16[7,64,1152]{2,1,0:T(8,128)(2,1)} %get-tuple-element.57), channel_id=1, source_target_pairs={{0,4},{1,5},{2,6},{3,7},{4,0},{5,1},{6,2},{7,3},{8,20},{9,21},{10,... | collective-permute-start | bytes 3096584 | tf_op jit(solution)/shard_map/ppermute | solution.py:57
  98.9 31.9 %collective-permute-start.1 = (bf16[7,64,1152]{2,1,0:T(8,128)(2,1)S(1)}, bf16[7,64,1152]{2,1,0:T(8,128)(2,1)S(1)}, u32[]{:S(2)}, u32[]{:S(2)}) collective-permute-start(bf16[7,64,1152]{2,1,0:T(8,128)(2,1)S(1)} %get-tuple-element.56), channel_id=1, source_target_pairs={{0,0},{1,1},{2,2},{3,3},{4,4},{5,5},{6,6},{7,7},{8,16},{9,17},{10,... | collective-permute-start | bytes 3096584 | tf_op jit(solution)/shard_map/ppermute | solution.py:57
  105.0 26.6 %collective-permute-start.3 = (bf16[7,64,1152]{2,1,0:T(8,128)(2,1)S(1)}, bf16[7,64,1152]{2,1,0:T(8,128)(2,1)}, u32[]{:S(2)}, u32[]{:S(2)}) collective-permute-start(bf16[7,64,1152]{2,1,0:T(8,128)(2,1)S(1)} %get-tuple-element.58), channel_id=1, source_target_pairs={{0,4},{1,5},{2,6},{3,7},{4,0},{5,1},{6,2},{7,3},{8,20},{9,21},{10,... | collective-permute-start | bytes 3096584 | tf_op jit(solution)/shard_map/ppermute | solution.py:57
  109.4 22.3 %collective-permute-start.4 = (bf16[7,64,1152]{2,1,0:T(8,128)(2,1)S(1)}, bf16[7,64,1152]{2,1,0:T(8,128)(2,1)}, u32[]{:S(2)}, u32[]{:S(2)}) collective-permute-start(bf16[7,64,1152]{2,1,0:T(8,128)(2,1)S(1)} %collective-permute-done.refs_1_.refs_0_), channel_id=1, source_target_pairs={{0,16},{1,17},{2,18},{3,19},{4,20},{5,21},{6,22},{7,23},{8,24},{9,... | collective-permute-start | bytes 3096584 | tf_op jit(solution)/shard_map/ppermute | solution.py:57
  109.4 22.3 %collective-permute-start.6 = (bf16[7,64,1152]{2,1,0:T(8,128)(2,1)S(1)}, bf16[7,64,1152]{2,1,0:T(8,128)(2,1)}, u32[]{:S(2)}, u32[]{:S(2)}) collective-permute-start(bf16[7,64,1152]{2,1,0:T(8,128)(2,1)S(1)} %collective-permute-done.2.refs_3_.refs_2_), channel_id=1, source_target_pairs={{0,16},{1,17},{2,18},{3,19},{4,20},{5,21},{6,22},{7,23},{8,24},{9,... | collective-permute-start | bytes 3096584 | tf_op jit(solution)/shard_map/ppermute | solution.py:57
  139.9 11.7 %collective-permute-start.8 = (bf16[608,256]{1,0:T(8,128)(2,1)S(1)}, bf16[608,256]{1,0:T(8,128)(2,1)S(1)}, u32[]{:S(2)}, u32[]{:S(2)}) collective-permute-start(bf16[608,256]{1,0:T(8,128)(2,1)S(1)} %get-tuple-element.62), channel_id=1, source_target_pairs={{0,1},{1,2},{2,3},{3,0},{4,5},{5,6},{6,7},{7,4},{8,9},{9,10},{10,1... | collective-permute-start | bytes 933896 | tf_op jit(solution)/shard_map/ppermute | solution.py:57
  141.4 10.2 %collective-permute-start.9 = (bf16[592,256]{1,0:T(8,128)(2,1)S(1)}, bf16[592,256]{1,0:T(8,128)(2,1)S(1)}, u32[]{:S(2)}, u32[]{:S(2)}) collective-permute-start(bf16[592,256]{1,0:T(8,128)(2,1)S(1)} %get-tuple-element.63), channel_id=1, source_target_pairs={{0,3},{1,0},{2,1},{3,2},{4,7},{5,4},{6,5},{7,6},{8,11},{9,8},{10,9... | collective-permute-start | bytes 909320 | tf_op jit(solution)/shard_map/ppermute | solution.py:57
  142.8 8.8 %collective-permute-start.10 = (bf16[592,256]{1,0:T(8,128)(2,1)S(1)}, bf16[592,256]{1,0:T(8,128)(2,1)S(1)}, u32[]{:S(2)}, u32[]{:S(2)}) collective-permute-start(bf16[592,256]{1,0:T(8,128)(2,1)S(1)} %get-tuple-element.64), channel_id=1, source_target_pairs={{0,4},{1,5},{2,6},{3,7},{4,0},{5,1},{6,2},{7,3},{8,12},{9,13},{10,... | collective-permute-start | bytes 909320 | tf_op jit(solution)/shard_map/ppermute | solution.py:57
  152.0 21.2 %collective-permute-start.12 = (bf16[1792,256]{1,0:T(8,128)(2,1)S(1)}, bf16[1792,256]{1,0:T(8,128)(2,1)S(1)}, u32[]{:S(2)}, u32[]{:S(2)}) collective-permute-start(bf16[1792,256]{1,0:T(8,128)(2,1)S(1)} %get-tuple-element.77), channel_id=1, source_target_pairs={{0,3},{1,0},{2,1},{3,2},{4,7},{5,4},{6,5},{7,6},{8,11},{9,8},{10,9... | collective-permute-start | bytes 2752520 | tf_op jit(solution)/shard_map/ppermute | solution.py:57
  153.5 21.8 %collective-permute-start.13 = (bf16[1792,256]{1,0:T(8,128)(2,1)S(1)}, bf16[1792,256]{1,0:T(8,128)(2,1)S(1)}, u32[]{:S(2)}, u32[]{:S(2)}) collective-permute-start(bf16[1792,256]{1,0:T(8,128)(2,1)S(1)} %get-tuple-element.78), channel_id=1, source_target_pairs={{0,1},{1,2},{2,3},{3,0},{4,5},{5,6},{6,7},{7,4},{8,9},{9,10},{10,1... | collective-permute-start | bytes 2752520 | tf_op jit(solution)/shard_map/ppermute | solution.py:57
  153.6 21.7 %collective-permute-start.11 = (bf16[1792,256]{1,0:T(8,128)(2,1)S(1)}, bf16[1792,256]{1,0:T(8,128)(2,1)S(1)}, u32[]{:S(2)}, u32[]{:S(2)}) collective-permute-start(bf16[1792,256]{1,0:T(8,128)(2,1)S(1)} %get-tuple-element.65), channel_id=1, source_target_pairs={{0,4},{1,5},{2,6},{3,7},{4,0},{5,1},{6,2},{7,3},{8,12},{9,13},{10,... | collective-permute-start | bytes 2752520 | tf_op jit(solution)/shard_map/ppermute | solution.py:57
  164.2 28.7 %collective-permute-start.16 = (bf16[1792,256]{1,0:T(8,128)(2,1)S(1)}, bf16[1792,256]{1,0:T(8,128)(2,1)S(1)}, u32[]{:S(2)}, u32[]{:S(2)}) collective-permute-start(bf16[1792,256]{1,0:T(8,128)(2,1)S(1)} %get-tuple-element.81), channel_id=1, source_target_pairs={{0,3},{1,0},{2,1},{3,2},{4,7},{5,4},{6,5},{7,6},{8,11},{9,8},{10,9... | collective-permute-start | bytes 2752520 | tf_op jit(solution)/shard_map/ppermute | solution.py:57
  175.7 19.7 %collective-permute-start.15 = (bf16[1792,256]{1,0:T(8,128)(2,1)S(1)}, bf16[1792,256]{1,0:T(8,128)(2,1)S(1)}, u32[]{:S(2)}, u32[]{:S(2)}) collective-permute-start(bf16[1792,256]{1,0:T(8,128)(2,1)S(1)} %get-tuple-element.80), channel_id=1, source_target_pairs={{0,4},{1,5},{2,6},{3,7},{4,0},{5,1},{6,2},{7,3},{8,12},{9,13},{10,... | collective-permute-start | bytes 2752520 | tf_op jit(solution)/shard_map/ppermute | solution.py:57
  176.8 20.6 %collective-permute-start.14 = (bf16[1792,256]{1,0:T(8,128)(2,1)S(1)}, bf16[1792,256]{1,0:T(8,128)(2,1)S(1)}, u32[]{:S(2)}, u32[]{:S(2)}) collective-permute-start(bf16[1792,256]{1,0:T(8,128)(2,1)S(1)} %get-tuple-element.79), channel_id=1, source_target_pairs={{0,1},{1,2},{2,3},{3,0},{4,5},{5,6},{6,7},{7,4},{8,9},{9,10},{10,1... | collective-permute-start | bytes 2752520 | tf_op jit(solution)/shard_map/ppermute | solution.py:57
  197.9 18.5 %collective-permute-start.19 = (bf16[1792,256]{1,0:T(8,128)(2,1)S(1)}, bf16[1792,256]{1,0:T(8,128)(2,1)S(1)}, u32[]{:S(2)}, u32[]{:S(2)}) collective-permute-start(bf16[1792,256]{1,0:T(8,128)(2,1)S(1)} %shard_map.59.refs_0_), channel_id=1, source_target_pairs={{0,4},{1,5},{2,6},{3,7},{4,0},{5,1},{6,2},{7,3},{8,12},{9,13},{10,... | collective-permute-start | bytes 2752520 | tf_op jit(solution)/shard_map/ppermute | solution.py:57
  198.4 18.2 %collective-permute-start.18 = (bf16[1792,256]{1,0:T(8,128)(2,1)S(1)}, bf16[1792,256]{1,0:T(8,128)(2,1)S(1)}, u32[]{:S(2)}, u32[]{:S(2)}) collective-permute-start(bf16[1792,256]{1,0:T(8,128)(2,1)S(1)} %shard_map.59.refs_0_), channel_id=1, source_target_pairs={{0,3},{1,0},{2,1},{3,2},{4,7},{5,4},{6,5},{7,6},{8,11},{9,8},{10,9... | collective-permute-start | bytes 2752520 | tf_op jit(solution)/shard_map/ppermute | solution.py:57
  198.4 21.1 %collective-permute-start.17 = (bf16[1792,256]{1,0:T(8,128)(2,1)S(1)}, bf16[1792,256]{1,0:T(8,128)(2,1)S(1)}, u32[]{:S(2)}, u32[]{:S(2)}) collective-permute-start(bf16[1792,256]{1,0:T(8,128)(2,1)S(1)} %shard_map.59.refs_0_), channel_id=1, source_target_pairs={{0,1},{1,2},{2,3},{3,0},{4,5},{5,6},{6,7},{7,4},{8,9},{9,10},{10,1... | collective-permute-start | bytes 2752520 | tf_op jit(solution)/shard_map/ppermute | solution.py:57
  216.4 22.0 %collective-permute-start.21 = (bf16[1792,256]{1,0:T(8,128)(2,1)S(1)}, bf16[1792,256]{1,0:T(8,128)(2,1)S(1)}, u32[]{:S(2)}, u32[]{:S(2)}) collective-permute-start(bf16[1792,256]{1,0:T(8,128)(2,1)S(1)} %collective-permute-done.19.refs_3_), channel_id=1, source_target_pairs={{0,1},{1,2},{2,3},{3,0},{4,5},{5,6},{6,7},{7,4},{8,9},{9,10},{10,1... | collective-permute-start | bytes 2752520 | tf_op jit(solution)/shard_map/ppermute | solution.py:57
  216.5 21.9 %collective-permute-start.22 = (bf16[1792,256]{1,0:T(8,128)(2,1)S(1)}, bf16[1792,256]{1,0:T(8,128)(2,1)S(1)}, u32[]{:S(2)}, u32[]{:S(2)}) collective-permute-start(bf16[1792,256]{1,0:T(8,128)(2,1)S(1)} %collective-permute-done.18.refs_2_), channel_id=1, source_target_pairs={{0,3},{1,0},{2,1},{3,2},{4,7},{5,4},{6,5},{7,6},{8,11},{9,8},{10,9... | collective-permute-start | bytes 2752520 | tf_op jit(solution)/shard_map/ppermute | solution.py:57
  219.1 19.4 %collective-permute-start.20 = (bf16[1792,256]{1,0:T(8,128)(2,1)S(1)}, bf16[1792,256]{1,0:T(8,128)(2,1)S(1)}, u32[]{:S(2)}, u32[]{:S(2)}) collective-permute-start(bf16[1792,256]{1,0:T(8,128)(2,1)S(1)} %collective-permute-done.18.refs_2_), channel_id=1, source_target_pairs={{0,4},{1,5},{2,6},{3,7},{4,0},{5,1},{6,2},{7,3},{8,12},{9,13},{10,... | collective-permute-start | bytes 2752520 | tf_op jit(solution)/shard_map/ppermute | solution.py:57
  220.5 37.3 %collective-permute-start.27 = (bf16[5376,256]{1,0:T(8,128)(2,1)S(1)}, bf16[5376,256]{1,0:T(8,128)(2,1)S(1)}, u32[]{:S(2)}, u32[]{:S(2)}) collective-permute-start(bf16[5376,256]{1,0:T(8,128)(2,1)S(1)} %pad_maximum_fusion), channel_id=1, source_target_pairs={{0,16},{1,17},{2,18},{3,19},{4,20},{5,21},{6,22},{7,23},{8,24},{9,... | collective-permute-start | bytes 8257544 | tf_op jit(solution)/shard_map/ppermute | solution.py:57
  238.6 20.7 %collective-permute-start.28 = (bf16[5376,256]{1,0:T(8,128)(2,1)S(1)}, bf16[5376,256]{1,0:T(8,128)(2,1)}, u32[]{:S(2)}, u32[]{:S(2)}) collective-permute-start(bf16[5376,256]{1,0:T(8,128)(2,1)S(1)} %pad_maximum_fusion.1), channel_id=1, source_target_pairs={{0,16},{1,17},{2,18},{3,19},{4,20},{5,21},{6,22},{7,23},{8,24},{9,... | collective-permute-start | bytes 8257544 | tf_op jit(solution)/shard_map/ppermute | solution.py:57
  242.3 12.0 %collective-permute-start.23 = (bf16[608,256]{1,0:T(8,128)(2,1)S(1)}, bf16[608,256]{1,0:T(8,128)(2,1)S(1)}, u32[]{:S(2)}, u32[]{:S(2)}) collective-permute-start(bf16[608,256]{1,0:T(8,128)(2,1)S(1)} %slice.17), channel_id=1, source_target_pairs={{0,3},{1,0},{2,1},{3,2},{4,7},{5,4},{6,5},{7,6},{8,11},{9,8},{10,9... | collective-permute-start | bytes 933896 | tf_op jit(solution)/shard_map/ppermute | solution.py:57
  243.4 9.0 %collective-permute-start.24 = (bf16[592,256]{1,0:T(8,128)(2,1)S(1)}, bf16[592,256]{1,0:T(8,128)(2,1)S(1)}, u32[]{:S(2)}, u32[]{:S(2)}) collective-permute-start(bf16[592,256]{1,0:T(8,128)(2,1)S(1)} %slice.18), channel_id=1, source_target_pairs={{0,1},{1,2},{2,3},{3,0},{4,5},{5,6},{6,7},{7,4},{8,9},{9,10},{10,1... | collective-permute-start | bytes 909320 | tf_op jit(solution)/shard_map/ppermute | solution.py:57
  244.0 10.3 %collective-permute-start.25 = (bf16[592,256]{1,0:T(8,128)(2,1)S(1)}, bf16[592,256]{1,0:T(8,128)(2,1)S(1)}, u32[]{:S(2)}, u32[]{:S(2)}) collective-permute-start(bf16[592,256]{1,0:T(8,128)(2,1)S(1)} %slice.19), channel_id=1, source_target_pairs={{0,4},{1,5},{2,6},{3,7},{4,0},{5,1},{6,2},{7,3},{8,12},{9,13},{10,... | collective-permute-start | bytes 909320 | tf_op jit(solution)/shard_map/ppermute | solution.py:57
  252.5 4.0 %collective-permute-start.26 = (bf16[1792,256]{1,0:T(8,128)(2,1)S(1)}, bf16[1792,256]{1,0:T(8,128)(2,1)S(1)}, u32[]{:S(2)}, u32[]{:S(2)}) collective-permute-start(bf16[1792,256]{1,0:T(8,128)(2,1)S(1)} %shard_map.59.refs_0_), channel_id=1, source_target_pairs={{0,16},{1,17},{2,18},{3,19},{4,20},{5,21},{6,22},{7,23},{8,24},{9,... | collective-permute-start | bytes 2752520 | tf_op jit(solution)/shard_map/ppermute | solution.py:57
  299.9 29.9 %collective-permute-start.30 = (bf16[4032,128]{1,0:T(8,128)(2,1)}, bf16[4032,128]{1,0:T(8,128)(2,1)S(1)}, u32[]{:S(2)}, u32[]{:S(2)}) collective-permute-start(bf16[4032,128]{1,0:T(8,128)(2,1)} %get-tuple-element.90), channel_id=1, source_target_pairs={{0,0},{1,1},{2,2},{3,3},{4,4},{5,5},{6,6},{7,7},{8,16},{9,17},{10,... | collective-permute-start | bytes 3096584 | tf_op jit(solution)/shard_map/ppermute | solution.py:57
  304.2 25.6 %collective-permute-start.31 = (bf16[4032,128]{1,0:T(8,128)(2,1)}, bf16[4032,128]{1,0:T(8,128)(2,1)S(1)}, u32[]{:S(2)}, u32[]{:S(2)}) collective-permute-start(bf16[4032,128]{1,0:T(8,128)(2,1)} %get-tuple-element.91), channel_id=1, source_target_pairs={{0,4},{1,5},{2,6},{3,7},{4,0},{5,1},{6,2},{7,3},{8,20},{9,21},{10,... | collective-permute-start | bytes 3096584 | tf_op jit(solution)/shard_map/ppermute | solution.py:57
  326.7 25.2 %collective-permute-start.32 = (bf16[4032,128]{1,0:T(8,128)(2,1)S(1)}, bf16[4032,128]{1,0:T(8,128)(2,1)S(1)}, u32[]{:S(2)}, u32[]{:S(2)}) collective-permute-start(bf16[4032,128]{1,0:T(8,128)(2,1)S(1)} %get-tuple-element.96), channel_id=1, source_target_pairs={{0,8},{1,9},{2,10},{3,11},{4,12},{5,13},{6,14},{7,15},{8,24},{9,25... | collective-permute-start | bytes 3096584 | tf_op jit(solution)/shard_map/ppermute | solution.py:57
  326.8 25.8 %collective-permute-start.33 = (bf16[4032,128]{1,0:T(8,128)(2,1)S(1)}, bf16[4032,128]{1,0:T(8,128)(2,1)S(1)}, u32[]{:S(2)}, u32[]{:S(2)}) collective-permute-start(bf16[4032,128]{1,0:T(8,128)(2,1)S(1)} %get-tuple-element.97), channel_id=1, source_target_pairs={{0,12},{1,13},{2,14},{3,15},{4,8},{5,9},{6,10},{7,11},{8,28},{9,29... | collective-permute-start | bytes 3096584 | tf_op jit(solution)/shard_map/ppermute | solution.py:57
  (26 other events, 276.7 us)

commit v3 on v2

--- a/solution.py
+++ b/solution.py
@@ -19,8 +19,7 @@
 HEIGHT = 896
 HALF = 1152
 TILE = 128
-PART = 64
-SENT = HALF // TILE * PART
+SPLIT = ((0, 80), (80, 48))
 LABEL = 16
 SIDE = 256
 BLOCKS = ROWS // SIDE
@@ -28,6 +27,7 @@
 CHUNK = HALF_BLOCKS * SIDE
 PARTS = ((0, 608), (608, 592), (1200, 592))
 WIDE = 640
+SHARE = 576
 AROUND = ROWS + CHUNK
 BACK_ROWS = 4032
 
@@ -87,10 +87,10 @@
         slot = details[o]
         for j in range(HALF // TILE):
             piece = held[slot, :, j * TILE : (j + 1) * TILE]
-            first[o, j * PART : (j + 1) * PART, :] = piece[:PART]
-            second[o, j * PART : (j + 1) * PART, :] = piece[PART:]
+            for (row, size), out in zip(SPLIT, (first, second)):
+                out[o, j * size : (j + 1) * size, :] = piece[row : row + size]
         place = jnp.full((LABEL, TILE), details[16 + o], jnp.int32)
-        first[o, SENT:, :] = place.astype(F32).astype(BF16)
+        first[o, first.shape[1] - LABEL :, :] = place.astype(F32).astype(BF16)
         for copy in copies(o):
             copy.start()
 
@@ -102,7 +102,8 @@
 
 def pack(details, tiles):
     n = details.shape[0] // 2
-    shapes = [(n, SENT + LABEL, TILE), (n, SENT, TILE)]
+    rows = [HALF // TILE * size for _, size in SPLIT]
+    shapes = [(n, rows[0] + LABEL, TILE), (n, rows[1], TILE)]
     return pl.pallas_call(
         pack_kernel,
         in_specs=[SMEM, HBM],
@@ -111,26 +112,27 @@
         scratch_shapes=[pltpu.VMEM(tiles.shape, BF16)]
         + [pltpu.VMEM(shape, BF16) for shape in shapes]
         + [pltpu.SemaphoreType.DMA((tiles.shape[0],)), pltpu.SemaphoreType.DMA((2, n))],
-        compiler_params=pltpu.CompilerParams(vmem_limit_bytes=32 * MIB),
-        cost_estimate=cost(0, 4 * n * SENT * TILE * 2),
+        compiler_params=pltpu.CompilerParams(vmem_limit_bytes=62 * MIB),
+        cost_estimate=cost(0, 4 * tiles.size),
     )(details, tiles)
 
 
 def momentum_kernel(part, info, arrived, momentum, *refs):
     new, half0, half1, tile, old, fresh, rounded, in_sems, out_sems = refs[-9:]
     n = HEIGHT // TILE
+    row, size = SPLIT[part]
 
     def place(t, r):
         half = (t + info[14]) % 2
         columns = pl.ds(pl.multiple_of(half * HALF, TILE), HALF)
-        return pl.ds(pl.multiple_of(r * TILE + part * PART, PART), PART), columns
+        return pl.ds(pl.multiple_of(r * TILE + row, 16), size), columns
 
     def reads(t, r):
         source = info[2 * r + (t + info[14]) % 2]
         i = t * n + r
         return (
             pltpu.make_async_copy(momentum.at[place(t, r)], old.at[i], in_sems.at[0, i]),
-            pltpu.make_async_copy(arrived.at[source, 0:SENT], tile.at[i], in_sems.at[1, i]),
+            pltpu.make_async_copy(arrived.at[source, 0 : HALF // TILE * size], tile.at[i], in_sems.at[1, i]),
         )
 
     def writes(t, r):
@@ -154,7 +156,7 @@
                 copy.wait()
             for j in range(HALF // TILE):
                 columns = slice(j * TILE, (j + 1) * TILE)
-                g = tile[i, j * PART : (j + 1) * PART, :].astype(F32)
+                g = tile[i, j * size : (j + 1) * size, :].astype(F32)
                 later = MOMENTUM_RATE * old[i, :, columns] + g
                 fresh[i, :, columns] = later
                 rounded[i, :, columns] = (g + MOMENTUM_RATE * later).astype(BF16)
@@ -172,25 +174,26 @@
 def update_momentum(info, arrived, momentum, part, so_far):
     more = () if so_far is None else (so_far,)
     n = 2 * HEIGHT // TILE
+    size = SPLIT[part][1]
     return pl.pallas_call(
         lambda *refs: momentum_kernel(part, *refs),
         in_specs=[SMEM] + [HBM] * (2 + len(more)),
         out_specs=[HBM] * 3,
         out_shape=[
             jax.ShapeDtypeStruct(momentum.shape, F32),
-            jax.ShapeDtypeStruct((n // 2, PART, HALF), BF16),
-            jax.ShapeDtypeStruct((n // 2, PART, HALF), BF16),
+            jax.ShapeDtypeStruct((n // 2, size, HALF), BF16),
+            jax.ShapeDtypeStruct((n // 2, size, HALF), BF16),
         ],
         scratch_shapes=[
-            pltpu.VMEM((n, SENT, TILE), BF16),
-            pltpu.VMEM((n, PART, HALF), F32),
-            pltpu.VMEM((n, PART, HALF), F32),
-            pltpu.VMEM((n, PART, HALF), BF16),
+            pltpu.VMEM((n, HALF // TILE * size, TILE), BF16),
+            pltpu.VMEM((n, size, HALF), F32),
+            pltpu.VMEM((n, size, HALF), F32),
+            pltpu.VMEM((n, size, HALF), BF16),
             pltpu.SemaphoreType.DMA((2, n)),
             pltpu.SemaphoreType.DMA((2, n)),
         ],
         input_output_aliases={3: 0} if more else {},
-        compiler_params=pltpu.CompilerParams(vmem_limit_bytes=32 * MIB),
+        compiler_params=pltpu.CompilerParams(vmem_limit_bytes=62 * MIB),
         cost_estimate=cost(0, HEIGHT * HALF * 12),
     )(info, arrived, momentum, *more)
 
@@ -203,12 +206,14 @@
         core = 1 - c if other else c
         z = 2 * core + (a + t) % 2
         src = block if columns is None else block.at[:, :, columns]
-        copies.append((src, panel.at[pl.ds(z * (HEIGHT // TILE), HEIGHT // TILE), part]))
+        row, size = SPLIT[part]
+        rows = pl.ds(z * (HEIGHT // TILE), HEIGHT // TILE)
+        copies.append((src, panel.at[rows, row : row + size]))
     return copies
 
 
 def panel_shape(width):
-    return pltpu.VMEM((ROWS // TILE, TILE // PART, PART, width), BF16)
+    return pltpu.VMEM((ROWS // TILE, TILE, width), BF16)
 
 
 def chip_at(info, flip, dy):
@@ -300,11 +305,14 @@
 
 
 def turn_kernel(info, *refs):
-    blocks, out, held, sems = refs[:8], refs[8], refs[9], refs[10]
-    shift = pl.multiple_of(512 * info[0], TILE)
+    blocks, out, held, flat, sems = refs[:8], *refs[8:]
+    c = info[0]
+    shift = pl.multiple_of(512 * c, TILE)
     load_all(panel_copies(info, blocks, held, pl.ds(shift, WIDE)), sems)
     for r in range(ROWS // TILE):
-        out[:, r * TILE : (r + 1) * TILE] = held[r].reshape(TILE, WIDE).T
+        flat[:, r * TILE : (r + 1) * TILE] = held[r].T
+    out[:512, :ROWS] = flat[pl.ds(pl.multiple_of(128 * c, 64), 512), :]
+    out[512:, :ROWS] = flat[pl.ds(pl.multiple_of(512 - 448 * c, 64), 64), :]
     out[:, ROWS:] = out[:, :CHUNK]
 
 
@@ -313,8 +321,8 @@
         turn_kernel,
         in_specs=[SMEM] + [HBM] * 8,
         out_specs=VMEM,
-        out_shape=jax.ShapeDtypeStruct((WIDE, AROUND), BF16),
-        scratch_shapes=[panel_shape(WIDE), pltpu.SemaphoreType.DMA((8,))],
+        out_shape=jax.ShapeDtypeStruct((SHARE, AROUND), BF16),
+        scratch_shapes=[panel_shape(WIDE), pltpu.VMEM((WIDE, ROWS), BF16), pltpu.SemaphoreType.DMA((8,))],
         compiler_params=pltpu.CompilerParams(vmem_limit_bytes=24 * MIB),
         cost_estimate=cost(0, 1.2e7),
     )(info, *blocks)
@@ -327,7 +335,7 @@
     own, ends, swapped = refs[:7], refs[7:10], refs[10:14]
     turned = refs[14]
     outs, rest_direct, rest_flipped, all_mixed, scales = refs[15:17], *refs[17:21]
-    direct, flipped, panel, mixed, stage, sems, panel_sem, out_sems, keep_sems = refs[21:]
+    direct, flipped, panel, mixed, stage, extra, sems, panel_sem, out_sems, keep_sems = refs[21:]
     c = info[0]
     panel_copy = pltpu.make_async_copy(turned, panel, panel_sem)
     panel_copy.start()
@@ -407,7 +415,7 @@
         result = scale * (COEF_LINEAR * panel[:, columns].astype(F32) + product(i, mixed))
         stage[pl.ds(pl.multiple_of(b * SIDE, SIDE), SIDE)] = result.astype(BF16).T
 
-    send_back(info, stage, outs, out_sems)
+    send_back(info, stage, extra, outs, out_sems)
     for copy in keeps:
         copy.wait()
 
@@ -419,22 +427,22 @@
     return result + jnp.dot(x[:, rest], flipped[...], preferred_element_type=F32)
 
 
-def send_back(info, stage, outs, sems):
-    c, a = info[0], info[2]
+def send_back(info, stage, extra, outs, sems):
+    a = info[2]
     sends = []
     for side, out in enumerate(outs):
         owner = 1 - a if side else a
         start = pl.multiple_of(owner * HEIGHT, 128)
         for j in range(4):
-            columns = pl.ds(pl.multiple_of((j + c) * TILE, TILE), TILE)
-            sends.append((stage.at[pl.ds(start, HEIGHT), columns], out.at[pl.ds(j * HEIGHT, HEIGHT)]))
-        columns = pl.ds(pl.multiple_of(4 * (1 - c) * TILE, TILE), TILE)
-        shared = pl.ds(pl.multiple_of(start + 448 * c, 64), 448)
-        sends.append((stage.at[shared, columns], out.at[pl.ds(4 * HEIGHT, 448)]))
+            rows = pl.ds(start, HEIGHT)
+            sends.append((stage.at[rows, j * TILE : (j + 1) * TILE], out.at[pl.ds(j * HEIGHT, HEIGHT)]))
+        halves = [stage[pl.ds(pl.multiple_of(start + row, 64), 448), 512:] for row in (0, 448)]
+        extra[side] = jnp.concatenate(halves, axis=1)
+        sends.append((extra.at[side], out.at[pl.ds(4 * HEIGHT, 448)]))
     load_all(sends, sems)
 
 
-def rest_kernel(info, direct, flipped, panel, all_mixed, scales, out0, out1, mixed, stage, sems):
+def rest_kernel(info, direct, flipped, panel, all_mixed, scales, out0, out1, mixed, stage, extra, sems):
     b = pl.program_id(0)
 
     @pl.when(b == 0)
@@ -448,7 +456,7 @@
 
     @pl.when(b == HALF_BLOCKS - 1)
     def _():
-        send_back(info, stage, (out0, out1), sems)
+        send_back(info, stage, extra, (out0, out1), sems)
 
 
 def apply_rest(info, direct, flipped, mixed, scales, turned):
@@ -460,16 +468,21 @@
             in_specs=[
                 pl.BlockSpec((1, 8 * SIDE, SIDE), lambda b, s: (b, 0, 0)),
                 pl.BlockSpec((1, 6 * SIDE, SIDE), lambda b, s: (b, 0, 0)),
-                pl.BlockSpec((WIDE, SIDE), lambda b, s: (0, (1 - s[0]) * HALF_BLOCKS + b)),
+                pl.BlockSpec((SHARE, SIDE), lambda b, s: (0, (1 - s[0]) * HALF_BLOCKS + b)),
                 HBM,
                 VMEM,
             ],
             out_specs=[HBM] * 2,
-            scratch_shapes=[pltpu.VMEM((WIDE, AROUND), BF16), pltpu.VMEM((CHUNK, WIDE), BF16), pltpu.SemaphoreType.DMA((10,))],
+            scratch_shapes=[
+                pltpu.VMEM((SHARE, AROUND), BF16),
+                pltpu.VMEM((CHUNK, SHARE), BF16),
+                pltpu.VMEM((2, 448, TILE), BF16),
+                pltpu.SemaphoreType.DMA((10,)),
+            ],
         ),
         out_shape=[jax.ShapeDtypeStruct((BACK_ROWS, TILE), BF16)] * 2,
-        compiler_params=pltpu.CompilerParams(vmem_limit_bytes=40 * MIB),
-        cost_estimate=cost(ROWS * ROWS * WIDE, 2e7),
+        compiler_params=pltpu.CompilerParams(vmem_limit_bytes=62 * MIB),
+        cost_estimate=cost(ROWS * ROWS * SHARE, 2e7),
     )(info, direct, flipped, turned, mixed, scales)
 
 
@@ -482,22 +495,23 @@
         + [
             jax.ShapeDtypeStruct((HALF_BLOCKS, 8 * SIDE, SIDE), BF16),
             jax.ShapeDtypeStruct((HALF_BLOCKS, 6 * SIDE, SIDE), BF16),
-            jax.ShapeDtypeStruct((WIDE, AROUND), BF16),
+            jax.ShapeDtypeStruct((SHARE, AROUND), BF16),
             jax.ShapeDtypeStruct((8, SIDE), F32),
         ],
         scratch_shapes=[
             pltpu.VMEM((BLOCKS, 8 * SIDE, SIDE), BF16),
             pltpu.VMEM((BLOCKS, 6 * SIDE, SIDE), BF16),
-            pltpu.VMEM((WIDE, AROUND), BF16),
-            pltpu.VMEM((WIDE, AROUND), BF16),
-            pltpu.VMEM((CHUNK, WIDE), BF16),
+            pltpu.VMEM((SHARE, AROUND), BF16),
+            pltpu.VMEM((SHARE, AROUND), BF16),
+            pltpu.VMEM((CHUNK, SHARE), BF16),
+            pltpu.VMEM((2, 448, TILE), BF16),
             pltpu.SemaphoreType.DMA((32,)),
             pltpu.SemaphoreType.DMA,
             pltpu.SemaphoreType.DMA((10,)),
             pltpu.SemaphoreType.DMA((3,)),
         ],
         compiler_params=pltpu.CompilerParams(vmem_limit_bytes=58 * MIB),
-        cost_estimate=cost(3 * ROWS * ROWS * WIDE, 4e7),
+        cost_estimate=cost(3 * ROWS * ROWS * SHARE, 4e7),
     )(info, *own, *ends, *swapped, turned)
 
 
@@ -509,9 +523,13 @@
         for j in range(4):
             start = pl.multiple_of((9 * side + j + 5 * core) * TILE, TILE)
             update[:, pl.ds(start, TILE)] = got[j * HEIGHT : (j + 1) * HEIGHT]
-        start = pl.multiple_of((9 * side + 4) * TILE, TILE)
-        rows = pl.ds(pl.multiple_of(448 * core, 64), 448)
-        update[rows, pl.ds(start, TILE)] = got[4 * HEIGHT :]
+    for s, (one, two) in enumerate(((r0, r2), (r1, r3))):
+        side = 1 - a if s else a
+        one, two = one[4 * HEIGHT :], two[4 * HEIGHT :]
+        low, high = jnp.where(m == 0, one, two), jnp.where(m == 0, two, one)
+        tile = pl.ds(pl.multiple_of((9 * side + 4) * TILE, TILE), TILE)
+        update[:448, tile] = jnp.concatenate([low[:, :64], high[:, :64]], axis=1)
+        update[448:, tile] = jnp.concatenate([low[:, 64:], high[:, 64:]], axis=1)
 
 
 def unpack(info, parts):
@@ -540,7 +558,7 @@
     lower, _ = lax.optimization_barrier((lower, upper))
     lower = lax.all_to_all(lower, PLANE, split_axis=0, concat_axis=0, tiled=True)
 
-    got_labels = upper[:, SENT, 0].astype(jnp.int32)
+    got_labels = upper[:, -1, 0].astype(jnp.int32)
     found = got_labels[None, :] == jnp.arange(tile_count, dtype=jnp.int32)[:, None]
     sources = jnp.sum(jnp.where(found, jnp.arange(16, dtype=jnp.int32)[None, :], 0), axis=1)
     details = jnp.concatenate([sources, zl[None].astype(jnp.int32)])

time: 357 us -> 350 us (0.980)
  local copies, waits for them, and re-layouts: 17.8 us -> 5.03 us
  blocking collectives: 39.4 us -> 46 us
  Pallas kernels: 109 us -> 104 us
  waiting for transfers between devices: 131 us -> 135 us
    unnamed x46 -> x44, local copies, waits for them, and re-layouts: 17.8 us -> 4.96 us
    ppermute x34, waiting for transfers between devices: 117 us -> 127 us  [move(): return lax.ppermute(x, AXES[1:], pairs)]
    all_to_all x1, blocking collectives: 39.4 us -> 46 us  [on_device(): lax.all_to_all(upper, PLANE, split_axis=0, concat_axis=0, tiled=True)]
    all_to_all x1, waiting for transfers between devices: 14.4 us -> 8.11 us  [on_device(): lax.all_to_all(lower, PLANE, split_axis=0, concat_axis=0, tiled=True)]
    pallas_call x1, Pallas kernels: 9.03 us -> 5.37 us  [pack(): pl.pallas_call(pack_kernel, in_specs=[SMEM, HBM], out_specs=[HBM] * 2, ou...]
  transfers between devices with their start and end apart: 35 -> 35, of which waited for: 19 -> 20; matrix products, arithmetic and copies ran while one was open for 0% -> 0% of each run, Pallas kernels for 14% -> 15%
where the time goes in v3:
time: 350 us; the launch traced here: 349 us
  waiting for transfers between devices  135 us (39%)
  Pallas kernels  104 us (30%)
  starting transfers between devices  53.8 us (15%)
  blocking collectives  46 us (13%)
  local copies, waits for them, and re-layouts  5.03 us (1%)
  other arithmetic  3.6 us (1%)
    ppermute x34, waiting for transfers between devices, move(): return lax.ppermute(x, AXES[1:], pairs)  127 us
    ppermute x34, starting transfers between devices, move(): return lax.ppermute(x, AXES[1:], pairs)  49.4 us
    all_to_all x1, blocking collectives, on_device(): lax.all_to_all(upper, PLANE, split_axis=0, concat_axis=0, tiled=True)  46 us
    pallas_call x1, Pallas kernels, apply_poly(): pl.pallas_call(apply_kernel, in_specs=[SMEM] + [HBM] * 15, out_specs=[HBM...  37.7 us
    pallas_call x3, Pallas kernels, gram_chunks(): pl.pallas_call(lambda *refs: gram_kernel(dests, *refs), in_specs=[SMEM] +...  22.8 us
    pallas_call x1, Pallas kernels, apply_rest(): pl.pallas_call(rest_kernel, grid_spec=pltpu.PrefetchScalarGridSpec(num_sc...  16.5 us
    pallas_call x2, Pallas kernels, update_momentum(): pl.pallas_call(lambda *refs: momentum_kernel(part, *refs), in_specs=[SMEM...  12.5 us
    all_to_all x1, waiting for transfers between devices, on_device(): lax.all_to_all(lower, PLANE, split_axis=0, concat_axis=0, tiled=True)  8.11 us
  transfers between devices with their start and end apart: 35, of which 20 were waited for; matrix products, arithmetic and copies ran while one was open for 0% of the time, Pallas kernels for 15%

profile of v3, /device:TPU:1, one launch (start us, length us, event | category | flops | bytes accessed | tf_op | source)
XLA Modules:
  0.0 348.6 jit_solution(774349557776958797)
XLA Ops:
  2.7 5.4 %shard_map.50 = (bf16[16,736,128]{2,1,0:T(8,128)(2,1)}, bf16[16,432,128]{2,1,0:T(8,128)(2,1)}) custom-call(s32[32]{0:T(128)} %pad_add_fusion.details, bf16[14,128,1152]{2,1,0:T(8,128)(2,1)} %tiles.1), custom_call_target="tpu_custom_call" | custom-call | bytes 8257536 | tf_op jit(solution)/shard_map/pallas_call | solution.py:107
  8.0 46.0 %all_to_all.10.refs_1_ = bf16[16,736,128]{2,1,0:T(8,128)(2,1)S(1)} all-to-all(bf16[16,736,128]{2,1,0:T(8,128)(2,1)} %get-tuple-element.50), channel_id=1, replica_groups=mesh['x'=4,'core'=2,'zm'=2,'zl'=2,'y'=4] {'zm','zl','y'}, dimensions={0} | all-to-all | bytes 6029312 | tf_op jit(solution)/shard_map/all_to_all | solution.py:557
  54.0 4.4 %all-to-all-start.1 = ((bf16[16,432,128]{2,1,0:T(8,128)(2,1)}), bf16[16,432,128]{2,1,0:T(8,128)(2,1)}, u32[]{:S(2)}, u32[]{:S(2)}) async-start(bf16[16,432,128]{2,1,0:T(8,128)(2,1)} %get-tuple-element.52), calls=%async_computation.1 | async-start | bytes 3538944 | tf_op jit(solution)/shard_map/all_to_all | solution.py:559
  59.5 7.1 %shard_map.51 = (f32[896,2304]{1,0:T(8,128)}, bf16[7,80,1152]{2,1,0:T(8,128)(2,1)}, bf16[7,80,1152]{2,1,0:T(8,128)(2,1)}) custom-call(s32[15]{0:T(128)} %pad_add_fusion.1.refs_0_, bf16[16,736,128]{2,1,0:T(8,128)(2,1)} %copy-done.8, f32[896,2304]{1,0:T(8,128)} %refs_2_.3), custom_call_target="tpu_custom_call" | custom-call | bytes 12386304 | tf_op jit(solution)/shard_map/pallas_call | solution.py:178
  66.6 6.6 %collective-permute-start = (bf16[7,80,1152]{2,1,0:T(8,128)(2,1)}, bf16[7,80,1152]{2,1,0:T(8,128)(2,1)S(1)}, u32[]{:S(2)}, u32[]{:S(2)}) collective-permute-start(bf16[7,80,1152]{2,1,0:T(8,128)(2,1)} %get-tuple-element.55), channel_id=1, source_target_pairs={{0,0},{1,1},{2,2},{3,3},{4,4},{5,5},{6,6},{7,7},{8,16},{9,17},{10,... | collective-permute-start | bytes 3870728 | tf_op jit(solution)/shard_map/ppermute | solution.py:57
  73.4 8.1 %all-to-all-done.1.refs_1_ = bf16[16,432,128]{2,1,0:T(8,128)(2,1)} async-done(((bf16[16,432,128]{2,1,0:T(8,128)(2,1)}), bf16[16,432,128]{2,1,0:T(8,128)(2,1)}, u32[]{:S(2)}, u32[]{:S(2)}) %all-to-all-start.1) | async-done | bytes 1769504 | tf_op jit(solution)/shard_map/all_to_all | solution.py:559
  81.5 5.4 %shard_map.52 = (f32[896,2304]{1,0:T(8,128)}, bf16[7,48,1152]{2,1,0:T(8,128)(2,1)}, bf16[7,48,1152]{2,1,0:T(8,128)(2,1)}) custom-call(s32[15]{0:T(128)} %pad_add_fusion.1.refs_0_, bf16[16,432,128]{2,1,0:T(8,128)(2,1)} %all-to-all-done.1.refs_1_, f32[896,2304]{1,0:T(8,128)} %refs_2_.3, ...), custom_call_target="tpu_custom_call", output_to_operand_aliasing={{0}: (3, {})} | custom-call | bytes 12386304 | tf_op jit(solution)/shard_map/pallas_call | solution.py:178
  86.9 7.1 %collective-permute-start.1 = (bf16[7,48,1152]{2,1,0:T(8,128)(2,1)}, bf16[7,48,1152]{2,1,0:T(8,128)(2,1)}, u32[]{:S(2)}, u32[]{:S(2)}) collective-permute-start(bf16[7,48,1152]{2,1,0:T(8,128)(2,1)} %get-tuple-element.56), channel_id=1, source_target_pairs={{0,0},{1,1},{2,2},{3,3},{4,4},{5,5},{6,6},{7,7},{8,16},{9,17},{10,... | collective-permute-start | bytes 2322440 | tf_op jit(solution)/shard_map/ppermute | solution.py:57
  94.1 15.8 %collective-permute-done.refs_1_.refs_0_ = bf16[7,80,1152]{2,1,0:T(8,128)(2,1)S(1)} collective-permute-done((bf16[7,80,1152]{2,1,0:T(8,128)(2,1)}, bf16[7,80,1152]{2,1,0:T(8,128)(2,1)S(1)}, u32[]{:S(2)}, u32[]{:S(2)}) %collective-permute-start) | collective-permute-done | bytes 1290272 | tf_op jit(solution)/shard_map/ppermute | solution.py:57
  110.4 15.3 %collective-permute-done.1.refs_2_.refs_1_ = bf16[7,48,1152]{2,1,0:T(8,128)(2,1)} collective-permute-done((bf16[7,48,1152]{2,1,0:T(8,128)(2,1)}, bf16[7,48,1152]{2,1,0:T(8,128)(2,1)}, u32[]{:S(2)}, u32[]{:S(2)}) %collective-permute-start.1) | collective-permute-done | bytes 774176 | tf_op jit(solution)/shard_map/ppermute | solution.py:57
  129.4 4.8 %shard_map.54 = (bf16[608,256]{1,0:T(8,128)(2,1)S(1)}, bf16[592,256]{1,0:T(8,128)(2,1)S(1)}, bf16[592,256]{1,0:T(8,128)(2,1)S(1)}) custom-call(s32[4]{0:T(128)S(1)} %pad_add_fusion.2.refs_0_.info, bf16[7,80,1152]{2,1,0:T(8,128)(2,1)S(1)} %collective-permute-done.refs_1_.refs_0_, bf16[7,48,1152]{2,1,0:T(8,128)(2,1)} %collective-permute-done.1.refs_2_.refs_1_, ...), custom_call_target="tpu_custom_call" | custom-call | flops 1056964608 | bytes 10135008 | tf_op jit(solution)/shard_map/pallas_call | solution.py:261
  137.8 8.5 %shard_map.53 = (f32[1792,256]{1,0:T(8,128)S(1)}, f32[1792,256]{1,0:T(8,128)S(1)}, f32[1792,256]{1,0:T(8,128)S(1)}) custom-call(s32[4]{0:T(128)S(1)} %pad_add_fusion.2.refs_0_.info, bf16[7,80,1152]{2,1,0:T(8,128)(2,1)S(1)} %collective-permute-done.refs_1_.refs_0_, bf16[7,48,1152]{2,1,0:T(8,128)(2,1)} %collective-permute-done.1.refs_2_.refs_1_, ...), custom_call_target="tpu_custom_call" | custom-call | flops 3170893824 | bytes 13805024 | tf_op jit(solution)/shard_map/pallas_call | solution.py:261
  148.8 9.6 %shard_map.56 = (f32[1792,256]{1,0:T(8,128)S(1)}, f32[1792,256]{1,0:T(8,128)S(1)}, bf16[1792,256]{1,0:T(8,128)(2,1)S(1)}, f32[1792,256]{1,0:T(8,128)S(1)}) custom-call(s32[4]{0:T(128)S(1)} %pad_add_fusion.2.refs_0_.info, bf16[7,80,1152]{2,1,0:T(8,128)(2,1)S(1)} %collective-permute-done.refs_1_.refs_0_, ...), custom_call_target="tpu_custom_call" | custom-call | flops 4227858432 | bytes 15640032 | tf_op jit(solution)/shard_map/pallas_call | solution.py:261
  158.4 2.4 collective-permute-start.16
  160.8 7.1 %collective-permute-done.12.g2 = bf16[1792,256]{1,0:T(8,128)(2,1)S(1)} collective-permute-done((bf16[1792,256]{1,0:T(8,128)(2,1)S(1)}, bf16[1792,256]{1,0:T(8,128)(2,1)S(1)}, u32[]{:S(2)}, u32[]{:S(2)}) %collective-permute-start.12) | collective-permute-done | bytes 917536 | tf_op jit(solution)/shard_map/ppermute | solution.py:57
  171.6 4.2 %shard_map.58.turned.refs_14_.panel = bf16[576,5376]{1,0:T(8,128)(2,1)S(1)} custom-call(s32[4]{0:T(128)S(1)} %pad_add_fusion.2.refs_0_.info, bf16[7,80,1152]{2,1,0:T(8,128)(2,1)S(1)} %copy-done.2, bf16[7,48,1152]{2,1,0:T(8,128)(2,1)} %collective-permute-done.1.refs_2_.refs_1_, bf16[7,80,1152]{2,1,0:T(8,128)(2,1)} %collective-permute-done.2.refs_3_.refs_2_, ...), custom_call_target="tpu_custom_call" | custom-call | bytes 12000000 | tf_op jit(solution)/shard_map/pallas_call | solution.py:320
  175.8 11.7 %collective-permute-done.16.v3 = bf16[1792,256]{1,0:T(8,128)(2,1)S(1)} collective-permute-done((bf16[1792,256]{1,0:T(8,128)(2,1)S(1)}, bf16[1792,256]{1,0:T(8,128)(2,1)S(1)}, u32[]{:S(2)}, u32[]{:S(2)}) %collective-permute-start.16) | collective-permute-done | bytes 917536 | tf_op jit(solution)/shard_map/ppermute | solution.py:57
  187.6 2.5 collective-permute-done.15.v2
  194.5 15.8 %collective-permute-done.19.refs_3_ = bf16[1792,256]{1,0:T(8,128)(2,1)S(1)} collective-permute-done((bf16[1792,256]{1,0:T(8,128)(2,1)S(1)}, bf16[1792,256]{1,0:T(8,128)(2,1)S(1)}, u32[]{:S(2)}, u32[]{:S(2)}) %collective-permute-start.19) | collective-permute-done | bytes 917536 | tf_op jit(solution)/shard_map/ppermute | solution.py:57
  215.1 5.1 %collective-permute-start.27 = (bf16[5376,256]{1,0:T(8,128)(2,1)S(1)}, bf16[5376,256]{1,0:T(8,128)(2,1)S(1)}, u32[]{:S(2)}, u32[]{:S(2)}) collective-permute-start(bf16[5376,256]{1,0:T(8,128)(2,1)S(1)} %pad_maximum_fusion), channel_id=1, source_target_pairs={{0,16},{1,17},{2,18},{3,19},{4,20},{5,21},{6,22},{7,23},{8,24},{9,... | collective-permute-start | bytes 8257544 | tf_op jit(solution)/shard_map/ppermute | solution.py:57
  220.2 13.5 %collective-permute-done.21.refs_5_ = bf16[1792,256]{1,0:T(8,128)(2,1)S(1)} collective-permute-done((bf16[1792,256]{1,0:T(8,128)(2,1)S(1)}, bf16[1792,256]{1,0:T(8,128)(2,1)S(1)}, u32[]{:S(2)}, u32[]{:S(2)}) %collective-permute-start.21) | collective-permute-done | bytes 917536 | tf_op jit(solution)/shard_map/ppermute | solution.py:57
  234.0 2.9 collective-permute-start.28
  239.0 7.3 %collective-permute-done.24.refs_8_ = bf16[592,256]{1,0:T(8,128)(2,1)S(1)} collective-permute-done((bf16[592,256]{1,0:T(8,128)(2,1)S(1)}, bf16[592,256]{1,0:T(8,128)(2,1)S(1)}, u32[]{:S(2)}, u32[]{:S(2)}) %collective-permute-start.24) | collective-permute-done | bytes 303136 | tf_op jit(solution)/shard_map/ppermute | solution.py:57
  255.0 37.7 %shard_map.60 = (bf16[4032,128]{1,0:T(8,128)(2,1)}, bf16[4032,128]{1,0:T(8,128)(2,1)}, bf16[7,2048,256]{2,1,0:T(8,128)(2,1)}, bf16[7,1536,256]{2,1,0:T(8,128)(2,...) custom-call(s32[4]{0:T(128)} %copy-done.6, bf16[1792,256]{1,0:T(8,128)(2,1)} %copy-done.5, bf16[1792,256]{1,0:T(8,128)(2,1)} %copy-done.14, ...), custom_call_target="tpu_custom_call" | custom-call | flops 22196256768 | bytes 40000000 | tf_op jit(solution)/shard_map/pallas_call | solution.py:490
  292.7 4.1 %collective-permute-start.30 = (bf16[4032,128]{1,0:T(8,128)(2,1)}, bf16[4032,128]{1,0:T(8,128)(2,1)S(1)}, u32[]{:S(2)}, u32[]{:S(2)}) collective-permute-start(bf16[4032,128]{1,0:T(8,128)(2,1)} %get-tuple-element.90), channel_id=1, source_target_pairs={{0,0},{1,1},{2,2},{3,3},{4,4},{5,5},{6,6},{7,7},{8,16},{9,17},{10,... | collective-permute-start | bytes 3096584 | tf_op jit(solution)/shard_map/ppermute | solution.py:57
  298.6 16.5 %shard_map.61 = (bf16[4032,128]{1,0:T(8,128)(2,1)}, bf16[4032,128]{1,0:T(8,128)(2,1)}) custom-call(s32[4]{0:T(128)} %copy-done.6, bf16[7,2048,256]{2,1,0:T(8,128)(2,1)} %get-tuple-element.92.direct, bf16[7,1536,256]{2,1,0:T(8,128)(2,1)} %get-tuple-element.93.flipped, bf16[576,5376]{1,0:T(8,128)(2,1)} %copy-done, ...), custom_call_target="tpu_custom_call" | custom-call | flops 7398752256 | bytes 20000000 | tf_op jit(solution)/shard_map/pallas_call | solution.py:463
  315.2 2.1 collective-permute-start.33
  317.3 4.2 %collective-permute-done.30.r0 = bf16[4032,128]{1,0:T(8,128)(2,1)S(1)} collective-permute-done((bf16[4032,128]{1,0:T(8,128)(2,1)}, bf16[4032,128]{1,0:T(8,128)(2,1)S(1)}, u32[]{:S(2)}, u32[]{:S(2)}) %collective-permute-start.30) | collective-permute-done | bytes 1032224 | tf_op jit(solution)/shard_map/ppermute | solution.py:57
  321.5 8.2 %collective-permute-done.31.r1 = bf16[4032,128]{1,0:T(8,128)(2,1)} collective-permute-done((bf16[4032,128]{1,0:T(8,128)(2,1)}, bf16[4032,128]{1,0:T(8,128)(2,1)}, u32[]{:S(2)}, u32[]{:S(2)}) %collective-permute-start.31) | collective-permute-done | bytes 1032224 | tf_op jit(solution)/shard_map/ppermute | solution.py:57
  329.7 11.8 %collective-permute-done.32.r2 = bf16[4032,128]{1,0:T(8,128)(2,1)S(1)} collective-permute-done((bf16[4032,128]{1,0:T(8,128)(2,1)}, bf16[4032,128]{1,0:T(8,128)(2,1)S(1)}, u32[]{:S(2)}, u32[]{:S(2)}) %collective-permute-start.32) | collective-permute-done | bytes 1032224 | tf_op jit(solution)/shard_map/ppermute | solution.py:57
  341.5 3.0 collective-permute-done.33.r3
  344.6 4.0 %shard_map.62 = bf16[896,2304]{1,0:T(8,128)(2,1)} custom-call(s32[4]{0:T(128)S(1)} %copy-done.7, bf16[4032,128]{1,0:T(8,128)(2,1)S(1)} %collective-permute-done.30.r0, bf16[4032,128]{1,0:T(8,128)(2,1)} %collective-permute-done.31.r1, bf16[4032,128]{1,0:T(8,128)(2,1)S(1)} %collective-permute-done.32.r2, bf16[4032,128]{1,0:T(8,128)(2,1)S(1)} %collective-permute-done.33.r3), custom_call_target="tpu_custom_call" | custom-call | bytes 8300000 | tf_op jit(solution)/shard_map/pallas_call | solution.py:536
  (111 shorter events, 39.2 us)
Async XLA Ops:
  54.0 27.5 %all-to-all-start.1 = ((bf16[16,432,128]{2,1,0:T(8,128)(2,1)}), bf16[16,432,128]{2,1,0:T(8,128)(2,1)}, u32[]{:S(2)}, u32[]{:S(2)}) async-start(bf16[16,432,128]{2,1,0:T(8,128)(2,1)} %get-tuple-element.52), calls=%async_computation.1 | async-start | bytes 3538944 | tf_op jit(solution)/shard_map/all_to_all | solution.py:559
  66.6 43.2 %collective-permute-start = (bf16[7,80,1152]{2,1,0:T(8,128)(2,1)}, bf16[7,80,1152]{2,1,0:T(8,128)(2,1)S(1)}, u32[]{:S(2)}, u32[]{:S(2)}) collective-permute-start(bf16[7,80,1152]{2,1,0:T(8,128)(2,1)} %get-tuple-element.55), channel_id=1, source_target_pairs={{0,0},{1,1},{2,2},{3,3},{4,4},{5,5},{6,6},{7,7},{8,16},{9,17},{10,... | collective-permute-start | bytes 3870728 | tf_op jit(solution)/shard_map/ppermute | solution.py:57
  73.3 36.6 %collective-permute-start.2 = (bf16[7,80,1152]{2,1,0:T(8,128)(2,1)}, bf16[7,80,1152]{2,1,0:T(8,128)(2,1)}, u32[]{:S(2)}, u32[]{:S(2)}) collective-permute-start(bf16[7,80,1152]{2,1,0:T(8,128)(2,1)} %get-tuple-element.57), channel_id=1, source_target_pairs={{0,4},{1,5},{2,6},{3,7},{4,0},{5,1},{6,2},{7,3},{8,20},{9,21},{10,... | collective-permute-start | bytes 3870728 | tf_op jit(solution)/shard_map/ppermute | solution.py:57
  86.9 38.8 %collective-permute-start.1 = (bf16[7,48,1152]{2,1,0:T(8,128)(2,1)}, bf16[7,48,1152]{2,1,0:T(8,128)(2,1)}, u32[]{:S(2)}, u32[]{:S(2)}) collective-permute-start(bf16[7,48,1152]{2,1,0:T(8,128)(2,1)} %get-tuple-element.56), channel_id=1, source_target_pairs={{0,0},{1,1},{2,2},{3,3},{4,4},{5,5},{6,6},{7,7},{8,16},{9,17},{10,... | collective-permute-start | bytes 2322440 | tf_op jit(solution)/shard_map/ppermute | solution.py:57
  93.9 31.8 %collective-permute-start.3 = (bf16[7,48,1152]{2,1,0:T(8,128)(2,1)}, bf16[7,48,1152]{2,1,0:T(8,128)(2,1)}, u32[]{:S(2)}, u32[]{:S(2)}) collective-permute-start(bf16[7,48,1152]{2,1,0:T(8,128)(2,1)} %get-tuple-element.58), channel_id=1, source_target_pairs={{0,4},{1,5},{2,6},{3,7},{4,0},{5,1},{6,2},{7,3},{8,20},{9,21},{10,... | collective-permute-start | bytes 2322440 | tf_op jit(solution)/shard_map/ppermute | solution.py:57
  109.9 16.4 %collective-permute-start.4 = (bf16[7,80,1152]{2,1,0:T(8,128)(2,1)S(1)}, bf16[7,80,1152]{2,1,0:T(8,128)(2,1)S(1)}, u32[]{:S(2)}, u32[]{:S(2)}) collective-permute-start(bf16[7,80,1152]{2,1,0:T(8,128)(2,1)S(1)} %collective-permute-done.refs_1_.refs_0_), channel_id=1, source_target_pairs={{0,16},{1,17},{2,18},{3,19},{4,20},{5,21},{6,22},{7,23},{8,24},{9,... | collective-permute-start | bytes 3870728 | tf_op jit(solution)/shard_map/ppermute | solution.py:57
  109.9 16.4 %collective-permute-start.6 = (bf16[7,80,1152]{2,1,0:T(8,128)(2,1)}, bf16[7,80,1152]{2,1,0:T(8,128)(2,1)}, u32[]{:S(2)}, u32[]{:S(2)}) collective-permute-start(bf16[7,80,1152]{2,1,0:T(8,128)(2,1)} %collective-permute-done.2.refs_3_.refs_2_), channel_id=1, source_target_pairs={{0,16},{1,17},{2,18},{3,19},{4,20},{5,21},{6,22},{7,23},{8,24},{9,... | collective-permute-start | bytes 3870728 | tf_op jit(solution)/shard_map/ppermute | solution.py:57
  134.2 12.1 %collective-permute-start.8 = (bf16[608,256]{1,0:T(8,128)(2,1)S(1)}, bf16[608,256]{1,0:T(8,128)(2,1)S(1)}, u32[]{:S(2)}, u32[]{:S(2)}) collective-permute-start(bf16[608,256]{1,0:T(8,128)(2,1)S(1)} %get-tuple-element.62), channel_id=1, source_target_pairs={{0,1},{1,2},{2,3},{3,0},{4,5},{5,6},{6,7},{7,4},{8,9},{9,10},{10,1... | collective-permute-start | bytes 933896 | tf_op jit(solution)/shard_map/ppermute | solution.py:57
  135.4 10.8 %collective-permute-start.9 = (bf16[592,256]{1,0:T(8,128)(2,1)S(1)}, bf16[592,256]{1,0:T(8,128)(2,1)S(1)}, u32[]{:S(2)}, u32[]{:S(2)}) collective-permute-start(bf16[592,256]{1,0:T(8,128)(2,1)S(1)} %get-tuple-element.63), channel_id=1, source_target_pairs={{0,3},{1,0},{2,1},{3,2},{4,7},{5,4},{6,5},{7,6},{8,11},{9,8},{10,9... | collective-permute-start | bytes 909320 | tf_op jit(solution)/shard_map/ppermute | solution.py:57
  136.9 9.4 %collective-permute-start.10 = (bf16[592,256]{1,0:T(8,128)(2,1)S(1)}, bf16[592,256]{1,0:T(8,128)(2,1)S(1)}, u32[]{:S(2)}, u32[]{:S(2)}) collective-permute-start(bf16[592,256]{1,0:T(8,128)(2,1)S(1)} %get-tuple-element.64), channel_id=1, source_target_pairs={{0,4},{1,5},{2,6},{3,7},{4,0},{5,1},{6,2},{7,3},{8,12},{9,13},{10,... | collective-permute-start | bytes 909320 | tf_op jit(solution)/shard_map/ppermute | solution.py:57
  146.7 21.2 %collective-permute-start.12 = (bf16[1792,256]{1,0:T(8,128)(2,1)S(1)}, bf16[1792,256]{1,0:T(8,128)(2,1)S(1)}, u32[]{:S(2)}, u32[]{:S(2)}) collective-permute-start(bf16[1792,256]{1,0:T(8,128)(2,1)S(1)} %get-tuple-element.77), channel_id=1, source_target_pairs={{0,3},{1,0},{2,1},{3,2},{4,7},{5,4},{6,5},{7,6},{8,11},{9,8},{10,9... | collective-permute-start | bytes 2752520 | tf_op jit(solution)/shard_map/ppermute | solution.py:57
  148.1 21.8 %collective-permute-start.13 = (bf16[1792,256]{1,0:T(8,128)(2,1)S(1)}, bf16[1792,256]{1,0:T(8,128)(2,1)S(1)}, u32[]{:S(2)}, u32[]{:S(2)}) collective-permute-start(bf16[1792,256]{1,0:T(8,128)(2,1)S(1)} %get-tuple-element.78), channel_id=1, source_target_pairs={{0,1},{1,2},{2,3},{3,0},{4,5},{5,6},{6,7},{7,4},{8,9},{9,10},{10,1... | collective-permute-start | bytes 2752520 | tf_op jit(solution)/shard_map/ppermute | solution.py:57
  148.2 21.7 %collective-permute-start.11 = (bf16[1792,256]{1,0:T(8,128)(2,1)S(1)}, bf16[1792,256]{1,0:T(8,128)(2,1)S(1)}, u32[]{:S(2)}, u32[]{:S(2)}) collective-permute-start(bf16[1792,256]{1,0:T(8,128)(2,1)S(1)} %get-tuple-element.65), channel_id=1, source_target_pairs={{0,4},{1,5},{2,6},{3,7},{4,0},{5,1},{6,2},{7,3},{8,12},{9,13},{10,... | collective-permute-start | bytes 2752520 | tf_op jit(solution)/shard_map/ppermute | solution.py:57
  158.4 29.2 %collective-permute-start.16 = (bf16[1792,256]{1,0:T(8,128)(2,1)S(1)}, bf16[1792,256]{1,0:T(8,128)(2,1)S(1)}, u32[]{:S(2)}, u32[]{:S(2)}) collective-permute-start(bf16[1792,256]{1,0:T(8,128)(2,1)S(1)} %get-tuple-element.81), channel_id=1, source_target_pairs={{0,3},{1,0},{2,1},{3,2},{4,7},{5,4},{6,5},{7,6},{8,11},{9,8},{10,9... | collective-permute-start | bytes 2752520 | tf_op jit(solution)/shard_map/ppermute | solution.py:57
  170.4 19.8 %collective-permute-start.15 = (bf16[1792,256]{1,0:T(8,128)(2,1)S(1)}, bf16[1792,256]{1,0:T(8,128)(2,1)S(1)}, u32[]{:S(2)}, u32[]{:S(2)}) collective-permute-start(bf16[1792,256]{1,0:T(8,128)(2,1)S(1)} %get-tuple-element.80), channel_id=1, source_target_pairs={{0,4},{1,5},{2,6},{3,7},{4,0},{5,1},{6,2},{7,3},{8,12},{9,13},{10,... | collective-permute-start | bytes 2752520 | tf_op jit(solution)/shard_map/ppermute | solution.py:57
  170.8 20.6 %collective-permute-start.14 = (bf16[1792,256]{1,0:T(8,128)(2,1)S(1)}, bf16[1792,256]{1,0:T(8,128)(2,1)S(1)}, u32[]{:S(2)}, u32[]{:S(2)}) collective-permute-start(bf16[1792,256]{1,0:T(8,128)(2,1)S(1)} %get-tuple-element.79), channel_id=1, source_target_pairs={{0,1},{1,2},{2,3},{3,0},{4,5},{5,6},{6,7},{7,4},{8,9},{9,10},{10,1... | collective-permute-start | bytes 2752520 | tf_op jit(solution)/shard_map/ppermute | solution.py:57
  191.8 18.5 %collective-permute-start.19 = (bf16[1792,256]{1,0:T(8,128)(2,1)S(1)}, bf16[1792,256]{1,0:T(8,128)(2,1)S(1)}, u32[]{:S(2)}, u32[]{:S(2)}) collective-permute-start(bf16[1792,256]{1,0:T(8,128)(2,1)S(1)} %shard_map.59.refs_0_), channel_id=1, source_target_pairs={{0,4},{1,5},{2,6},{3,7},{4,0},{5,1},{6,2},{7,3},{8,12},{9,13},{10,... | collective-permute-start | bytes 2752520 | tf_op jit(solution)/shard_map/ppermute | solution.py:57
  193.0 18.2 %collective-permute-start.18 = (bf16[1792,256]{1,0:T(8,128)(2,1)S(1)}, bf16[1792,256]{1,0:T(8,128)(2,1)S(1)}, u32[]{:S(2)}, u32[]{:S(2)}) collective-permute-start(bf16[1792,256]{1,0:T(8,128)(2,1)S(1)} %shard_map.59.refs_0_), channel_id=1, source_target_pairs={{0,3},{1,0},{2,1},{3,2},{4,7},{5,4},{6,5},{7,6},{8,11},{9,8},{10,9... | collective-permute-start | bytes 2752520 | tf_op jit(solution)/shard_map/ppermute | solution.py:57
  193.0 21.2 %collective-permute-start.17 = (bf16[1792,256]{1,0:T(8,128)(2,1)S(1)}, bf16[1792,256]{1,0:T(8,128)(2,1)S(1)}, u32[]{:S(2)}, u32[]{:S(2)}) collective-permute-start(bf16[1792,256]{1,0:T(8,128)(2,1)S(1)} %shard_map.59.refs_0_), channel_id=1, source_target_pairs={{0,1},{1,2},{2,3},{3,0},{4,5},{5,6},{6,7},{7,4},{8,9},{9,10},{10,1... | collective-permute-start | bytes 2752520 | tf_op jit(solution)/shard_map/ppermute | solution.py:57
  210.3 23.5 %collective-permute-start.21 = (bf16[1792,256]{1,0:T(8,128)(2,1)S(1)}, bf16[1792,256]{1,0:T(8,128)(2,1)S(1)}, u32[]{:S(2)}, u32[]{:S(2)}) collective-permute-start(bf16[1792,256]{1,0:T(8,128)(2,1)S(1)} %collective-permute-done.19.refs_3_), channel_id=1, source_target_pairs={{0,1},{1,2},{2,3},{3,0},{4,5},{5,6},{6,7},{7,4},{8,9},{9,10},{10,1... | collective-permute-start | bytes 2752520 | tf_op jit(solution)/shard_map/ppermute | solution.py:57
  211.2 22.6 %collective-permute-start.22 = (bf16[1792,256]{1,0:T(8,128)(2,1)S(1)}, bf16[1792,256]{1,0:T(8,128)(2,1)S(1)}, u32[]{:S(2)}, u32[]{:S(2)}) collective-permute-start(bf16[1792,256]{1,0:T(8,128)(2,1)S(1)} %collective-permute-done.18.refs_2_), channel_id=1, source_target_pairs={{0,3},{1,0},{2,1},{3,2},{4,7},{5,4},{6,5},{7,6},{8,11},{9,8},{10,9... | collective-permute-start | bytes 2752520 | tf_op jit(solution)/shard_map/ppermute | solution.py:57
  213.0 20.8 %collective-permute-start.20 = (bf16[1792,256]{1,0:T(8,128)(2,1)S(1)}, bf16[1792,256]{1,0:T(8,128)(2,1)S(1)}, u32[]{:S(2)}, u32[]{:S(2)}) collective-permute-start(bf16[1792,256]{1,0:T(8,128)(2,1)S(1)} %collective-permute-done.18.refs_2_), channel_id=1, source_target_pairs={{0,4},{1,5},{2,6},{3,7},{4,0},{5,1},{6,2},{7,3},{8,12},{9,13},{10,... | collective-permute-start | bytes 2752520 | tf_op jit(solution)/shard_map/ppermute | solution.py:57
  215.1 36.5 %collective-permute-start.27 = (bf16[5376,256]{1,0:T(8,128)(2,1)S(1)}, bf16[5376,256]{1,0:T(8,128)(2,1)S(1)}, u32[]{:S(2)}, u32[]{:S(2)}) collective-permute-start(bf16[5376,256]{1,0:T(8,128)(2,1)S(1)} %pad_maximum_fusion), channel_id=1, source_target_pairs={{0,16},{1,17},{2,18},{3,19},{4,20},{5,21},{6,22},{7,23},{8,24},{9,... | collective-permute-start | bytes 8257544 | tf_op jit(solution)/shard_map/ppermute | solution.py:57
  234.0 19.2 %collective-permute-start.28 = (bf16[5376,256]{1,0:T(8,128)(2,1)S(1)}, bf16[5376,256]{1,0:T(8,128)(2,1)S(1)}, u32[]{:S(2)}, u32[]{:S(2)}) collective-permute-start(bf16[5376,256]{1,0:T(8,128)(2,1)S(1)} %pad_maximum_fusion.1), channel_id=1, source_target_pairs={{0,16},{1,17},{2,18},{3,19},{4,20},{5,21},{6,22},{7,23},{8,24},{9,... | collective-permute-start | bytes 8257544 | tf_op jit(solution)/shard_map/ppermute | solution.py:57
  237.0 11.3 %collective-permute-start.23 = (bf16[608,256]{1,0:T(8,128)(2,1)S(1)}, bf16[608,256]{1,0:T(8,128)(2,1)S(1)}, u32[]{:S(2)}, u32[]{:S(2)}) collective-permute-start(bf16[608,256]{1,0:T(8,128)(2,1)S(1)} %slice.17), channel_id=1, source_target_pairs={{0,3},{1,0},{2,1},{3,2},{4,7},{5,4},{6,5},{7,6},{8,11},{9,8},{10,9... | collective-permute-start | bytes 933896 | tf_op jit(solution)/shard_map/ppermute | solution.py:57
  237.3 9.0 %collective-permute-start.24 = (bf16[592,256]{1,0:T(8,128)(2,1)S(1)}, bf16[592,256]{1,0:T(8,128)(2,1)S(1)}, u32[]{:S(2)}, u32[]{:S(2)}) collective-permute-start(bf16[592,256]{1,0:T(8,128)(2,1)S(1)} %slice.18), channel_id=1, source_target_pairs={{0,1},{1,2},{2,3},{3,0},{4,5},{5,6},{6,7},{7,4},{8,9},{9,10},{10,1... | collective-permute-start | bytes 909320 | tf_op jit(solution)/shard_map/ppermute | solution.py:57
  238.6 9.6 %collective-permute-start.25 = (bf16[592,256]{1,0:T(8,128)(2,1)S(1)}, bf16[592,256]{1,0:T(8,128)(2,1)S(1)}, u32[]{:S(2)}, u32[]{:S(2)}) collective-permute-start(bf16[592,256]{1,0:T(8,128)(2,1)S(1)} %slice.19), channel_id=1, source_target_pairs={{0,4},{1,5},{2,6},{3,7},{4,0},{5,1},{6,2},{7,3},{8,12},{9,13},{10,... | collective-permute-start | bytes 909320 | tf_op jit(solution)/shard_map/ppermute | solution.py:57
  246.3 4.0 %collective-permute-start.26 = (bf16[1792,256]{1,0:T(8,128)(2,1)S(1)}, bf16[1792,256]{1,0:T(8,128)(2,1)S(1)}, u32[]{:S(2)}, u32[]{:S(2)}) collective-permute-start(bf16[1792,256]{1,0:T(8,128)(2,1)S(1)} %shard_map.59.refs_0_), channel_id=1, source_target_pairs={{0,16},{1,17},{2,18},{3,19},{4,20},{5,21},{6,22},{7,23},{8,24},{9,... | collective-permute-start | bytes 2752520 | tf_op jit(solution)/shard_map/ppermute | solution.py:57
  292.7 28.8 %collective-permute-start.30 = (bf16[4032,128]{1,0:T(8,128)(2,1)}, bf16[4032,128]{1,0:T(8,128)(2,1)S(1)}, u32[]{:S(2)}, u32[]{:S(2)}) collective-permute-start(bf16[4032,128]{1,0:T(8,128)(2,1)} %get-tuple-element.90), channel_id=1, source_target_pairs={{0,0},{1,1},{2,2},{3,3},{4,4},{5,5},{6,6},{7,7},{8,16},{9,17},{10,... | collective-permute-start | bytes 3096584 | tf_op jit(solution)/shard_map/ppermute | solution.py:57
  296.8 32.9 %collective-permute-start.31 = (bf16[4032,128]{1,0:T(8,128)(2,1)}, bf16[4032,128]{1,0:T(8,128)(2,1)}, u32[]{:S(2)}, u32[]{:S(2)}) collective-permute-start(bf16[4032,128]{1,0:T(8,128)(2,1)} %get-tuple-element.91), channel_id=1, source_target_pairs={{0,4},{1,5},{2,6},{3,7},{4,0},{5,1},{6,2},{7,3},{8,20},{9,21},{10,... | collective-permute-start | bytes 3096584 | tf_op jit(solution)/shard_map/ppermute | solution.py:57
  315.1 26.4 %collective-permute-start.32 = (bf16[4032,128]{1,0:T(8,128)(2,1)}, bf16[4032,128]{1,0:T(8,128)(2,1)S(1)}, u32[]{:S(2)}, u32[]{:S(2)}) collective-permute-start(bf16[4032,128]{1,0:T(8,128)(2,1)} %get-tuple-element.96), channel_id=1, source_target_pairs={{0,8},{1,9},{2,10},{3,11},{4,12},{5,13},{6,14},{7,15},{8,24},{9,25... | collective-permute-start | bytes 3096584 | tf_op jit(solution)/shard_map/ppermute | solution.py:57
  315.2 29.3 %collective-permute-start.33 = (bf16[4032,128]{1,0:T(8,128)(2,1)}, bf16[4032,128]{1,0:T(8,128)(2,1)S(1)}, u32[]{:S(2)}, u32[]{:S(2)}) collective-permute-start(bf16[4032,128]{1,0:T(8,128)(2,1)} %get-tuple-element.97), channel_id=1, source_target_pairs={{0,12},{1,13},{2,14},{3,15},{4,8},{5,9},{6,10},{7,11},{8,28},{9,29... | collective-permute-start | bytes 3096584 | tf_op jit(solution)/shard_map/ppermute | solution.py:57
  (25 other events, 283.7 us)

commit v4 on v3

--- a/solution.py
+++ b/solution.py
@@ -73,8 +73,24 @@
     return move(x, lambda c, m, a, y: (1 - c, m, a, y))
 
 
-def pack_kernel(details, tiles, upper, lower, held, first, second, sems, out_sems):
-    load_all([(tiles.at[i], held.at[i]) for i in range(tiles.shape[0])], sems)
+def pack_kernel(ids, tiles, upper, lower, slots, places, held, first, second, sems, out_sems):
+    n = tiles.shape[0]
+    loads = [pltpu.make_async_copy(tiles.at[i], held.at[i], sems.at[i]) for i in range(n)]
+    for load in loads:
+        load.start()
+    for o in range(upper.shape[0]):
+        slots[o] = 0
+        places[o] = -1
+
+    @pl.loop(0, n)
+    def _(i):
+        row, column = ids[i] // 8, ids[i] % 8
+        owner = row // 7 * 4 + column // 2
+        slots[owner] = i
+        places[owner] = row % 7 * 2 + column % 2
+
+    for load in loads:
+        load.wait()
 
     def copies(o):
         return (
@@ -84,12 +100,12 @@
 
     @pl.loop(0, upper.shape[0])
     def _(o):
-        slot = details[o]
+        slot = slots[o]
         for j in range(HALF // TILE):
             piece = held[slot, :, j * TILE : (j + 1) * TILE]
             for (row, size), out in zip(SPLIT, (first, second)):
                 out[o, j * size : (j + 1) * size, :] = piece[row : row + size]
-        place = jnp.full((LABEL, TILE), details[16 + o], jnp.int32)
+        place = jnp.full((LABEL, TILE), places[o], jnp.int32)
         first[o, first.shape[1] - LABEL :, :] = place.astype(F32).astype(BF16)
         for copy in copies(o):
             copy.start()
@@ -100,8 +116,8 @@
             copy.wait()
 
 
-def pack(details, tiles):
-    n = details.shape[0] // 2
+def pack(ids, tiles):
+    n = 16
     rows = [HALF // TILE * size for _, size in SPLIT]
     shapes = [(n, rows[0] + LABEL, TILE), (n, rows[1], TILE)]
     return pl.pallas_call(
@@ -109,12 +125,13 @@
         in_specs=[SMEM, HBM],
         out_specs=[HBM] * 2,
         out_shape=[jax.ShapeDtypeStruct(shape, BF16) for shape in shapes],
-        scratch_shapes=[pltpu.VMEM(tiles.shape, BF16)]
+        scratch_shapes=[pltpu.SMEM((n,), jnp.int32)] * 2
+        + [pltpu.VMEM(tiles.shape, BF16)]
         + [pltpu.VMEM(shape, BF16) for shape in shapes]
         + [pltpu.SemaphoreType.DMA((tiles.shape[0],)), pltpu.SemaphoreType.DMA((2, n))],
         compiler_params=pltpu.CompilerParams(vmem_limit_bytes=62 * MIB),
         cost_estimate=cost(0, 4 * tiles.size),
-    )(details, tiles)
+    )(ids, tiles)
 
 
 def momentum_kernel(part, info, arrived, momentum, *refs):
@@ -334,11 +351,10 @@
 def apply_kernel(info, *refs):
     own, ends, swapped = refs[:7], refs[7:10], refs[10:14]
     turned = refs[14]
-    outs, rest_direct, rest_flipped, all_mixed, scales = refs[15:17], *refs[17:21]
-    direct, flipped, panel, mixed, stage, extra, sems, panel_sem, out_sems, keep_sems = refs[21:]
+    out, near_direct, near_flipped, rest_direct, rest_flipped, all_mixed, scales = refs[15:22]
+    direct, flipped, mixed, stage, extra, sems, out_sems, keep_sems = refs[22:]
+    panel = turned
     c = info[0]
-    panel_copy = pltpu.make_async_copy(turned, panel, panel_sem)
-    panel_copy.start()
     pieces = [(c, ref, 0, rel) for ref, rel in zip(own, SOURCES)]
     pieces += [(1 - c, swapped[0], 0, SOURCES[0]), (1 - c, swapped[3], 0, SOURCES[7])]
     pieces += [(1 - c, swapped[1 + n // 3], n % 3 * CHUNK, SOURCES[1 + n]) for n in range(6)]
@@ -368,9 +384,15 @@
         pltpu.make_async_copy(whole, whole, sems.at[n]).wait()
     for copy in last:
         copy.wait()
-    panel_copy.wait()
-
-    total = jnp.zeros((), F32)
+
+    near = near_start(info, 1)
+    other = (1 - c) * HALF_BLOCKS
+    keeps = [
+        pltpu.make_async_copy(direct.at[pl.ds(near, 4)], near_direct, keep_sems.at[0]),
+        pltpu.make_async_copy(direct.at[pl.ds(other, HALF_BLOCKS)], rest_direct, keep_sems.at[1]),
+    ]
+    for copy in keeps:
+        copy.start()
     on = lax.broadcasted_iota(jnp.int32, (SIDE, SIDE), 0) == lax.broadcasted_iota(jnp.int32, (SIDE, SIDE), 1)
     diagonal = jnp.zeros((SIDE, SIDE), F32)
     for i in range(BLOCKS):
@@ -397,27 +419,31 @@
         def _():
             mixed[:, pl.ds(pl.multiple_of(i * SIDE + ROWS, SIDE), SIDE)] = mix
 
-    other = (1 - c) * HALF_BLOCKS
     scale = math.sqrt(COLS) * factor
     scales[...] = jnp.concatenate([scale] * 4 + [square] * 4)
-    keeps = [
-        pltpu.make_async_copy(direct.at[pl.ds(other, HALF_BLOCKS)], rest_direct, keep_sems.at[0]),
-        pltpu.make_async_copy(flipped.at[pl.ds(other, HALF_BLOCKS)], rest_flipped, keep_sems.at[1]),
-        pltpu.make_async_copy(mixed, all_mixed, keep_sems.at[2]),
+    more = [
+        pltpu.make_async_copy(flipped.at[pl.ds(near, 4)], near_flipped, keep_sems.at[2]),
+        pltpu.make_async_copy(flipped.at[pl.ds(other, HALF_BLOCKS)], rest_flipped, keep_sems.at[3]),
+        pltpu.make_async_copy(mixed, all_mixed, keep_sems.at[4]),
     ]
-    for copy in keeps:
+    for copy in more:
         copy.start()
 
-    @pl.loop(0, HALF_BLOCKS)
+    @pl.loop(0, 4)
     def _(b):
-        i = c * HALF_BLOCKS + b
+        i = near_start(info, 0) + b
         columns = pl.ds(pl.multiple_of(i * SIDE, SIDE), SIDE)
         result = scale * (COEF_LINEAR * panel[:, columns].astype(F32) + product(i, mixed))
         stage[pl.ds(pl.multiple_of(b * SIDE, SIDE), SIDE)] = result.astype(BF16).T
 
-    send_back(info, stage, extra, outs, out_sems)
-    for copy in keeps:
+    send_back(stage, extra, [(info[2] * TILE, out)], out_sems)
+    for copy in keeps + more:
         copy.wait()
+
+
+def near_start(info, side):
+    a = info[2]
+    return info[0] * HALF_BLOCKS + 3 * (1 - a if side else a)
 
 
 def gram_times(i, x, direct, flipped):
@@ -427,72 +453,80 @@
     return result + jnp.dot(x[:, rest], flipped[...], preferred_element_type=F32)
 
 
-def send_back(info, stage, extra, outs, sems):
-    a = info[2]
+def send_back(stage, extra, outs, sems):
     sends = []
-    for side, out in enumerate(outs):
-        owner = 1 - a if side else a
-        start = pl.multiple_of(owner * HEIGHT, 128)
+    for n, (start, out) in enumerate(outs):
         for j in range(4):
-            rows = pl.ds(start, HEIGHT)
+            rows = pl.ds(pl.multiple_of(start, 128), HEIGHT)
             sends.append((stage.at[rows, j * TILE : (j + 1) * TILE], out.at[pl.ds(j * HEIGHT, HEIGHT)]))
         halves = [stage[pl.ds(pl.multiple_of(start + row, 64), 448), 512:] for row in (0, 448)]
-        extra[side] = jnp.concatenate(halves, axis=1)
-        sends.append((extra.at[side], out.at[pl.ds(4 * HEIGHT, 448)]))
+        extra[n] = jnp.concatenate(halves, axis=1)
+        sends.append((extra.at[n], out.at[pl.ds(4 * HEIGHT, 448)]))
     load_all(sends, sems)
 
 
-def rest_kernel(info, direct, flipped, panel, all_mixed, scales, out0, out1, mixed, stage, extra, sems):
+def rest_start(near, info):
+    return near_start(info, 1) if near else (1 - info[0]) * HALF_BLOCKS
+
+
+def rest_kernel(near, info, direct, flipped, panel, all_mixed, scales, *refs):
+    outs, (mixed, stage, extra, sems) = refs[:-4], refs[-4:]
     b = pl.program_id(0)
 
     @pl.when(b == 0)
     def _():
         load_all([(all_mixed, mixed)], sems)
 
-    i = (1 - info[0]) * HALF_BLOCKS + b
+    i = rest_start(near, info) + b
     product = gram_times(i, mixed, direct.at[0], flipped.at[0]) * scales[4:5]
     result = scales[0:1] * (COEF_LINEAR * panel[...].astype(F32) + product)
     stage[pl.ds(pl.multiple_of(b * SIDE, SIDE), SIDE)] = result.astype(BF16).T
 
-    @pl.when(b == HALF_BLOCKS - 1)
+    @pl.when(b == pl.num_programs(0) - 1)
     def _():
-        send_back(info, stage, extra, (out0, out1), sems)
-
-
-def apply_rest(info, direct, flipped, mixed, scales, turned):
-    return pl.pallas_call(
-        rest_kernel,
+        a = info[2]
+        starts = [(1 - a) * TILE] if near else [a * HEIGHT, (1 - a) * HEIGHT]
+        send_back(stage, extra, list(zip(starts, outs)), sems)
+
+
+def apply_rest(near, info, direct, flipped, mixed, scales, turned):
+    n = direct.shape[0]
+    count = 1 if near else 2
+    return pl.pallas_call(
+        lambda *refs: rest_kernel(near, *refs),
         grid_spec=pltpu.PrefetchScalarGridSpec(
             num_scalar_prefetch=1,
-            grid=(HALF_BLOCKS,),
+            grid=(n,),
             in_specs=[
                 pl.BlockSpec((1, 8 * SIDE, SIDE), lambda b, s: (b, 0, 0)),
                 pl.BlockSpec((1, 6 * SIDE, SIDE), lambda b, s: (b, 0, 0)),
-                pl.BlockSpec((SHARE, SIDE), lambda b, s: (0, (1 - s[0]) * HALF_BLOCKS + b)),
+                pl.BlockSpec((SHARE, SIDE), lambda b, s: (0, rest_start(near, s) + b)),
                 HBM,
                 VMEM,
             ],
-            out_specs=[HBM] * 2,
+            out_specs=[HBM] * count,
             scratch_shapes=[
                 pltpu.VMEM((SHARE, AROUND), BF16),
-                pltpu.VMEM((CHUNK, SHARE), BF16),
+                pltpu.VMEM((n * SIDE, SHARE), BF16),
                 pltpu.VMEM((2, 448, TILE), BF16),
                 pltpu.SemaphoreType.DMA((10,)),
             ],
         ),
-        out_shape=[jax.ShapeDtypeStruct((BACK_ROWS, TILE), BF16)] * 2,
+        out_shape=[jax.ShapeDtypeStruct((BACK_ROWS, TILE), BF16)] * count,
         compiler_params=pltpu.CompilerParams(vmem_limit_bytes=62 * MIB),
-        cost_estimate=cost(ROWS * ROWS * SHARE, 2e7),
+        cost_estimate=cost(n * 2 * SIDE * ROWS * SHARE, 2e7),
     )(info, direct, flipped, turned, mixed, scales)
 
 
 def apply_poly(info, own, ends, swapped, turned):
     return pl.pallas_call(
         apply_kernel,
-        in_specs=[SMEM] + [HBM] * 15,
-        out_specs=[HBM] * 5 + [VMEM],
-        out_shape=[jax.ShapeDtypeStruct((BACK_ROWS, TILE), BF16)] * 2
-        + [
+        in_specs=[SMEM] + [ANY] * 14 + [VMEM],
+        out_specs=[HBM] * 6 + [VMEM],
+        out_shape=[
+            jax.ShapeDtypeStruct((BACK_ROWS, TILE), BF16),
+            jax.ShapeDtypeStruct((4, 8 * SIDE, SIDE), BF16),
+            jax.ShapeDtypeStruct((4, 6 * SIDE, SIDE), BF16),
             jax.ShapeDtypeStruct((HALF_BLOCKS, 8 * SIDE, SIDE), BF16),
             jax.ShapeDtypeStruct((HALF_BLOCKS, 6 * SIDE, SIDE), BF16),
             jax.ShapeDtypeStruct((SHARE, AROUND), BF16),
@@ -502,15 +536,13 @@
             pltpu.VMEM((BLOCKS, 8 * SIDE, SIDE), BF16),
             pltpu.VMEM((BLOCKS, 6 * SIDE, SIDE), BF16),
             pltpu.VMEM((SHARE, AROUND), BF16),
-            pltpu.VMEM((SHARE, AROUND), BF16),
-            pltpu.VMEM((CHUNK, SHARE), BF16),
-            pltpu.VMEM((2, 448, TILE), BF16),
+            pltpu.VMEM((4 * SIDE, SHARE), BF16),
+            pltpu.VMEM((1, 448, TILE), BF16),
             pltpu.SemaphoreType.DMA((32,)),
-            pltpu.SemaphoreType.DMA,
-            pltpu.SemaphoreType.DMA((10,)),
-            pltpu.SemaphoreType.DMA((3,)),
+            pltpu.SemaphoreType.DMA((5,)),
+            pltpu.SemaphoreType.DMA((5,)),
         ],
-        compiler_params=pltpu.CompilerParams(vmem_limit_bytes=58 * MIB),
+        compiler_params=pltpu.CompilerParams(vmem_limit_bytes=44 * MIB),
         cost_estimate=cost(3 * ROWS * ROWS * SHARE, 4e7),
     )(info, *own, *ends, *swapped, turned)
 
@@ -548,12 +580,7 @@
     info = jnp.stack([core, zm, zl, y]).astype(jnp.int32)
     tile_count = grad_tiles.shape[0]
 
-    owners = tile_ids // 8 // 7 * 4 + tile_ids % 8 // 2
-    places = tile_ids // 8 % 7 * 2 + tile_ids % 2
-    matches = owners[:, None] == jnp.arange(16, dtype=jnp.int32)[None, :]
-    slots = jnp.sum(jnp.where(matches, jnp.arange(tile_count, dtype=jnp.int32)[:, None], 0), axis=0)
-    labels = jnp.sum(jnp.where(matches, places[:, None] + 1, 0), axis=0) - 1
-    upper, lower = pack(jnp.concatenate([slots, labels]), grad_tiles)
+    upper, lower = pack(tile_ids, grad_tiles)
     upper = lax.all_to_all(upper, PLANE, split_axis=0, concat_axis=0, tiled=True)
     lower, _ = lax.optimization_barrier((lower, upper))
     lower = lax.all_to_all(lower, PLANE, split_axis=0, concat_axis=0, tiled=True)
@@ -603,8 +630,12 @@
         swap(jnp.concatenate([a1, a2, a3])),
         swap(jnp.concatenate(ends)),
     )
-    *sent, direct, flipped, mixed, scales = apply_poly(info, (mine, low, high, pair, a1, a2, a3), ends, swapped, turned)
-    sent += apply_rest(info, direct, flipped, mixed, scales, turned)
+    first, *near_rows, rest_direct, rest_flipped, mixed, scales = apply_poly(
+        info, (mine, low, high, pair, a1, a2, a3), ends, swapped, turned
+    )
+    (second,) = apply_rest(True, info, *near_rows, mixed, scales, turned)
+    later, _ = lax.optimization_barrier((mixed, second))
+    sent = (first, second, *apply_rest(False, info, rest_direct, rest_flipped, later, scales, turned))
 
     parts = (
         move(sent[0], lambda c, m, a, y: (m, c, a, y)),

time: 350 us -> 368 us (1.051)
  Pallas kernels: 104 us -> 120 us
  waiting for transfers between devices: 135 us -> 141 us
    pallas_call x2 -> x3, Pallas kernels: 54.3 us -> 70.3 us  [the longest x1 41.8 us: apply_poly(): pl.pallas_call(apply_kernel, in_specs=[SMEM] + [ANY] * 14 + [VMEM], out_s...]
    ppermute x34, waiting for transfers between devices: 127 us -> 133 us  [move(): return lax.ppermute(x, AXES[1:], pairs)]
  transfers between devices with their start and end apart: 35 -> 35, of which waited for: 20 -> 19; matrix products, arithmetic and copies ran while one was open for 0% -> 0% of each run, Pallas kernels for 15% -> 14%
where the time goes in v4:
time: 368 us; the launch traced here: 367 us
  waiting for transfers between devices  141 us (38%)
  Pallas kernels  120 us (33%)
  starting transfers between devices  52.8 us (14%)
  blocking collectives  46 us (12%)
  local copies, waits for them, and re-layouts  4.69 us (1%)
    ppermute x34, waiting for transfers between devices, move(): return lax.ppermute(x, AXES[1:], pairs)  133 us
    ppermute x34, starting transfers between devices, move(): return lax.ppermute(x, AXES[1:], pairs)  48.3 us
    all_to_all x1, blocking collectives, on_device(): lax.all_to_all(upper, PLANE, split_axis=0, concat_axis=0, tiled=True)  46 us
    pallas_call x1, Pallas kernels, apply_poly(): pl.pallas_call(apply_kernel, in_specs=[SMEM] + [ANY] * 14 + [VMEM], out_s...  41.8 us
    pallas_call x2, Pallas kernels, apply_rest(): pl.pallas_call(lambda *refs: rest_kernel(near, *refs), grid_spec=pltpu.Pr...  28.5 us
    pallas_call x3, Pallas kernels, gram_chunks(): pl.pallas_call(lambda *refs: gram_kernel(dests, *refs), in_specs=[SMEM] +...  22.8 us
    pallas_call x2, Pallas kernels, update_momentum(): pl.pallas_call(lambda *refs: momentum_kernel(part, *refs), in_specs=[SMEM...  12.5 us
    all_to_all x1, waiting for transfers between devices, on_device(): lax.all_to_all(lower, PLANE, split_axis=0, concat_axis=0, tiled=True)  8.07 us
  transfers between devices with their start and end apart: 35, of which 19 were waited for; matrix products, arithmetic and copies ran while one was open for 0% of the time, Pallas kernels for 14%

profile of v4, /device:TPU:1, one launch (start us, length us, event | category | flops | bytes accessed | tf_op | source)
XLA Modules:
  0.0 366.9 jit_solution(809104658339996208)
XLA Ops:
  0.6 5.4 %shard_map.50 = (bf16[16,736,128]{2,1,0:T(8,128)(2,1)}, bf16[16,432,128]{2,1,0:T(8,128)(2,1)}) custom-call(s32[14]{0:T(128)} %ids.1, bf16[14,128,1152]{2,1,0:T(8,128)(2,1)} %tiles.1), custom_call_target="tpu_custom_call" | custom-call | bytes 8257536 | tf_op jit(solution)/shard_map/pallas_call | solution.py:123
  6.0 46.0 %all_to_all.10.refs_1_ = bf16[16,736,128]{2,1,0:T(8,128)(2,1)S(1)} all-to-all(bf16[16,736,128]{2,1,0:T(8,128)(2,1)} %get-tuple-element.52), channel_id=1, replica_groups=mesh['x'=4,'core'=2,'zm'=2,'zl'=2,'y'=4] {'zm','zl','y'}, dimensions={0} | all-to-all | bytes 6029312 | tf_op jit(solution)/shard_map/all_to_all | solution.py:584
  52.0 4.4 %all-to-all-start.1 = ((bf16[16,432,128]{2,1,0:T(8,128)(2,1)}), bf16[16,432,128]{2,1,0:T(8,128)(2,1)}, u32[]{:S(2)}, u32[]{:S(2)}) async-start(bf16[16,432,128]{2,1,0:T(8,128)(2,1)} %get-tuple-element.54), calls=%async_computation.1 | async-start | bytes 3538944 | tf_op jit(solution)/shard_map/all_to_all | solution.py:586
  57.5 7.1 %shard_map.51 = (f32[896,2304]{1,0:T(8,128)}, bf16[7,80,1152]{2,1,0:T(8,128)(2,1)}, bf16[7,80,1152]{2,1,0:T(8,128)(2,1)}) custom-call(s32[15]{0:T(128)} %pad_add_fusion.refs_0_, bf16[16,736,128]{2,1,0:T(8,128)(2,1)} %copy-done.5, f32[896,2304]{1,0:T(8,128)} %refs_2_.3), custom_call_target="tpu_custom_call" | custom-call | bytes 12386304 | tf_op jit(solution)/shard_map/pallas_call | solution.py:195
  64.6 6.6 %collective-permute-start = (bf16[7,80,1152]{2,1,0:T(8,128)(2,1)}, bf16[7,80,1152]{2,1,0:T(8,128)(2,1)S(1)}, u32[]{:S(2)}, u32[]{:S(2)}) collective-permute-start(bf16[7,80,1152]{2,1,0:T(8,128)(2,1)} %get-tuple-element.57), channel_id=1, source_target_pairs={{0,0},{1,1},{2,2},{3,3},{4,4},{5,5},{6,6},{7,7},{8,16},{9,17},{10,... | collective-permute-start | bytes 3870728 | tf_op jit(solution)/shard_map/ppermute | solution.py:57
  71.4 8.1 %all-to-all-done.1.refs_1_ = bf16[16,432,128]{2,1,0:T(8,128)(2,1)} async-done(((bf16[16,432,128]{2,1,0:T(8,128)(2,1)}), bf16[16,432,128]{2,1,0:T(8,128)(2,1)}, u32[]{:S(2)}, u32[]{:S(2)}) %all-to-all-start.1) | async-done | bytes 1769504 | tf_op jit(solution)/shard_map/all_to_all | solution.py:586
  79.4 5.4 %shard_map.52 = (f32[896,2304]{1,0:T(8,128)}, bf16[7,48,1152]{2,1,0:T(8,128)(2,1)}, bf16[7,48,1152]{2,1,0:T(8,128)(2,1)}) custom-call(s32[15]{0:T(128)} %pad_add_fusion.refs_0_, bf16[16,432,128]{2,1,0:T(8,128)(2,1)} %all-to-all-done.1.refs_1_, f32[896,2304]{1,0:T(8,128)} %refs_2_.3, ...), custom_call_target="tpu_custom_call", output_to_operand_aliasing={{0}: (3, {})} | custom-call | bytes 12386304 | tf_op jit(solution)/shard_map/pallas_call | solution.py:195
  84.8 7.1 %collective-permute-start.1 = (bf16[7,48,1152]{2,1,0:T(8,128)(2,1)}, bf16[7,48,1152]{2,1,0:T(8,128)(2,1)}, u32[]{:S(2)}, u32[]{:S(2)}) collective-permute-start(bf16[7,48,1152]{2,1,0:T(8,128)(2,1)} %get-tuple-element.58), channel_id=1, source_target_pairs={{0,0},{1,1},{2,2},{3,3},{4,4},{5,5},{6,6},{7,7},{8,16},{9,17},{10,... | collective-permute-start | bytes 2322440 | tf_op jit(solution)/shard_map/ppermute | solution.py:57
  92.1 15.8 %collective-permute-done.refs_1_.refs_0_ = bf16[7,80,1152]{2,1,0:T(8,128)(2,1)S(1)} collective-permute-done((bf16[7,80,1152]{2,1,0:T(8,128)(2,1)}, bf16[7,80,1152]{2,1,0:T(8,128)(2,1)S(1)}, u32[]{:S(2)}, u32[]{:S(2)}) %collective-permute-start) | collective-permute-done | bytes 1290272 | tf_op jit(solution)/shard_map/ppermute | solution.py:57
  108.3 15.3 %collective-permute-done.1.refs_2_.refs_1_ = bf16[7,48,1152]{2,1,0:T(8,128)(2,1)} collective-permute-done((bf16[7,48,1152]{2,1,0:T(8,128)(2,1)}, bf16[7,48,1152]{2,1,0:T(8,128)(2,1)}, u32[]{:S(2)}, u32[]{:S(2)}) %collective-permute-start.1) | collective-permute-done | bytes 774176 | tf_op jit(solution)/shard_map/ppermute | solution.py:57
  124.2 2.0 collective-permute-done.5.refs_6_.refs_5_
  127.4 4.8 %shard_map.54 = (bf16[608,256]{1,0:T(8,128)(2,1)S(1)}, bf16[592,256]{1,0:T(8,128)(2,1)S(1)}, bf16[592,256]{1,0:T(8,128)(2,1)S(1)}) custom-call(s32[4]{0:T(128)S(1)} %pad_add_fusion.1.refs_0_.info, bf16[7,80,1152]{2,1,0:T(8,128)(2,1)S(1)} %collective-permute-done.refs_1_.refs_0_, bf16[7,48,1152]{2,1,0:T(8,128)(2,1)} %collective-permute-done.1.refs_2_.refs_1_, ...), custom_call_target="tpu_custom_call" | custom-call | flops 1056964608 | bytes 10135008 | tf_op jit(solution)/shard_map/pallas_call | solution.py:278
  135.8 8.5 %shard_map.53 = (f32[1792,256]{1,0:T(8,128)S(1)}, f32[1792,256]{1,0:T(8,128)S(1)}, f32[1792,256]{1,0:T(8,128)S(1)}) custom-call(s32[4]{0:T(128)S(1)} %pad_add_fusion.1.refs_0_.info, bf16[7,80,1152]{2,1,0:T(8,128)(2,1)S(1)} %collective-permute-done.refs_1_.refs_0_, bf16[7,48,1152]{2,1,0:T(8,128)(2,1)} %collective-permute-done.1.refs_2_.refs_1_, ...), custom_call_target="tpu_custom_call" | custom-call | flops 3170893824 | bytes 13805024 | tf_op jit(solution)/shard_map/pallas_call | solution.py:278
  146.7 9.6 %shard_map.56 = (f32[1792,256]{1,0:T(8,128)S(1)}, f32[1792,256]{1,0:T(8,128)S(1)}, bf16[1792,256]{1,0:T(8,128)(2,1)S(1)}, f32[1792,256]{1,0:T(8,128)S(1)}) custom-call(s32[4]{0:T(128)S(1)} %pad_add_fusion.1.refs_0_.info, bf16[7,80,1152]{2,1,0:T(8,128)(2,1)S(1)} %collective-permute-done.refs_1_.refs_0_, ...), custom_call_target="tpu_custom_call" | custom-call | flops 4227858432 | bytes 15640032 | tf_op jit(solution)/shard_map/pallas_call | solution.py:278
  156.3 2.4 collective-permute-start.16
  158.8 7.2 %collective-permute-done.12.g2 = bf16[1792,256]{1,0:T(8,128)(2,1)S(1)} collective-permute-done((bf16[1792,256]{1,0:T(8,128)(2,1)S(1)}, bf16[1792,256]{1,0:T(8,128)(2,1)S(1)}, u32[]{:S(2)}, u32[]{:S(2)}) %collective-permute-start.12) | collective-permute-done | bytes 917536 | tf_op jit(solution)/shard_map/ppermute | solution.py:57
  168.7 4.2 %shard_map.58.turned.refs_14_.refs_3_ = bf16[576,5376]{1,0:T(8,128)(2,1)S(1)} custom-call(s32[4]{0:T(128)S(1)} %pad_add_fusion.1.refs_0_.info, bf16[7,80,1152]{2,1,0:T(8,128)(2,1)S(1)} %collective-permute-done.refs_1_.refs_0_, bf16[7,48,1152]{2,1,0:T(8,128)(2,1)} %collective-permute-done.1.refs_2_.refs_1_, ...), custom_call_target="tpu_custom_call" | custom-call | bytes 12000000 | tf_op jit(solution)/shard_map/pallas_call | solution.py:337
  172.9 12.7 %collective-permute-done.16.v3 = bf16[1792,256]{1,0:T(8,128)(2,1)S(1)} collective-permute-done((bf16[1792,256]{1,0:T(8,128)(2,1)S(1)}, bf16[1792,256]{1,0:T(8,128)(2,1)S(1)}, u32[]{:S(2)}, u32[]{:S(2)}) %collective-permute-start.16) | collective-permute-done | bytes 917536 | tf_op jit(solution)/shard_map/ppermute | solution.py:57
  185.6 2.4 collective-permute-done.15.v2
  192.3 15.9 %collective-permute-done.19.refs_3_ = bf16[1792,256]{1,0:T(8,128)(2,1)S(1)} collective-permute-done((bf16[1792,256]{1,0:T(8,128)(2,1)S(1)}, bf16[1792,256]{1,0:T(8,128)(2,1)S(1)}, u32[]{:S(2)}, u32[]{:S(2)}) %collective-permute-start.19) | collective-permute-done | bytes 917536 | tf_op jit(solution)/shard_map/ppermute | solution.py:57
  212.2 5.3 %collective-permute-start.27 = (bf16[5376,256]{1,0:T(8,128)(2,1)S(1)}, bf16[5376,256]{1,0:T(8,128)(2,1)S(1)}, u32[]{:S(2)}, u32[]{:S(2)}) collective-permute-start(bf16[5376,256]{1,0:T(8,128)(2,1)S(1)} %pad_maximum_fusion), channel_id=1, source_target_pairs={{0,16},{1,17},{2,18},{3,19},{4,20},{5,21},{6,22},{7,23},{8,24},{9,... | collective-permute-start | bytes 8257544 | tf_op jit(solution)/shard_map/ppermute | solution.py:57
  217.4 14.2 %collective-permute-done.21.refs_5_ = bf16[1792,256]{1,0:T(8,128)(2,1)S(1)} collective-permute-done((bf16[1792,256]{1,0:T(8,128)(2,1)S(1)}, bf16[1792,256]{1,0:T(8,128)(2,1)S(1)}, u32[]{:S(2)}, u32[]{:S(2)}) %collective-permute-start.21) | collective-permute-done | bytes 917536 | tf_op jit(solution)/shard_map/ppermute | solution.py:57
  231.8 3.0 collective-permute-start.28
  236.9 8.1 %collective-permute-done.24.refs_8_ = bf16[592,256]{1,0:T(8,128)(2,1)S(1)} collective-permute-done((bf16[592,256]{1,0:T(8,128)(2,1)S(1)}, bf16[592,256]{1,0:T(8,128)(2,1)S(1)}, u32[]{:S(2)}, u32[]{:S(2)}) %collective-permute-start.24) | collective-permute-done | bytes 303136 | tf_op jit(solution)/shard_map/ppermute | solution.py:57
  252.6 41.8 %shard_map.60 = (bf16[4032,128]{1,0:T(8,128)(2,1)S(1)}, bf16[4,2048,256]{2,1,0:T(8,128)(2,1)}, bf16[4,1536,256]{2,1,0:T(8,128)(2,1)}, bf16[7,2048,256]{2,1,0:T(8...) custom-call(s32[4]{0:T(128)S(1)} %pad_add_fusion.1.refs_0_.info, ...), custom_call_target="tpu_custom_call" | custom-call | flops 22196256768 | bytes 40000000 | tf_op jit(solution)/shard_map/pallas_call | solution.py:522
  296.0 12.0 %shard_map.61 = bf16[4032,128]{1,0:T(8,128)(2,1)} custom-call(s32[4]{0:T(128)} %copy-done.1, bf16[4,2048,256]{2,1,0:T(8,128)(2,1)} %get-tuple-element.93.refs_1_, bf16[4,1536,256]{2,1,0:T(8,128)(2,1)} %get-tuple-element.94.refs_2_, bf16[576,5376]{1,0:T(8,128)(2,1)} %copy-done, bf16[576,5376]{1,0:T(8,128)(2,1)} %get-tuple-element.99.refs_4_, f32[8,256]{1,0:T(8,128)} %copy-done.3), custom_call_target="tpu_custom_call" | custom-call | flops 4227858432 | bytes 20000000 | tf_op jit(solution)/shard_map/pallas_call | solution.py:495
  309.7 16.5 %shard_map.62 = (bf16[4032,128]{1,0:T(8,128)(2,1)}, bf16[4032,128]{1,0:T(8,128)(2,1)}) custom-call(s32[4]{0:T(128)} %copy-done.1, bf16[7,2048,256]{2,1,0:T(8,128)(2,1)} %get-tuple-element.97.refs_1_, bf16[7,1536,256]{2,1,0:T(8,128)(2,1)} %get-tuple-element.98.refs_2_, bf16[576,5376]{1,0:T(8,128)(2,1)} %copy-done, ...), custom_call_target="tpu_custom_call" | custom-call | flops 7398752256 | bytes 20000000 | tf_op jit(solution)/shard_map/pallas_call | solution.py:495
  326.4 2.0 collective-permute-start.33
  328.4 3.7 %collective-permute-start.30 = (bf16[4032,128]{1,0:T(8,128)(2,1)}, bf16[4032,128]{1,0:T(8,128)(2,1)S(1)}, u32[]{:S(2)}, u32[]{:S(2)}) collective-permute-start(bf16[4032,128]{1,0:T(8,128)(2,1)} %copy-done.4), channel_id=1, source_target_pairs={{0,0},{1,1},{2,2},{3,3},{4,4},{5,5},{6,6},{7,7},{8,16},{9,17},{10,... | collective-permute-start | bytes 3096584 | tf_op jit(solution)/shard_map/ppermute | solution.py:57
  332.2 19.0 %collective-permute-done.32.r2 = bf16[4032,128]{1,0:T(8,128)(2,1)S(1)} collective-permute-done((bf16[4032,128]{1,0:T(8,128)(2,1)}, bf16[4032,128]{1,0:T(8,128)(2,1)S(1)}, u32[]{:S(2)}, u32[]{:S(2)}) %collective-permute-start.32) | collective-permute-done | bytes 1032224 | tf_op jit(solution)/shard_map/ppermute | solution.py:57
  352.4 11.2 %collective-permute-done.30.r0 = bf16[4032,128]{1,0:T(8,128)(2,1)S(1)} collective-permute-done((bf16[4032,128]{1,0:T(8,128)(2,1)}, bf16[4032,128]{1,0:T(8,128)(2,1)S(1)}, u32[]{:S(2)}, u32[]{:S(2)}) %collective-permute-start.30) | collective-permute-done | bytes 1032224 | tf_op jit(solution)/shard_map/ppermute | solution.py:57
  363.6 3.3 shard_map.63
  (79 shorter events, 35.3 us)
Async XLA Ops:
  52.0 27.5 %all-to-all-start.1 = ((bf16[16,432,128]{2,1,0:T(8,128)(2,1)}), bf16[16,432,128]{2,1,0:T(8,128)(2,1)}, u32[]{:S(2)}, u32[]{:S(2)}) async-start(bf16[16,432,128]{2,1,0:T(8,128)(2,1)} %get-tuple-element.54), calls=%async_computation.1 | async-start | bytes 3538944 | tf_op jit(solution)/shard_map/all_to_all | solution.py:586
  64.6 43.2 %collective-permute-start = (bf16[7,80,1152]{2,1,0:T(8,128)(2,1)}, bf16[7,80,1152]{2,1,0:T(8,128)(2,1)S(1)}, u32[]{:S(2)}, u32[]{:S(2)}) collective-permute-start(bf16[7,80,1152]{2,1,0:T(8,128)(2,1)} %get-tuple-element.57), channel_id=1, source_target_pairs={{0,0},{1,1},{2,2},{3,3},{4,4},{5,5},{6,6},{7,7},{8,16},{9,17},{10,... | collective-permute-start | bytes 3870728 | tf_op jit(solution)/shard_map/ppermute | solution.py:57
  71.3 36.6 %collective-permute-start.2 = (bf16[7,80,1152]{2,1,0:T(8,128)(2,1)}, bf16[7,80,1152]{2,1,0:T(8,128)(2,1)}, u32[]{:S(2)}, u32[]{:S(2)}) collective-permute-start(bf16[7,80,1152]{2,1,0:T(8,128)(2,1)} %get-tuple-element.59), channel_id=1, source_target_pairs={{0,4},{1,5},{2,6},{3,7},{4,0},{5,1},{6,2},{7,3},{8,20},{9,21},{10,... | collective-permute-start | bytes 3870728 | tf_op jit(solution)/shard_map/ppermute | solution.py:57
  84.8 38.8 %collective-permute-start.1 = (bf16[7,48,1152]{2,1,0:T(8,128)(2,1)}, bf16[7,48,1152]{2,1,0:T(8,128)(2,1)}, u32[]{:S(2)}, u32[]{:S(2)}) collective-permute-start(bf16[7,48,1152]{2,1,0:T(8,128)(2,1)} %get-tuple-element.58), channel_id=1, source_target_pairs={{0,0},{1,1},{2,2},{3,3},{4,4},{5,5},{6,6},{7,7},{8,16},{9,17},{10,... | collective-permute-start | bytes 2322440 | tf_op jit(solution)/shard_map/ppermute | solution.py:57
  91.9 31.8 %collective-permute-start.3 = (bf16[7,48,1152]{2,1,0:T(8,128)(2,1)}, bf16[7,48,1152]{2,1,0:T(8,128)(2,1)}, u32[]{:S(2)}, u32[]{:S(2)}) collective-permute-start(bf16[7,48,1152]{2,1,0:T(8,128)(2,1)} %get-tuple-element.60), channel_id=1, source_target_pairs={{0,4},{1,5},{2,6},{3,7},{4,0},{5,1},{6,2},{7,3},{8,20},{9,21},{10,... | collective-permute-start | bytes 2322440 | tf_op jit(solution)/shard_map/ppermute | solution.py:57
  107.8 16.4 %collective-permute-start.4 = (bf16[7,80,1152]{2,1,0:T(8,128)(2,1)S(1)}, bf16[7,80,1152]{2,1,0:T(8,128)(2,1)S(1)}, u32[]{:S(2)}, u32[]{:S(2)}) collective-permute-start(bf16[7,80,1152]{2,1,0:T(8,128)(2,1)S(1)} %collective-permute-done.refs_1_.refs_0_), channel_id=1, source_target_pairs={{0,16},{1,17},{2,18},{3,19},{4,20},{5,21},{6,22},{7,23},{8,24},{9,... | collective-permute-start | bytes 3870728 | tf_op jit(solution)/shard_map/ppermute | solution.py:57
  107.8 16.4 %collective-permute-start.6 = (bf16[7,80,1152]{2,1,0:T(8,128)(2,1)}, bf16[7,80,1152]{2,1,0:T(8,128)(2,1)}, u32[]{:S(2)}, u32[]{:S(2)}) collective-permute-start(bf16[7,80,1152]{2,1,0:T(8,128)(2,1)} %collective-permute-done.2.refs_3_.refs_2_), channel_id=1, source_target_pairs={{0,16},{1,17},{2,18},{3,19},{4,20},{5,21},{6,22},{7,23},{8,24},{9,... | collective-permute-start | bytes 3870728 | tf_op jit(solution)/shard_map/ppermute | solution.py:57
  123.6 3.7 %collective-permute-start.7 = (bf16[7,48,1152]{2,1,0:T(8,128)(2,1)}, bf16[7,48,1152]{2,1,0:T(8,128)(2,1)}, u32[]{:S(2)}, u32[]{:S(2)}) collective-permute-start(bf16[7,48,1152]{2,1,0:T(8,128)(2,1)} %collective-permute-done.3.refs_4_.refs_3_), channel_id=1, source_target_pairs={{0,16},{1,17},{2,18},{3,19},{4,20},{5,21},{6,22},{7,23},{8,24},{9,... | collective-permute-start | bytes 2322440 | tf_op jit(solution)/shard_map/ppermute | solution.py:57
  132.1 12.2 %collective-permute-start.8 = (bf16[608,256]{1,0:T(8,128)(2,1)S(1)}, bf16[608,256]{1,0:T(8,128)(2,1)S(1)}, u32[]{:S(2)}, u32[]{:S(2)}) collective-permute-start(bf16[608,256]{1,0:T(8,128)(2,1)S(1)} %get-tuple-element.64), channel_id=1, source_target_pairs={{0,1},{1,2},{2,3},{3,0},{4,5},{5,6},{6,7},{7,4},{8,9},{9,10},{10,1... | collective-permute-start | bytes 933896 | tf_op jit(solution)/shard_map/ppermute | solution.py:57
  133.4 10.9 %collective-permute-start.9 = (bf16[592,256]{1,0:T(8,128)(2,1)S(1)}, bf16[592,256]{1,0:T(8,128)(2,1)S(1)}, u32[]{:S(2)}, u32[]{:S(2)}) collective-permute-start(bf16[592,256]{1,0:T(8,128)(2,1)S(1)} %get-tuple-element.65), channel_id=1, source_target_pairs={{0,3},{1,0},{2,1},{3,2},{4,7},{5,4},{6,5},{7,6},{8,11},{9,8},{10,9... | collective-permute-start | bytes 909320 | tf_op jit(solution)/shard_map/ppermute | solution.py:57
  134.9 9.4 %collective-permute-start.10 = (bf16[592,256]{1,0:T(8,128)(2,1)S(1)}, bf16[592,256]{1,0:T(8,128)(2,1)S(1)}, u32[]{:S(2)}, u32[]{:S(2)}) collective-permute-start(bf16[592,256]{1,0:T(8,128)(2,1)S(1)} %get-tuple-element.66), channel_id=1, source_target_pairs={{0,4},{1,5},{2,6},{3,7},{4,0},{5,1},{6,2},{7,3},{8,12},{9,13},{10,... | collective-permute-start | bytes 909320 | tf_op jit(solution)/shard_map/ppermute | solution.py:57
  144.6 21.3 %collective-permute-start.12 = (bf16[1792,256]{1,0:T(8,128)(2,1)S(1)}, bf16[1792,256]{1,0:T(8,128)(2,1)S(1)}, u32[]{:S(2)}, u32[]{:S(2)}) collective-permute-start(bf16[1792,256]{1,0:T(8,128)(2,1)S(1)} %get-tuple-element.79), channel_id=1, source_target_pairs={{0,3},{1,0},{2,1},{3,2},{4,7},{5,4},{6,5},{7,6},{8,11},{9,8},{10,9... | collective-permute-start | bytes 2752520 | tf_op jit(solution)/shard_map/ppermute | solution.py:57
  146.1 21.8 %collective-permute-start.13 = (bf16[1792,256]{1,0:T(8,128)(2,1)S(1)}, bf16[1792,256]{1,0:T(8,128)(2,1)S(1)}, u32[]{:S(2)}, u32[]{:S(2)}) collective-permute-start(bf16[1792,256]{1,0:T(8,128)(2,1)S(1)} %get-tuple-element.80), channel_id=1, source_target_pairs={{0,1},{1,2},{2,3},{3,0},{4,5},{5,6},{6,7},{7,4},{8,9},{9,10},{10,1... | collective-permute-start | bytes 2752520 | tf_op jit(solution)/shard_map/ppermute | solution.py:57
  146.2 21.7 %collective-permute-start.11 = (bf16[1792,256]{1,0:T(8,128)(2,1)S(1)}, bf16[1792,256]{1,0:T(8,128)(2,1)S(1)}, u32[]{:S(2)}, u32[]{:S(2)}) collective-permute-start(bf16[1792,256]{1,0:T(8,128)(2,1)S(1)} %get-tuple-element.67), channel_id=1, source_target_pairs={{0,4},{1,5},{2,6},{3,7},{4,0},{5,1},{6,2},{7,3},{8,12},{9,13},{10,... | collective-permute-start | bytes 2752520 | tf_op jit(solution)/shard_map/ppermute | solution.py:57
  156.3 29.3 %collective-permute-start.16 = (bf16[1792,256]{1,0:T(8,128)(2,1)S(1)}, bf16[1792,256]{1,0:T(8,128)(2,1)S(1)}, u32[]{:S(2)}, u32[]{:S(2)}) collective-permute-start(bf16[1792,256]{1,0:T(8,128)(2,1)S(1)} %get-tuple-element.83), channel_id=1, source_target_pairs={{0,3},{1,0},{2,1},{3,2},{4,7},{5,4},{6,5},{7,6},{8,11},{9,8},{10,9... | collective-permute-start | bytes 2752520 | tf_op jit(solution)/shard_map/ppermute | solution.py:57
  168.3 19.7 %collective-permute-start.15 = (bf16[1792,256]{1,0:T(8,128)(2,1)S(1)}, bf16[1792,256]{1,0:T(8,128)(2,1)S(1)}, u32[]{:S(2)}, u32[]{:S(2)}) collective-permute-start(bf16[1792,256]{1,0:T(8,128)(2,1)S(1)} %get-tuple-element.82), channel_id=1, source_target_pairs={{0,4},{1,5},{2,6},{3,7},{4,0},{5,1},{6,2},{7,3},{8,12},{9,13},{10,... | collective-permute-start | bytes 2752520 | tf_op jit(solution)/shard_map/ppermute | solution.py:57
  168.7 20.6 %collective-permute-start.14 = (bf16[1792,256]{1,0:T(8,128)(2,1)S(1)}, bf16[1792,256]{1,0:T(8,128)(2,1)S(1)}, u32[]{:S(2)}, u32[]{:S(2)}) collective-permute-start(bf16[1792,256]{1,0:T(8,128)(2,1)S(1)} %get-tuple-element.81), channel_id=1, source_target_pairs={{0,1},{1,2},{2,3},{3,0},{4,5},{5,6},{6,7},{7,4},{8,9},{9,10},{10,1... | collective-permute-start | bytes 2752520 | tf_op jit(solution)/shard_map/ppermute | solution.py:57
  189.6 18.5 %collective-permute-start.19 = (bf16[1792,256]{1,0:T(8,128)(2,1)S(1)}, bf16[1792,256]{1,0:T(8,128)(2,1)S(1)}, u32[]{:S(2)}, u32[]{:S(2)}) collective-permute-start(bf16[1792,256]{1,0:T(8,128)(2,1)S(1)} %shard_map.59.refs_0_), channel_id=1, source_target_pairs={{0,4},{1,5},{2,6},{3,7},{4,0},{5,1},{6,2},{7,3},{8,12},{9,13},{10,... | collective-permute-start | bytes 2752520 | tf_op jit(solution)/shard_map/ppermute | solution.py:57
  190.9 18.2 %collective-permute-start.18 = (bf16[1792,256]{1,0:T(8,128)(2,1)S(1)}, bf16[1792,256]{1,0:T(8,128)(2,1)S(1)}, u32[]{:S(2)}, u32[]{:S(2)}) collective-permute-start(bf16[1792,256]{1,0:T(8,128)(2,1)S(1)} %shard_map.59.refs_0_), channel_id=1, source_target_pairs={{0,3},{1,0},{2,1},{3,2},{4,7},{5,4},{6,5},{7,6},{8,11},{9,8},{10,9... | collective-permute-start | bytes 2752520 | tf_op jit(solution)/shard_map/ppermute | solution.py:57
  190.9 21.1 %collective-permute-start.17 = (bf16[1792,256]{1,0:T(8,128)(2,1)S(1)}, bf16[1792,256]{1,0:T(8,128)(2,1)S(1)}, u32[]{:S(2)}, u32[]{:S(2)}) collective-permute-start(bf16[1792,256]{1,0:T(8,128)(2,1)S(1)} %shard_map.59.refs_0_), channel_id=1, source_target_pairs={{0,1},{1,2},{2,3},{3,0},{4,5},{5,6},{6,7},{7,4},{8,9},{9,10},{10,1... | collective-permute-start | bytes 2752520 | tf_op jit(solution)/shard_map/ppermute | solution.py:57
  208.2 23.4 %collective-permute-start.21 = (bf16[1792,256]{1,0:T(8,128)(2,1)S(1)}, bf16[1792,256]{1,0:T(8,128)(2,1)S(1)}, u32[]{:S(2)}, u32[]{:S(2)}) collective-permute-start(bf16[1792,256]{1,0:T(8,128)(2,1)S(1)} %collective-permute-done.19.refs_3_), channel_id=1, source_target_pairs={{0,1},{1,2},{2,3},{3,0},{4,5},{5,6},{6,7},{7,4},{8,9},{9,10},{10,1... | collective-permute-start | bytes 2752520 | tf_op jit(solution)/shard_map/ppermute | solution.py:57
  209.0 22.6 %collective-permute-start.22 = (bf16[1792,256]{1,0:T(8,128)(2,1)S(1)}, bf16[1792,256]{1,0:T(8,128)(2,1)S(1)}, u32[]{:S(2)}, u32[]{:S(2)}) collective-permute-start(bf16[1792,256]{1,0:T(8,128)(2,1)S(1)} %collective-permute-done.18.refs_2_), channel_id=1, source_target_pairs={{0,3},{1,0},{2,1},{3,2},{4,7},{5,4},{6,5},{7,6},{8,11},{9,8},{10,9... | collective-permute-start | bytes 2752520 | tf_op jit(solution)/shard_map/ppermute | solution.py:57
  210.9 20.7 %collective-permute-start.20 = (bf16[1792,256]{1,0:T(8,128)(2,1)S(1)}, bf16[1792,256]{1,0:T(8,128)(2,1)S(1)}, u32[]{:S(2)}, u32[]{:S(2)}) collective-permute-start(bf16[1792,256]{1,0:T(8,128)(2,1)S(1)} %collective-permute-done.18.refs_2_), channel_id=1, source_target_pairs={{0,4},{1,5},{2,6},{3,7},{4,0},{5,1},{6,2},{7,3},{8,12},{9,13},{10,... | collective-permute-start | bytes 2752520 | tf_op jit(solution)/shard_map/ppermute | solution.py:57
  212.2 37.4 %collective-permute-start.27 = (bf16[5376,256]{1,0:T(8,128)(2,1)S(1)}, bf16[5376,256]{1,0:T(8,128)(2,1)S(1)}, u32[]{:S(2)}, u32[]{:S(2)}) collective-permute-start(bf16[5376,256]{1,0:T(8,128)(2,1)S(1)} %pad_maximum_fusion), channel_id=1, source_target_pairs={{0,16},{1,17},{2,18},{3,19},{4,20},{5,21},{6,22},{7,23},{8,24},{9,... | collective-permute-start | bytes 8257544 | tf_op jit(solution)/shard_map/ppermute | solution.py:57
  231.8 17.7 %collective-permute-start.28 = (bf16[5376,256]{1,0:T(8,128)(2,1)S(1)}, bf16[5376,256]{1,0:T(8,128)(2,1)S(1)}, u32[]{:S(2)}, u32[]{:S(2)}) collective-permute-start(bf16[5376,256]{1,0:T(8,128)(2,1)S(1)} %pad_maximum_fusion.1), channel_id=1, source_target_pairs={{0,16},{1,17},{2,18},{3,19},{4,20},{5,21},{6,22},{7,23},{8,24},{9,... | collective-permute-start | bytes 8257544 | tf_op jit(solution)/shard_map/ppermute | solution.py:57
  234.8 11.3 %collective-permute-start.23 = (bf16[608,256]{1,0:T(8,128)(2,1)S(1)}, bf16[608,256]{1,0:T(8,128)(2,1)S(1)}, u32[]{:S(2)}, u32[]{:S(2)}) collective-permute-start(bf16[608,256]{1,0:T(8,128)(2,1)S(1)} %slice.17), channel_id=1, source_target_pairs={{0,3},{1,0},{2,1},{3,2},{4,7},{5,4},{6,5},{7,6},{8,11},{9,8},{10,9... | collective-permute-start | bytes 933896 | tf_op jit(solution)/shard_map/ppermute | solution.py:57
  235.2 9.8 %collective-permute-start.24 = (bf16[592,256]{1,0:T(8,128)(2,1)S(1)}, bf16[592,256]{1,0:T(8,128)(2,1)S(1)}, u32[]{:S(2)}, u32[]{:S(2)}) collective-permute-start(bf16[592,256]{1,0:T(8,128)(2,1)S(1)} %slice.18), channel_id=1, source_target_pairs={{0,1},{1,2},{2,3},{3,0},{4,5},{5,6},{6,7},{7,4},{8,9},{9,10},{10,1... | collective-permute-start | bytes 909320 | tf_op jit(solution)/shard_map/ppermute | solution.py:57
  236.4 9.7 %collective-permute-start.25 = (bf16[592,256]{1,0:T(8,128)(2,1)S(1)}, bf16[592,256]{1,0:T(8,128)(2,1)S(1)}, u32[]{:S(2)}, u32[]{:S(2)}) collective-permute-start(bf16[592,256]{1,0:T(8,128)(2,1)S(1)} %slice.19), channel_id=1, source_target_pairs={{0,4},{1,5},{2,6},{3,7},{4,0},{5,1},{6,2},{7,3},{8,12},{9,13},{10,... | collective-permute-start | bytes 909320 | tf_op jit(solution)/shard_map/ppermute | solution.py:57
  308.0 44.4 %collective-permute-start.31 = (bf16[4032,128]{1,0:T(8,128)(2,1)}, bf16[4032,128]{1,0:T(8,128)(2,1)S(1)}, u32[]{:S(2)}, u32[]{:S(2)}) collective-permute-start(bf16[4032,128]{1,0:T(8,128)(2,1)} %shard_map.61), channel_id=1, source_target_pairs={{0,4},{1,5},{2,6},{3,7},{4,0},{5,1},{6,2},{7,3},{8,20},{9,21},{10,... | collective-permute-start | bytes 3096584 | tf_op jit(solution)/shard_map/ppermute | solution.py:57
  326.2 25.0 %collective-permute-start.32 = (bf16[4032,128]{1,0:T(8,128)(2,1)}, bf16[4032,128]{1,0:T(8,128)(2,1)S(1)}, u32[]{:S(2)}, u32[]{:S(2)}) collective-permute-start(bf16[4032,128]{1,0:T(8,128)(2,1)} %get-tuple-element.100), channel_id=1, source_target_pairs={{0,8},{1,9},{2,10},{3,11},{4,12},{5,13},{6,14},{7,15},{8,24},{9,25... | collective-permute-start | bytes 3096584 | tf_op jit(solution)/shard_map/ppermute | solution.py:57
  326.4 26.0 %collective-permute-start.33 = (bf16[4032,128]{1,0:T(8,128)(2,1)}, bf16[4032,128]{1,0:T(8,128)(2,1)S(1)}, u32[]{:S(2)}, u32[]{:S(2)}) collective-permute-start(bf16[4032,128]{1,0:T(8,128)(2,1)} %get-tuple-element.101), channel_id=1, source_target_pairs={{0,12},{1,13},{2,14},{3,15},{4,8},{5,9},{6,10},{7,11},{8,28},{9,29... | collective-permute-start | bytes 3096584 | tf_op jit(solution)/shard_map/ppermute | solution.py:57
  328.4 35.2 %collective-permute-start.30 = (bf16[4032,128]{1,0:T(8,128)(2,1)}, bf16[4032,128]{1,0:T(8,128)(2,1)S(1)}, u32[]{:S(2)}, u32[]{:S(2)}) collective-permute-start(bf16[4032,128]{1,0:T(8,128)(2,1)} %copy-done.4), channel_id=1, source_target_pairs={{0,0},{1,1},{2,2},{3,3},{4,4},{5,5},{6,6},{7,7},{8,16},{9,17},{10,... | collective-permute-start | bytes 3096584 | tf_op jit(solution)/shard_map/ppermute | solution.py:57
  (11 other events, 214.2 us)

commit v5 on v4

--- a/solution.py
+++ b/solution.py
@@ -27,9 +27,9 @@
 CHUNK = HALF_BLOCKS * SIDE
 PARTS = ((0, 608), (608, 592), (1200, 592))
 WIDE = 640
-SHARE = 576
+SHARES = (320, 256)
 AROUND = ROWS + CHUNK
-BACK_ROWS = 4032
+BACK_ROWS = (2240, 1792)
 
 AXES = ("x", "core", "zm", "zl", "y")
 PLANE = ("zm", "zl", "y")
@@ -304,7 +304,7 @@
     v2[...] = (p2[...] + g2[...].astype(F32)).astype(BF16)
 
 
-def last_sums_kernel(p, v1, v2, v3, turned, out):
+def last_sums_kernel(p, v1, v2, v3, first, second, out):
     total = p[...] + (v1[...].astype(F32) + v2[...].astype(F32) + v3[...].astype(F32))
     out[...] = total.astype(BF16)
 
@@ -322,23 +322,26 @@
 
 
 def turn_kernel(info, *refs):
-    blocks, out, held, flat, sems = refs[:8], *refs[8:]
+    blocks, (first, second, held, flat, sems) = refs[:8], refs[8:]
     c = info[0]
     shift = pl.multiple_of(512 * c, TILE)
     load_all(panel_copies(info, blocks, held, pl.ds(shift, WIDE)), sems)
     for r in range(ROWS // TILE):
         flat[:, r * TILE : (r + 1) * TILE] = held[r].T
-    out[:512, :ROWS] = flat[pl.ds(pl.multiple_of(128 * c, 64), 512), :]
-    out[512:, :ROWS] = flat[pl.ds(pl.multiple_of(512 - 448 * c, 64), 64), :]
-    out[:, ROWS:] = out[:, :CHUNK]
+    start = 128 * c
+    first[: 2 * TILE, :ROWS] = flat[pl.ds(pl.multiple_of(start, 128), 2 * TILE), :]
+    first[2 * TILE :, :ROWS] = flat[pl.ds(pl.multiple_of(512 - 448 * c, 64), 64), :]
+    second[:, :ROWS] = flat[pl.ds(pl.multiple_of(start + 2 * TILE, 128), 2 * TILE), :]
+    for out in (first, second):
+        out[:, ROWS:] = out[:, :CHUNK]
 
 
 def turned_panel(info, blocks):
     return pl.pallas_call(
         turn_kernel,
         in_specs=[SMEM] + [HBM] * 8,
-        out_specs=VMEM,
-        out_shape=jax.ShapeDtypeStruct((SHARE, AROUND), BF16),
+        out_specs=[VMEM] * 2,
+        out_shape=[jax.ShapeDtypeStruct((share, AROUND), BF16) for share in SHARES],
         scratch_shapes=[panel_shape(WIDE), pltpu.VMEM((WIDE, ROWS), BF16), pltpu.SemaphoreType.DMA((8,))],
         compiler_params=pltpu.CompilerParams(vmem_limit_bytes=24 * MIB),
         cost_estimate=cost(0, 1.2e7),
@@ -351,10 +354,11 @@
 def apply_kernel(info, *refs):
     own, ends, swapped = refs[:7], refs[7:10], refs[10:14]
     turned = refs[14]
-    out, near_direct, near_flipped, rest_direct, rest_flipped, all_mixed, scales = refs[15:22]
-    direct, flipped, mixed, stage, extra, sems, out_sems, keep_sems = refs[22:]
-    panel = turned
+    outs, all_direct, all_flipped, scales = refs[15:19], *refs[19:22]
+    direct, flipped, panel, mixed, stage, extra, sems, panel_sem, out_sems, keep_sems = refs[22:]
     c = info[0]
+    panel_copy = pltpu.make_async_copy(turned, panel, panel_sem)
+    panel_copy.start()
     pieces = [(c, ref, 0, rel) for ref, rel in zip(own, SOURCES)]
     pieces += [(1 - c, swapped[0], 0, SOURCES[0]), (1 - c, swapped[3], 0, SOURCES[7])]
     pieces += [(1 - c, swapped[1 + n // 3], n % 3 * CHUNK, SOURCES[1 + n]) for n in range(6)]
@@ -384,15 +388,9 @@
         pltpu.make_async_copy(whole, whole, sems.at[n]).wait()
     for copy in last:
         copy.wait()
-
-    near = near_start(info, 1)
-    other = (1 - c) * HALF_BLOCKS
-    keeps = [
-        pltpu.make_async_copy(direct.at[pl.ds(near, 4)], near_direct, keep_sems.at[0]),
-        pltpu.make_async_copy(direct.at[pl.ds(other, HALF_BLOCKS)], rest_direct, keep_sems.at[1]),
-    ]
-    for copy in keeps:
-        copy.start()
+    panel_copy.wait()
+
+    total = jnp.zeros((), F32)
     on = lax.broadcasted_iota(jnp.int32, (SIDE, SIDE), 0) == lax.broadcasted_iota(jnp.int32, (SIDE, SIDE), 1)
     diagonal = jnp.zeros((SIDE, SIDE), F32)
     for i in range(BLOCKS):
@@ -402,162 +400,166 @@
     factor = math.sqrt(ROWS) / (2.0 * (jnp.sqrt(total) + EPSILON))
     square = factor * factor
 
-    def product(i, x):
-        return gram_times(i, x, direct.at[i], flipped.at[i]) * square
-
-    @pl.loop(0, BLOCKS)
-    def _(i):
+    scale = math.sqrt(COLS) * factor
+    scales[...] = jnp.concatenate([scale] * 4 + [square] * 4)
+    keep = pltpu.make_async_copy(direct, all_direct, keep_sems.at[0])
+    keep.start()
+
+    def flip(i):
         for e in range(1, 7):
             far = (i + e) % BLOCKS
             flipped[i, (e - 1) * SIDE : e * SIDE, :] = direct[far, (7 - e) * SIDE : (8 - e) * SIDE, :].T
+
+    first_product(square, panel, direct, flipped, mixed, flip)
+    keep_more = pltpu.make_async_copy(flipped, all_flipped, keep_sems.at[1])
+    keep_more.start()
+    second_product(info, scale, square, panel, direct, flipped, mixed, stage, extra, outs, out_sems)
+    keep.wait()
+    keep_more.wait()
+
+
+def gram_times(i, x, direct, flipped):
+    first = pl.ds(pl.multiple_of((i + 7) % BLOCKS * SIDE, SIDE), 8 * SIDE)
+    rest = pl.ds(pl.multiple_of((i + 1) % BLOCKS * SIDE, SIDE), 6 * SIDE)
+    result = jnp.dot(x[:, first], direct[i], preferred_element_type=F32)
+    return result + jnp.dot(x[:, rest], flipped[i], preferred_element_type=F32)
+
+
+def first_product(square, panel, direct, flipped, mixed, ready):
+    @pl.loop(0, BLOCKS)
+    def _(i):
+        ready(i)
         columns = pl.ds(pl.multiple_of(i * SIDE, SIDE), SIDE)
-        mix = COEF_CUBIC * panel[:, columns].astype(F32) + COEF_QUINTIC * product(i, panel)
-        mix = mix.astype(BF16)
+        product = gram_times(i, panel, direct, flipped) * square
+        mix = (COEF_CUBIC * panel[:, columns].astype(F32) + COEF_QUINTIC * product).astype(BF16)
         mixed[:, columns] = mix
 
         @pl.when(i < HALF_BLOCKS)
         def _():
             mixed[:, pl.ds(pl.multiple_of(i * SIDE + ROWS, SIDE), SIDE)] = mix
 
-    scale = math.sqrt(COLS) * factor
-    scales[...] = jnp.concatenate([scale] * 4 + [square] * 4)
-    more = [
-        pltpu.make_async_copy(flipped.at[pl.ds(near, 4)], near_flipped, keep_sems.at[2]),
-        pltpu.make_async_copy(flipped.at[pl.ds(other, HALF_BLOCKS)], rest_flipped, keep_sems.at[3]),
-        pltpu.make_async_copy(mixed, all_mixed, keep_sems.at[4]),
-    ]
-    for copy in more:
-        copy.start()
-
-    @pl.loop(0, 4)
-    def _(b):
-        i = near_start(info, 0) + b
-        columns = pl.ds(pl.multiple_of(i * SIDE, SIDE), SIDE)
-        result = scale * (COEF_LINEAR * panel[:, columns].astype(F32) + product(i, mixed))
-        stage[pl.ds(pl.multiple_of(b * SIDE, SIDE), SIDE)] = result.astype(BF16).T
-
-    send_back(stage, extra, [(info[2] * TILE, out)], out_sems)
-    for copy in keeps + more:
-        copy.wait()
-
-
-def near_start(info, side):
-    a = info[2]
-    return info[0] * HALF_BLOCKS + 3 * (1 - a if side else a)
-
-
-def gram_times(i, x, direct, flipped):
-    first = pl.ds(pl.multiple_of((i + 7) % BLOCKS * SIDE, SIDE), 8 * SIDE)
-    rest = pl.ds(pl.multiple_of((i + 1) % BLOCKS * SIDE, SIDE), 6 * SIDE)
-    result = jnp.dot(x[:, first], direct[...], preferred_element_type=F32)
-    return result + jnp.dot(x[:, rest], flipped[...], preferred_element_type=F32)
-
-
-def send_back(stage, extra, outs, sems):
+
+def second_product(info, scale, square, panel, direct, flipped, mixed, stage, extra, outs, sems):
+    c, a = info[0], info[2]
     sends = []
-    for n, (start, out) in enumerate(outs):
-        for j in range(4):
-            rows = pl.ds(pl.multiple_of(start, 128), HEIGHT)
-            sends.append((stage.at[rows, j * TILE : (j + 1) * TILE], out.at[pl.ds(j * HEIGHT, HEIGHT)]))
-        halves = [stage[pl.ds(pl.multiple_of(start + row, 64), 448), 512:] for row in (0, 448)]
-        extra[n] = jnp.concatenate(halves, axis=1)
-        sends.append((extra.at[n], out.at[pl.ds(4 * HEIGHT, 448)]))
-    load_all(sends, sems)
-
-
-def rest_start(near, info):
-    return near_start(info, 1) if near else (1 - info[0]) * HALF_BLOCKS
-
-
-def rest_kernel(near, info, direct, flipped, panel, all_mixed, scales, *refs):
-    outs, (mixed, stage, extra, sems) = refs[:-4], refs[-4:]
-    b = pl.program_id(0)
-
-    @pl.when(b == 0)
-    def _():
-        load_all([(all_mixed, mixed)], sems)
-
-    i = rest_start(near, info) + b
-    product = gram_times(i, mixed, direct.at[0], flipped.at[0]) * scales[4:5]
-    result = scales[0:1] * (COEF_LINEAR * panel[...].astype(F32) + product)
-    stage[pl.ds(pl.multiple_of(b * SIDE, SIDE), SIDE)] = result.astype(BF16).T
-
-    @pl.when(b == pl.num_programs(0) - 1)
-    def _():
-        a = info[2]
-        starts = [(1 - a) * TILE] if near else [a * HEIGHT, (1 - a) * HEIGHT]
-        send_back(stage, extra, list(zip(starts, outs)), sems)
-
-
-def apply_rest(near, info, direct, flipped, mixed, scales, turned):
-    n = direct.shape[0]
-    count = 1 if near else 2
-    return pl.pallas_call(
-        lambda *refs: rest_kernel(near, *refs),
-        grid_spec=pltpu.PrefetchScalarGridSpec(
-            num_scalar_prefetch=1,
-            grid=(n,),
-            in_specs=[
-                pl.BlockSpec((1, 8 * SIDE, SIDE), lambda b, s: (b, 0, 0)),
-                pl.BlockSpec((1, 6 * SIDE, SIDE), lambda b, s: (b, 0, 0)),
-                pl.BlockSpec((SHARE, SIDE), lambda b, s: (0, rest_start(near, s) + b)),
-                HBM,
-                VMEM,
-            ],
-            out_specs=[HBM] * count,
-            scratch_shapes=[
-                pltpu.VMEM((SHARE, AROUND), BF16),
-                pltpu.VMEM((n * SIDE, SHARE), BF16),
-                pltpu.VMEM((2, 448, TILE), BF16),
-                pltpu.SemaphoreType.DMA((10,)),
-            ],
-        ),
-        out_shape=[jax.ShapeDtypeStruct((BACK_ROWS, TILE), BF16)] * count,
-        compiler_params=pltpu.CompilerParams(vmem_limit_bytes=62 * MIB),
-        cost_estimate=cost(n * 2 * SIDE * ROWS * SHARE, 2e7),
-    )(info, direct, flipped, turned, mixed, scales)
+    for turn in range(2):
+        half = 1 - c if turn else c
+
+        @pl.loop(0, HALF_BLOCKS)
+        def _(b):
+            i = half * HALF_BLOCKS + b
+            columns = pl.ds(pl.multiple_of(i * SIDE, SIDE), SIDE)
+            product = gram_times(i, mixed, direct, flipped) * square
+            result = scale * (COEF_LINEAR * panel[:, columns].astype(F32) + product)
+            stage[turn, pl.ds(pl.multiple_of(b * SIDE, SIDE), SIDE)] = result.astype(BF16).T
+
+        for side in range(2):
+            out = outs[2 * turn + side]
+            start = pl.multiple_of((1 - a if side else a) * HEIGHT, 128)
+            pieces = [
+                (stage.at[turn, pl.ds(start, HEIGHT), j * TILE : (j + 1) * TILE], out.at[pl.ds(j * HEIGHT, HEIGHT)])
+                for j in range(2)
+            ]
+            if extra is not None:
+                halves = [stage[turn, pl.ds(pl.multiple_of(start + row, 64), 448), 2 * TILE :] for row in (0, 448)]
+                extra[2 * turn + side] = jnp.concatenate(halves, axis=1)
+                pieces.append((extra.at[2 * turn + side], out.at[pl.ds(2 * HEIGHT, 448)]))
+            for piece in pieces:
+                sends.append(pltpu.make_async_copy(*piece, sems.at[len(sends)]))
+                sends[-1].start()
+    for send in sends:
+        send.wait()
+
+
+def rest_kernel(info, all_direct, all_flipped, turned, scales, *refs):
+    outs, (direct, flipped, panel, mixed, stage, sems, panel_sem, out_sems) = refs[:4], refs[4:]
+
+    def loads(i):
+        return (
+            pltpu.make_async_copy(all_direct.at[i], direct.at[i], sems.at[0, i]),
+            pltpu.make_async_copy(all_flipped.at[i], flipped.at[i], sems.at[1, i]),
+        )
+
+    panel_copy = pltpu.make_async_copy(turned, panel, panel_sem)
+    panel_copy.start()
+    for i in range(BLOCKS):
+        for load in loads(i):
+            load.start()
+    panel_copy.wait()
+    scale, square = scales[0:1], scales[4:5]
+
+    def arrive(i):
+        for load in loads(i):
+            load.wait()
+
+    first_product(square, panel, direct, flipped, mixed, arrive)
+    second_product(info, scale, square, panel, direct, flipped, mixed, stage, None, outs, out_sems)
+
+
+def apply_rest(info, direct, flipped, scales, turned):
+    share = SHARES[1]
+    return pl.pallas_call(
+        rest_kernel,
+        in_specs=[SMEM] + [HBM] * 3 + [VMEM],
+        out_specs=[HBM] * 4,
+        out_shape=[jax.ShapeDtypeStruct((BACK_ROWS[1], TILE), BF16)] * 4,
+        scratch_shapes=[
+            pltpu.VMEM((BLOCKS, 8 * SIDE, SIDE), BF16),
+            pltpu.VMEM((BLOCKS, 6 * SIDE, SIDE), BF16),
+            pltpu.VMEM((share, AROUND), BF16),
+            pltpu.VMEM((share, AROUND), BF16),
+            pltpu.VMEM((2, CHUNK, share), BF16),
+            pltpu.SemaphoreType.DMA((2, BLOCKS)),
+            pltpu.SemaphoreType.DMA,
+            pltpu.SemaphoreType.DMA((8,)),
+        ],
+        compiler_params=pltpu.CompilerParams(vmem_limit_bytes=58 * MIB),
+        cost_estimate=cost(4 * ROWS * ROWS * share, 3e7),
+    )(info, direct, flipped, turned, scales)
 
 
 def apply_poly(info, own, ends, swapped, turned):
+    share = SHARES[0]
     return pl.pallas_call(
         apply_kernel,
-        in_specs=[SMEM] + [ANY] * 14 + [VMEM],
+        in_specs=[SMEM] + [HBM] * 15,
         out_specs=[HBM] * 6 + [VMEM],
-        out_shape=[
-            jax.ShapeDtypeStruct((BACK_ROWS, TILE), BF16),
-            jax.ShapeDtypeStruct((4, 8 * SIDE, SIDE), BF16),
-            jax.ShapeDtypeStruct((4, 6 * SIDE, SIDE), BF16),
-            jax.ShapeDtypeStruct((HALF_BLOCKS, 8 * SIDE, SIDE), BF16),
-            jax.ShapeDtypeStruct((HALF_BLOCKS, 6 * SIDE, SIDE), BF16),
-            jax.ShapeDtypeStruct((SHARE, AROUND), BF16),
+        out_shape=[jax.ShapeDtypeStruct((BACK_ROWS[0], TILE), BF16)] * 4
+        + [
+            jax.ShapeDtypeStruct((BLOCKS, 8 * SIDE, SIDE), BF16),
+            jax.ShapeDtypeStruct((BLOCKS, 6 * SIDE, SIDE), BF16),
             jax.ShapeDtypeStruct((8, SIDE), F32),
         ],
         scratch_shapes=[
             pltpu.VMEM((BLOCKS, 8 * SIDE, SIDE), BF16),
             pltpu.VMEM((BLOCKS, 6 * SIDE, SIDE), BF16),
-            pltpu.VMEM((SHARE, AROUND), BF16),
-            pltpu.VMEM((4 * SIDE, SHARE), BF16),
-            pltpu.VMEM((1, 448, TILE), BF16),
+            pltpu.VMEM((share, AROUND), BF16),
+            pltpu.VMEM((share, AROUND), BF16),
+            pltpu.VMEM((2, CHUNK, share), BF16),
+            pltpu.VMEM((4, 448, TILE), BF16),
             pltpu.SemaphoreType.DMA((32,)),
-            pltpu.SemaphoreType.DMA((5,)),
-            pltpu.SemaphoreType.DMA((5,)),
+            pltpu.SemaphoreType.DMA,
+            pltpu.SemaphoreType.DMA((12,)),
+            pltpu.SemaphoreType.DMA((2,)),
         ],
-        compiler_params=pltpu.CompilerParams(vmem_limit_bytes=44 * MIB),
-        cost_estimate=cost(3 * ROWS * ROWS * SHARE, 4e7),
+        compiler_params=pltpu.CompilerParams(vmem_limit_bytes=58 * MIB),
+        cost_estimate=cost(4 * ROWS * ROWS * share, 4e7),
     )(info, *own, *ends, *swapped, turned)
 
 
-def unpack_kernel(info, r0, r1, r2, r3, update):
+def unpack_kernel(info, *refs):
+    firsts, seconds, update = refs[:4], refs[4:8], refs[8]
     m, a = info[1], info[2]
-    for s, got in enumerate((r0, r1, r2, r3)):
+    for s in range(4):
         core = 1 - m if s >= 2 else m
         side = 1 - a if s % 2 else a
         for j in range(4):
             start = pl.multiple_of((9 * side + j + 5 * core) * TILE, TILE)
-            update[:, pl.ds(start, TILE)] = got[j * HEIGHT : (j + 1) * HEIGHT]
-    for s, (one, two) in enumerate(((r0, r2), (r1, r3))):
+            got = (firsts, seconds)[j // 2][s]
+            update[:, pl.ds(start, TILE)] = got[j % 2 * HEIGHT : (j % 2 + 1) * HEIGHT]
+    for s in range(2):
         side = 1 - a if s else a
-        one, two = one[4 * HEIGHT :], two[4 * HEIGHT :]
+        one, two = firsts[s][2 * HEIGHT :], firsts[s + 2][2 * HEIGHT :]
         low, high = jnp.where(m == 0, one, two), jnp.where(m == 0, two, one)
         tile = pl.ds(pl.multiple_of((9 * side + 4) * TILE, TILE), TILE)
         update[:448, tile] = jnp.concatenate([low[:, :64], high[:, :64]], axis=1)
@@ -567,7 +569,7 @@
 def unpack(info, parts):
     return pl.pallas_call(
         unpack_kernel,
-        in_specs=[SMEM] + [VMEM] * 4,
+        in_specs=[SMEM] + [VMEM] * 8,
         out_specs=VMEM,
         out_shape=jax.ShapeDtypeStruct((HEIGHT, 2304), BF16),
         compiler_params=pltpu.CompilerParams(vmem_limit_bytes=32 * MIB),
@@ -617,7 +619,7 @@
     w1, w2 = up(v1), across(v2)
     later, _ = lax.optimization_barrier((blocks, v1))
     turned = turned_panel(info, later)
-    (mine,) = in_vmem(last_sums_kernel, [chunk()], center, w1, w2, near, after=(turned,))
+    (mine,) = in_vmem(last_sums_kernel, [chunk()], center, w1, w2, near, after=turned)
 
     low, high, pair = up(mine), down(mine), across(mine)
     a1, a2, a3 = across(high), up(pair), down(high)
@@ -630,20 +632,22 @@
         swap(jnp.concatenate([a1, a2, a3])),
         swap(jnp.concatenate(ends)),
     )
-    first, *near_rows, rest_direct, rest_flipped, mixed, scales = apply_poly(
-        info, (mine, low, high, pair, a1, a2, a3), ends, swapped, turned
+    *sent, direct, flipped, scales = apply_poly(
+        info, (mine, low, high, pair, a1, a2, a3), ends, swapped, turned[0]
     )
-    (second,) = apply_rest(True, info, *near_rows, mixed, scales, turned)
-    later, _ = lax.optimization_barrier((mixed, second))
-    sent = (first, second, *apply_rest(False, info, rest_direct, rest_flipped, later, scales, turned))
-
-    parts = (
-        move(sent[0], lambda c, m, a, y: (m, c, a, y)),
-        move(sent[1], lambda c, m, a, y: (m, c, 1 - a, y)),
-        move(sent[2], lambda c, m, a, y: (m, 1 - c, a, y)),
-        move(sent[3], lambda c, m, a, y: (m, 1 - c, 1 - a, y)),
-    )
-    return new_momentum, unpack(info, parts)
+
+    def to_owners(sent):
+        return (
+            move(sent[0], lambda c, m, a, y: (m, c, a, y)),
+            move(sent[1], lambda c, m, a, y: (m, c, 1 - a, y)),
+            move(sent[2], lambda c, m, a, y: (m, 1 - c, a, y)),
+            move(sent[3], lambda c, m, a, y: (m, 1 - c, 1 - a, y)),
+        )
+
+    firsts = to_owners(sent)
+    sent = apply_rest(info, direct, flipped, scales, turned[1])
+    sent, firsts = lax.optimization_barrier((sent, firsts))
+    return new_momentum, unpack(info, firsts + to_owners(sent))
 
 
 def solution(mesh):

time: 368 us -> 353 us (0.959)
  waiting for transfers between devices: 141 us -> 129 us
  Pallas kernels: 120 us -> 112 us
  starting transfers between devices: 52.8 us -> 60.4 us
    ppermute x34 -> x38, waiting for transfers between devices: 133 us -> 121 us  [move(): return lax.ppermute(x, AXES[1:], pairs)]
    ppermute x34 -> x38, starting transfers between devices: 48.3 us -> 56 us  [move(): return lax.ppermute(x, AXES[1:], pairs)]
    pallas_call x5 -> x4, Pallas kernels: 77.8 us -> 70.4 us  [the longest x1 32.8 us: apply_poly(): pl.pallas_call(apply_kernel, in_specs=[SMEM] + [HBM] * 15, out_specs=[HBM...]
  transfers between devices with their start and end apart: 35 -> 39, of which waited for: 19 -> 19; matrix products, arithmetic and copies ran while one was open for 0% -> 0% of each run, Pallas kernels for 14% -> 19%
where the time goes in v5:
time: 353 us; the launch traced here: 352 us
  waiting for transfers between devices  129 us (37%)
  Pallas kernels  112 us (32%)
  starting transfers between devices  60.4 us (17%)
  blocking collectives  46 us (13%)
    ppermute x38, waiting for transfers between devices, move(): return lax.ppermute(x, AXES[1:], pairs)  121 us
    ppermute x38, starting transfers between devices, move(): return lax.ppermute(x, AXES[1:], pairs)  56 us
    all_to_all x1, blocking collectives, on_device(): lax.all_to_all(upper, PLANE, split_axis=0, concat_axis=0, tiled=True)  46 us
    pallas_call x1, Pallas kernels, apply_poly(): pl.pallas_call(apply_kernel, in_specs=[SMEM] + [HBM] * 15, out_specs=[HBM...  32.8 us
    pallas_call x1, Pallas kernels, apply_rest(): pl.pallas_call(rest_kernel, in_specs=[SMEM] + [HBM] * 3 + [VMEM], out_spe...  30.1 us
    pallas_call x3, Pallas kernels, gram_chunks(): pl.pallas_call(lambda *refs: gram_kernel(dests, *refs), in_specs=[SMEM] +...  22.8 us
    pallas_call x2, Pallas kernels, update_momentum(): pl.pallas_call(lambda *refs: momentum_kernel(part, *refs), in_specs=[SMEM...  12.5 us
    all_to_all x1, waiting for transfers between devices, on_device(): lax.all_to_all(lower, PLANE, split_axis=0, concat_axis=0, tiled=True)  7.97 us
  transfers between devices with their start and end apart: 39, of which 19 were waited for; matrix products, arithmetic and copies ran while one was open for 0% of the time, Pallas kernels for 19%

profile of v5, /device:TPU:1, one launch (start us, length us, event | category | flops | bytes accessed | tf_op | source)
XLA Modules:
  0.0 352.4 jit_solution(5317467661717596241)
XLA Ops:
  0.6 5.4 %shard_map.50 = (bf16[16,736,128]{2,1,0:T(8,128)(2,1)}, bf16[16,432,128]{2,1,0:T(8,128)(2,1)}) custom-call(s32[14]{0:T(128)} %ids.1, bf16[14,128,1152]{2,1,0:T(8,128)(2,1)} %tiles.1), custom_call_target="tpu_custom_call" | custom-call | bytes 8257536 | tf_op jit(solution)/shard_map/pallas_call | solution.py:123
  6.0 46.0 %all_to_all.10.refs_1_ = bf16[16,736,128]{2,1,0:T(8,128)(2,1)S(1)} all-to-all(bf16[16,736,128]{2,1,0:T(8,128)(2,1)} %get-tuple-element.63), channel_id=1, replica_groups=mesh['x'=4,'core'=2,'zm'=2,'zl'=2,'y'=4] {'zm','zl','y'}, dimensions={0} | all-to-all | bytes 6029312 | tf_op jit(solution)/shard_map/all_to_all | solution.py:586
  52.0 4.4 %all-to-all-start.1 = ((bf16[16,432,128]{2,1,0:T(8,128)(2,1)}), bf16[16,432,128]{2,1,0:T(8,128)(2,1)}, u32[]{:S(2)}, u32[]{:S(2)}) async-start(bf16[16,432,128]{2,1,0:T(8,128)(2,1)} %get-tuple-element.65), calls=%async_computation.1 | async-start | bytes 3538944 | tf_op jit(solution)/shard_map/all_to_all | solution.py:588
  57.6 7.1 %shard_map.51 = (f32[896,2304]{1,0:T(8,128)}, bf16[7,80,1152]{2,1,0:T(8,128)(2,1)}, bf16[7,80,1152]{2,1,0:T(8,128)(2,1)}) custom-call(s32[15]{0:T(128)} %pad_add_fusion.refs_0_, bf16[16,736,128]{2,1,0:T(8,128)(2,1)} %copy-done.5, f32[896,2304]{1,0:T(8,128)} %refs_2_.3), custom_call_target="tpu_custom_call" | custom-call | bytes 12386304 | tf_op jit(solution)/shard_map/pallas_call | solution.py:195
  64.7 6.6 %collective-permute-start = (bf16[7,80,1152]{2,1,0:T(8,128)(2,1)}, bf16[7,80,1152]{2,1,0:T(8,128)(2,1)S(1)}, u32[]{:S(2)}, u32[]{:S(2)}) collective-permute-start(bf16[7,80,1152]{2,1,0:T(8,128)(2,1)} %get-tuple-element.68), channel_id=1, source_target_pairs={{0,0},{1,1},{2,2},{3,3},{4,4},{5,5},{6,6},{7,7},{8,16},{9,17},{10,... | collective-permute-start | bytes 3870728 | tf_op jit(solution)/shard_map/ppermute | solution.py:57
  71.5 8.0 %all-to-all-done.1.refs_1_ = bf16[16,432,128]{2,1,0:T(8,128)(2,1)} async-done(((bf16[16,432,128]{2,1,0:T(8,128)(2,1)}), bf16[16,432,128]{2,1,0:T(8,128)(2,1)}, u32[]{:S(2)}, u32[]{:S(2)}) %all-to-all-start.1) | async-done | bytes 1769504 | tf_op jit(solution)/shard_map/all_to_all | solution.py:588
  79.4 5.4 %shard_map.52 = (f32[896,2304]{1,0:T(8,128)}, bf16[7,48,1152]{2,1,0:T(8,128)(2,1)}, bf16[7,48,1152]{2,1,0:T(8,128)(2,1)}) custom-call(s32[15]{0:T(128)} %pad_add_fusion.refs_0_, bf16[16,432,128]{2,1,0:T(8,128)(2,1)} %all-to-all-done.1.refs_1_, f32[896,2304]{1,0:T(8,128)} %refs_2_.3, ...), custom_call_target="tpu_custom_call", output_to_operand_aliasing={{0}: (3, {})} | custom-call | bytes 12386304 | tf_op jit(solution)/shard_map/pallas_call | solution.py:195
  84.8 7.1 %collective-permute-start.1 = (bf16[7,48,1152]{2,1,0:T(8,128)(2,1)}, bf16[7,48,1152]{2,1,0:T(8,128)(2,1)}, u32[]{:S(2)}, u32[]{:S(2)}) collective-permute-start(bf16[7,48,1152]{2,1,0:T(8,128)(2,1)} %get-tuple-element.69), channel_id=1, source_target_pairs={{0,0},{1,1},{2,2},{3,3},{4,4},{5,5},{6,6},{7,7},{8,16},{9,17},{10,... | collective-permute-start | bytes 2322440 | tf_op jit(solution)/shard_map/ppermute | solution.py:57
  92.1 15.8 %collective-permute-done.refs_1_.refs_0_ = bf16[7,80,1152]{2,1,0:T(8,128)(2,1)S(1)} collective-permute-done((bf16[7,80,1152]{2,1,0:T(8,128)(2,1)}, bf16[7,80,1152]{2,1,0:T(8,128)(2,1)S(1)}, u32[]{:S(2)}, u32[]{:S(2)}) %collective-permute-start) | collective-permute-done | bytes 1290272 | tf_op jit(solution)/shard_map/ppermute | solution.py:57
  108.4 15.3 %collective-permute-done.1.refs_2_.refs_1_ = bf16[7,48,1152]{2,1,0:T(8,128)(2,1)} collective-permute-done((bf16[7,48,1152]{2,1,0:T(8,128)(2,1)}, bf16[7,48,1152]{2,1,0:T(8,128)(2,1)}, u32[]{:S(2)}, u32[]{:S(2)}) %collective-permute-start.1) | collective-permute-done | bytes 774176 | tf_op jit(solution)/shard_map/ppermute | solution.py:57
  127.4 4.8 %shard_map.54 = (bf16[608,256]{1,0:T(8,128)(2,1)S(1)}, bf16[592,256]{1,0:T(8,128)(2,1)S(1)}, bf16[592,256]{1,0:T(8,128)(2,1)S(1)}) custom-call(s32[4]{0:T(128)S(1)} %pad_add_fusion.1.refs_0_.info, bf16[7,80,1152]{2,1,0:T(8,128)(2,1)S(1)} %collective-permute-done.refs_1_.refs_0_, bf16[7,48,1152]{2,1,0:T(8,128)(2,1)} %collective-permute-done.1.refs_2_.refs_1_, ...), custom_call_target="tpu_custom_call" | custom-call | flops 1056964608 | bytes 10135008 | tf_op jit(solution)/shard_map/pallas_call | solution.py:278
  135.8 8.5 %shard_map.53 = (f32[1792,256]{1,0:T(8,128)S(1)}, f32[1792,256]{1,0:T(8,128)S(1)}, f32[1792,256]{1,0:T(8,128)S(1)}) custom-call(s32[4]{0:T(128)S(1)} %pad_add_fusion.1.refs_0_.info, bf16[7,80,1152]{2,1,0:T(8,128)(2,1)S(1)} %collective-permute-done.refs_1_.refs_0_, bf16[7,48,1152]{2,1,0:T(8,128)(2,1)} %collective-permute-done.1.refs_2_.refs_1_, ...), custom_call_target="tpu_custom_call" | custom-call | flops 3170893824 | bytes 13805024 | tf_op jit(solution)/shard_map/pallas_call | solution.py:278
  146.7 9.6 %shard_map.56 = (f32[1792,256]{1,0:T(8,128)S(1)}, f32[1792,256]{1,0:T(8,128)S(1)}, bf16[1792,256]{1,0:T(8,128)(2,1)S(1)}, f32[1792,256]{1,0:T(8,128)S(1)}) custom-call(s32[4]{0:T(128)S(1)} %pad_add_fusion.1.refs_0_.info, bf16[7,80,1152]{2,1,0:T(8,128)(2,1)S(1)} %collective-permute-done.refs_1_.refs_0_, ...), custom_call_target="tpu_custom_call" | custom-call | flops 4227858432 | bytes 15640032 | tf_op jit(solution)/shard_map/pallas_call | solution.py:278
  156.3 2.4 collective-permute-start.16
  158.8 7.1 %collective-permute-done.12.g2 = bf16[1792,256]{1,0:T(8,128)(2,1)S(1)} collective-permute-done((bf16[1792,256]{1,0:T(8,128)(2,1)S(1)}, bf16[1792,256]{1,0:T(8,128)(2,1)S(1)}, u32[]{:S(2)}, u32[]{:S(2)}) %collective-permute-start.12) | collective-permute-done | bytes 917536 | tf_op jit(solution)/shard_map/ppermute | solution.py:57
  168.7 4.2 %shard_map.58 = (bf16[320,5376]{1,0:T(8,128)(2,1)S(1)}, bf16[256,5376]{1,0:T(8,128)(2,1)S(1)}) custom-call(s32[4]{0:T(128)S(1)} %pad_add_fusion.1.refs_0_.info, bf16[7,80,1152]{2,1,0:T(8,128)(2,1)S(1)} %collective-permute-done.refs_1_.refs_0_, bf16[7,48,1152]{2,1,0:T(8,128)(2,1)} %collective-permute-done.1.refs_2_.refs_1_, ...), custom_call_target="tpu_custom_call" | custom-call | bytes 12000000 | tf_op jit(solution)/shard_map/pallas_call | solution.py:340
  172.9 12.7 %collective-permute-done.16.v3 = bf16[1792,256]{1,0:T(8,128)(2,1)S(1)} collective-permute-done((bf16[1792,256]{1,0:T(8,128)(2,1)S(1)}, bf16[1792,256]{1,0:T(8,128)(2,1)S(1)}, u32[]{:S(2)}, u32[]{:S(2)}) %collective-permute-start.16) | collective-permute-done | bytes 917536 | tf_op jit(solution)/shard_map/ppermute | solution.py:57
  185.6 2.4 collective-permute-done.15.v2
  192.4 15.8 %collective-permute-done.19.refs_3_ = bf16[1792,256]{1,0:T(8,128)(2,1)S(1)} collective-permute-done((bf16[1792,256]{1,0:T(8,128)(2,1)S(1)}, bf16[1792,256]{1,0:T(8,128)(2,1)S(1)}, u32[]{:S(2)}, u32[]{:S(2)}) %collective-permute-start.19) | collective-permute-done | bytes 917536 | tf_op jit(solution)/shard_map/ppermute | solution.py:57
  212.2 5.2 %collective-permute-start.27 = (bf16[5376,256]{1,0:T(8,128)(2,1)S(1)}, bf16[5376,256]{1,0:T(8,128)(2,1)S(1)}, u32[]{:S(2)}, u32[]{:S(2)}) collective-permute-start(bf16[5376,256]{1,0:T(8,128)(2,1)S(1)} %pad_maximum_fusion), channel_id=1, source_target_pairs={{0,16},{1,17},{2,18},{3,19},{4,20},{5,21},{6,22},{7,23},{8,24},{9,... | collective-permute-start | bytes 8257544 | tf_op jit(solution)/shard_map/ppermute | solution.py:57
  217.5 14.2 %collective-permute-done.21.refs_5_ = bf16[1792,256]{1,0:T(8,128)(2,1)S(1)} collective-permute-done((bf16[1792,256]{1,0:T(8,128)(2,1)S(1)}, bf16[1792,256]{1,0:T(8,128)(2,1)S(1)}, u32[]{:S(2)}, u32[]{:S(2)}) %collective-permute-start.21) | collective-permute-done | bytes 917536 | tf_op jit(solution)/shard_map/ppermute | solution.py:57
  231.9 3.0 collective-permute-start.28
  237.0 7.4 %collective-permute-done.24.refs_8_ = bf16[592,256]{1,0:T(8,128)(2,1)S(1)} collective-permute-done((bf16[592,256]{1,0:T(8,128)(2,1)S(1)}, bf16[592,256]{1,0:T(8,128)(2,1)S(1)}, u32[]{:S(2)}, u32[]{:S(2)}) %collective-permute-start.24) | collective-permute-done | bytes 303136 | tf_op jit(solution)/shard_map/ppermute | solution.py:57
  251.4 32.8 %shard_map.60 = (bf16[2240,128]{1,0:T(8,128)(2,1)}, bf16[2240,128]{1,0:T(8,128)(2,1)}, bf16[2240,128]{1,0:T(8,128)(2,1)}, bf16[2240,128]{1,0:T(8,128)(2,1)}, bf1...) custom-call(s32[4]{0:T(128)} %copy-done.3, bf16[1792,256]{1,0:T(8,128)(2,1)} %copy-done.2, ...), custom_call_target="tpu_custom_call" | custom-call | flops 16441671680 | bytes 40000000 | tf_op jit(solution)/shard_map/pallas_call | solution.py:523
  284.2 4.1 %collective-permute-start.30 = (bf16[2240,128]{1,0:T(8,128)(2,1)}, bf16[2240,128]{1,0:T(8,128)(2,1)S(1)}, u32[]{:S(2)}, u32[]{:S(2)}) collective-permute-start(bf16[2240,128]{1,0:T(8,128)(2,1)} %get-tuple-element.112), channel_id=1, source_target_pairs={{0,0},{1,1},{2,2},{3,3},{4,4},{5,5},{6,6},{7,7},{8,16},{9,17},{10,... | collective-permute-start | bytes 1720328 | tf_op jit(solution)/shard_map/ppermute | solution.py:57
  290.1 2.2 collective-permute-start.33
  292.3 30.1 %shard_map.61 = (bf16[1792,128]{1,0:T(8,128)(2,1)}, bf16[1792,128]{1,0:T(8,128)(2,1)}, bf16[1792,128]{1,0:T(8,128)(2,1)}, bf16[1792,128]{1,0:T(8,128)(2,1)}) custom-call(s32[4]{0:T(128)} %copy-done.3, bf16[14,2048,256]{2,1,0:T(8,128)(2,1)} %get-tuple-element.105.all_direct, bf16[14,1536,256]{2,1,0:T(8,128)(2,1)} %get-tuple-element.106.all_flipped, ...), custom_call_target="tpu_custom_call" | custom-call | flops 13153337344 | bytes 30000000 | tf_op jit(solution)/shard_map/pallas_call | solution.py:501
  322.4 2.7 collective-permute-start.34
  325.1 2.0 collective-permute-start.35
  329.0 10.0 %collective-permute-done.34.refs_4_ = bf16[1792,128]{1,0:T(8,128)(2,1)S(1)} collective-permute-done((bf16[1792,128]{1,0:T(8,128)(2,1)}, bf16[1792,128]{1,0:T(8,128)(2,1)S(1)}, u32[]{:S(2)}, u32[]{:S(2)}) %collective-permute-start.34) | collective-permute-done | bytes 458784 | tf_op jit(solution)/shard_map/ppermute | solution.py:57
  339.0 9.3 %collective-permute-done.35.refs_5_ = bf16[1792,128]{1,0:T(8,128)(2,1)S(1)} collective-permute-done((bf16[1792,128]{1,0:T(8,128)(2,1)}, bf16[1792,128]{1,0:T(8,128)(2,1)S(1)}, u32[]{:S(2)}, u32[]{:S(2)}) %collective-permute-start.35) | collective-permute-done | bytes 458784 | tf_op jit(solution)/shard_map/ppermute | solution.py:57
  349.0 3.3 shard_map.62
  (106 shorter events, 36.5 us)
Async XLA Ops:
  52.0 27.5 %all-to-all-start.1 = ((bf16[16,432,128]{2,1,0:T(8,128)(2,1)}), bf16[16,432,128]{2,1,0:T(8,128)(2,1)}, u32[]{:S(2)}, u32[]{:S(2)}) async-start(bf16[16,432,128]{2,1,0:T(8,128)(2,1)} %get-tuple-element.65), calls=%async_computation.1 | async-start | bytes 3538944 | tf_op jit(solution)/shard_map/all_to_all | solution.py:588
  64.7 43.1 %collective-permute-start = (bf16[7,80,1152]{2,1,0:T(8,128)(2,1)}, bf16[7,80,1152]{2,1,0:T(8,128)(2,1)S(1)}, u32[]{:S(2)}, u32[]{:S(2)}) collective-permute-start(bf16[7,80,1152]{2,1,0:T(8,128)(2,1)} %get-tuple-element.68), channel_id=1, source_target_pairs={{0,0},{1,1},{2,2},{3,3},{4,4},{5,5},{6,6},{7,7},{8,16},{9,17},{10,... | collective-permute-start | bytes 3870728 | tf_op jit(solution)/shard_map/ppermute | solution.py:57
  71.4 36.5 %collective-permute-start.2 = (bf16[7,80,1152]{2,1,0:T(8,128)(2,1)}, bf16[7,80,1152]{2,1,0:T(8,128)(2,1)}, u32[]{:S(2)}, u32[]{:S(2)}) collective-permute-start(bf16[7,80,1152]{2,1,0:T(8,128)(2,1)} %get-tuple-element.70), channel_id=1, source_target_pairs={{0,4},{1,5},{2,6},{3,7},{4,0},{5,1},{6,2},{7,3},{8,20},{9,21},{10,... | collective-permute-start | bytes 3870728 | tf_op jit(solution)/shard_map/ppermute | solution.py:57
  84.8 38.8 %collective-permute-start.1 = (bf16[7,48,1152]{2,1,0:T(8,128)(2,1)}, bf16[7,48,1152]{2,1,0:T(8,128)(2,1)}, u32[]{:S(2)}, u32[]{:S(2)}) collective-permute-start(bf16[7,48,1152]{2,1,0:T(8,128)(2,1)} %get-tuple-element.69), channel_id=1, source_target_pairs={{0,0},{1,1},{2,2},{3,3},{4,4},{5,5},{6,6},{7,7},{8,16},{9,17},{10,... | collective-permute-start | bytes 2322440 | tf_op jit(solution)/shard_map/ppermute | solution.py:57
  91.9 31.8 %collective-permute-start.3 = (bf16[7,48,1152]{2,1,0:T(8,128)(2,1)}, bf16[7,48,1152]{2,1,0:T(8,128)(2,1)}, u32[]{:S(2)}, u32[]{:S(2)}) collective-permute-start(bf16[7,48,1152]{2,1,0:T(8,128)(2,1)} %get-tuple-element.71), channel_id=1, source_target_pairs={{0,4},{1,5},{2,6},{3,7},{4,0},{5,1},{6,2},{7,3},{8,20},{9,21},{10,... | collective-permute-start | bytes 2322440 | tf_op jit(solution)/shard_map/ppermute | solution.py:57
  107.8 16.4 %collective-permute-start.4 = (bf16[7,80,1152]{2,1,0:T(8,128)(2,1)S(1)}, bf16[7,80,1152]{2,1,0:T(8,128)(2,1)S(1)}, u32[]{:S(2)}, u32[]{:S(2)}) collective-permute-start(bf16[7,80,1152]{2,1,0:T(8,128)(2,1)S(1)} %collective-permute-done.refs_1_.refs_0_), channel_id=1, source_target_pairs={{0,16},{1,17},{2,18},{3,19},{4,20},{5,21},{6,22},{7,23},{8,24},{9,... | collective-permute-start | bytes 3870728 | tf_op jit(solution)/shard_map/ppermute | solution.py:57
  107.8 16.4 %collective-permute-start.6 = (bf16[7,80,1152]{2,1,0:T(8,128)(2,1)}, bf16[7,80,1152]{2,1,0:T(8,128)(2,1)}, u32[]{:S(2)}, u32[]{:S(2)}) collective-permute-start(bf16[7,80,1152]{2,1,0:T(8,128)(2,1)} %collective-permute-done.2.refs_3_.refs_2_), channel_id=1, source_target_pairs={{0,16},{1,17},{2,18},{3,19},{4,20},{5,21},{6,22},{7,23},{8,24},{9,... | collective-permute-start | bytes 3870728 | tf_op jit(solution)/shard_map/ppermute | solution.py:57
  132.1 12.2 %collective-permute-start.8 = (bf16[608,256]{1,0:T(8,128)(2,1)S(1)}, bf16[608,256]{1,0:T(8,128)(2,1)S(1)}, u32[]{:S(2)}, u32[]{:S(2)}) collective-permute-start(bf16[608,256]{1,0:T(8,128)(2,1)S(1)} %get-tuple-element.75), channel_id=1, source_target_pairs={{0,1},{1,2},{2,3},{3,0},{4,5},{5,6},{6,7},{7,4},{8,9},{9,10},{10,1... | collective-permute-start | bytes 933896 | tf_op jit(solution)/shard_map/ppermute | solution.py:57
  133.4 10.9 %collective-permute-start.9 = (bf16[592,256]{1,0:T(8,128)(2,1)S(1)}, bf16[592,256]{1,0:T(8,128)(2,1)S(1)}, u32[]{:S(2)}, u32[]{:S(2)}) collective-permute-start(bf16[592,256]{1,0:T(8,128)(2,1)S(1)} %get-tuple-element.76), channel_id=1, source_target_pairs={{0,3},{1,0},{2,1},{3,2},{4,7},{5,4},{6,5},{7,6},{8,11},{9,8},{10,9... | collective-permute-start | bytes 909320 | tf_op jit(solution)/shard_map/ppermute | solution.py:57
  144.7 21.3 %collective-permute-start.12 = (bf16[1792,256]{1,0:T(8,128)(2,1)S(1)}, bf16[1792,256]{1,0:T(8,128)(2,1)S(1)}, u32[]{:S(2)}, u32[]{:S(2)}) collective-permute-start(bf16[1792,256]{1,0:T(8,128)(2,1)S(1)} %get-tuple-element.90), channel_id=1, source_target_pairs={{0,3},{1,0},{2,1},{3,2},{4,7},{5,4},{6,5},{7,6},{8,11},{9,8},{10,9... | collective-permute-start | bytes 2752520 | tf_op jit(solution)/shard_map/ppermute | solution.py:57
  146.1 21.8 %collective-permute-start.13 = (bf16[1792,256]{1,0:T(8,128)(2,1)S(1)}, bf16[1792,256]{1,0:T(8,128)(2,1)S(1)}, u32[]{:S(2)}, u32[]{:S(2)}) collective-permute-start(bf16[1792,256]{1,0:T(8,128)(2,1)S(1)} %get-tuple-element.91), channel_id=1, source_target_pairs={{0,1},{1,2},{2,3},{3,0},{4,5},{5,6},{6,7},{7,4},{8,9},{9,10},{10,1... | collective-permute-start | bytes 2752520 | tf_op jit(solution)/shard_map/ppermute | solution.py:57
  146.2 21.7 %collective-permute-start.11 = (bf16[1792,256]{1,0:T(8,128)(2,1)S(1)}, bf16[1792,256]{1,0:T(8,128)(2,1)S(1)}, u32[]{:S(2)}, u32[]{:S(2)}) collective-permute-start(bf16[1792,256]{1,0:T(8,128)(2,1)S(1)} %get-tuple-element.78), channel_id=1, source_target_pairs={{0,4},{1,5},{2,6},{3,7},{4,0},{5,1},{6,2},{7,3},{8,12},{9,13},{10,... | collective-permute-start | bytes 2752520 | tf_op jit(solution)/shard_map/ppermute | solution.py:57
  156.3 29.2 %collective-permute-start.16 = (bf16[1792,256]{1,0:T(8,128)(2,1)S(1)}, bf16[1792,256]{1,0:T(8,128)(2,1)S(1)}, u32[]{:S(2)}, u32[]{:S(2)}) collective-permute-start(bf16[1792,256]{1,0:T(8,128)(2,1)S(1)} %get-tuple-element.94), channel_id=1, source_target_pairs={{0,3},{1,0},{2,1},{3,2},{4,7},{5,4},{6,5},{7,6},{8,11},{9,8},{10,9... | collective-permute-start | bytes 2752520 | tf_op jit(solution)/shard_map/ppermute | solution.py:57
  168.3 19.7 %collective-permute-start.15 = (bf16[1792,256]{1,0:T(8,128)(2,1)S(1)}, bf16[1792,256]{1,0:T(8,128)(2,1)S(1)}, u32[]{:S(2)}, u32[]{:S(2)}) collective-permute-start(bf16[1792,256]{1,0:T(8,128)(2,1)S(1)} %get-tuple-element.93), channel_id=1, source_target_pairs={{0,4},{1,5},{2,6},{3,7},{4,0},{5,1},{6,2},{7,3},{8,12},{9,13},{10,... | collective-permute-start | bytes 2752520 | tf_op jit(solution)/shard_map/ppermute | solution.py:57
  168.7 20.6 %collective-permute-start.14 = (bf16[1792,256]{1,0:T(8,128)(2,1)S(1)}, bf16[1792,256]{1,0:T(8,128)(2,1)S(1)}, u32[]{:S(2)}, u32[]{:S(2)}) collective-permute-start(bf16[1792,256]{1,0:T(8,128)(2,1)S(1)} %get-tuple-element.92), channel_id=1, source_target_pairs={{0,1},{1,2},{2,3},{3,0},{4,5},{5,6},{6,7},{7,4},{8,9},{9,10},{10,1... | collective-permute-start | bytes 2752520 | tf_op jit(solution)/shard_map/ppermute | solution.py:57
  189.7 18.5 %collective-permute-start.19 = (bf16[1792,256]{1,0:T(8,128)(2,1)S(1)}, bf16[1792,256]{1,0:T(8,128)(2,1)S(1)}, u32[]{:S(2)}, u32[]{:S(2)}) collective-permute-start(bf16[1792,256]{1,0:T(8,128)(2,1)S(1)} %shard_map.59.refs_0_), channel_id=1, source_target_pairs={{0,4},{1,5},{2,6},{3,7},{4,0},{5,1},{6,2},{7,3},{8,12},{9,13},{10,... | collective-permute-start | bytes 2752520 | tf_op jit(solution)/shard_map/ppermute | solution.py:57
  190.9 18.2 %collective-permute-start.18 = (bf16[1792,256]{1,0:T(8,128)(2,1)S(1)}, bf16[1792,256]{1,0:T(8,128)(2,1)S(1)}, u32[]{:S(2)}, u32[]{:S(2)}) collective-permute-start(bf16[1792,256]{1,0:T(8,128)(2,1)S(1)} %shard_map.59.refs_0_), channel_id=1, source_target_pairs={{0,3},{1,0},{2,1},{3,2},{4,7},{5,4},{6,5},{7,6},{8,11},{9,8},{10,9... | collective-permute-start | bytes 2752520 | tf_op jit(solution)/shard_map/ppermute | solution.py:57
  190.9 21.1 %collective-permute-start.17 = (bf16[1792,256]{1,0:T(8,128)(2,1)S(1)}, bf16[1792,256]{1,0:T(8,128)(2,1)S(1)}, u32[]{:S(2)}, u32[]{:S(2)}) collective-permute-start(bf16[1792,256]{1,0:T(8,128)(2,1)S(1)} %shard_map.59.refs_0_), channel_id=1, source_target_pairs={{0,1},{1,2},{2,3},{3,0},{4,5},{5,6},{6,7},{7,4},{8,9},{9,10},{10,1... | collective-permute-start | bytes 2752520 | tf_op jit(solution)/shard_map/ppermute | solution.py:57
  208.2 23.5 %collective-permute-start.21 = (bf16[1792,256]{1,0:T(8,128)(2,1)S(1)}, bf16[1792,256]{1,0:T(8,128)(2,1)S(1)}, u32[]{:S(2)}, u32[]{:S(2)}) collective-permute-start(bf16[1792,256]{1,0:T(8,128)(2,1)S(1)} %collective-permute-done.19.refs_3_), channel_id=1, source_target_pairs={{0,1},{1,2},{2,3},{3,0},{4,5},{5,6},{6,7},{7,4},{8,9},{9,10},{10,1... | collective-permute-start | bytes 2752520 | tf_op jit(solution)/shard_map/ppermute | solution.py:57
  209.1 22.6 %collective-permute-start.22 = (bf16[1792,256]{1,0:T(8,128)(2,1)S(1)}, bf16[1792,256]{1,0:T(8,128)(2,1)S(1)}, u32[]{:S(2)}, u32[]{:S(2)}) collective-permute-start(bf16[1792,256]{1,0:T(8,128)(2,1)S(1)} %collective-permute-done.18.refs_2_), channel_id=1, source_target_pairs={{0,3},{1,0},{2,1},{3,2},{4,7},{5,4},{6,5},{7,6},{8,11},{9,8},{10,9... | collective-permute-start | bytes 2752520 | tf_op jit(solution)/shard_map/ppermute | solution.py:57
  210.9 20.8 %collective-permute-start.20 = (bf16[1792,256]{1,0:T(8,128)(2,1)S(1)}, bf16[1792,256]{1,0:T(8,128)(2,1)S(1)}, u32[]{:S(2)}, u32[]{:S(2)}) collective-permute-start(bf16[1792,256]{1,0:T(8,128)(2,1)S(1)} %collective-permute-done.18.refs_2_), channel_id=1, source_target_pairs={{0,4},{1,5},{2,6},{3,7},{4,0},{5,1},{6,2},{7,3},{8,12},{9,13},{10,... | collective-permute-start | bytes 2752520 | tf_op jit(solution)/shard_map/ppermute | solution.py:57
  212.2 37.4 %collective-permute-start.27 = (bf16[5376,256]{1,0:T(8,128)(2,1)S(1)}, bf16[5376,256]{1,0:T(8,128)(2,1)S(1)}, u32[]{:S(2)}, u32[]{:S(2)}) collective-permute-start(bf16[5376,256]{1,0:T(8,128)(2,1)S(1)} %pad_maximum_fusion), channel_id=1, source_target_pairs={{0,16},{1,17},{2,18},{3,19},{4,20},{5,21},{6,22},{7,23},{8,24},{9,... | collective-permute-start | bytes 8257544 | tf_op jit(solution)/shard_map/ppermute | solution.py:57
  231.9 19.2 %collective-permute-start.28 = (bf16[5376,256]{1,0:T(8,128)(2,1)S(1)}, bf16[5376,256]{1,0:T(8,128)(2,1)}, u32[]{:S(2)}, u32[]{:S(2)}) collective-permute-start(bf16[5376,256]{1,0:T(8,128)(2,1)S(1)} %pad_maximum_fusion.1), channel_id=1, source_target_pairs={{0,16},{1,17},{2,18},{3,19},{4,20},{5,21},{6,22},{7,23},{8,24},{9,... | collective-permute-start | bytes 8257544 | tf_op jit(solution)/shard_map/ppermute | solution.py:57
  234.9 11.3 %collective-permute-start.23 = (bf16[608,256]{1,0:T(8,128)(2,1)S(1)}, bf16[608,256]{1,0:T(8,128)(2,1)S(1)}, u32[]{:S(2)}, u32[]{:S(2)}) collective-permute-start(bf16[608,256]{1,0:T(8,128)(2,1)S(1)} %slice.17), channel_id=1, source_target_pairs={{0,3},{1,0},{2,1},{3,2},{4,7},{5,4},{6,5},{7,6},{8,11},{9,8},{10,9... | collective-permute-start | bytes 933896 | tf_op jit(solution)/shard_map/ppermute | solution.py:57
  284.2 38.2 %collective-permute-start.30 = (bf16[2240,128]{1,0:T(8,128)(2,1)}, bf16[2240,128]{1,0:T(8,128)(2,1)S(1)}, u32[]{:S(2)}, u32[]{:S(2)}) collective-permute-start(bf16[2240,128]{1,0:T(8,128)(2,1)} %get-tuple-element.112), channel_id=1, source_target_pairs={{0,0},{1,1},{2,2},{3,3},{4,4},{5,5},{6,6},{7,7},{8,16},{9,17},{10,... | collective-permute-start | bytes 1720328 | tf_op jit(solution)/shard_map/ppermute | solution.py:57
  288.4 34.0 %collective-permute-start.31 = (bf16[2240,128]{1,0:T(8,128)(2,1)}, bf16[2240,128]{1,0:T(8,128)(2,1)S(1)}, u32[]{:S(2)}, u32[]{:S(2)}) collective-permute-start(bf16[2240,128]{1,0:T(8,128)(2,1)} %get-tuple-element.113), channel_id=1, source_target_pairs={{0,4},{1,5},{2,6},{3,7},{4,0},{5,1},{6,2},{7,3},{8,20},{9,21},{10,... | collective-permute-start | bytes 1720328 | tf_op jit(solution)/shard_map/ppermute | solution.py:57
  290.1 32.4 %collective-permute-start.32 = (bf16[2240,128]{1,0:T(8,128)(2,1)}, bf16[2240,128]{1,0:T(8,128)(2,1)S(1)}, u32[]{:S(2)}, u32[]{:S(2)}) collective-permute-start(bf16[2240,128]{1,0:T(8,128)(2,1)} %get-tuple-element.114), channel_id=1, source_target_pairs={{0,8},{1,9},{2,10},{3,11},{4,12},{5,13},{6,14},{7,15},{8,24},{9,25... | collective-permute-start | bytes 1720328 | tf_op jit(solution)/shard_map/ppermute | solution.py:57
  290.1 32.4 %collective-permute-start.33 = (bf16[2240,128]{1,0:T(8,128)(2,1)}, bf16[2240,128]{1,0:T(8,128)(2,1)S(1)}, u32[]{:S(2)}, u32[]{:S(2)}) collective-permute-start(bf16[2240,128]{1,0:T(8,128)(2,1)} %get-tuple-element.115), channel_id=1, source_target_pairs={{0,12},{1,13},{2,14},{3,15},{4,8},{5,9},{6,10},{7,11},{8,28},{9,29... | collective-permute-start | bytes 1720328 | tf_op jit(solution)/shard_map/ppermute | solution.py:57
  322.4 16.6 %collective-permute-start.34 = (bf16[1792,128]{1,0:T(8,128)(2,1)}, bf16[1792,128]{1,0:T(8,128)(2,1)S(1)}, u32[]{:S(2)}, u32[]{:S(2)}) collective-permute-start(bf16[1792,128]{1,0:T(8,128)(2,1)} %get-tuple-element.120), channel_id=1, source_target_pairs={{0,0},{1,1},{2,2},{3,3},{4,4},{5,5},{6,6},{7,7},{8,16},{9,17},{10,... | collective-permute-start | bytes 1376264 | tf_op jit(solution)/shard_map/ppermute | solution.py:57
  325.1 23.2 %collective-permute-start.35 = (bf16[1792,128]{1,0:T(8,128)(2,1)}, bf16[1792,128]{1,0:T(8,128)(2,1)S(1)}, u32[]{:S(2)}, u32[]{:S(2)}) collective-permute-start(bf16[1792,128]{1,0:T(8,128)(2,1)} %get-tuple-element.121), channel_id=1, source_target_pairs={{0,4},{1,5},{2,6},{3,7},{4,0},{5,1},{6,2},{7,3},{8,20},{9,21},{10,... | collective-permute-start | bytes 1376264 | tf_op jit(solution)/shard_map/ppermute | solution.py:57
  327.1 21.1 %collective-permute-start.36 = (bf16[1792,128]{1,0:T(8,128)(2,1)}, bf16[1792,128]{1,0:T(8,128)(2,1)S(1)}, u32[]{:S(2)}, u32[]{:S(2)}) collective-permute-start(bf16[1792,128]{1,0:T(8,128)(2,1)} %get-tuple-element.122), channel_id=1, source_target_pairs={{0,8},{1,9},{2,10},{3,11},{4,12},{5,13},{6,14},{7,15},{8,24},{9,25... | collective-permute-start | bytes 1376264 | tf_op jit(solution)/shard_map/ppermute | solution.py:57
  327.1 21.9 %collective-permute-start.37 = (bf16[1792,128]{1,0:T(8,128)(2,1)}, bf16[1792,128]{1,0:T(8,128)(2,1)S(1)}, u32[]{:S(2)}, u32[]{:S(2)}) collective-permute-start(bf16[1792,128]{1,0:T(8,128)(2,1)} %get-tuple-element.123), channel_id=1, source_target_pairs={{0,12},{1,13},{2,14},{3,15},{4,8},{5,9},{6,10},{7,11},{8,28},{9,29... | collective-permute-start | bytes 1376264 | tf_op jit(solution)/shard_map/ppermute | solution.py:57
  (25 other events, 336.5 us)

commit v6 on v3

--- a/solution.py
+++ b/solution.py
@@ -73,8 +73,24 @@
     return move(x, lambda c, m, a, y: (1 - c, m, a, y))
 
 
-def pack_kernel(details, tiles, upper, lower, held, first, second, sems, out_sems):
-    load_all([(tiles.at[i], held.at[i]) for i in range(tiles.shape[0])], sems)
+def pack_kernel(ids, tiles, upper, lower, slots, places, held, first, second, sems, out_sems):
+    n = tiles.shape[0]
+    loads = [pltpu.make_async_copy(tiles.at[i], held.at[i], sems.at[i]) for i in range(n)]
+    for load in loads:
+        load.start()
+    for o in range(upper.shape[0]):
+        slots[o] = 0
+        places[o] = -1
+
+    @pl.loop(0, n)
+    def _(i):
+        row, column = ids[i] // 8, ids[i] % 8
+        owner = row // 7 * 4 + column // 2
+        slots[owner] = i
+        places[owner] = row % 7 * 2 + column % 2
+
+    for load in loads:
+        load.wait()
 
     def copies(o):
         return (
@@ -84,12 +100,12 @@
 
     @pl.loop(0, upper.shape[0])
     def _(o):
-        slot = details[o]
+        slot = slots[o]
         for j in range(HALF // TILE):
             piece = held[slot, :, j * TILE : (j + 1) * TILE]
             for (row, size), out in zip(SPLIT, (first, second)):
                 out[o, j * size : (j + 1) * size, :] = piece[row : row + size]
-        place = jnp.full((LABEL, TILE), details[16 + o], jnp.int32)
+        place = jnp.full((LABEL, TILE), places[o], jnp.int32)
         first[o, first.shape[1] - LABEL :, :] = place.astype(F32).astype(BF16)
         for copy in copies(o):
             copy.start()
@@ -100,8 +116,8 @@
             copy.wait()
 
 
-def pack(details, tiles):
-    n = details.shape[0] // 2
+def pack(ids, tiles):
+    n = 16
     rows = [HALF // TILE * size for _, size in SPLIT]
     shapes = [(n, rows[0] + LABEL, TILE), (n, rows[1], TILE)]
     return pl.pallas_call(
@@ -109,12 +125,13 @@
         in_specs=[SMEM, HBM],
         out_specs=[HBM] * 2,
         out_shape=[jax.ShapeDtypeStruct(shape, BF16) for shape in shapes],
-        scratch_shapes=[pltpu.VMEM(tiles.shape, BF16)]
+        scratch_shapes=[pltpu.SMEM((n,), jnp.int32)] * 2
+        + [pltpu.VMEM(tiles.shape, BF16)]
         + [pltpu.VMEM(shape, BF16) for shape in shapes]
         + [pltpu.SemaphoreType.DMA((tiles.shape[0],)), pltpu.SemaphoreType.DMA((2, n))],
         compiler_params=pltpu.CompilerParams(vmem_limit_bytes=62 * MIB),
         cost_estimate=cost(0, 4 * tiles.size),
-    )(details, tiles)
+    )(ids, tiles)
 
 
 def momentum_kernel(part, info, arrived, momentum, *refs):
@@ -548,12 +565,7 @@
     info = jnp.stack([core, zm, zl, y]).astype(jnp.int32)
     tile_count = grad_tiles.shape[0]
 
-    owners = tile_ids // 8 // 7 * 4 + tile_ids % 8 // 2
-    places = tile_ids // 8 % 7 * 2 + tile_ids % 2
-    matches = owners[:, None] == jnp.arange(16, dtype=jnp.int32)[None, :]
-    slots = jnp.sum(jnp.where(matches, jnp.arange(tile_count, dtype=jnp.int32)[:, None], 0), axis=0)
-    labels = jnp.sum(jnp.where(matches, places[:, None] + 1, 0), axis=0) - 1
-    upper, lower = pack(jnp.concatenate([slots, labels]), grad_tiles)
+    upper, lower = pack(tile_ids, grad_tiles)
     upper = lax.all_to_all(upper, PLANE, split_axis=0, concat_axis=0, tiled=True)
     lower, _ = lax.optimization_barrier((lower, upper))
     lower = lax.all_to_all(lower, PLANE, split_axis=0, concat_axis=0, tiled=True)
@@ -594,15 +606,14 @@
 
     low, high, pair = up(mine), down(mine), across(mine)
     a1, a2, a3 = across(high), up(pair), down(high)
+    swap_mine, swap_near = swap(mine), swap(jnp.concatenate([low, high, pair]))
+    a1, a2, a3, swap_near = lax.optimization_barrier((a1, a2, a3, swap_near))
     ends = tuple(
         send(x[row : row + size]) for send, x, (row, size) in zip((down, up, across), (a1, a2, a3), PARTS)
     )
-    swapped = (
-        swap(mine),
-        swap(jnp.concatenate([low, high, pair])),
-        swap(jnp.concatenate([a1, a2, a3])),
-        swap(jnp.concatenate(ends)),
-    )
+    swap_far = swap(jnp.concatenate([a1, a2, a3]))
+    ends, swap_far = lax.optimization_barrier((ends, swap_far))
+    swapped = (swap_mine, swap_near, swap_far, swap(jnp.concatenate(ends)))
     *sent, direct, flipped, mixed, scales = apply_poly(info, (mine, low, high, pair, a1, a2, a3), ends, swapped, turned)
     sent += apply_rest(info, direct, flipped, mixed, scales, turned)
 

time: 350 us -> 354 us (1.011)
  waiting for transfers between devices: 135 us -> 143 us
    ppermute x34, waiting for transfers between devices: 127 us -> 135 us  [move(): return lax.ppermute(x, AXES[1:], pairs)]
  transfers between devices with their start and end apart: 35 -> 35, of which waited for: 20 -> 22; matrix products, arithmetic and copies ran while one was open for 0% -> 0% of each run, Pallas kernels for 15% -> 15%
where the time goes in v6:
time: 354 us; the launch traced here: 353 us
  waiting for transfers between devices  143 us (40%)
  Pallas kernels  104 us (29%)
  starting transfers between devices  52.3 us (15%)
  blocking collectives  46 us (13%)
  local copies, waits for them, and re-layouts  4.27 us (1%)
    ppermute x34, waiting for transfers between devices, move(): return lax.ppermute(x, AXES[1:], pairs)  135 us
    ppermute x34, starting transfers between devices, move(): return lax.ppermute(x, AXES[1:], pairs)  47.9 us
    all_to_all x1, blocking collectives, on_device(): lax.all_to_all(upper, PLANE, split_axis=0, concat_axis=0, tiled=True)  46 us
    pallas_call x1, Pallas kernels, apply_poly(): pl.pallas_call(apply_kernel, in_specs=[SMEM] + [HBM] * 15, out_specs=[HBM...  37.7 us
    pallas_call x3, Pallas kernels, gram_chunks(): pl.pallas_call(lambda *refs: gram_kernel(dests, *refs), in_specs=[SMEM] +...  22.8 us
    pallas_call x1, Pallas kernels, apply_rest(): pl.pallas_call(rest_kernel, grid_spec=pltpu.PrefetchScalarGridSpec(num_sc...  16.6 us
    pallas_call x2, Pallas kernels, update_momentum(): pl.pallas_call(lambda *refs: momentum_kernel(part, *refs), in_specs=[SMEM...  12.5 us
    all_to_all x1, waiting for transfers between devices, on_device(): lax.all_to_all(lower, PLANE, split_axis=0, concat_axis=0, tiled=True)  8.08 us
  transfers between devices with their start and end apart: 35, of which 22 were waited for; matrix products, arithmetic and copies ran while one was open for 0% of the time, Pallas kernels for 15%

profile of v6, /device:TPU:1, one launch (start us, length us, event | category | flops | bytes accessed | tf_op | source)
XLA Modules:
  0.0 352.5 jit_solution(7765505642149578901)
XLA Ops:
  0.6 5.4 %shard_map.50 = (bf16[16,736,128]{2,1,0:T(8,128)(2,1)}, bf16[16,432,128]{2,1,0:T(8,128)(2,1)}) custom-call(s32[14]{0:T(128)} %ids.1, bf16[14,128,1152]{2,1,0:T(8,128)(2,1)} %tiles.1), custom_call_target="tpu_custom_call" | custom-call | bytes 8257536 | tf_op jit(solution)/shard_map/pallas_call | solution.py:123
  6.0 46.0 %all_to_all.10.refs_1_ = bf16[16,736,128]{2,1,0:T(8,128)(2,1)S(1)} all-to-all(bf16[16,736,128]{2,1,0:T(8,128)(2,1)} %get-tuple-element.58), channel_id=1, replica_groups=mesh['x'=4,'core'=2,'zm'=2,'zl'=2,'y'=4] {'zm','zl','y'}, dimensions={0} | all-to-all | bytes 6029312 | tf_op jit(solution)/shard_map/all_to_all | solution.py:569
  52.0 4.4 %all-to-all-start.1 = ((bf16[16,432,128]{2,1,0:T(8,128)(2,1)}), bf16[16,432,128]{2,1,0:T(8,128)(2,1)}, u32[]{:S(2)}, u32[]{:S(2)}) async-start(bf16[16,432,128]{2,1,0:T(8,128)(2,1)} %get-tuple-element.60), calls=%async_computation.1 | async-start | bytes 3538944 | tf_op jit(solution)/shard_map/all_to_all | solution.py:571
  57.5 7.1 %shard_map.51 = (f32[896,2304]{1,0:T(8,128)}, bf16[7,80,1152]{2,1,0:T(8,128)(2,1)}, bf16[7,80,1152]{2,1,0:T(8,128)(2,1)}) custom-call(s32[15]{0:T(128)} %pad_add_fusion.refs_0_, bf16[16,736,128]{2,1,0:T(8,128)(2,1)} %copy-done.8, f32[896,2304]{1,0:T(8,128)} %refs_2_.3), custom_call_target="tpu_custom_call" | custom-call | bytes 12386304 | tf_op jit(solution)/shard_map/pallas_call | solution.py:195
  64.6 6.6 %collective-permute-start = (bf16[7,80,1152]{2,1,0:T(8,128)(2,1)}, bf16[7,80,1152]{2,1,0:T(8,128)(2,1)S(1)}, u32[]{:S(2)}, u32[]{:S(2)}) collective-permute-start(bf16[7,80,1152]{2,1,0:T(8,128)(2,1)} %get-tuple-element.63), channel_id=1, source_target_pairs={{0,0},{1,1},{2,2},{3,3},{4,4},{5,5},{6,6},{7,7},{8,16},{9,17},{10,... | collective-permute-start | bytes 3870728 | tf_op jit(solution)/shard_map/ppermute | solution.py:57
  71.4 8.1 %all-to-all-done.1.refs_1_ = bf16[16,432,128]{2,1,0:T(8,128)(2,1)} async-done(((bf16[16,432,128]{2,1,0:T(8,128)(2,1)}), bf16[16,432,128]{2,1,0:T(8,128)(2,1)}, u32[]{:S(2)}, u32[]{:S(2)}) %all-to-all-start.1) | async-done | bytes 1769504 | tf_op jit(solution)/shard_map/all_to_all | solution.py:571
  79.4 5.4 %shard_map.52 = (f32[896,2304]{1,0:T(8,128)}, bf16[7,48,1152]{2,1,0:T(8,128)(2,1)}, bf16[7,48,1152]{2,1,0:T(8,128)(2,1)}) custom-call(s32[15]{0:T(128)} %pad_add_fusion.refs_0_, bf16[16,432,128]{2,1,0:T(8,128)(2,1)} %all-to-all-done.1.refs_1_, f32[896,2304]{1,0:T(8,128)} %refs_2_.3, ...), custom_call_target="tpu_custom_call", output_to_operand_aliasing={{0}: (3, {})} | custom-call | bytes 12386304 | tf_op jit(solution)/shard_map/pallas_call | solution.py:195
  84.9 7.1 %collective-permute-start.1 = (bf16[7,48,1152]{2,1,0:T(8,128)(2,1)}, bf16[7,48,1152]{2,1,0:T(8,128)(2,1)}, u32[]{:S(2)}, u32[]{:S(2)}) collective-permute-start(bf16[7,48,1152]{2,1,0:T(8,128)(2,1)} %get-tuple-element.64), channel_id=1, source_target_pairs={{0,0},{1,1},{2,2},{3,3},{4,4},{5,5},{6,6},{7,7},{8,16},{9,17},{10,... | collective-permute-start | bytes 2322440 | tf_op jit(solution)/shard_map/ppermute | solution.py:57
  92.1 15.8 %collective-permute-done.refs_1_.refs_0_ = bf16[7,80,1152]{2,1,0:T(8,128)(2,1)S(1)} collective-permute-done((bf16[7,80,1152]{2,1,0:T(8,128)(2,1)}, bf16[7,80,1152]{2,1,0:T(8,128)(2,1)S(1)}, u32[]{:S(2)}, u32[]{:S(2)}) %collective-permute-start) | collective-permute-done | bytes 1290272 | tf_op jit(solution)/shard_map/ppermute | solution.py:57
  108.4 15.3 %collective-permute-done.1.refs_2_.refs_1_ = bf16[7,48,1152]{2,1,0:T(8,128)(2,1)} collective-permute-done((bf16[7,48,1152]{2,1,0:T(8,128)(2,1)}, bf16[7,48,1152]{2,1,0:T(8,128)(2,1)}, u32[]{:S(2)}, u32[]{:S(2)}) %collective-permute-start.1) | collective-permute-done | bytes 774176 | tf_op jit(solution)/shard_map/ppermute | solution.py:57
  127.4 4.8 %shard_map.54 = (bf16[608,256]{1,0:T(8,128)(2,1)S(1)}, bf16[592,256]{1,0:T(8,128)(2,1)S(1)}, bf16[592,256]{1,0:T(8,128)(2,1)S(1)}) custom-call(s32[4]{0:T(128)S(1)} %pad_add_fusion.1.refs_0_.info, bf16[7,80,1152]{2,1,0:T(8,128)(2,1)S(1)} %collective-permute-done.refs_1_.refs_0_, bf16[7,48,1152]{2,1,0:T(8,128)(2,1)} %collective-permute-done.1.refs_2_.refs_1_, ...), custom_call_target="tpu_custom_call" | custom-call | flops 1056964608 | bytes 10135008 | tf_op jit(solution)/shard_map/pallas_call | solution.py:278
  135.8 8.5 %shard_map.53 = (f32[1792,256]{1,0:T(8,128)S(1)}, f32[1792,256]{1,0:T(8,128)S(1)}, f32[1792,256]{1,0:T(8,128)S(1)}) custom-call(s32[4]{0:T(128)S(1)} %pad_add_fusion.1.refs_0_.info, bf16[7,80,1152]{2,1,0:T(8,128)(2,1)S(1)} %collective-permute-done.refs_1_.refs_0_, bf16[7,48,1152]{2,1,0:T(8,128)(2,1)} %collective-permute-done.1.refs_2_.refs_1_, ...), custom_call_target="tpu_custom_call" | custom-call | flops 3170893824 | bytes 13805024 | tf_op jit(solution)/shard_map/pallas_call | solution.py:278
  146.7 9.6 %shard_map.56 = (f32[1792,256]{1,0:T(8,128)S(1)}, f32[1792,256]{1,0:T(8,128)S(1)}, bf16[1792,256]{1,0:T(8,128)(2,1)S(1)}, f32[1792,256]{1,0:T(8,128)S(1)}) custom-call(s32[4]{0:T(128)S(1)} %pad_add_fusion.1.refs_0_.info, bf16[7,80,1152]{2,1,0:T(8,128)(2,1)S(1)} %collective-permute-done.refs_1_.refs_0_, ...), custom_call_target="tpu_custom_call" | custom-call | flops 4227858432 | bytes 15640032 | tf_op jit(solution)/shard_map/pallas_call | solution.py:278
  156.4 2.4 collective-permute-start.16
  158.8 7.1 %collective-permute-done.12.g2 = bf16[1792,256]{1,0:T(8,128)(2,1)S(1)} collective-permute-done((bf16[1792,256]{1,0:T(8,128)(2,1)S(1)}, bf16[1792,256]{1,0:T(8,128)(2,1)S(1)}, u32[]{:S(2)}, u32[]{:S(2)}) %collective-permute-start.12) | collective-permute-done | bytes 917536 | tf_op jit(solution)/shard_map/ppermute | solution.py:57
  169.5 4.2 %shard_map.58.turned.refs_14_.panel = bf16[576,5376]{1,0:T(8,128)(2,1)S(1)} custom-call(s32[4]{0:T(128)S(1)} %pad_add_fusion.1.refs_0_.info, bf16[7,80,1152]{2,1,0:T(8,128)(2,1)S(1)} %copy-done.2, bf16[7,48,1152]{2,1,0:T(8,128)(2,1)} %collective-permute-done.1.refs_2_.refs_1_, bf16[7,80,1152]{2,1,0:T(8,128)(2,1)} %collective-permute-done.2.refs_3_.refs_2_, ...), custom_call_target="tpu_custom_call" | custom-call | bytes 12000000 | tf_op jit(solution)/shard_map/pallas_call | solution.py:337
  173.8 11.8 %collective-permute-done.16.v3 = bf16[1792,256]{1,0:T(8,128)(2,1)S(1)} collective-permute-done((bf16[1792,256]{1,0:T(8,128)(2,1)S(1)}, bf16[1792,256]{1,0:T(8,128)(2,1)S(1)}, u32[]{:S(2)}, u32[]{:S(2)}) %collective-permute-start.16) | collective-permute-done | bytes 917536 | tf_op jit(solution)/shard_map/ppermute | solution.py:57
  185.6 2.4 collective-permute-done.15.v2
  192.3 16.0 %collective-permute-done.19.refs_3_ = bf16[1792,256]{1,0:T(8,128)(2,1)S(1)} collective-permute-done((bf16[1792,256]{1,0:T(8,128)(2,1)S(1)}, bf16[1792,256]{1,0:T(8,128)(2,1)S(1)}, u32[]{:S(2)}, u32[]{:S(2)}) %collective-permute-start.19) | collective-permute-done | bytes 917536 | tf_op jit(solution)/shard_map/ppermute | solution.py:57
  210.9 4.9 %collective-permute-start.23 = (bf16[5376,256]{1,0:T(8,128)(2,1)S(1)}, bf16[5376,256]{1,0:T(8,128)(2,1)S(1)}, u32[]{:S(2)}, u32[]{:S(2)}) collective-permute-start(bf16[5376,256]{1,0:T(8,128)(2,1)S(1)} %pad_maximum_fusion), channel_id=1, source_target_pairs={{0,16},{1,17},{2,18},{3,19},{4,20},{5,21},{6,22},{7,23},{8,24},{9,... | collective-permute-start | bytes 8257544 | tf_op jit(solution)/shard_map/ppermute | solution.py:57
  216.0 2.4 collective-permute-start.22
  218.9 20.0 %collective-permute-done.21.refs_5_ = bf16[1792,256]{1,0:T(8,128)(2,1)S(1)} collective-permute-done((bf16[1792,256]{1,0:T(8,128)(2,1)S(1)}, bf16[1792,256]{1,0:T(8,128)(2,1)S(1)}, u32[]{:S(2)}, u32[]{:S(2)}) %collective-permute-start.21) | collective-permute-done | bytes 917536 | tf_op jit(solution)/shard_map/ppermute | solution.py:57
  246.1 6.9 %collective-permute-done.26.refs_9_ = bf16[592,256]{1,0:T(8,128)(2,1)S(1)} collective-permute-done((bf16[592,256]{1,0:T(8,128)(2,1)S(1)}, bf16[592,256]{1,0:T(8,128)(2,1)S(1)}, u32[]{:S(2)}, u32[]{:S(2)}) %collective-permute-start.26) | collective-permute-done | bytes 303136 | tf_op jit(solution)/shard_map/ppermute | solution.py:57
  259.0 37.7 %shard_map.60 = (bf16[4032,128]{1,0:T(8,128)(2,1)}, bf16[4032,128]{1,0:T(8,128)(2,1)}, bf16[7,2048,256]{2,1,0:T(8,128)(2,1)}, bf16[7,1536,256]{2,1,0:T(8,128)(2,...) custom-call(s32[4]{0:T(128)} %copy-done.6, bf16[1792,256]{1,0:T(8,128)(2,1)} %copy-done.5, bf16[1792,256]{1,0:T(8,128)(2,1)} %copy-done.14, ...), custom_call_target="tpu_custom_call" | custom-call | flops 22196256768 | bytes 40000000 | tf_op jit(solution)/shard_map/pallas_call | solution.py:507
  296.8 4.0 %collective-permute-start.30 = (bf16[4032,128]{1,0:T(8,128)(2,1)}, bf16[4032,128]{1,0:T(8,128)(2,1)S(1)}, u32[]{:S(2)}, u32[]{:S(2)}) collective-permute-start(bf16[4032,128]{1,0:T(8,128)(2,1)} %get-tuple-element.106), channel_id=1, source_target_pairs={{0,0},{1,1},{2,2},{3,3},{4,4},{5,5},{6,6},{7,7},{8,16},{9,17},{10,... | collective-permute-start | bytes 3096584 | tf_op jit(solution)/shard_map/ppermute | solution.py:57
  302.4 16.6 %shard_map.61 = (bf16[4032,128]{1,0:T(8,128)(2,1)}, bf16[4032,128]{1,0:T(8,128)(2,1)}) custom-call(s32[4]{0:T(128)} %copy-done.6, bf16[7,2048,256]{2,1,0:T(8,128)(2,1)} %get-tuple-element.108.direct, bf16[7,1536,256]{2,1,0:T(8,128)(2,1)} %get-tuple-element.109.flipped, bf16[576,5376]{1,0:T(8,128)(2,1)} %copy-done, ...), custom_call_target="tpu_custom_call" | custom-call | flops 7398752256 | bytes 20000000 | tf_op jit(solution)/shard_map/pallas_call | solution.py:480
  319.1 2.1 collective-permute-start.33
  321.2 4.3 %collective-permute-done.30.r0 = bf16[4032,128]{1,0:T(8,128)(2,1)S(1)} collective-permute-done((bf16[4032,128]{1,0:T(8,128)(2,1)}, bf16[4032,128]{1,0:T(8,128)(2,1)S(1)}, u32[]{:S(2)}, u32[]{:S(2)}) %collective-permute-start.30) | collective-permute-done | bytes 1032224 | tf_op jit(solution)/shard_map/ppermute | solution.py:57
  325.5 7.7 %collective-permute-done.31.r1 = bf16[4032,128]{1,0:T(8,128)(2,1)} collective-permute-done((bf16[4032,128]{1,0:T(8,128)(2,1)}, bf16[4032,128]{1,0:T(8,128)(2,1)}, u32[]{:S(2)}, u32[]{:S(2)}) %collective-permute-start.31) | collective-permute-done | bytes 1032224 | tf_op jit(solution)/shard_map/ppermute | solution.py:57
  333.3 12.7 %collective-permute-done.32.r2 = bf16[4032,128]{1,0:T(8,128)(2,1)S(1)} collective-permute-done((bf16[4032,128]{1,0:T(8,128)(2,1)}, bf16[4032,128]{1,0:T(8,128)(2,1)S(1)}, u32[]{:S(2)}, u32[]{:S(2)}) %collective-permute-start.32) | collective-permute-done | bytes 1032224 | tf_op jit(solution)/shard_map/ppermute | solution.py:57
  346.0 2.5 collective-permute-done.33.r3
  348.5 4.0 %shard_map.62 = bf16[896,2304]{1,0:T(8,128)(2,1)} custom-call(s32[4]{0:T(128)S(1)} %copy-done.7, bf16[4032,128]{1,0:T(8,128)(2,1)S(1)} %collective-permute-done.30.r0, bf16[4032,128]{1,0:T(8,128)(2,1)} %collective-permute-done.31.r1, bf16[4032,128]{1,0:T(8,128)(2,1)S(1)} %collective-permute-done.32.r2, bf16[4032,128]{1,0:T(8,128)(2,1)S(1)} %collective-permute-done.33.r3), custom_call_target="tpu_custom_call" | custom-call | bytes 8300000 | tf_op jit(solution)/shard_map/pallas_call | solution.py:553
  (106 shorter events, 37.7 us)
Async XLA Ops:
  52.0 27.5 %all-to-all-start.1 = ((bf16[16,432,128]{2,1,0:T(8,128)(2,1)}), bf16[16,432,128]{2,1,0:T(8,128)(2,1)}, u32[]{:S(2)}, u32[]{:S(2)}) async-start(bf16[16,432,128]{2,1,0:T(8,128)(2,1)} %get-tuple-element.60), calls=%async_computation.1 | async-start | bytes 3538944 | tf_op jit(solution)/shard_map/all_to_all | solution.py:571
  64.6 43.2 %collective-permute-start = (bf16[7,80,1152]{2,1,0:T(8,128)(2,1)}, bf16[7,80,1152]{2,1,0:T(8,128)(2,1)S(1)}, u32[]{:S(2)}, u32[]{:S(2)}) collective-permute-start(bf16[7,80,1152]{2,1,0:T(8,128)(2,1)} %get-tuple-element.63), channel_id=1, source_target_pairs={{0,0},{1,1},{2,2},{3,3},{4,4},{5,5},{6,6},{7,7},{8,16},{9,17},{10,... | collective-permute-start | bytes 3870728 | tf_op jit(solution)/shard_map/ppermute | solution.py:57
  71.3 36.6 %collective-permute-start.2 = (bf16[7,80,1152]{2,1,0:T(8,128)(2,1)}, bf16[7,80,1152]{2,1,0:T(8,128)(2,1)}, u32[]{:S(2)}, u32[]{:S(2)}) collective-permute-start(bf16[7,80,1152]{2,1,0:T(8,128)(2,1)} %get-tuple-element.65), channel_id=1, source_target_pairs={{0,4},{1,5},{2,6},{3,7},{4,0},{5,1},{6,2},{7,3},{8,20},{9,21},{10,... | collective-permute-start | bytes 3870728 | tf_op jit(solution)/shard_map/ppermute | solution.py:57
  84.9 38.8 %collective-permute-start.1 = (bf16[7,48,1152]{2,1,0:T(8,128)(2,1)}, bf16[7,48,1152]{2,1,0:T(8,128)(2,1)}, u32[]{:S(2)}, u32[]{:S(2)}) collective-permute-start(bf16[7,48,1152]{2,1,0:T(8,128)(2,1)} %get-tuple-element.64), channel_id=1, source_target_pairs={{0,0},{1,1},{2,2},{3,3},{4,4},{5,5},{6,6},{7,7},{8,16},{9,17},{10,... | collective-permute-start | bytes 2322440 | tf_op jit(solution)/shard_map/ppermute | solution.py:57
  91.9 31.7 %collective-permute-start.3 = (bf16[7,48,1152]{2,1,0:T(8,128)(2,1)}, bf16[7,48,1152]{2,1,0:T(8,128)(2,1)}, u32[]{:S(2)}, u32[]{:S(2)}) collective-permute-start(bf16[7,48,1152]{2,1,0:T(8,128)(2,1)} %get-tuple-element.66), channel_id=1, source_target_pairs={{0,4},{1,5},{2,6},{3,7},{4,0},{5,1},{6,2},{7,3},{8,20},{9,21},{10,... | collective-permute-start | bytes 2322440 | tf_op jit(solution)/shard_map/ppermute | solution.py:57
  107.8 16.4 %collective-permute-start.4 = (bf16[7,80,1152]{2,1,0:T(8,128)(2,1)S(1)}, bf16[7,80,1152]{2,1,0:T(8,128)(2,1)S(1)}, u32[]{:S(2)}, u32[]{:S(2)}) collective-permute-start(bf16[7,80,1152]{2,1,0:T(8,128)(2,1)S(1)} %collective-permute-done.refs_1_.refs_0_), channel_id=1, source_target_pairs={{0,16},{1,17},{2,18},{3,19},{4,20},{5,21},{6,22},{7,23},{8,24},{9,... | collective-permute-start | bytes 3870728 | tf_op jit(solution)/shard_map/ppermute | solution.py:57
  107.9 16.4 %collective-permute-start.6 = (bf16[7,80,1152]{2,1,0:T(8,128)(2,1)}, bf16[7,80,1152]{2,1,0:T(8,128)(2,1)}, u32[]{:S(2)}, u32[]{:S(2)}) collective-permute-start(bf16[7,80,1152]{2,1,0:T(8,128)(2,1)} %collective-permute-done.2.refs_3_.refs_2_), channel_id=1, source_target_pairs={{0,16},{1,17},{2,18},{3,19},{4,20},{5,21},{6,22},{7,23},{8,24},{9,... | collective-permute-start | bytes 3870728 | tf_op jit(solution)/shard_map/ppermute | solution.py:57
  132.1 12.2 %collective-permute-start.8 = (bf16[608,256]{1,0:T(8,128)(2,1)S(1)}, bf16[608,256]{1,0:T(8,128)(2,1)S(1)}, u32[]{:S(2)}, u32[]{:S(2)}) collective-permute-start(bf16[608,256]{1,0:T(8,128)(2,1)S(1)} %get-tuple-element.70), channel_id=1, source_target_pairs={{0,1},{1,2},{2,3},{3,0},{4,5},{5,6},{6,7},{7,4},{8,9},{9,10},{10,1... | collective-permute-start | bytes 933896 | tf_op jit(solution)/shard_map/ppermute | solution.py:57
  133.4 10.9 %collective-permute-start.9 = (bf16[592,256]{1,0:T(8,128)(2,1)S(1)}, bf16[592,256]{1,0:T(8,128)(2,1)S(1)}, u32[]{:S(2)}, u32[]{:S(2)}) collective-permute-start(bf16[592,256]{1,0:T(8,128)(2,1)S(1)} %get-tuple-element.71), channel_id=1, source_target_pairs={{0,3},{1,0},{2,1},{3,2},{4,7},{5,4},{6,5},{7,6},{8,11},{9,8},{10,9... | collective-permute-start | bytes 909320 | tf_op jit(solution)/shard_map/ppermute | solution.py:57
  134.9 9.4 %collective-permute-start.10 = (bf16[592,256]{1,0:T(8,128)(2,1)S(1)}, bf16[592,256]{1,0:T(8,128)(2,1)S(1)}, u32[]{:S(2)}, u32[]{:S(2)}) collective-permute-start(bf16[592,256]{1,0:T(8,128)(2,1)S(1)} %get-tuple-element.72), channel_id=1, source_target_pairs={{0,4},{1,5},{2,6},{3,7},{4,0},{5,1},{6,2},{7,3},{8,12},{9,13},{10,... | collective-permute-start | bytes 909320 | tf_op jit(solution)/shard_map/ppermute | solution.py:57
  144.7 21.3 %collective-permute-start.12 = (bf16[1792,256]{1,0:T(8,128)(2,1)S(1)}, bf16[1792,256]{1,0:T(8,128)(2,1)S(1)}, u32[]{:S(2)}, u32[]{:S(2)}) collective-permute-start(bf16[1792,256]{1,0:T(8,128)(2,1)S(1)} %get-tuple-element.85), channel_id=1, source_target_pairs={{0,3},{1,0},{2,1},{3,2},{4,7},{5,4},{6,5},{7,6},{8,11},{9,8},{10,9... | collective-permute-start | bytes 2752520 | tf_op jit(solution)/shard_map/ppermute | solution.py:57
  146.1 21.8 %collective-permute-start.13 = (bf16[1792,256]{1,0:T(8,128)(2,1)S(1)}, bf16[1792,256]{1,0:T(8,128)(2,1)S(1)}, u32[]{:S(2)}, u32[]{:S(2)}) collective-permute-start(bf16[1792,256]{1,0:T(8,128)(2,1)S(1)} %get-tuple-element.86), channel_id=1, source_target_pairs={{0,1},{1,2},{2,3},{3,0},{4,5},{5,6},{6,7},{7,4},{8,9},{9,10},{10,1... | collective-permute-start | bytes 2752520 | tf_op jit(solution)/shard_map/ppermute | solution.py:57
  146.2 21.6 %collective-permute-start.11 = (bf16[1792,256]{1,0:T(8,128)(2,1)S(1)}, bf16[1792,256]{1,0:T(8,128)(2,1)S(1)}, u32[]{:S(2)}, u32[]{:S(2)}) collective-permute-start(bf16[1792,256]{1,0:T(8,128)(2,1)S(1)} %get-tuple-element.73), channel_id=1, source_target_pairs={{0,4},{1,5},{2,6},{3,7},{4,0},{5,1},{6,2},{7,3},{8,12},{9,13},{10,... | collective-permute-start | bytes 2752520 | tf_op jit(solution)/shard_map/ppermute | solution.py:57
  156.4 29.2 %collective-permute-start.16 = (bf16[1792,256]{1,0:T(8,128)(2,1)S(1)}, bf16[1792,256]{1,0:T(8,128)(2,1)S(1)}, u32[]{:S(2)}, u32[]{:S(2)}) collective-permute-start(bf16[1792,256]{1,0:T(8,128)(2,1)S(1)} %get-tuple-element.89), channel_id=1, source_target_pairs={{0,3},{1,0},{2,1},{3,2},{4,7},{5,4},{6,5},{7,6},{8,11},{9,8},{10,9... | collective-permute-start | bytes 2752520 | tf_op jit(solution)/shard_map/ppermute | solution.py:57
  168.3 19.7 %collective-permute-start.15 = (bf16[1792,256]{1,0:T(8,128)(2,1)S(1)}, bf16[1792,256]{1,0:T(8,128)(2,1)S(1)}, u32[]{:S(2)}, u32[]{:S(2)}) collective-permute-start(bf16[1792,256]{1,0:T(8,128)(2,1)S(1)} %get-tuple-element.88), channel_id=1, source_target_pairs={{0,4},{1,5},{2,6},{3,7},{4,0},{5,1},{6,2},{7,3},{8,12},{9,13},{10,... | collective-permute-start | bytes 2752520 | tf_op jit(solution)/shard_map/ppermute | solution.py:57
  168.7 20.6 %collective-permute-start.14 = (bf16[1792,256]{1,0:T(8,128)(2,1)S(1)}, bf16[1792,256]{1,0:T(8,128)(2,1)S(1)}, u32[]{:S(2)}, u32[]{:S(2)}) collective-permute-start(bf16[1792,256]{1,0:T(8,128)(2,1)S(1)} %get-tuple-element.87), channel_id=1, source_target_pairs={{0,1},{1,2},{2,3},{3,0},{4,5},{5,6},{6,7},{7,4},{8,9},{9,10},{10,1... | collective-permute-start | bytes 2752520 | tf_op jit(solution)/shard_map/ppermute | solution.py:57
  189.8 18.6 %collective-permute-start.19 = (bf16[1792,256]{1,0:T(8,128)(2,1)S(1)}, bf16[1792,256]{1,0:T(8,128)(2,1)S(1)}, u32[]{:S(2)}, u32[]{:S(2)}) collective-permute-start(bf16[1792,256]{1,0:T(8,128)(2,1)S(1)} %shard_map.59.refs_0_), channel_id=1, source_target_pairs={{0,4},{1,5},{2,6},{3,7},{4,0},{5,1},{6,2},{7,3},{8,12},{9,13},{10,... | collective-permute-start | bytes 2752520 | tf_op jit(solution)/shard_map/ppermute | solution.py:57
  190.9 18.1 %collective-permute-start.18 = (bf16[1792,256]{1,0:T(8,128)(2,1)S(1)}, bf16[1792,256]{1,0:T(8,128)(2,1)S(1)}, u32[]{:S(2)}, u32[]{:S(2)}) collective-permute-start(bf16[1792,256]{1,0:T(8,128)(2,1)S(1)} %shard_map.59.refs_0_), channel_id=1, source_target_pairs={{0,3},{1,0},{2,1},{3,2},{4,7},{5,4},{6,5},{7,6},{8,11},{9,8},{10,9... | collective-permute-start | bytes 2752520 | tf_op jit(solution)/shard_map/ppermute | solution.py:57
  190.9 19.1 %collective-permute-start.17 = (bf16[1792,256]{1,0:T(8,128)(2,1)S(1)}, bf16[1792,256]{1,0:T(8,128)(2,1)S(1)}, u32[]{:S(2)}, u32[]{:S(2)}) collective-permute-start(bf16[1792,256]{1,0:T(8,128)(2,1)S(1)} %shard_map.59.refs_0_), channel_id=1, source_target_pairs={{0,1},{1,2},{2,3},{3,0},{4,5},{5,6},{6,7},{7,4},{8,9},{9,10},{10,1... | collective-permute-start | bytes 2752520 | tf_op jit(solution)/shard_map/ppermute | solution.py:57
  210.9 28.9 %collective-permute-start.23 = (bf16[5376,256]{1,0:T(8,128)(2,1)S(1)}, bf16[5376,256]{1,0:T(8,128)(2,1)S(1)}, u32[]{:S(2)}, u32[]{:S(2)}) collective-permute-start(bf16[5376,256]{1,0:T(8,128)(2,1)S(1)} %pad_maximum_fusion), channel_id=1, source_target_pairs={{0,16},{1,17},{2,18},{3,19},{4,20},{5,21},{6,22},{7,23},{8,24},{9,... | collective-permute-start | bytes 8257544 | tf_op jit(solution)/shard_map/ppermute | solution.py:57
  215.8 23.2 %collective-permute-start.21 = (bf16[1792,256]{1,0:T(8,128)(2,1)S(1)}, bf16[1792,256]{1,0:T(8,128)(2,1)S(1)}, u32[]{:S(2)}, u32[]{:S(2)}) collective-permute-start(bf16[1792,256]{1,0:T(8,128)(2,1)S(1)} %collective-permute-done.19.refs_3_), channel_id=1, source_target_pairs={{0,1},{1,2},{2,3},{3,0},{4,5},{5,6},{6,7},{7,4},{8,9},{9,10},{10,1... | collective-permute-start | bytes 2752520 | tf_op jit(solution)/shard_map/ppermute | solution.py:57
  216.0 22.9 %collective-permute-start.22 = (bf16[1792,256]{1,0:T(8,128)(2,1)S(1)}, bf16[1792,256]{1,0:T(8,128)(2,1)S(1)}, u32[]{:S(2)}, u32[]{:S(2)}) collective-permute-start(bf16[1792,256]{1,0:T(8,128)(2,1)S(1)} %collective-permute-done.18.refs_2_), channel_id=1, source_target_pairs={{0,3},{1,0},{2,1},{3,2},{4,7},{5,4},{6,5},{7,6},{8,11},{9,8},{10,9... | collective-permute-start | bytes 2752520 | tf_op jit(solution)/shard_map/ppermute | solution.py:57
  218.5 21.3 %collective-permute-start.20 = (bf16[1792,256]{1,0:T(8,128)(2,1)S(1)}, bf16[1792,256]{1,0:T(8,128)(2,1)S(1)}, u32[]{:S(2)}, u32[]{:S(2)}) collective-permute-start(bf16[1792,256]{1,0:T(8,128)(2,1)S(1)} %collective-permute-done.18.refs_2_), channel_id=1, source_target_pairs={{0,4},{1,5},{2,6},{3,7},{4,0},{5,1},{6,2},{7,3},{8,12},{9,13},{10,... | collective-permute-start | bytes 2752520 | tf_op jit(solution)/shard_map/ppermute | solution.py:57
  241.7 12.7 %collective-permute-start.27 = (bf16[5376,256]{1,0:T(8,128)(2,1)S(1)}, bf16[5376,256]{1,0:T(8,128)(2,1)S(1)}, u32[]{:S(2)}, u32[]{:S(2)}) collective-permute-start(bf16[5376,256]{1,0:T(8,128)(2,1)S(1)} %pad_maximum_fusion.1), channel_id=1, source_target_pairs={{0,16},{1,17},{2,18},{3,19},{4,20},{5,21},{6,22},{7,23},{8,24},{9,... | collective-permute-start | bytes 8257544 | tf_op jit(solution)/shard_map/ppermute | solution.py:57
  243.1 11.3 %collective-permute-start.24 = (bf16[608,256]{1,0:T(8,128)(2,1)S(1)}, bf16[608,256]{1,0:T(8,128)(2,1)S(1)}, u32[]{:S(2)}, u32[]{:S(2)}) collective-permute-start(bf16[608,256]{1,0:T(8,128)(2,1)S(1)} %slice.13), channel_id=1, source_target_pairs={{0,3},{1,0},{2,1},{3,2},{4,7},{5,4},{6,5},{7,6},{8,11},{9,8},{10,9... | collective-permute-start | bytes 933896 | tf_op jit(solution)/shard_map/ppermute | solution.py:57
  244.5 8.6 %collective-permute-start.26 = (bf16[592,256]{1,0:T(8,128)(2,1)S(1)}, bf16[592,256]{1,0:T(8,128)(2,1)S(1)}, u32[]{:S(2)}, u32[]{:S(2)}) collective-permute-start(bf16[592,256]{1,0:T(8,128)(2,1)S(1)} %slice.15), channel_id=1, source_target_pairs={{0,4},{1,5},{2,6},{3,7},{4,0},{5,1},{6,2},{7,3},{8,12},{9,13},{10,... | collective-permute-start | bytes 909320 | tf_op jit(solution)/shard_map/ppermute | solution.py:57
  245.0 9.4 %collective-permute-start.25 = (bf16[592,256]{1,0:T(8,128)(2,1)S(1)}, bf16[592,256]{1,0:T(8,128)(2,1)S(1)}, u32[]{:S(2)}, u32[]{:S(2)}) collective-permute-start(bf16[592,256]{1,0:T(8,128)(2,1)S(1)} %slice.14), channel_id=1, source_target_pairs={{0,1},{1,2},{2,3},{3,0},{4,5},{5,6},{6,7},{7,4},{8,9},{9,10},{10,1... | collective-permute-start | bytes 909320 | tf_op jit(solution)/shard_map/ppermute | solution.py:57
  245.2 10.7 %collective-permute-start.28 = (bf16[1792,256]{1,0:T(8,128)(2,1)S(1)}, bf16[1792,256]{1,0:T(8,128)(2,1)S(1)}, u32[]{:S(2)}, u32[]{:S(2)}) collective-permute-start(bf16[1792,256]{1,0:T(8,128)(2,1)S(1)} %shard_map.59.refs_0_), channel_id=1, source_target_pairs={{0,16},{1,17},{2,18},{3,19},{4,20},{5,21},{6,22},{7,23},{8,24},{9,... | collective-permute-start | bytes 2752520 | tf_op jit(solution)/shard_map/ppermute | solution.py:57
  296.8 28.8 %collective-permute-start.30 = (bf16[4032,128]{1,0:T(8,128)(2,1)}, bf16[4032,128]{1,0:T(8,128)(2,1)S(1)}, u32[]{:S(2)}, u32[]{:S(2)}) collective-permute-start(bf16[4032,128]{1,0:T(8,128)(2,1)} %get-tuple-element.106), channel_id=1, source_target_pairs={{0,0},{1,1},{2,2},{3,3},{4,4},{5,5},{6,6},{7,7},{8,16},{9,17},{10,... | collective-permute-start | bytes 3096584 | tf_op jit(solution)/shard_map/ppermute | solution.py:57
  300.8 32.5 %collective-permute-start.31 = (bf16[4032,128]{1,0:T(8,128)(2,1)}, bf16[4032,128]{1,0:T(8,128)(2,1)}, u32[]{:S(2)}, u32[]{:S(2)}) collective-permute-start(bf16[4032,128]{1,0:T(8,128)(2,1)} %get-tuple-element.107), channel_id=1, source_target_pairs={{0,4},{1,5},{2,6},{3,7},{4,0},{5,1},{6,2},{7,3},{8,20},{9,21},{10,... | collective-permute-start | bytes 3096584 | tf_op jit(solution)/shard_map/ppermute | solution.py:57
  319.0 27.0 %collective-permute-start.32 = (bf16[4032,128]{1,0:T(8,128)(2,1)}, bf16[4032,128]{1,0:T(8,128)(2,1)S(1)}, u32[]{:S(2)}, u32[]{:S(2)}) collective-permute-start(bf16[4032,128]{1,0:T(8,128)(2,1)} %get-tuple-element.112), channel_id=1, source_target_pairs={{0,8},{1,9},{2,10},{3,11},{4,12},{5,13},{6,14},{7,15},{8,24},{9,25... | collective-permute-start | bytes 3096584 | tf_op jit(solution)/shard_map/ppermute | solution.py:57
  319.1 29.4 %collective-permute-start.33 = (bf16[4032,128]{1,0:T(8,128)(2,1)}, bf16[4032,128]{1,0:T(8,128)(2,1)S(1)}, u32[]{:S(2)}, u32[]{:S(2)}) collective-permute-start(bf16[4032,128]{1,0:T(8,128)(2,1)} %get-tuple-element.113), channel_id=1, source_target_pairs={{0,12},{1,13},{2,14},{3,15},{4,8},{5,9},{6,10},{7,11},{8,28},{9,29... | collective-permute-start | bytes 3096584 | tf_op jit(solution)/shard_map/ppermute | solution.py:57
  (25 other events, 293.9 us)

commit v7 on v6

--- a/solution.py
+++ b/solution.py
@@ -606,14 +606,12 @@
 
     low, high, pair = up(mine), down(mine), across(mine)
     a1, a2, a3 = across(high), up(pair), down(high)
-    swap_mine, swap_near = swap(mine), swap(jnp.concatenate([low, high, pair]))
-    a1, a2, a3, swap_near = lax.optimization_barrier((a1, a2, a3, swap_near))
     ends = tuple(
         send(x[row : row + size]) for send, x, (row, size) in zip((down, up, across), (a1, a2, a3), PARTS)
     )
-    swap_far = swap(jnp.concatenate([a1, a2, a3]))
-    ends, swap_far = lax.optimization_barrier((ends, swap_far))
-    swapped = (swap_mine, swap_near, swap_far, swap(jnp.concatenate(ends)))
+    swapped = (swap(mine), swap(jnp.concatenate([low, high, pair])), swap(jnp.concatenate([a1, a2, a3])))
+    ends, swapped = lax.optimization_barrier((ends, swapped))
+    swapped += (swap(jnp.concatenate(ends)),)
     *sent, direct, flipped, mixed, scales = apply_poly(info, (mine, low, high, pair, a1, a2, a3), ends, swapped, turned)
     sent += apply_rest(info, direct, flipped, mixed, scales, turned)
 

time: 354 us -> 348 us (0.983)
  waiting for transfers between devices: 143 us -> 138 us
    ppermute x34, waiting for transfers between devices: 135 us -> 130 us  [move(): return lax.ppermute(x, AXES[1:], pairs)]
  transfers between devices with their start and end apart: 35 -> 35, of which waited for: 22 -> 21; matrix products, arithmetic and copies ran while one was open for 0% -> 0% of each run, Pallas kernels for 15% -> 15%
where the time goes in v7:
time: 348 us; the launch traced here: 347 us
  waiting for transfers between devices  138 us (40%)
  Pallas kernels  104 us (30%)
  starting transfers between devices  53.1 us (15%)
  blocking collectives  46 us (13%)
    ppermute x34, waiting for transfers between devices, move(): return lax.ppermute(x, AXES[1:], pairs)  130 us
    ppermute x34, starting transfers between devices, move(): return lax.ppermute(x, AXES[1:], pairs)  48.7 us
    all_to_all x1, blocking collectives, on_device(): lax.all_to_all(upper, PLANE, split_axis=0, concat_axis=0, tiled=True)  46 us
    pallas_call x1, Pallas kernels, apply_poly(): pl.pallas_call(apply_kernel, in_specs=[SMEM] + [HBM] * 15, out_specs=[HBM...  37.7 us
    pallas_call x3, Pallas kernels, gram_chunks(): pl.pallas_call(lambda *refs: gram_kernel(dests, *refs), in_specs=[SMEM] +...  22.8 us
    pallas_call x1, Pallas kernels, apply_rest(): pl.pallas_call(rest_kernel, grid_spec=pltpu.PrefetchScalarGridSpec(num_sc...  16.6 us
    pallas_call x2, Pallas kernels, update_momentum(): pl.pallas_call(lambda *refs: momentum_kernel(part, *refs), in_specs=[SMEM...  12.5 us
    all_to_all x1, waiting for transfers between devices, on_device(): lax.all_to_all(lower, PLANE, split_axis=0, concat_axis=0, tiled=True)  8.08 us
  transfers between devices with their start and end apart: 35, of which 21 were waited for; matrix products, arithmetic and copies ran while one was open for 0% of the time, Pallas kernels for 15%

profile of v7, /device:TPU:1, one launch (start us, length us, event | category | flops | bytes accessed | tf_op | source)
XLA Modules:
  0.0 347.2 jit_solution(9701952827133333809)
XLA Ops:
  0.6 5.4 %shard_map.50 = (bf16[16,736,128]{2,1,0:T(8,128)(2,1)}, bf16[16,432,128]{2,1,0:T(8,128)(2,1)}) custom-call(s32[14]{0:T(128)} %ids.1, bf16[14,128,1152]{2,1,0:T(8,128)(2,1)} %tiles.1), custom_call_target="tpu_custom_call" | custom-call | bytes 8257536 | tf_op jit(solution)/shard_map/pallas_call | solution.py:123
  6.0 46.0 %all_to_all.10.refs_1_ = bf16[16,736,128]{2,1,0:T(8,128)(2,1)S(1)} all-to-all(bf16[16,736,128]{2,1,0:T(8,128)(2,1)} %get-tuple-element.56), channel_id=1, replica_groups=mesh['x'=4,'core'=2,'zm'=2,'zl'=2,'y'=4] {'zm','zl','y'}, dimensions={0} | all-to-all | bytes 6029312 | tf_op jit(solution)/shard_map/all_to_all | solution.py:569
  52.0 4.4 %all-to-all-start.1 = ((bf16[16,432,128]{2,1,0:T(8,128)(2,1)}), bf16[16,432,128]{2,1,0:T(8,128)(2,1)}, u32[]{:S(2)}, u32[]{:S(2)}) async-start(bf16[16,432,128]{2,1,0:T(8,128)(2,1)} %get-tuple-element.58), calls=%async_computation.1 | async-start | bytes 3538944 | tf_op jit(solution)/shard_map/all_to_all | solution.py:571
  57.5 7.1 %shard_map.51 = (f32[896,2304]{1,0:T(8,128)}, bf16[7,80,1152]{2,1,0:T(8,128)(2,1)}, bf16[7,80,1152]{2,1,0:T(8,128)(2,1)}) custom-call(s32[15]{0:T(128)} %pad_add_fusion.refs_0_, bf16[16,736,128]{2,1,0:T(8,128)(2,1)} %copy-done.8, f32[896,2304]{1,0:T(8,128)} %refs_2_.3), custom_call_target="tpu_custom_call" | custom-call | bytes 12386304 | tf_op jit(solution)/shard_map/pallas_call | solution.py:195
  64.6 6.6 %collective-permute-start = (bf16[7,80,1152]{2,1,0:T(8,128)(2,1)}, bf16[7,80,1152]{2,1,0:T(8,128)(2,1)S(1)}, u32[]{:S(2)}, u32[]{:S(2)}) collective-permute-start(bf16[7,80,1152]{2,1,0:T(8,128)(2,1)} %get-tuple-element.61), channel_id=1, source_target_pairs={{0,0},{1,1},{2,2},{3,3},{4,4},{5,5},{6,6},{7,7},{8,16},{9,17},{10,... | collective-permute-start | bytes 3870728 | tf_op jit(solution)/shard_map/ppermute | solution.py:57
  71.4 8.1 %all-to-all-done.1.refs_1_ = bf16[16,432,128]{2,1,0:T(8,128)(2,1)} async-done(((bf16[16,432,128]{2,1,0:T(8,128)(2,1)}), bf16[16,432,128]{2,1,0:T(8,128)(2,1)}, u32[]{:S(2)}, u32[]{:S(2)}) %all-to-all-start.1) | async-done | bytes 1769504 | tf_op jit(solution)/shard_map/all_to_all | solution.py:571
  79.4 5.4 %shard_map.52 = (f32[896,2304]{1,0:T(8,128)}, bf16[7,48,1152]{2,1,0:T(8,128)(2,1)}, bf16[7,48,1152]{2,1,0:T(8,128)(2,1)}) custom-call(s32[15]{0:T(128)} %pad_add_fusion.refs_0_, bf16[16,432,128]{2,1,0:T(8,128)(2,1)} %all-to-all-done.1.refs_1_, f32[896,2304]{1,0:T(8,128)} %refs_2_.3, ...), custom_call_target="tpu_custom_call", output_to_operand_aliasing={{0}: (3, {})} | custom-call | bytes 12386304 | tf_op jit(solution)/shard_map/pallas_call | solution.py:195
  84.9 7.1 %collective-permute-start.1 = (bf16[7,48,1152]{2,1,0:T(8,128)(2,1)}, bf16[7,48,1152]{2,1,0:T(8,128)(2,1)}, u32[]{:S(2)}, u32[]{:S(2)}) collective-permute-start(bf16[7,48,1152]{2,1,0:T(8,128)(2,1)} %get-tuple-element.62), channel_id=1, source_target_pairs={{0,0},{1,1},{2,2},{3,3},{4,4},{5,5},{6,6},{7,7},{8,16},{9,17},{10,... | collective-permute-start | bytes 2322440 | tf_op jit(solution)/shard_map/ppermute | solution.py:57
  92.1 15.8 %collective-permute-done.refs_1_.refs_0_ = bf16[7,80,1152]{2,1,0:T(8,128)(2,1)S(1)} collective-permute-done((bf16[7,80,1152]{2,1,0:T(8,128)(2,1)}, bf16[7,80,1152]{2,1,0:T(8,128)(2,1)S(1)}, u32[]{:S(2)}, u32[]{:S(2)}) %collective-permute-start) | collective-permute-done | bytes 1290272 | tf_op jit(solution)/shard_map/ppermute | solution.py:57
  108.4 15.3 %collective-permute-done.1.refs_2_.refs_1_ = bf16[7,48,1152]{2,1,0:T(8,128)(2,1)} collective-permute-done((bf16[7,48,1152]{2,1,0:T(8,128)(2,1)}, bf16[7,48,1152]{2,1,0:T(8,128)(2,1)}, u32[]{:S(2)}, u32[]{:S(2)}) %collective-permute-start.1) | collective-permute-done | bytes 774176 | tf_op jit(solution)/shard_map/ppermute | solution.py:57
  127.4 4.8 %shard_map.54 = (bf16[608,256]{1,0:T(8,128)(2,1)S(1)}, bf16[592,256]{1,0:T(8,128)(2,1)S(1)}, bf16[592,256]{1,0:T(8,128)(2,1)S(1)}) custom-call(s32[4]{0:T(128)S(1)} %pad_add_fusion.1.refs_0_.info, bf16[7,80,1152]{2,1,0:T(8,128)(2,1)S(1)} %collective-permute-done.refs_1_.refs_0_, bf16[7,48,1152]{2,1,0:T(8,128)(2,1)} %collective-permute-done.1.refs_2_.refs_1_, ...), custom_call_target="tpu_custom_call" | custom-call | flops 1056964608 | bytes 10135008 | tf_op jit(solution)/shard_map/pallas_call | solution.py:278
  135.8 8.5 %shard_map.53 = (f32[1792,256]{1,0:T(8,128)S(1)}, f32[1792,256]{1,0:T(8,128)S(1)}, f32[1792,256]{1,0:T(8,128)S(1)}) custom-call(s32[4]{0:T(128)S(1)} %pad_add_fusion.1.refs_0_.info, bf16[7,80,1152]{2,1,0:T(8,128)(2,1)S(1)} %collective-permute-done.refs_1_.refs_0_, bf16[7,48,1152]{2,1,0:T(8,128)(2,1)} %collective-permute-done.1.refs_2_.refs_1_, ...), custom_call_target="tpu_custom_call" | custom-call | flops 3170893824 | bytes 13805024 | tf_op jit(solution)/shard_map/pallas_call | solution.py:278
  146.7 9.6 %shard_map.56 = (f32[1792,256]{1,0:T(8,128)S(1)}, f32[1792,256]{1,0:T(8,128)S(1)}, bf16[1792,256]{1,0:T(8,128)(2,1)S(1)}, f32[1792,256]{1,0:T(8,128)S(1)}) custom-call(s32[4]{0:T(128)S(1)} %pad_add_fusion.1.refs_0_.info, bf16[7,80,1152]{2,1,0:T(8,128)(2,1)S(1)} %collective-permute-done.refs_1_.refs_0_, ...), custom_call_target="tpu_custom_call" | custom-call | flops 4227858432 | bytes 15640032 | tf_op jit(solution)/shard_map/pallas_call | solution.py:278
  158.8 7.1 %collective-permute-done.12.g2 = bf16[1792,256]{1,0:T(8,128)(2,1)S(1)} collective-permute-done((bf16[1792,256]{1,0:T(8,128)(2,1)S(1)}, bf16[1792,256]{1,0:T(8,128)(2,1)S(1)}, u32[]{:S(2)}, u32[]{:S(2)}) %collective-permute-start.12) | collective-permute-done | bytes 917536 | tf_op jit(solution)/shard_map/ppermute | solution.py:57
  169.5 4.2 %shard_map.58.turned.refs_14_.panel = bf16[576,5376]{1,0:T(8,128)(2,1)S(1)} custom-call(s32[4]{0:T(128)S(1)} %pad_add_fusion.1.refs_0_.info, bf16[7,80,1152]{2,1,0:T(8,128)(2,1)S(1)} %copy-done.2, bf16[7,48,1152]{2,1,0:T(8,128)(2,1)} %collective-permute-done.1.refs_2_.refs_1_, bf16[7,80,1152]{2,1,0:T(8,128)(2,1)} %collective-permute-done.2.refs_3_.refs_2_, ...), custom_call_target="tpu_custom_call" | custom-call | bytes 12000000 | tf_op jit(solution)/shard_map/pallas_call | solution.py:337
  173.8 11.8 %collective-permute-done.16.v3 = bf16[1792,256]{1,0:T(8,128)(2,1)S(1)} collective-permute-done((bf16[1792,256]{1,0:T(8,128)(2,1)S(1)}, bf16[1792,256]{1,0:T(8,128)(2,1)S(1)}, u32[]{:S(2)}, u32[]{:S(2)}) %collective-permute-start.16) | collective-permute-done | bytes 917536 | tf_op jit(solution)/shard_map/ppermute | solution.py:57
  192.3 16.0 %collective-permute-done.19.refs_3_ = bf16[1792,256]{1,0:T(8,128)(2,1)S(1)} collective-permute-done((bf16[1792,256]{1,0:T(8,128)(2,1)S(1)}, bf16[1792,256]{1,0:T(8,128)(2,1)S(1)}, u32[]{:S(2)}, u32[]{:S(2)}) %collective-permute-start.19) | collective-permute-done | bytes 917536 | tf_op jit(solution)/shard_map/ppermute | solution.py:57
  212.9 5.2 %collective-permute-start.27 = (bf16[5376,256]{1,0:T(8,128)(2,1)S(1)}, bf16[5376,256]{1,0:T(8,128)(2,1)S(1)}, u32[]{:S(2)}, u32[]{:S(2)}) collective-permute-start(bf16[5376,256]{1,0:T(8,128)(2,1)S(1)} %pad_maximum_fusion), channel_id=1, source_target_pairs={{0,16},{1,17},{2,18},{3,19},{4,20},{5,21},{6,22},{7,23},{8,24},{9,... | collective-permute-start | bytes 8257544 | tf_op jit(solution)/shard_map/ppermute | solution.py:57
  218.1 13.4 %collective-permute-done.21.refs_5_ = bf16[1792,256]{1,0:T(8,128)(2,1)S(1)} collective-permute-done((bf16[1792,256]{1,0:T(8,128)(2,1)S(1)}, bf16[1792,256]{1,0:T(8,128)(2,1)S(1)}, u32[]{:S(2)}, u32[]{:S(2)}) %collective-permute-start.21) | collective-permute-done | bytes 917536 | tf_op jit(solution)/shard_map/ppermute | solution.py:57
  231.7 3.1 collective-permute-start.28
  236.6 4.2 %collective-permute-done.26.refs_10_ = bf16[1792,256]{1,0:T(8,128)(2,1)S(1)} collective-permute-done((bf16[1792,256]{1,0:T(8,128)(2,1)S(1)}, bf16[1792,256]{1,0:T(8,128)(2,1)S(1)}, u32[]{:S(2)}, u32[]{:S(2)}) %collective-permute-start.26) | collective-permute-done | bytes 917536 | tf_op jit(solution)/shard_map/ppermute | solution.py:57
  241.3 3.3 collective-permute-done.24.refs_8_
  244.6 4.7 %collective-permute-done.25.refs_9_ = bf16[592,256]{1,0:T(8,128)(2,1)S(1)} collective-permute-done((bf16[592,256]{1,0:T(8,128)(2,1)S(1)}, bf16[592,256]{1,0:T(8,128)(2,1)S(1)}, u32[]{:S(2)}, u32[]{:S(2)}) %collective-permute-start.25) | collective-permute-done | bytes 303136 | tf_op jit(solution)/shard_map/ppermute | solution.py:57
  253.7 37.7 %shard_map.60 = (bf16[4032,128]{1,0:T(8,128)(2,1)}, bf16[4032,128]{1,0:T(8,128)(2,1)}, bf16[7,2048,256]{2,1,0:T(8,128)(2,1)}, bf16[7,1536,256]{2,1,0:T(8,128)(2,...) custom-call(s32[4]{0:T(128)} %copy-done.6, bf16[1792,256]{1,0:T(8,128)(2,1)} %copy-done.5, bf16[1792,256]{1,0:T(8,128)(2,1)} %copy-done.14, ...), custom_call_target="tpu_custom_call" | custom-call | flops 22196256768 | bytes 40000000 | tf_op jit(solution)/shard_map/pallas_call | solution.py:507
  291.4 3.9 %collective-permute-start.30 = (bf16[4032,128]{1,0:T(8,128)(2,1)}, bf16[4032,128]{1,0:T(8,128)(2,1)S(1)}, u32[]{:S(2)}, u32[]{:S(2)}) collective-permute-start(bf16[4032,128]{1,0:T(8,128)(2,1)} %get-tuple-element.102), channel_id=1, source_target_pairs={{0,0},{1,1},{2,2},{3,3},{4,4},{5,5},{6,6},{7,7},{8,16},{9,17},{10,... | collective-permute-start | bytes 3096584 | tf_op jit(solution)/shard_map/ppermute | solution.py:57
  296.5 16.6 %shard_map.61 = (bf16[4032,128]{1,0:T(8,128)(2,1)}, bf16[4032,128]{1,0:T(8,128)(2,1)}) custom-call(s32[4]{0:T(128)} %copy-done.6, bf16[7,2048,256]{2,1,0:T(8,128)(2,1)} %get-tuple-element.104.direct, bf16[7,1536,256]{2,1,0:T(8,128)(2,1)} %get-tuple-element.105.flipped, bf16[576,5376]{1,0:T(8,128)(2,1)} %copy-done, ...), custom_call_target="tpu_custom_call" | custom-call | flops 7398752256 | bytes 20000000 | tf_op jit(solution)/shard_map/pallas_call | solution.py:480
  313.2 2.6 collective-permute-start.33
  315.8 4.4 %collective-permute-done.30.r0 = bf16[4032,128]{1,0:T(8,128)(2,1)S(1)} collective-permute-done((bf16[4032,128]{1,0:T(8,128)(2,1)}, bf16[4032,128]{1,0:T(8,128)(2,1)S(1)}, u32[]{:S(2)}, u32[]{:S(2)}) %collective-permute-start.30) | collective-permute-done | bytes 1032224 | tf_op jit(solution)/shard_map/ppermute | solution.py:57
  320.3 9.1 %collective-permute-done.31.r1 = bf16[4032,128]{1,0:T(8,128)(2,1)} collective-permute-done((bf16[4032,128]{1,0:T(8,128)(2,1)}, bf16[4032,128]{1,0:T(8,128)(2,1)}, u32[]{:S(2)}, u32[]{:S(2)}) %collective-permute-start.31) | collective-permute-done | bytes 1032224 | tf_op jit(solution)/shard_map/ppermute | solution.py:57
  329.4 10.3 %collective-permute-done.32.r2 = bf16[4032,128]{1,0:T(8,128)(2,1)S(1)} collective-permute-done((bf16[4032,128]{1,0:T(8,128)(2,1)}, bf16[4032,128]{1,0:T(8,128)(2,1)S(1)}, u32[]{:S(2)}, u32[]{:S(2)}) %collective-permute-start.32) | collective-permute-done | bytes 1032224 | tf_op jit(solution)/shard_map/ppermute | solution.py:57
  339.6 3.5 %collective-permute-done.33.r3 = bf16[4032,128]{1,0:T(8,128)(2,1)S(1)} collective-permute-done((bf16[4032,128]{1,0:T(8,128)(2,1)}, bf16[4032,128]{1,0:T(8,128)(2,1)S(1)}, u32[]{:S(2)}, u32[]{:S(2)}) %collective-permute-start.33) | collective-permute-done | bytes 1032224 | tf_op jit(solution)/shard_map/ppermute | solution.py:57
  343.2 4.0 %shard_map.62 = bf16[896,2304]{1,0:T(8,128)(2,1)} custom-call(s32[4]{0:T(128)S(1)} %copy-done.7, bf16[4032,128]{1,0:T(8,128)(2,1)S(1)} %collective-permute-done.30.r0, bf16[4032,128]{1,0:T(8,128)(2,1)} %collective-permute-done.31.r1, bf16[4032,128]{1,0:T(8,128)(2,1)S(1)} %collective-permute-done.32.r2, bf16[4032,128]{1,0:T(8,128)(2,1)S(1)} %collective-permute-done.33.r3), custom_call_target="tpu_custom_call" | custom-call | bytes 8300000 | tf_op jit(solution)/shard_map/pallas_call | solution.py:553
  (106 shorter events, 37.1 us)
Async XLA Ops:
  52.0 27.5 %all-to-all-start.1 = ((bf16[16,432,128]{2,1,0:T(8,128)(2,1)}), bf16[16,432,128]{2,1,0:T(8,128)(2,1)}, u32[]{:S(2)}, u32[]{:S(2)}) async-start(bf16[16,432,128]{2,1,0:T(8,128)(2,1)} %get-tuple-element.58), calls=%async_computation.1 | async-start | bytes 3538944 | tf_op jit(solution)/shard_map/all_to_all | solution.py:571
  64.6 43.2 %collective-permute-start = (bf16[7,80,1152]{2,1,0:T(8,128)(2,1)}, bf16[7,80,1152]{2,1,0:T(8,128)(2,1)S(1)}, u32[]{:S(2)}, u32[]{:S(2)}) collective-permute-start(bf16[7,80,1152]{2,1,0:T(8,128)(2,1)} %get-tuple-element.61), channel_id=1, source_target_pairs={{0,0},{1,1},{2,2},{3,3},{4,4},{5,5},{6,6},{7,7},{8,16},{9,17},{10,... | collective-permute-start | bytes 3870728 | tf_op jit(solution)/shard_map/ppermute | solution.py:57
  71.3 36.6 %collective-permute-start.2 = (bf16[7,80,1152]{2,1,0:T(8,128)(2,1)}, bf16[7,80,1152]{2,1,0:T(8,128)(2,1)}, u32[]{:S(2)}, u32[]{:S(2)}) collective-permute-start(bf16[7,80,1152]{2,1,0:T(8,128)(2,1)} %get-tuple-element.63), channel_id=1, source_target_pairs={{0,4},{1,5},{2,6},{3,7},{4,0},{5,1},{6,2},{7,3},{8,20},{9,21},{10,... | collective-permute-start | bytes 3870728 | tf_op jit(solution)/shard_map/ppermute | solution.py:57
  84.9 38.8 %collective-permute-start.1 = (bf16[7,48,1152]{2,1,0:T(8,128)(2,1)}, bf16[7,48,1152]{2,1,0:T(8,128)(2,1)}, u32[]{:S(2)}, u32[]{:S(2)}) collective-permute-start(bf16[7,48,1152]{2,1,0:T(8,128)(2,1)} %get-tuple-element.62), channel_id=1, source_target_pairs={{0,0},{1,1},{2,2},{3,3},{4,4},{5,5},{6,6},{7,7},{8,16},{9,17},{10,... | collective-permute-start | bytes 2322440 | tf_op jit(solution)/shard_map/ppermute | solution.py:57
  91.9 31.7 %collective-permute-start.3 = (bf16[7,48,1152]{2,1,0:T(8,128)(2,1)}, bf16[7,48,1152]{2,1,0:T(8,128)(2,1)}, u32[]{:S(2)}, u32[]{:S(2)}) collective-permute-start(bf16[7,48,1152]{2,1,0:T(8,128)(2,1)} %get-tuple-element.64), channel_id=1, source_target_pairs={{0,4},{1,5},{2,6},{3,7},{4,0},{5,1},{6,2},{7,3},{8,20},{9,21},{10,... | collective-permute-start | bytes 2322440 | tf_op jit(solution)/shard_map/ppermute | solution.py:57
  107.8 16.4 %collective-permute-start.4 = (bf16[7,80,1152]{2,1,0:T(8,128)(2,1)S(1)}, bf16[7,80,1152]{2,1,0:T(8,128)(2,1)S(1)}, u32[]{:S(2)}, u32[]{:S(2)}) collective-permute-start(bf16[7,80,1152]{2,1,0:T(8,128)(2,1)S(1)} %collective-permute-done.refs_1_.refs_0_), channel_id=1, source_target_pairs={{0,16},{1,17},{2,18},{3,19},{4,20},{5,21},{6,22},{7,23},{8,24},{9,... | collective-permute-start | bytes 3870728 | tf_op jit(solution)/shard_map/ppermute | solution.py:57
  107.9 16.4 %collective-permute-start.6 = (bf16[7,80,1152]{2,1,0:T(8,128)(2,1)}, bf16[7,80,1152]{2,1,0:T(8,128)(2,1)}, u32[]{:S(2)}, u32[]{:S(2)}) collective-permute-start(bf16[7,80,1152]{2,1,0:T(8,128)(2,1)} %collective-permute-done.2.refs_3_.refs_2_), channel_id=1, source_target_pairs={{0,16},{1,17},{2,18},{3,19},{4,20},{5,21},{6,22},{7,23},{8,24},{9,... | collective-permute-start | bytes 3870728 | tf_op jit(solution)/shard_map/ppermute | solution.py:57
  132.1 12.2 %collective-permute-start.8 = (bf16[608,256]{1,0:T(8,128)(2,1)S(1)}, bf16[608,256]{1,0:T(8,128)(2,1)S(1)}, u32[]{:S(2)}, u32[]{:S(2)}) collective-permute-start(bf16[608,256]{1,0:T(8,128)(2,1)S(1)} %get-tuple-element.68), channel_id=1, source_target_pairs={{0,1},{1,2},{2,3},{3,0},{4,5},{5,6},{6,7},{7,4},{8,9},{9,10},{10,1... | collective-permute-start | bytes 933896 | tf_op jit(solution)/shard_map/ppermute | solution.py:57
  133.4 10.9 %collective-permute-start.9 = (bf16[592,256]{1,0:T(8,128)(2,1)S(1)}, bf16[592,256]{1,0:T(8,128)(2,1)S(1)}, u32[]{:S(2)}, u32[]{:S(2)}) collective-permute-start(bf16[592,256]{1,0:T(8,128)(2,1)S(1)} %get-tuple-element.69), channel_id=1, source_target_pairs={{0,3},{1,0},{2,1},{3,2},{4,7},{5,4},{6,5},{7,6},{8,11},{9,8},{10,9... | collective-permute-start | bytes 909320 | tf_op jit(solution)/shard_map/ppermute | solution.py:57
  134.9 9.4 %collective-permute-start.10 = (bf16[592,256]{1,0:T(8,128)(2,1)S(1)}, bf16[592,256]{1,0:T(8,128)(2,1)S(1)}, u32[]{:S(2)}, u32[]{:S(2)}) collective-permute-start(bf16[592,256]{1,0:T(8,128)(2,1)S(1)} %get-tuple-element.70), channel_id=1, source_target_pairs={{0,4},{1,5},{2,6},{3,7},{4,0},{5,1},{6,2},{7,3},{8,12},{9,13},{10,... | collective-permute-start | bytes 909320 | tf_op jit(solution)/shard_map/ppermute | solution.py:57
  144.7 21.3 %collective-permute-start.12 = (bf16[1792,256]{1,0:T(8,128)(2,1)S(1)}, bf16[1792,256]{1,0:T(8,128)(2,1)S(1)}, u32[]{:S(2)}, u32[]{:S(2)}) collective-permute-start(bf16[1792,256]{1,0:T(8,128)(2,1)S(1)} %get-tuple-element.83), channel_id=1, source_target_pairs={{0,3},{1,0},{2,1},{3,2},{4,7},{5,4},{6,5},{7,6},{8,11},{9,8},{10,9... | collective-permute-start | bytes 2752520 | tf_op jit(solution)/shard_map/ppermute | solution.py:57
  146.1 21.8 %collective-permute-start.13 = (bf16[1792,256]{1,0:T(8,128)(2,1)S(1)}, bf16[1792,256]{1,0:T(8,128)(2,1)S(1)}, u32[]{:S(2)}, u32[]{:S(2)}) collective-permute-start(bf16[1792,256]{1,0:T(8,128)(2,1)S(1)} %get-tuple-element.84), channel_id=1, source_target_pairs={{0,1},{1,2},{2,3},{3,0},{4,5},{5,6},{6,7},{7,4},{8,9},{9,10},{10,1... | collective-permute-start | bytes 2752520 | tf_op jit(solution)/shard_map/ppermute | solution.py:57
  146.2 21.6 %collective-permute-start.11 = (bf16[1792,256]{1,0:T(8,128)(2,1)S(1)}, bf16[1792,256]{1,0:T(8,128)(2,1)S(1)}, u32[]{:S(2)}, u32[]{:S(2)}) collective-permute-start(bf16[1792,256]{1,0:T(8,128)(2,1)S(1)} %get-tuple-element.71), channel_id=1, source_target_pairs={{0,4},{1,5},{2,6},{3,7},{4,0},{5,1},{6,2},{7,3},{8,12},{9,13},{10,... | collective-permute-start | bytes 2752520 | tf_op jit(solution)/shard_map/ppermute | solution.py:57
  156.4 29.2 %collective-permute-start.16 = (bf16[1792,256]{1,0:T(8,128)(2,1)S(1)}, bf16[1792,256]{1,0:T(8,128)(2,1)S(1)}, u32[]{:S(2)}, u32[]{:S(2)}) collective-permute-start(bf16[1792,256]{1,0:T(8,128)(2,1)S(1)} %get-tuple-element.87), channel_id=1, source_target_pairs={{0,3},{1,0},{2,1},{3,2},{4,7},{5,4},{6,5},{7,6},{8,11},{9,8},{10,9... | collective-permute-start | bytes 2752520 | tf_op jit(solution)/shard_map/ppermute | solution.py:57
  168.3 19.7 %collective-permute-start.15 = (bf16[1792,256]{1,0:T(8,128)(2,1)S(1)}, bf16[1792,256]{1,0:T(8,128)(2,1)S(1)}, u32[]{:S(2)}, u32[]{:S(2)}) collective-permute-start(bf16[1792,256]{1,0:T(8,128)(2,1)S(1)} %get-tuple-element.86), channel_id=1, source_target_pairs={{0,4},{1,5},{2,6},{3,7},{4,0},{5,1},{6,2},{7,3},{8,12},{9,13},{10,... | collective-permute-start | bytes 2752520 | tf_op jit(solution)/shard_map/ppermute | solution.py:57
  168.7 20.6 %collective-permute-start.14 = (bf16[1792,256]{1,0:T(8,128)(2,1)S(1)}, bf16[1792,256]{1,0:T(8,128)(2,1)S(1)}, u32[]{:S(2)}, u32[]{:S(2)}) collective-permute-start(bf16[1792,256]{1,0:T(8,128)(2,1)S(1)} %get-tuple-element.85), channel_id=1, source_target_pairs={{0,1},{1,2},{2,3},{3,0},{4,5},{5,6},{6,7},{7,4},{8,9},{9,10},{10,1... | collective-permute-start | bytes 2752520 | tf_op jit(solution)/shard_map/ppermute | solution.py:57
  189.8 18.6 %collective-permute-start.19 = (bf16[1792,256]{1,0:T(8,128)(2,1)S(1)}, bf16[1792,256]{1,0:T(8,128)(2,1)S(1)}, u32[]{:S(2)}, u32[]{:S(2)}) collective-permute-start(bf16[1792,256]{1,0:T(8,128)(2,1)S(1)} %shard_map.59.refs_0_), channel_id=1, source_target_pairs={{0,4},{1,5},{2,6},{3,7},{4,0},{5,1},{6,2},{7,3},{8,12},{9,13},{10,... | collective-permute-start | bytes 2752520 | tf_op jit(solution)/shard_map/ppermute | solution.py:57
  190.9 18.1 %collective-permute-start.18 = (bf16[1792,256]{1,0:T(8,128)(2,1)S(1)}, bf16[1792,256]{1,0:T(8,128)(2,1)S(1)}, u32[]{:S(2)}, u32[]{:S(2)}) collective-permute-start(bf16[1792,256]{1,0:T(8,128)(2,1)S(1)} %shard_map.59.refs_0_), channel_id=1, source_target_pairs={{0,3},{1,0},{2,1},{3,2},{4,7},{5,4},{6,5},{7,6},{8,11},{9,8},{10,9... | collective-permute-start | bytes 2752520 | tf_op jit(solution)/shard_map/ppermute | solution.py:57
  190.9 21.1 %collective-permute-start.17 = (bf16[1792,256]{1,0:T(8,128)(2,1)S(1)}, bf16[1792,256]{1,0:T(8,128)(2,1)S(1)}, u32[]{:S(2)}, u32[]{:S(2)}) collective-permute-start(bf16[1792,256]{1,0:T(8,128)(2,1)S(1)} %shard_map.59.refs_0_), channel_id=1, source_target_pairs={{0,1},{1,2},{2,3},{3,0},{4,5},{5,6},{6,7},{7,4},{8,9},{9,10},{10,1... | collective-permute-start | bytes 2752520 | tf_op jit(solution)/shard_map/ppermute | solution.py:57
  208.3 23.1 %collective-permute-start.21 = (bf16[1792,256]{1,0:T(8,128)(2,1)S(1)}, bf16[1792,256]{1,0:T(8,128)(2,1)S(1)}, u32[]{:S(2)}, u32[]{:S(2)}) collective-permute-start(bf16[1792,256]{1,0:T(8,128)(2,1)S(1)} %collective-permute-done.19.refs_3_), channel_id=1, source_target_pairs={{0,1},{1,2},{2,3},{3,0},{4,5},{5,6},{6,7},{7,4},{8,9},{9,10},{10,1... | collective-permute-start | bytes 2752520 | tf_op jit(solution)/shard_map/ppermute | solution.py:57
  209.0 22.5 %collective-permute-start.22 = (bf16[1792,256]{1,0:T(8,128)(2,1)S(1)}, bf16[1792,256]{1,0:T(8,128)(2,1)S(1)}, u32[]{:S(2)}, u32[]{:S(2)}) collective-permute-start(bf16[1792,256]{1,0:T(8,128)(2,1)S(1)} %collective-permute-done.18.refs_2_), channel_id=1, source_target_pairs={{0,3},{1,0},{2,1},{3,2},{4,7},{5,4},{6,5},{7,6},{8,11},{9,8},{10,9... | collective-permute-start | bytes 2752520 | tf_op jit(solution)/shard_map/ppermute | solution.py:57
  211.0 20.5 %collective-permute-start.20 = (bf16[1792,256]{1,0:T(8,128)(2,1)S(1)}, bf16[1792,256]{1,0:T(8,128)(2,1)S(1)}, u32[]{:S(2)}, u32[]{:S(2)}) collective-permute-start(bf16[1792,256]{1,0:T(8,128)(2,1)S(1)} %collective-permute-done.18.refs_2_), channel_id=1, source_target_pairs={{0,4},{1,5},{2,6},{3,7},{4,0},{5,1},{6,2},{7,3},{8,12},{9,13},{10,... | collective-permute-start | bytes 2752520 | tf_op jit(solution)/shard_map/ppermute | solution.py:57
  212.9 36.3 %collective-permute-start.27 = (bf16[5376,256]{1,0:T(8,128)(2,1)S(1)}, bf16[5376,256]{1,0:T(8,128)(2,1)S(1)}, u32[]{:S(2)}, u32[]{:S(2)}) collective-permute-start(bf16[5376,256]{1,0:T(8,128)(2,1)S(1)} %pad_maximum_fusion), channel_id=1, source_target_pairs={{0,16},{1,17},{2,18},{3,19},{4,20},{5,21},{6,22},{7,23},{8,24},{9,... | collective-permute-start | bytes 8257544 | tf_op jit(solution)/shard_map/ppermute | solution.py:57
  231.7 17.6 %collective-permute-start.28 = (bf16[5376,256]{1,0:T(8,128)(2,1)S(1)}, bf16[5376,256]{1,0:T(8,128)(2,1)S(1)}, u32[]{:S(2)}, u32[]{:S(2)}) collective-permute-start(bf16[5376,256]{1,0:T(8,128)(2,1)S(1)} %pad_maximum_fusion.1), channel_id=1, source_target_pairs={{0,16},{1,17},{2,18},{3,19},{4,20},{5,21},{6,22},{7,23},{8,24},{9,... | collective-permute-start | bytes 8257544 | tf_op jit(solution)/shard_map/ppermute | solution.py:57
  234.8 6.0 %collective-permute-start.26 = (bf16[1792,256]{1,0:T(8,128)(2,1)S(1)}, bf16[1792,256]{1,0:T(8,128)(2,1)S(1)}, u32[]{:S(2)}, u32[]{:S(2)}) collective-permute-start(bf16[1792,256]{1,0:T(8,128)(2,1)S(1)} %shard_map.59.refs_0_), channel_id=1, source_target_pairs={{0,16},{1,17},{2,18},{3,19},{4,20},{5,21},{6,22},{7,23},{8,24},{9,... | collective-permute-start | bytes 2752520 | tf_op jit(solution)/shard_map/ppermute | solution.py:57
  234.9 14.3 %collective-permute-start.23 = (bf16[608,256]{1,0:T(8,128)(2,1)S(1)}, bf16[608,256]{1,0:T(8,128)(2,1)S(1)}, u32[]{:S(2)}, u32[]{:S(2)}) collective-permute-start(bf16[608,256]{1,0:T(8,128)(2,1)S(1)} %slice.17), channel_id=1, source_target_pairs={{0,3},{1,0},{2,1},{3,2},{4,7},{5,4},{6,5},{7,6},{8,11},{9,8},{10,9... | collective-permute-start | bytes 933896 | tf_op jit(solution)/shard_map/ppermute | solution.py:57
  235.5 9.1 %collective-permute-start.24 = (bf16[592,256]{1,0:T(8,128)(2,1)S(1)}, bf16[592,256]{1,0:T(8,128)(2,1)S(1)}, u32[]{:S(2)}, u32[]{:S(2)}) collective-permute-start(bf16[592,256]{1,0:T(8,128)(2,1)S(1)} %slice.18), channel_id=1, source_target_pairs={{0,1},{1,2},{2,3},{3,0},{4,5},{5,6},{6,7},{7,4},{8,9},{9,10},{10,1... | collective-permute-start | bytes 909320 | tf_op jit(solution)/shard_map/ppermute | solution.py:57
  240.8 8.4 %collective-permute-start.25 = (bf16[592,256]{1,0:T(8,128)(2,1)S(1)}, bf16[592,256]{1,0:T(8,128)(2,1)S(1)}, u32[]{:S(2)}, u32[]{:S(2)}) collective-permute-start(bf16[592,256]{1,0:T(8,128)(2,1)S(1)} %slice.19), channel_id=1, source_target_pairs={{0,4},{1,5},{2,6},{3,7},{4,0},{5,1},{6,2},{7,3},{8,12},{9,13},{10,... | collective-permute-start | bytes 909320 | tf_op jit(solution)/shard_map/ppermute | solution.py:57
  291.4 28.9 %collective-permute-start.30 = (bf16[4032,128]{1,0:T(8,128)(2,1)}, bf16[4032,128]{1,0:T(8,128)(2,1)S(1)}, u32[]{:S(2)}, u32[]{:S(2)}) collective-permute-start(bf16[4032,128]{1,0:T(8,128)(2,1)} %get-tuple-element.102), channel_id=1, source_target_pairs={{0,0},{1,1},{2,2},{3,3},{4,4},{5,5},{6,6},{7,7},{8,16},{9,17},{10,... | collective-permute-start | bytes 3096584 | tf_op jit(solution)/shard_map/ppermute | solution.py:57
  295.3 34.0 %collective-permute-start.31 = (bf16[4032,128]{1,0:T(8,128)(2,1)}, bf16[4032,128]{1,0:T(8,128)(2,1)}, u32[]{:S(2)}, u32[]{:S(2)}) collective-permute-start(bf16[4032,128]{1,0:T(8,128)(2,1)} %get-tuple-element.103), channel_id=1, source_target_pairs={{0,4},{1,5},{2,6},{3,7},{4,0},{5,1},{6,2},{7,3},{8,20},{9,21},{10,... | collective-permute-start | bytes 3096584 | tf_op jit(solution)/shard_map/ppermute | solution.py:57
  313.1 26.5 %collective-permute-start.32 = (bf16[4032,128]{1,0:T(8,128)(2,1)}, bf16[4032,128]{1,0:T(8,128)(2,1)S(1)}, u32[]{:S(2)}, u32[]{:S(2)}) collective-permute-start(bf16[4032,128]{1,0:T(8,128)(2,1)} %get-tuple-element.108), channel_id=1, source_target_pairs={{0,8},{1,9},{2,10},{3,11},{4,12},{5,13},{6,14},{7,15},{8,24},{9,25... | collective-permute-start | bytes 3096584 | tf_op jit(solution)/shard_map/ppermute | solution.py:57
  313.2 30.0 %collective-permute-start.33 = (bf16[4032,128]{1,0:T(8,128)(2,1)}, bf16[4032,128]{1,0:T(8,128)(2,1)S(1)}, u32[]{:S(2)}, u32[]{:S(2)}) collective-permute-start(bf16[4032,128]{1,0:T(8,128)(2,1)} %get-tuple-element.109), channel_id=1, source_target_pairs={{0,12},{1,13},{2,14},{3,15},{4,8},{5,9},{6,10},{7,11},{8,28},{9,29... | collective-permute-start | bytes 3096584 | tf_op jit(solution)/shard_map/ppermute | solution.py:57
  (25 other events, 284.2 us)

commit v8 on v7

--- a/solution.py
+++ b/solution.py
@@ -349,16 +349,16 @@
 
 
 def apply_kernel(info, *refs):
-    own, ends, swapped = refs[:7], refs[7:10], refs[10:14]
-    turned = refs[14]
-    outs, rest_direct, rest_flipped, all_mixed, scales = refs[15:17], *refs[17:21]
-    direct, flipped, panel, mixed, stage, extra, sems, panel_sem, out_sems, keep_sems = refs[21:]
+    own, ends, swapped = refs[:7], refs[7:10], refs[10:13]
+    turned = refs[13]
+    outs, rest_direct, rest_flipped, all_mixed, scales = refs[14:16], *refs[16:20]
+    direct, flipped, panel, mixed, stage, extra, sems, panel_sem, out_sems, keep_sems = refs[20:]
     c = info[0]
     panel_copy = pltpu.make_async_copy(turned, panel, panel_sem)
     panel_copy.start()
     pieces = [(c, ref, 0, rel) for ref, rel in zip(own, SOURCES)]
-    pieces += [(1 - c, swapped[0], 0, SOURCES[0]), (1 - c, swapped[3], 0, SOURCES[7])]
-    pieces += [(1 - c, swapped[1 + n // 3], n % 3 * CHUNK, SOURCES[1 + n]) for n in range(6)]
+    pieces += [(1 - c, swapped[n // 4], n % 4 * CHUNK, SOURCES[n]) for n in range(7)]
+    pieces.append((1 - c, swapped[2], 0, SOURCES[7]))
     for n, (core, ref, row, rel) in enumerate(pieces):
         d = chip_at(info, *rel)
 
@@ -506,7 +506,7 @@
 def apply_poly(info, own, ends, swapped, turned):
     return pl.pallas_call(
         apply_kernel,
-        in_specs=[SMEM] + [HBM] * 15,
+        in_specs=[SMEM] + [HBM] * 14,
         out_specs=[HBM] * 5 + [VMEM],
         out_shape=[jax.ShapeDtypeStruct((BACK_ROWS, TILE), BF16)] * 2
         + [
@@ -609,7 +609,7 @@
     ends = tuple(
         send(x[row : row + size]) for send, x, (row, size) in zip((down, up, across), (a1, a2, a3), PARTS)
     )
-    swapped = (swap(mine), swap(jnp.concatenate([low, high, pair])), swap(jnp.concatenate([a1, a2, a3])))
+    swapped = (swap(jnp.concatenate([mine, low, high, pair])), swap(jnp.concatenate([a1, a2, a3])))
     ends, swapped = lax.optimization_barrier((ends, swapped))
     swapped += (swap(jnp.concatenate(ends)),)
     *sent, direct, flipped, mixed, scales = apply_poly(info, (mine, low, high, pair, a1, a2, a3), ends, swapped, turned)

time: 348 us -> 346 us (level)
  waiting for transfers between devices: 138 us -> 132 us
    ppermute x34 -> x33, waiting for transfers between devices: 130 us -> 123 us  [move(): return lax.ppermute(x, AXES[1:], pairs)]
    ppermute x34 -> x33, starting transfers between devices: 48.7 us -> 51.7 us  [move(): return lax.ppermute(x, AXES[1:], pairs)]
  transfers between devices with their start and end apart: 35 -> 34, of which waited for: 21 -> 18; matrix products, arithmetic and copies ran while one was open for 0% -> 1% of each run, Pallas kernels for 15% -> 15%
where the time goes in v8:
time: 346 us; the launch traced here: 345 us
  waiting for transfers between devices  132 us (38%)
  Pallas kernels  104 us (30%)
  starting transfers between devices  56.1 us (16%)
  blocking collectives  46 us (13%)
  local copies, waits for them, and re-layouts  3.58 us (1%)
    ppermute x33, waiting for transfers between devices, move(): return lax.ppermute(x, AXES[1:], pairs)  123 us
    ppermute x33, starting transfers between devices, move(): return lax.ppermute(x, AXES[1:], pairs)  51.7 us
    all_to_all x1, blocking collectives, on_device(): lax.all_to_all(upper, PLANE, split_axis=0, concat_axis=0, tiled=True)  46 us
    pallas_call x1, Pallas kernels, apply_poly(): pl.pallas_call(apply_kernel, in_specs=[SMEM] + [HBM] * 14, out_specs=[HBM...  37.7 us
    pallas_call x3, Pallas kernels, gram_chunks(): pl.pallas_call(lambda *refs: gram_kernel(dests, *refs), in_specs=[SMEM] +...  22.8 us
    pallas_call x1, Pallas kernels, apply_rest(): pl.pallas_call(rest_kernel, grid_spec=pltpu.PrefetchScalarGridSpec(num_sc...  16.5 us
    pallas_call x2, Pallas kernels, update_momentum(): pl.pallas_call(lambda *refs: momentum_kernel(part, *refs), in_specs=[SMEM...  12.5 us
    all_to_all x1, waiting for transfers between devices, on_device(): lax.all_to_all(lower, PLANE, split_axis=0, concat_axis=0, tiled=True)  8.07 us
  transfers between devices with their start and end apart: 34, of which 18 were waited for; matrix products, arithmetic and copies ran while one was open for 1% of the time, Pallas kernels for 15%

profile of v8, /device:TPU:1, one launch (start us, length us, event | category | flops | bytes accessed | tf_op | source)
XLA Modules:
  0.0 344.7 jit_solution(6406007806510207722)
XLA Ops:
  0.6 5.4 %shard_map.50 = (bf16[16,736,128]{2,1,0:T(8,128)(2,1)}, bf16[16,432,128]{2,1,0:T(8,128)(2,1)}) custom-call(s32[14]{0:T(128)} %ids.1, bf16[14,128,1152]{2,1,0:T(8,128)(2,1)} %tiles.1), custom_call_target="tpu_custom_call" | custom-call | bytes 8257536 | tf_op jit(solution)/shard_map/pallas_call | solution.py:123
  6.0 46.0 %all_to_all.10.refs_1_ = bf16[16,736,128]{2,1,0:T(8,128)(2,1)S(1)} all-to-all(bf16[16,736,128]{2,1,0:T(8,128)(2,1)} %get-tuple-element.55), channel_id=1, replica_groups=mesh['x'=4,'core'=2,'zm'=2,'zl'=2,'y'=4] {'zm','zl','y'}, dimensions={0} | all-to-all | bytes 6029312 | tf_op jit(solution)/shard_map/all_to_all | solution.py:569
  52.0 4.4 %all-to-all-start.1 = ((bf16[16,432,128]{2,1,0:T(8,128)(2,1)}), bf16[16,432,128]{2,1,0:T(8,128)(2,1)}, u32[]{:S(2)}, u32[]{:S(2)}) async-start(bf16[16,432,128]{2,1,0:T(8,128)(2,1)} %get-tuple-element.57), calls=%async_computation.1 | async-start | bytes 3538944 | tf_op jit(solution)/shard_map/all_to_all | solution.py:571
  57.5 7.1 %shard_map.51 = (f32[896,2304]{1,0:T(8,128)}, bf16[7,80,1152]{2,1,0:T(8,128)(2,1)}, bf16[7,80,1152]{2,1,0:T(8,128)(2,1)}) custom-call(s32[15]{0:T(128)} %pad_add_fusion.refs_0_, bf16[16,736,128]{2,1,0:T(8,128)(2,1)} %copy-done.8, f32[896,2304]{1,0:T(8,128)} %refs_2_.3), custom_call_target="tpu_custom_call" | custom-call | bytes 12386304 | tf_op jit(solution)/shard_map/pallas_call | solution.py:195
  64.6 6.6 %collective-permute-start = (bf16[7,80,1152]{2,1,0:T(8,128)(2,1)}, bf16[7,80,1152]{2,1,0:T(8,128)(2,1)S(1)}, u32[]{:S(2)}, u32[]{:S(2)}) collective-permute-start(bf16[7,80,1152]{2,1,0:T(8,128)(2,1)} %get-tuple-element.60), channel_id=1, source_target_pairs={{0,0},{1,1},{2,2},{3,3},{4,4},{5,5},{6,6},{7,7},{8,16},{9,17},{10,... | collective-permute-start | bytes 3870728 | tf_op jit(solution)/shard_map/ppermute | solution.py:57
  71.4 8.1 %all-to-all-done.1.refs_1_ = bf16[16,432,128]{2,1,0:T(8,128)(2,1)} async-done(((bf16[16,432,128]{2,1,0:T(8,128)(2,1)}), bf16[16,432,128]{2,1,0:T(8,128)(2,1)}, u32[]{:S(2)}, u32[]{:S(2)}) %all-to-all-start.1) | async-done | bytes 1769504 | tf_op jit(solution)/shard_map/all_to_all | solution.py:571
  79.4 5.4 %shard_map.52 = (f32[896,2304]{1,0:T(8,128)}, bf16[7,48,1152]{2,1,0:T(8,128)(2,1)}, bf16[7,48,1152]{2,1,0:T(8,128)(2,1)}) custom-call(s32[15]{0:T(128)} %pad_add_fusion.refs_0_, bf16[16,432,128]{2,1,0:T(8,128)(2,1)} %all-to-all-done.1.refs_1_, f32[896,2304]{1,0:T(8,128)} %refs_2_.3, ...), custom_call_target="tpu_custom_call", output_to_operand_aliasing={{0}: (3, {})} | custom-call | bytes 12386304 | tf_op jit(solution)/shard_map/pallas_call | solution.py:195
  84.8 7.1 %collective-permute-start.1 = (bf16[7,48,1152]{2,1,0:T(8,128)(2,1)}, bf16[7,48,1152]{2,1,0:T(8,128)(2,1)}, u32[]{:S(2)}, u32[]{:S(2)}) collective-permute-start(bf16[7,48,1152]{2,1,0:T(8,128)(2,1)} %get-tuple-element.61), channel_id=1, source_target_pairs={{0,0},{1,1},{2,2},{3,3},{4,4},{5,5},{6,6},{7,7},{8,16},{9,17},{10,... | collective-permute-start | bytes 2322440 | tf_op jit(solution)/shard_map/ppermute | solution.py:57
  92.1 15.8 %collective-permute-done.refs_1_.refs_0_ = bf16[7,80,1152]{2,1,0:T(8,128)(2,1)S(1)} collective-permute-done((bf16[7,80,1152]{2,1,0:T(8,128)(2,1)}, bf16[7,80,1152]{2,1,0:T(8,128)(2,1)S(1)}, u32[]{:S(2)}, u32[]{:S(2)}) %collective-permute-start) | collective-permute-done | bytes 1290272 | tf_op jit(solution)/shard_map/ppermute | solution.py:57
  108.3 15.3 %collective-permute-done.1.refs_2_.refs_1_ = bf16[7,48,1152]{2,1,0:T(8,128)(2,1)} collective-permute-done((bf16[7,48,1152]{2,1,0:T(8,128)(2,1)}, bf16[7,48,1152]{2,1,0:T(8,128)(2,1)}, u32[]{:S(2)}, u32[]{:S(2)}) %collective-permute-start.1) | collective-permute-done | bytes 774176 | tf_op jit(solution)/shard_map/ppermute | solution.py:57
  127.3 4.8 %shard_map.54 = (bf16[608,256]{1,0:T(8,128)(2,1)S(1)}, bf16[592,256]{1,0:T(8,128)(2,1)S(1)}, bf16[592,256]{1,0:T(8,128)(2,1)S(1)}) custom-call(s32[4]{0:T(128)S(1)} %pad_add_fusion.1.refs_0_.info, bf16[7,80,1152]{2,1,0:T(8,128)(2,1)S(1)} %collective-permute-done.refs_1_.refs_0_, bf16[7,48,1152]{2,1,0:T(8,128)(2,1)} %collective-permute-done.1.refs_2_.refs_1_, ...), custom_call_target="tpu_custom_call" | custom-call | flops 1056964608 | bytes 10135008 | tf_op jit(solution)/shard_map/pallas_call | solution.py:278
  135.8 8.5 %shard_map.53 = (f32[1792,256]{1,0:T(8,128)S(1)}, f32[1792,256]{1,0:T(8,128)S(1)}, f32[1792,256]{1,0:T(8,128)S(1)}) custom-call(s32[4]{0:T(128)S(1)} %pad_add_fusion.1.refs_0_.info, bf16[7,80,1152]{2,1,0:T(8,128)(2,1)S(1)} %collective-permute-done.refs_1_.refs_0_, bf16[7,48,1152]{2,1,0:T(8,128)(2,1)} %collective-permute-done.1.refs_2_.refs_1_, ...), custom_call_target="tpu_custom_call" | custom-call | flops 3170893824 | bytes 13805024 | tf_op jit(solution)/shard_map/pallas_call | solution.py:278
  146.7 9.6 %shard_map.56 = (f32[1792,256]{1,0:T(8,128)S(1)}, f32[1792,256]{1,0:T(8,128)S(1)}, bf16[1792,256]{1,0:T(8,128)(2,1)S(1)}, f32[1792,256]{1,0:T(8,128)S(1)}) custom-call(s32[4]{0:T(128)S(1)} %pad_add_fusion.1.refs_0_.info, bf16[7,80,1152]{2,1,0:T(8,128)(2,1)S(1)} %collective-permute-done.refs_1_.refs_0_, ...), custom_call_target="tpu_custom_call" | custom-call | flops 4227858432 | bytes 15640032 | tf_op jit(solution)/shard_map/pallas_call | solution.py:278
  156.3 2.5 collective-permute-start.16
  158.8 7.1 %collective-permute-done.12.g2 = bf16[1792,256]{1,0:T(8,128)(2,1)S(1)} collective-permute-done((bf16[1792,256]{1,0:T(8,128)(2,1)S(1)}, bf16[1792,256]{1,0:T(8,128)(2,1)S(1)}, u32[]{:S(2)}, u32[]{:S(2)}) %collective-permute-start.12) | collective-permute-done | bytes 917536 | tf_op jit(solution)/shard_map/ppermute | solution.py:57
  168.8 4.2 %shard_map.58.turned.refs_13_.panel = bf16[576,5376]{1,0:T(8,128)(2,1)S(1)} custom-call(s32[4]{0:T(128)S(1)} %pad_add_fusion.1.refs_0_.info, bf16[7,80,1152]{2,1,0:T(8,128)(2,1)S(1)} %copy-done.2, bf16[7,48,1152]{2,1,0:T(8,128)(2,1)} %collective-permute-done.1.refs_2_.refs_1_, bf16[7,80,1152]{2,1,0:T(8,128)(2,1)} %collective-permute-done.2.refs_3_.refs_2_, ...), custom_call_target="tpu_custom_call" | custom-call | bytes 12000000 | tf_op jit(solution)/shard_map/pallas_call | solution.py:337
  173.0 12.5 %collective-permute-done.16.v3 = bf16[1792,256]{1,0:T(8,128)(2,1)S(1)} collective-permute-done((bf16[1792,256]{1,0:T(8,128)(2,1)S(1)}, bf16[1792,256]{1,0:T(8,128)(2,1)S(1)}, u32[]{:S(2)}, u32[]{:S(2)}) %collective-permute-start.16) | collective-permute-done | bytes 917536 | tf_op jit(solution)/shard_map/ppermute | solution.py:57
  185.5 2.6 collective-permute-done.15.v2
  192.5 15.9 %collective-permute-done.18.refs_2_ = bf16[1792,256]{1,0:T(8,128)(2,1)S(1)} collective-permute-done((bf16[1792,256]{1,0:T(8,128)(2,1)S(1)}, bf16[1792,256]{1,0:T(8,128)(2,1)S(1)}, u32[]{:S(2)}, u32[]{:S(2)}) %collective-permute-start.18) | collective-permute-done | bytes 917536 | tf_op jit(solution)/shard_map/ppermute | solution.py:57
  212.1 6.1 %collective-permute-start.26 = (bf16[7168,256]{1,0:T(8,128)(2,1)S(1)}, bf16[7168,256]{1,0:T(8,128)(2,1)S(1)}, u32[]{:S(2)}, u32[]{:S(2)}) collective-permute-start(bf16[7168,256]{1,0:T(8,128)(2,1)S(1)} %pad_maximum_fusion), channel_id=1, source_target_pairs={{0,16},{1,17},{2,18},{3,19},{4,20},{5,21},{6,22},{7,23},{8,24},{9,... | collective-permute-start | bytes 11010056 | tf_op jit(solution)/shard_map/ppermute | solution.py:57
  218.2 10.9 %collective-permute-done.21.refs_5_ = bf16[1792,256]{1,0:T(8,128)(2,1)S(1)} collective-permute-done((bf16[1792,256]{1,0:T(8,128)(2,1)S(1)}, bf16[1792,256]{1,0:T(8,128)(2,1)S(1)}, u32[]{:S(2)}, u32[]{:S(2)}) %collective-permute-start.21) | collective-permute-done | bytes 917536 | tf_op jit(solution)/shard_map/ppermute | solution.py:57
  229.3 5.8 %collective-permute-start.27 = (bf16[5376,256]{1,0:T(8,128)(2,1)S(1)}, bf16[5376,256]{1,0:T(8,128)(2,1)S(1)}, u32[]{:S(2)}, u32[]{:S(2)}) collective-permute-start(bf16[5376,256]{1,0:T(8,128)(2,1)S(1)} %pad_maximum_fusion.1), channel_id=1, source_target_pairs={{0,16},{1,17},{2,18},{3,19},{4,20},{5,21},{6,22},{7,23},{8,24},{9,... | collective-permute-start | bytes 8257544 | tf_op jit(solution)/shard_map/ppermute | solution.py:57
  237.2 8.1 %collective-permute-done.24.refs_8_ = bf16[592,256]{1,0:T(8,128)(2,1)S(1)} collective-permute-done((bf16[592,256]{1,0:T(8,128)(2,1)S(1)}, bf16[592,256]{1,0:T(8,128)(2,1)S(1)}, u32[]{:S(2)}, u32[]{:S(2)}) %collective-permute-start.24) | collective-permute-done | bytes 303136 | tf_op jit(solution)/shard_map/ppermute | solution.py:57
  251.2 37.7 %shard_map.60 = (bf16[4032,128]{1,0:T(8,128)(2,1)}, bf16[4032,128]{1,0:T(8,128)(2,1)}, bf16[7,2048,256]{2,1,0:T(8,128)(2,1)}, bf16[7,1536,256]{2,1,0:T(8,128)(2,...) custom-call(s32[4]{0:T(128)} %copy-done.6, bf16[1792,256]{1,0:T(8,128)(2,1)} %copy-done.5, bf16[1792,256]{1,0:T(8,128)(2,1)} %copy-done.14, ...), custom_call_target="tpu_custom_call" | custom-call | flops 22196256768 | bytes 40000000 | tf_op jit(solution)/shard_map/pallas_call | solution.py:507
  288.9 3.8 %collective-permute-start.29 = (bf16[4032,128]{1,0:T(8,128)(2,1)}, bf16[4032,128]{1,0:T(8,128)(2,1)S(1)}, u32[]{:S(2)}, u32[]{:S(2)}) collective-permute-start(bf16[4032,128]{1,0:T(8,128)(2,1)} %get-tuple-element.100), channel_id=1, source_target_pairs={{0,0},{1,1},{2,2},{3,3},{4,4},{5,5},{6,6},{7,7},{8,16},{9,17},{10,... | collective-permute-start | bytes 3096584 | tf_op jit(solution)/shard_map/ppermute | solution.py:57
  293.9 16.5 %shard_map.61 = (bf16[4032,128]{1,0:T(8,128)(2,1)}, bf16[4032,128]{1,0:T(8,128)(2,1)}) custom-call(s32[4]{0:T(128)} %copy-done.6, bf16[7,2048,256]{2,1,0:T(8,128)(2,1)} %get-tuple-element.102.direct, bf16[7,1536,256]{2,1,0:T(8,128)(2,1)} %get-tuple-element.103.flipped, bf16[576,5376]{1,0:T(8,128)(2,1)} %copy-done, ...), custom_call_target="tpu_custom_call" | custom-call | flops 7398752256 | bytes 20000000 | tf_op jit(solution)/shard_map/pallas_call | solution.py:480
  310.5 2.6 collective-permute-start.32
  313.2 4.6 %collective-permute-done.29.r0 = bf16[4032,128]{1,0:T(8,128)(2,1)S(1)} collective-permute-done((bf16[4032,128]{1,0:T(8,128)(2,1)}, bf16[4032,128]{1,0:T(8,128)(2,1)S(1)}, u32[]{:S(2)}, u32[]{:S(2)}) %collective-permute-start.29) | collective-permute-done | bytes 1032224 | tf_op jit(solution)/shard_map/ppermute | solution.py:57
  317.8 9.3 %collective-permute-done.30.r1 = bf16[4032,128]{1,0:T(8,128)(2,1)} collective-permute-done((bf16[4032,128]{1,0:T(8,128)(2,1)}, bf16[4032,128]{1,0:T(8,128)(2,1)}, u32[]{:S(2)}, u32[]{:S(2)}) %collective-permute-start.30) | collective-permute-done | bytes 1032224 | tf_op jit(solution)/shard_map/ppermute | solution.py:57
  327.1 9.8 %collective-permute-done.31.r2 = bf16[4032,128]{1,0:T(8,128)(2,1)S(1)} collective-permute-done((bf16[4032,128]{1,0:T(8,128)(2,1)}, bf16[4032,128]{1,0:T(8,128)(2,1)S(1)}, u32[]{:S(2)}, u32[]{:S(2)}) %collective-permute-start.31) | collective-permute-done | bytes 1032224 | tf_op jit(solution)/shard_map/ppermute | solution.py:57
  336.9 3.7 %collective-permute-done.32.r3 = bf16[4032,128]{1,0:T(8,128)(2,1)S(1)} collective-permute-done((bf16[4032,128]{1,0:T(8,128)(2,1)}, bf16[4032,128]{1,0:T(8,128)(2,1)S(1)}, u32[]{:S(2)}, u32[]{:S(2)}) %collective-permute-start.32) | collective-permute-done | bytes 1032224 | tf_op jit(solution)/shard_map/ppermute | solution.py:57
  340.6 4.0 %shard_map.62 = bf16[896,2304]{1,0:T(8,128)(2,1)} custom-call(s32[4]{0:T(128)S(1)} %copy-done.7, bf16[4032,128]{1,0:T(8,128)(2,1)S(1)} %collective-permute-done.29.r0, bf16[4032,128]{1,0:T(8,128)(2,1)} %collective-permute-done.30.r1, bf16[4032,128]{1,0:T(8,128)(2,1)S(1)} %collective-permute-done.31.r2, bf16[4032,128]{1,0:T(8,128)(2,1)S(1)} %collective-permute-done.32.r3), custom_call_target="tpu_custom_call" | custom-call | bytes 8300000 | tf_op jit(solution)/shard_map/pallas_call | solution.py:553
  (102 shorter events, 32.0 us)
Async XLA Ops:
  52.0 27.4 %all-to-all-start.1 = ((bf16[16,432,128]{2,1,0:T(8,128)(2,1)}), bf16[16,432,128]{2,1,0:T(8,128)(2,1)}, u32[]{:S(2)}, u32[]{:S(2)}) async-start(bf16[16,432,128]{2,1,0:T(8,128)(2,1)} %get-tuple-element.57), calls=%async_computation.1 | async-start | bytes 3538944 | tf_op jit(solution)/shard_map/all_to_all | solution.py:571
  64.6 43.2 %collective-permute-start = (bf16[7,80,1152]{2,1,0:T(8,128)(2,1)}, bf16[7,80,1152]{2,1,0:T(8,128)(2,1)S(1)}, u32[]{:S(2)}, u32[]{:S(2)}) collective-permute-start(bf16[7,80,1152]{2,1,0:T(8,128)(2,1)} %get-tuple-element.60), channel_id=1, source_target_pairs={{0,0},{1,1},{2,2},{3,3},{4,4},{5,5},{6,6},{7,7},{8,16},{9,17},{10,... | collective-permute-start | bytes 3870728 | tf_op jit(solution)/shard_map/ppermute | solution.py:57
  71.3 36.6 %collective-permute-start.2 = (bf16[7,80,1152]{2,1,0:T(8,128)(2,1)}, bf16[7,80,1152]{2,1,0:T(8,128)(2,1)}, u32[]{:S(2)}, u32[]{:S(2)}) collective-permute-start(bf16[7,80,1152]{2,1,0:T(8,128)(2,1)} %get-tuple-element.62), channel_id=1, source_target_pairs={{0,4},{1,5},{2,6},{3,7},{4,0},{5,1},{6,2},{7,3},{8,20},{9,21},{10,... | collective-permute-start | bytes 3870728 | tf_op jit(solution)/shard_map/ppermute | solution.py:57
  84.8 38.8 %collective-permute-start.1 = (bf16[7,48,1152]{2,1,0:T(8,128)(2,1)}, bf16[7,48,1152]{2,1,0:T(8,128)(2,1)}, u32[]{:S(2)}, u32[]{:S(2)}) collective-permute-start(bf16[7,48,1152]{2,1,0:T(8,128)(2,1)} %get-tuple-element.61), channel_id=1, source_target_pairs={{0,0},{1,1},{2,2},{3,3},{4,4},{5,5},{6,6},{7,7},{8,16},{9,17},{10,... | collective-permute-start | bytes 2322440 | tf_op jit(solution)/shard_map/ppermute | solution.py:57
  91.9 31.7 %collective-permute-start.3 = (bf16[7,48,1152]{2,1,0:T(8,128)(2,1)}, bf16[7,48,1152]{2,1,0:T(8,128)(2,1)}, u32[]{:S(2)}, u32[]{:S(2)}) collective-permute-start(bf16[7,48,1152]{2,1,0:T(8,128)(2,1)} %get-tuple-element.63), channel_id=1, source_target_pairs={{0,4},{1,5},{2,6},{3,7},{4,0},{5,1},{6,2},{7,3},{8,20},{9,21},{10,... | collective-permute-start | bytes 2322440 | tf_op jit(solution)/shard_map/ppermute | solution.py:57
  107.8 16.4 %collective-permute-start.4 = (bf16[7,80,1152]{2,1,0:T(8,128)(2,1)S(1)}, bf16[7,80,1152]{2,1,0:T(8,128)(2,1)S(1)}, u32[]{:S(2)}, u32[]{:S(2)}) collective-permute-start(bf16[7,80,1152]{2,1,0:T(8,128)(2,1)S(1)} %collective-permute-done.refs_1_.refs_0_), channel_id=1, source_target_pairs={{0,16},{1,17},{2,18},{3,19},{4,20},{5,21},{6,22},{7,23},{8,24},{9,... | collective-permute-start | bytes 3870728 | tf_op jit(solution)/shard_map/ppermute | solution.py:57
  107.8 16.4 %collective-permute-start.6 = (bf16[7,80,1152]{2,1,0:T(8,128)(2,1)}, bf16[7,80,1152]{2,1,0:T(8,128)(2,1)}, u32[]{:S(2)}, u32[]{:S(2)}) collective-permute-start(bf16[7,80,1152]{2,1,0:T(8,128)(2,1)} %collective-permute-done.2.refs_3_.refs_2_), channel_id=1, source_target_pairs={{0,16},{1,17},{2,18},{3,19},{4,20},{5,21},{6,22},{7,23},{8,24},{9,... | collective-permute-start | bytes 3870728 | tf_op jit(solution)/shard_map/ppermute | solution.py:57
  123.6 3.7 %collective-permute-start.7 = (bf16[7,48,1152]{2,1,0:T(8,128)(2,1)}, bf16[7,48,1152]{2,1,0:T(8,128)(2,1)}, u32[]{:S(2)}, u32[]{:S(2)}) collective-permute-start(bf16[7,48,1152]{2,1,0:T(8,128)(2,1)} %collective-permute-done.3.refs_4_.refs_3_), channel_id=1, source_target_pairs={{0,16},{1,17},{2,18},{3,19},{4,20},{5,21},{6,22},{7,23},{8,24},{9,... | collective-permute-start | bytes 2322440 | tf_op jit(solution)/shard_map/ppermute | solution.py:57
  132.1 12.2 %collective-permute-start.8 = (bf16[608,256]{1,0:T(8,128)(2,1)S(1)}, bf16[608,256]{1,0:T(8,128)(2,1)S(1)}, u32[]{:S(2)}, u32[]{:S(2)}) collective-permute-start(bf16[608,256]{1,0:T(8,128)(2,1)S(1)} %get-tuple-element.67), channel_id=1, source_target_pairs={{0,1},{1,2},{2,3},{3,0},{4,5},{5,6},{6,7},{7,4},{8,9},{9,10},{10,1... | collective-permute-start | bytes 933896 | tf_op jit(solution)/shard_map/ppermute | solution.py:57
  133.4 10.9 %collective-permute-start.9 = (bf16[592,256]{1,0:T(8,128)(2,1)S(1)}, bf16[592,256]{1,0:T(8,128)(2,1)S(1)}, u32[]{:S(2)}, u32[]{:S(2)}) collective-permute-start(bf16[592,256]{1,0:T(8,128)(2,1)S(1)} %get-tuple-element.68), channel_id=1, source_target_pairs={{0,3},{1,0},{2,1},{3,2},{4,7},{5,4},{6,5},{7,6},{8,11},{9,8},{10,9... | collective-permute-start | bytes 909320 | tf_op jit(solution)/shard_map/ppermute | solution.py:57
  134.9 9.4 %collective-permute-start.10 = (bf16[592,256]{1,0:T(8,128)(2,1)S(1)}, bf16[592,256]{1,0:T(8,128)(2,1)S(1)}, u32[]{:S(2)}, u32[]{:S(2)}) collective-permute-start(bf16[592,256]{1,0:T(8,128)(2,1)S(1)} %get-tuple-element.69), channel_id=1, source_target_pairs={{0,4},{1,5},{2,6},{3,7},{4,0},{5,1},{6,2},{7,3},{8,12},{9,13},{10,... | collective-permute-start | bytes 909320 | tf_op jit(solution)/shard_map/ppermute | solution.py:57
  144.6 21.2 %collective-permute-start.12 = (bf16[1792,256]{1,0:T(8,128)(2,1)S(1)}, bf16[1792,256]{1,0:T(8,128)(2,1)S(1)}, u32[]{:S(2)}, u32[]{:S(2)}) collective-permute-start(bf16[1792,256]{1,0:T(8,128)(2,1)S(1)} %get-tuple-element.82), channel_id=1, source_target_pairs={{0,3},{1,0},{2,1},{3,2},{4,7},{5,4},{6,5},{7,6},{8,11},{9,8},{10,9... | collective-permute-start | bytes 2752520 | tf_op jit(solution)/shard_map/ppermute | solution.py:57
  146.1 21.8 %collective-permute-start.13 = (bf16[1792,256]{1,0:T(8,128)(2,1)S(1)}, bf16[1792,256]{1,0:T(8,128)(2,1)S(1)}, u32[]{:S(2)}, u32[]{:S(2)}) collective-permute-start(bf16[1792,256]{1,0:T(8,128)(2,1)S(1)} %get-tuple-element.83), channel_id=1, source_target_pairs={{0,1},{1,2},{2,3},{3,0},{4,5},{5,6},{6,7},{7,4},{8,9},{9,10},{10,1... | collective-permute-start | bytes 2752520 | tf_op jit(solution)/shard_map/ppermute | solution.py:57
  146.2 21.7 %collective-permute-start.11 = (bf16[1792,256]{1,0:T(8,128)(2,1)S(1)}, bf16[1792,256]{1,0:T(8,128)(2,1)S(1)}, u32[]{:S(2)}, u32[]{:S(2)}) collective-permute-start(bf16[1792,256]{1,0:T(8,128)(2,1)S(1)} %get-tuple-element.70), channel_id=1, source_target_pairs={{0,4},{1,5},{2,6},{3,7},{4,0},{5,1},{6,2},{7,3},{8,12},{9,13},{10,... | collective-permute-start | bytes 2752520 | tf_op jit(solution)/shard_map/ppermute | solution.py:57
  156.3 29.2 %collective-permute-start.16 = (bf16[1792,256]{1,0:T(8,128)(2,1)S(1)}, bf16[1792,256]{1,0:T(8,128)(2,1)S(1)}, u32[]{:S(2)}, u32[]{:S(2)}) collective-permute-start(bf16[1792,256]{1,0:T(8,128)(2,1)S(1)} %get-tuple-element.86), channel_id=1, source_target_pairs={{0,3},{1,0},{2,1},{3,2},{4,7},{5,4},{6,5},{7,6},{8,11},{9,8},{10,9... | collective-permute-start | bytes 2752520 | tf_op jit(solution)/shard_map/ppermute | solution.py:57
  168.4 19.8 %collective-permute-start.15 = (bf16[1792,256]{1,0:T(8,128)(2,1)S(1)}, bf16[1792,256]{1,0:T(8,128)(2,1)S(1)}, u32[]{:S(2)}, u32[]{:S(2)}) collective-permute-start(bf16[1792,256]{1,0:T(8,128)(2,1)S(1)} %get-tuple-element.85), channel_id=1, source_target_pairs={{0,4},{1,5},{2,6},{3,7},{4,0},{5,1},{6,2},{7,3},{8,12},{9,13},{10,... | collective-permute-start | bytes 2752520 | tf_op jit(solution)/shard_map/ppermute | solution.py:57
  168.8 20.6 %collective-permute-start.14 = (bf16[1792,256]{1,0:T(8,128)(2,1)S(1)}, bf16[1792,256]{1,0:T(8,128)(2,1)S(1)}, u32[]{:S(2)}, u32[]{:S(2)}) collective-permute-start(bf16[1792,256]{1,0:T(8,128)(2,1)S(1)} %get-tuple-element.84), channel_id=1, source_target_pairs={{0,1},{1,2},{2,3},{3,0},{4,5},{5,6},{6,7},{7,4},{8,9},{9,10},{10,1... | collective-permute-start | bytes 2752520 | tf_op jit(solution)/shard_map/ppermute | solution.py:57
  189.8 18.5 %collective-permute-start.18 = (bf16[1792,256]{1,0:T(8,128)(2,1)S(1)}, bf16[1792,256]{1,0:T(8,128)(2,1)S(1)}, u32[]{:S(2)}, u32[]{:S(2)}) collective-permute-start(bf16[1792,256]{1,0:T(8,128)(2,1)S(1)} %shard_map.59.refs_0_), channel_id=1, source_target_pairs={{0,3},{1,0},{2,1},{3,2},{4,7},{5,4},{6,5},{7,6},{8,11},{9,8},{10,9... | collective-permute-start | bytes 2752520 | tf_op jit(solution)/shard_map/ppermute | solution.py:57
  189.9 20.9 %collective-permute-start.19 = (bf16[1792,256]{1,0:T(8,128)(2,1)S(1)}, bf16[1792,256]{1,0:T(8,128)(2,1)S(1)}, u32[]{:S(2)}, u32[]{:S(2)}) collective-permute-start(bf16[1792,256]{1,0:T(8,128)(2,1)S(1)} %shard_map.59.refs_0_), channel_id=1, source_target_pairs={{0,4},{1,5},{2,6},{3,7},{4,0},{5,1},{6,2},{7,3},{8,12},{9,13},{10,... | collective-permute-start | bytes 2752520 | tf_op jit(solution)/shard_map/ppermute | solution.py:57
  191.1 19.9 %collective-permute-start.17 = (bf16[1792,256]{1,0:T(8,128)(2,1)S(1)}, bf16[1792,256]{1,0:T(8,128)(2,1)S(1)}, u32[]{:S(2)}, u32[]{:S(2)}) collective-permute-start(bf16[1792,256]{1,0:T(8,128)(2,1)S(1)} %shard_map.59.refs_0_), channel_id=1, source_target_pairs={{0,1},{1,2},{2,3},{3,0},{4,5},{5,6},{6,7},{7,4},{8,9},{9,10},{10,1... | collective-permute-start | bytes 2752520 | tf_op jit(solution)/shard_map/ppermute | solution.py:57
  208.4 20.7 %collective-permute-start.22 = (bf16[1792,256]{1,0:T(8,128)(2,1)S(1)}, bf16[1792,256]{1,0:T(8,128)(2,1)S(1)}, u32[]{:S(2)}, u32[]{:S(2)}) collective-permute-start(bf16[1792,256]{1,0:T(8,128)(2,1)S(1)} %collective-permute-done.18.refs_2_), channel_id=1, source_target_pairs={{0,3},{1,0},{2,1},{3,2},{4,7},{5,4},{6,5},{7,6},{8,11},{9,8},{10,9... | collective-permute-start | bytes 2752520 | tf_op jit(solution)/shard_map/ppermute | solution.py:57
  209.6 19.4 %collective-permute-start.20 = (bf16[1792,256]{1,0:T(8,128)(2,1)S(1)}, bf16[1792,256]{1,0:T(8,128)(2,1)S(1)}, u32[]{:S(2)}, u32[]{:S(2)}) collective-permute-start(bf16[1792,256]{1,0:T(8,128)(2,1)S(1)} %collective-permute-done.18.refs_2_), channel_id=1, source_target_pairs={{0,4},{1,5},{2,6},{3,7},{4,0},{5,1},{6,2},{7,3},{8,12},{9,13},{10,... | collective-permute-start | bytes 2752520 | tf_op jit(solution)/shard_map/ppermute | solution.py:57
  210.8 18.3 %collective-permute-start.21 = (bf16[1792,256]{1,0:T(8,128)(2,1)S(1)}, bf16[1792,256]{1,0:T(8,128)(2,1)S(1)}, u32[]{:S(2)}, u32[]{:S(2)}) collective-permute-start(bf16[1792,256]{1,0:T(8,128)(2,1)S(1)} %collective-permute-done.19.refs_3_), channel_id=1, source_target_pairs={{0,1},{1,2},{2,3},{3,0},{4,5},{5,6},{6,7},{7,4},{8,9},{9,10},{10,1... | collective-permute-start | bytes 2752520 | tf_op jit(solution)/shard_map/ppermute | solution.py:57
  212.1 34.8 %collective-permute-start.26 = (bf16[7168,256]{1,0:T(8,128)(2,1)S(1)}, bf16[7168,256]{1,0:T(8,128)(2,1)S(1)}, u32[]{:S(2)}, u32[]{:S(2)}) collective-permute-start(bf16[7168,256]{1,0:T(8,128)(2,1)S(1)} %pad_maximum_fusion), channel_id=1, source_target_pairs={{0,16},{1,17},{2,18},{3,19},{4,20},{5,21},{6,22},{7,23},{8,24},{9,... | collective-permute-start | bytes 11010056 | tf_op jit(solution)/shard_map/ppermute | solution.py:57
  229.3 16.0 %collective-permute-start.27 = (bf16[5376,256]{1,0:T(8,128)(2,1)S(1)}, bf16[5376,256]{1,0:T(8,128)(2,1)S(1)}, u32[]{:S(2)}, u32[]{:S(2)}) collective-permute-start(bf16[5376,256]{1,0:T(8,128)(2,1)S(1)} %pad_maximum_fusion.1), channel_id=1, source_target_pairs={{0,16},{1,17},{2,18},{3,19},{4,20},{5,21},{6,22},{7,23},{8,24},{9,... | collective-permute-start | bytes 8257544 | tf_op jit(solution)/shard_map/ppermute | solution.py:57
  235.1 10.2 %collective-permute-start.23 = (bf16[608,256]{1,0:T(8,128)(2,1)S(1)}, bf16[608,256]{1,0:T(8,128)(2,1)S(1)}, u32[]{:S(2)}, u32[]{:S(2)}) collective-permute-start(bf16[608,256]{1,0:T(8,128)(2,1)S(1)} %slice.17), channel_id=1, source_target_pairs={{0,3},{1,0},{2,1},{3,2},{4,7},{5,4},{6,5},{7,6},{8,11},{9,8},{10,9... | collective-permute-start | bytes 933896 | tf_op jit(solution)/shard_map/ppermute | solution.py:57
  235.2 10.1 %collective-permute-start.24 = (bf16[592,256]{1,0:T(8,128)(2,1)S(1)}, bf16[592,256]{1,0:T(8,128)(2,1)S(1)}, u32[]{:S(2)}, u32[]{:S(2)}) collective-permute-start(bf16[592,256]{1,0:T(8,128)(2,1)S(1)} %slice.18), channel_id=1, source_target_pairs={{0,1},{1,2},{2,3},{3,0},{4,5},{5,6},{6,7},{7,4},{8,9},{9,10},{10,1... | collective-permute-start | bytes 909320 | tf_op jit(solution)/shard_map/ppermute | solution.py:57
  236.8 8.5 %collective-permute-start.25 = (bf16[592,256]{1,0:T(8,128)(2,1)S(1)}, bf16[592,256]{1,0:T(8,128)(2,1)S(1)}, u32[]{:S(2)}, u32[]{:S(2)}) collective-permute-start(bf16[592,256]{1,0:T(8,128)(2,1)S(1)} %slice.19), channel_id=1, source_target_pairs={{0,4},{1,5},{2,6},{3,7},{4,0},{5,1},{6,2},{7,3},{8,12},{9,13},{10,... | collective-permute-start | bytes 909320 | tf_op jit(solution)/shard_map/ppermute | solution.py:57
  288.9 28.9 %collective-permute-start.29 = (bf16[4032,128]{1,0:T(8,128)(2,1)}, bf16[4032,128]{1,0:T(8,128)(2,1)S(1)}, u32[]{:S(2)}, u32[]{:S(2)}) collective-permute-start(bf16[4032,128]{1,0:T(8,128)(2,1)} %get-tuple-element.100), channel_id=1, source_target_pairs={{0,0},{1,1},{2,2},{3,3},{4,4},{5,5},{6,6},{7,7},{8,16},{9,17},{10,... | collective-permute-start | bytes 3096584 | tf_op jit(solution)/shard_map/ppermute | solution.py:57
  292.7 34.4 %collective-permute-start.30 = (bf16[4032,128]{1,0:T(8,128)(2,1)}, bf16[4032,128]{1,0:T(8,128)(2,1)}, u32[]{:S(2)}, u32[]{:S(2)}) collective-permute-start(bf16[4032,128]{1,0:T(8,128)(2,1)} %get-tuple-element.101), channel_id=1, source_target_pairs={{0,4},{1,5},{2,6},{3,7},{4,0},{5,1},{6,2},{7,3},{8,20},{9,21},{10,... | collective-permute-start | bytes 3096584 | tf_op jit(solution)/shard_map/ppermute | solution.py:57
  310.5 26.4 %collective-permute-start.31 = (bf16[4032,128]{1,0:T(8,128)(2,1)}, bf16[4032,128]{1,0:T(8,128)(2,1)S(1)}, u32[]{:S(2)}, u32[]{:S(2)}) collective-permute-start(bf16[4032,128]{1,0:T(8,128)(2,1)} %get-tuple-element.106), channel_id=1, source_target_pairs={{0,8},{1,9},{2,10},{3,11},{4,12},{5,13},{6,14},{7,15},{8,24},{9,25... | collective-permute-start | bytes 3096584 | tf_op jit(solution)/shard_map/ppermute | solution.py:57
  310.5 30.1 %collective-permute-start.32 = (bf16[4032,128]{1,0:T(8,128)(2,1)}, bf16[4032,128]{1,0:T(8,128)(2,1)S(1)}, u32[]{:S(2)}, u32[]{:S(2)}) collective-permute-start(bf16[4032,128]{1,0:T(8,128)(2,1)} %get-tuple-element.107), channel_id=1, source_target_pairs={{0,12},{1,13},{2,14},{3,15},{4,8},{5,9},{6,10},{7,11},{8,28},{9,29... | collective-permute-start | bytes 3096584 | tf_op jit(solution)/shard_map/ppermute | solution.py:57
  (23 other events, 274.2 us)

commit v9 on v8

--- a/solution.py
+++ b/solution.py
@@ -610,8 +610,8 @@
         send(x[row : row + size]) for send, x, (row, size) in zip((down, up, across), (a1, a2, a3), PARTS)
     )
     swapped = (swap(jnp.concatenate([mine, low, high, pair])), swap(jnp.concatenate([a1, a2, a3])))
-    ends, swapped = lax.optimization_barrier((ends, swapped))
-    swapped += (swap(jnp.concatenate(ends)),)
+    ends, near_swap = lax.optimization_barrier((ends, swapped[0]))
+    swapped = (near_swap, swapped[1], swap(jnp.concatenate(ends)))
     *sent, direct, flipped, mixed, scales = apply_poly(info, (mine, low, high, pair, a1, a2, a3), ends, swapped, turned)
     sent += apply_rest(info, direct, flipped, mixed, scales, turned)
 

time: 346 us -> 352 us (1.017)
  waiting for transfers between devices: 132 us -> 142 us
  starting transfers between devices: 56.1 us -> 51.6 us
    ppermute x33, waiting for transfers between devices: 123 us -> 134 us  [move(): return lax.ppermute(x, AXES[1:], pairs)]
    ppermute x33, starting transfers between devices: 51.7 us -> 47.2 us  [move(): return lax.ppermute(x, AXES[1:], pairs)]
  transfers between devices with their start and end apart: 34 -> 34, of which waited for: 18 -> 20; matrix products, arithmetic and copies ran while one was open for 1% -> 0% of each run, Pallas kernels for 15% -> 15%
where the time goes in v9:
time: 352 us; the launch traced here: 351 us
  waiting for transfers between devices  142 us (40%)
  Pallas kernels  104 us (30%)
  starting transfers between devices  51.6 us (15%)
  blocking collectives  46 us (13%)
    ppermute x33, waiting for transfers between devices, move(): return lax.ppermute(x, AXES[1:], pairs)  134 us
    ppermute x33, starting transfers between devices, move(): return lax.ppermute(x, AXES[1:], pairs)  47.2 us
    all_to_all x1, blocking collectives, on_device(): lax.all_to_all(upper, PLANE, split_axis=0, concat_axis=0, tiled=True)  46 us
    pallas_call x1, Pallas kernels, apply_poly(): pl.pallas_call(apply_kernel, in_specs=[SMEM] + [HBM] * 14, out_specs=[HBM...  37.7 us
    pallas_call x3, Pallas kernels, gram_chunks(): pl.pallas_call(lambda *refs: gram_kernel(dests, *refs), in_specs=[SMEM] +...  22.8 us
    pallas_call x1, Pallas kernels, apply_rest(): pl.pallas_call(rest_kernel, grid_spec=pltpu.PrefetchScalarGridSpec(num_sc...  16.5 us
    pallas_call x2, Pallas kernels, update_momentum(): pl.pallas_call(lambda *refs: momentum_kernel(part, *refs), in_specs=[SMEM...  12.5 us
    all_to_all x1, waiting for transfers between devices, on_device(): lax.all_to_all(lower, PLANE, split_axis=0, concat_axis=0, tiled=True)  8.07 us
  transfers between devices with their start and end apart: 34, of which 20 were waited for; matrix products, arithmetic and copies ran while one was open for 0% of the time, Pallas kernels for 15%

profile of v9, /device:TPU:1, one launch (start us, length us, event | category | flops | bytes accessed | tf_op | source)
XLA Modules:
  0.0 351.0 jit_solution(15992889273008187801)
XLA Ops:
  0.6 5.4 %shard_map.50 = (bf16[16,736,128]{2,1,0:T(8,128)(2,1)}, bf16[16,432,128]{2,1,0:T(8,128)(2,1)}) custom-call(s32[14]{0:T(128)} %ids.1, bf16[14,128,1152]{2,1,0:T(8,128)(2,1)} %tiles.1), custom_call_target="tpu_custom_call" | custom-call | bytes 8257536 | tf_op jit(solution)/shard_map/pallas_call | solution.py:123
  6.0 46.0 %all_to_all.10.refs_1_ = bf16[16,736,128]{2,1,0:T(8,128)(2,1)S(1)} all-to-all(bf16[16,736,128]{2,1,0:T(8,128)(2,1)} %get-tuple-element.54), channel_id=1, replica_groups=mesh['x'=4,'core'=2,'zm'=2,'zl'=2,'y'=4] {'zm','zl','y'}, dimensions={0} | all-to-all | bytes 6029312 | tf_op jit(solution)/shard_map/all_to_all | solution.py:569
  52.0 4.4 %all-to-all-start.1 = ((bf16[16,432,128]{2,1,0:T(8,128)(2,1)}), bf16[16,432,128]{2,1,0:T(8,128)(2,1)}, u32[]{:S(2)}, u32[]{:S(2)}) async-start(bf16[16,432,128]{2,1,0:T(8,128)(2,1)} %get-tuple-element.56), calls=%async_computation.1 | async-start | bytes 3538944 | tf_op jit(solution)/shard_map/all_to_all | solution.py:571
  57.5 7.1 %shard_map.51 = (f32[896,2304]{1,0:T(8,128)}, bf16[7,80,1152]{2,1,0:T(8,128)(2,1)}, bf16[7,80,1152]{2,1,0:T(8,128)(2,1)}) custom-call(s32[15]{0:T(128)} %pad_add_fusion.refs_0_, bf16[16,736,128]{2,1,0:T(8,128)(2,1)} %copy-done.8, f32[896,2304]{1,0:T(8,128)} %refs_2_.3), custom_call_target="tpu_custom_call" | custom-call | bytes 12386304 | tf_op jit(solution)/shard_map/pallas_call | solution.py:195
  64.6 6.6 %collective-permute-start = (bf16[7,80,1152]{2,1,0:T(8,128)(2,1)}, bf16[7,80,1152]{2,1,0:T(8,128)(2,1)S(1)}, u32[]{:S(2)}, u32[]{:S(2)}) collective-permute-start(bf16[7,80,1152]{2,1,0:T(8,128)(2,1)} %get-tuple-element.59), channel_id=1, source_target_pairs={{0,0},{1,1},{2,2},{3,3},{4,4},{5,5},{6,6},{7,7},{8,16},{9,17},{10,... | collective-permute-start | bytes 3870728 | tf_op jit(solution)/shard_map/ppermute | solution.py:57
  71.4 8.1 %all-to-all-done.1.refs_1_ = bf16[16,432,128]{2,1,0:T(8,128)(2,1)} async-done(((bf16[16,432,128]{2,1,0:T(8,128)(2,1)}), bf16[16,432,128]{2,1,0:T(8,128)(2,1)}, u32[]{:S(2)}, u32[]{:S(2)}) %all-to-all-start.1) | async-done | bytes 1769504 | tf_op jit(solution)/shard_map/all_to_all | solution.py:571
  79.4 5.4 %shard_map.52 = (f32[896,2304]{1,0:T(8,128)}, bf16[7,48,1152]{2,1,0:T(8,128)(2,1)}, bf16[7,48,1152]{2,1,0:T(8,128)(2,1)}) custom-call(s32[15]{0:T(128)} %pad_add_fusion.refs_0_, bf16[16,432,128]{2,1,0:T(8,128)(2,1)} %all-to-all-done.1.refs_1_, f32[896,2304]{1,0:T(8,128)} %refs_2_.3, ...), custom_call_target="tpu_custom_call", output_to_operand_aliasing={{0}: (3, {})} | custom-call | bytes 12386304 | tf_op jit(solution)/shard_map/pallas_call | solution.py:195
  84.8 7.1 %collective-permute-start.1 = (bf16[7,48,1152]{2,1,0:T(8,128)(2,1)}, bf16[7,48,1152]{2,1,0:T(8,128)(2,1)}, u32[]{:S(2)}, u32[]{:S(2)}) collective-permute-start(bf16[7,48,1152]{2,1,0:T(8,128)(2,1)} %get-tuple-element.60), channel_id=1, source_target_pairs={{0,0},{1,1},{2,2},{3,3},{4,4},{5,5},{6,6},{7,7},{8,16},{9,17},{10,... | collective-permute-start | bytes 2322440 | tf_op jit(solution)/shard_map/ppermute | solution.py:57
  92.1 15.8 %collective-permute-done.refs_1_.refs_0_ = bf16[7,80,1152]{2,1,0:T(8,128)(2,1)S(1)} collective-permute-done((bf16[7,80,1152]{2,1,0:T(8,128)(2,1)}, bf16[7,80,1152]{2,1,0:T(8,128)(2,1)S(1)}, u32[]{:S(2)}, u32[]{:S(2)}) %collective-permute-start) | collective-permute-done | bytes 1290272 | tf_op jit(solution)/shard_map/ppermute | solution.py:57
  108.3 15.3 %collective-permute-done.1.refs_2_.refs_1_ = bf16[7,48,1152]{2,1,0:T(8,128)(2,1)} collective-permute-done((bf16[7,48,1152]{2,1,0:T(8,128)(2,1)}, bf16[7,48,1152]{2,1,0:T(8,128)(2,1)}, u32[]{:S(2)}, u32[]{:S(2)}) %collective-permute-start.1) | collective-permute-done | bytes 774176 | tf_op jit(solution)/shard_map/ppermute | solution.py:57
  127.3 4.8 %shard_map.54 = (bf16[608,256]{1,0:T(8,128)(2,1)S(1)}, bf16[592,256]{1,0:T(8,128)(2,1)S(1)}, bf16[592,256]{1,0:T(8,128)(2,1)S(1)}) custom-call(s32[4]{0:T(128)S(1)} %pad_add_fusion.1.refs_0_.info, bf16[7,80,1152]{2,1,0:T(8,128)(2,1)S(1)} %collective-permute-done.refs_1_.refs_0_, bf16[7,48,1152]{2,1,0:T(8,128)(2,1)} %collective-permute-done.1.refs_2_.refs_1_, ...), custom_call_target="tpu_custom_call" | custom-call | flops 1056964608 | bytes 10135008 | tf_op jit(solution)/shard_map/pallas_call | solution.py:278
  135.8 8.5 %shard_map.53 = (f32[1792,256]{1,0:T(8,128)S(1)}, f32[1792,256]{1,0:T(8,128)S(1)}, f32[1792,256]{1,0:T(8,128)S(1)}) custom-call(s32[4]{0:T(128)S(1)} %pad_add_fusion.1.refs_0_.info, bf16[7,80,1152]{2,1,0:T(8,128)(2,1)S(1)} %collective-permute-done.refs_1_.refs_0_, bf16[7,48,1152]{2,1,0:T(8,128)(2,1)} %collective-permute-done.1.refs_2_.refs_1_, ...), custom_call_target="tpu_custom_call" | custom-call | flops 3170893824 | bytes 13805024 | tf_op jit(solution)/shard_map/pallas_call | solution.py:278
  146.7 9.6 %shard_map.56 = (f32[1792,256]{1,0:T(8,128)S(1)}, f32[1792,256]{1,0:T(8,128)S(1)}, bf16[1792,256]{1,0:T(8,128)(2,1)S(1)}, f32[1792,256]{1,0:T(8,128)S(1)}) custom-call(s32[4]{0:T(128)S(1)} %pad_add_fusion.1.refs_0_.info, bf16[7,80,1152]{2,1,0:T(8,128)(2,1)S(1)} %collective-permute-done.refs_1_.refs_0_, ...), custom_call_target="tpu_custom_call" | custom-call | flops 4227858432 | bytes 15640032 | tf_op jit(solution)/shard_map/pallas_call | solution.py:278
  156.3 2.5 collective-permute-start.16
  158.8 7.1 %collective-permute-done.12.g2 = bf16[1792,256]{1,0:T(8,128)(2,1)S(1)} collective-permute-done((bf16[1792,256]{1,0:T(8,128)(2,1)S(1)}, bf16[1792,256]{1,0:T(8,128)(2,1)S(1)}, u32[]{:S(2)}, u32[]{:S(2)}) %collective-permute-start.12) | collective-permute-done | bytes 917536 | tf_op jit(solution)/shard_map/ppermute | solution.py:57
  168.8 4.2 %shard_map.58.turned.refs_13_.panel = bf16[576,5376]{1,0:T(8,128)(2,1)S(1)} custom-call(s32[4]{0:T(128)S(1)} %pad_add_fusion.1.refs_0_.info, bf16[7,80,1152]{2,1,0:T(8,128)(2,1)S(1)} %copy-done.2, bf16[7,48,1152]{2,1,0:T(8,128)(2,1)} %collective-permute-done.1.refs_2_.refs_1_, bf16[7,80,1152]{2,1,0:T(8,128)(2,1)} %collective-permute-done.2.refs_3_.refs_2_, ...), custom_call_target="tpu_custom_call" | custom-call | bytes 12000000 | tf_op jit(solution)/shard_map/pallas_call | solution.py:337
  173.0 12.5 %collective-permute-done.16.v3 = bf16[1792,256]{1,0:T(8,128)(2,1)S(1)} collective-permute-done((bf16[1792,256]{1,0:T(8,128)(2,1)S(1)}, bf16[1792,256]{1,0:T(8,128)(2,1)S(1)}, u32[]{:S(2)}, u32[]{:S(2)}) %collective-permute-start.16) | collective-permute-done | bytes 917536 | tf_op jit(solution)/shard_map/ppermute | solution.py:57
  185.5 2.6 collective-permute-done.15.v2
  192.5 15.9 %collective-permute-done.19.refs_3_ = bf16[1792,256]{1,0:T(8,128)(2,1)S(1)} collective-permute-done((bf16[1792,256]{1,0:T(8,128)(2,1)S(1)}, bf16[1792,256]{1,0:T(8,128)(2,1)S(1)}, u32[]{:S(2)}, u32[]{:S(2)}) %collective-permute-start.19) | collective-permute-done | bytes 917536 | tf_op jit(solution)/shard_map/ppermute | solution.py:57
  211.1 4.8 %collective-permute-start.26 = (bf16[7168,256]{1,0:T(8,128)(2,1)S(1)}, bf16[7168,256]{1,0:T(8,128)(2,1)S(1)}, u32[]{:S(2)}, u32[]{:S(2)}) collective-permute-start(bf16[7168,256]{1,0:T(8,128)(2,1)S(1)} %pad_maximum_fusion), channel_id=1, source_target_pairs={{0,16},{1,17},{2,18},{3,19},{4,20},{5,21},{6,22},{7,23},{8,24},{9,... | collective-permute-start | bytes 11010056 | tf_op jit(solution)/shard_map/ppermute | solution.py:57
  216.2 2.4 collective-permute-start.22
  219.0 20.2 %collective-permute-done.21.refs_5_ = bf16[1792,256]{1,0:T(8,128)(2,1)S(1)} collective-permute-done((bf16[1792,256]{1,0:T(8,128)(2,1)S(1)}, bf16[1792,256]{1,0:T(8,128)(2,1)S(1)}, u32[]{:S(2)}, u32[]{:S(2)}) %collective-permute-start.21) | collective-permute-done | bytes 917536 | tf_op jit(solution)/shard_map/ppermute | solution.py:57
  243.8 9.0 %collective-permute-done.24.refs_8_ = bf16[592,256]{1,0:T(8,128)(2,1)S(1)} collective-permute-done((bf16[592,256]{1,0:T(8,128)(2,1)S(1)}, bf16[592,256]{1,0:T(8,128)(2,1)S(1)}, u32[]{:S(2)}, u32[]{:S(2)}) %collective-permute-start.24) | collective-permute-done | bytes 303136 | tf_op jit(solution)/shard_map/ppermute | solution.py:57
  257.2 37.7 %shard_map.60 = (bf16[4032,128]{1,0:T(8,128)(2,1)}, bf16[4032,128]{1,0:T(8,128)(2,1)}, bf16[7,2048,256]{2,1,0:T(8,128)(2,1)}, bf16[7,1536,256]{2,1,0:T(8,128)(2,...) custom-call(s32[4]{0:T(128)} %copy-done.6, bf16[1792,256]{1,0:T(8,128)(2,1)} %copy-done.5, bf16[1792,256]{1,0:T(8,128)(2,1)} %copy-done.14, ...), custom_call_target="tpu_custom_call" | custom-call | flops 22196256768 | bytes 40000000 | tf_op jit(solution)/shard_map/pallas_call | solution.py:507
  294.9 4.5 %collective-permute-start.29 = (bf16[4032,128]{1,0:T(8,128)(2,1)}, bf16[4032,128]{1,0:T(8,128)(2,1)S(1)}, u32[]{:S(2)}, u32[]{:S(2)}) collective-permute-start(bf16[4032,128]{1,0:T(8,128)(2,1)} %get-tuple-element.98), channel_id=1, source_target_pairs={{0,0},{1,1},{2,2},{3,3},{4,4},{5,5},{6,6},{7,7},{8,16},{9,17},{10,... | collective-permute-start | bytes 3096584 | tf_op jit(solution)/shard_map/ppermute | solution.py:57
  299.9 16.5 %shard_map.61 = (bf16[4032,128]{1,0:T(8,128)(2,1)}, bf16[4032,128]{1,0:T(8,128)(2,1)}) custom-call(s32[4]{0:T(128)} %copy-done.6, bf16[7,2048,256]{2,1,0:T(8,128)(2,1)} %get-tuple-element.100.direct, bf16[7,1536,256]{2,1,0:T(8,128)(2,1)} %get-tuple-element.101.flipped, bf16[576,5376]{1,0:T(8,128)(2,1)} %copy-done, ...), custom_call_target="tpu_custom_call" | custom-call | flops 7398752256 | bytes 20000000 | tf_op jit(solution)/shard_map/pallas_call | solution.py:480
  316.5 3.4 collective-permute-start.32
  319.9 3.9 %collective-permute-done.29.r0 = bf16[4032,128]{1,0:T(8,128)(2,1)S(1)} collective-permute-done((bf16[4032,128]{1,0:T(8,128)(2,1)}, bf16[4032,128]{1,0:T(8,128)(2,1)S(1)}, u32[]{:S(2)}, u32[]{:S(2)}) %collective-permute-start.29) | collective-permute-done | bytes 1032224 | tf_op jit(solution)/shard_map/ppermute | solution.py:57
  323.8 10.8 %collective-permute-done.30.r1 = bf16[4032,128]{1,0:T(8,128)(2,1)} collective-permute-done((bf16[4032,128]{1,0:T(8,128)(2,1)}, bf16[4032,128]{1,0:T(8,128)(2,1)}, u32[]{:S(2)}, u32[]{:S(2)}) %collective-permute-start.30) | collective-permute-done | bytes 1032224 | tf_op jit(solution)/shard_map/ppermute | solution.py:57
  334.5 8.3 %collective-permute-done.31.r2 = bf16[4032,128]{1,0:T(8,128)(2,1)S(1)} collective-permute-done((bf16[4032,128]{1,0:T(8,128)(2,1)}, bf16[4032,128]{1,0:T(8,128)(2,1)S(1)}, u32[]{:S(2)}, u32[]{:S(2)}) %collective-permute-start.31) | collective-permute-done | bytes 1032224 | tf_op jit(solution)/shard_map/ppermute | solution.py:57
  342.9 4.1 %collective-permute-done.32.r3 = bf16[4032,128]{1,0:T(8,128)(2,1)S(1)} collective-permute-done((bf16[4032,128]{1,0:T(8,128)(2,1)}, bf16[4032,128]{1,0:T(8,128)(2,1)S(1)}, u32[]{:S(2)}, u32[]{:S(2)}) %collective-permute-start.32) | collective-permute-done | bytes 1032224 | tf_op jit(solution)/shard_map/ppermute | solution.py:57
  347.0 4.0 %shard_map.62 = bf16[896,2304]{1,0:T(8,128)(2,1)} custom-call(s32[4]{0:T(128)S(1)} %copy-done.7, bf16[4032,128]{1,0:T(8,128)(2,1)S(1)} %collective-permute-done.29.r0, bf16[4032,128]{1,0:T(8,128)(2,1)} %collective-permute-done.30.r1, bf16[4032,128]{1,0:T(8,128)(2,1)S(1)} %collective-permute-done.31.r2, bf16[4032,128]{1,0:T(8,128)(2,1)S(1)} %collective-permute-done.32.r3), custom_call_target="tpu_custom_call" | custom-call | bytes 8300000 | tf_op jit(solution)/shard_map/pallas_call | solution.py:553
  (102 shorter events, 31.7 us)
Async XLA Ops:
  52.0 27.4 %all-to-all-start.1 = ((bf16[16,432,128]{2,1,0:T(8,128)(2,1)}), bf16[16,432,128]{2,1,0:T(8,128)(2,1)}, u32[]{:S(2)}, u32[]{:S(2)}) async-start(bf16[16,432,128]{2,1,0:T(8,128)(2,1)} %get-tuple-element.56), calls=%async_computation.1 | async-start | bytes 3538944 | tf_op jit(solution)/shard_map/all_to_all | solution.py:571
  64.6 43.2 %collective-permute-start = (bf16[7,80,1152]{2,1,0:T(8,128)(2,1)}, bf16[7,80,1152]{2,1,0:T(8,128)(2,1)S(1)}, u32[]{:S(2)}, u32[]{:S(2)}) collective-permute-start(bf16[7,80,1152]{2,1,0:T(8,128)(2,1)} %get-tuple-element.59), channel_id=1, source_target_pairs={{0,0},{1,1},{2,2},{3,3},{4,4},{5,5},{6,6},{7,7},{8,16},{9,17},{10,... | collective-permute-start | bytes 3870728 | tf_op jit(solution)/shard_map/ppermute | solution.py:57
  71.3 36.6 %collective-permute-start.2 = (bf16[7,80,1152]{2,1,0:T(8,128)(2,1)}, bf16[7,80,1152]{2,1,0:T(8,128)(2,1)}, u32[]{:S(2)}, u32[]{:S(2)}) collective-permute-start(bf16[7,80,1152]{2,1,0:T(8,128)(2,1)} %get-tuple-element.61), channel_id=1, source_target_pairs={{0,4},{1,5},{2,6},{3,7},{4,0},{5,1},{6,2},{7,3},{8,20},{9,21},{10,... | collective-permute-start | bytes 3870728 | tf_op jit(solution)/shard_map/ppermute | solution.py:57
  84.8 38.8 %collective-permute-start.1 = (bf16[7,48,1152]{2,1,0:T(8,128)(2,1)}, bf16[7,48,1152]{2,1,0:T(8,128)(2,1)}, u32[]{:S(2)}, u32[]{:S(2)}) collective-permute-start(bf16[7,48,1152]{2,1,0:T(8,128)(2,1)} %get-tuple-element.60), channel_id=1, source_target_pairs={{0,0},{1,1},{2,2},{3,3},{4,4},{5,5},{6,6},{7,7},{8,16},{9,17},{10,... | collective-permute-start | bytes 2322440 | tf_op jit(solution)/shard_map/ppermute | solution.py:57
  91.9 31.7 %collective-permute-start.3 = (bf16[7,48,1152]{2,1,0:T(8,128)(2,1)}, bf16[7,48,1152]{2,1,0:T(8,128)(2,1)}, u32[]{:S(2)}, u32[]{:S(2)}) collective-permute-start(bf16[7,48,1152]{2,1,0:T(8,128)(2,1)} %get-tuple-element.62), channel_id=1, source_target_pairs={{0,4},{1,5},{2,6},{3,7},{4,0},{5,1},{6,2},{7,3},{8,20},{9,21},{10,... | collective-permute-start | bytes 2322440 | tf_op jit(solution)/shard_map/ppermute | solution.py:57
  107.8 16.4 %collective-permute-start.4 = (bf16[7,80,1152]{2,1,0:T(8,128)(2,1)S(1)}, bf16[7,80,1152]{2,1,0:T(8,128)(2,1)S(1)}, u32[]{:S(2)}, u32[]{:S(2)}) collective-permute-start(bf16[7,80,1152]{2,1,0:T(8,128)(2,1)S(1)} %collective-permute-done.refs_1_.refs_0_), channel_id=1, source_target_pairs={{0,16},{1,17},{2,18},{3,19},{4,20},{5,21},{6,22},{7,23},{8,24},{9,... | collective-permute-start | bytes 3870728 | tf_op jit(solution)/shard_map/ppermute | solution.py:57
  107.8 16.4 %collective-permute-start.6 = (bf16[7,80,1152]{2,1,0:T(8,128)(2,1)}, bf16[7,80,1152]{2,1,0:T(8,128)(2,1)}, u32[]{:S(2)}, u32[]{:S(2)}) collective-permute-start(bf16[7,80,1152]{2,1,0:T(8,128)(2,1)} %collective-permute-done.2.refs_3_.refs_2_), channel_id=1, source_target_pairs={{0,16},{1,17},{2,18},{3,19},{4,20},{5,21},{6,22},{7,23},{8,24},{9,... | collective-permute-start | bytes 3870728 | tf_op jit(solution)/shard_map/ppermute | solution.py:57
  123.6 3.7 %collective-permute-start.7 = (bf16[7,48,1152]{2,1,0:T(8,128)(2,1)}, bf16[7,48,1152]{2,1,0:T(8,128)(2,1)}, u32[]{:S(2)}, u32[]{:S(2)}) collective-permute-start(bf16[7,48,1152]{2,1,0:T(8,128)(2,1)} %collective-permute-done.3.refs_4_.refs_3_), channel_id=1, source_target_pairs={{0,16},{1,17},{2,18},{3,19},{4,20},{5,21},{6,22},{7,23},{8,24},{9,... | collective-permute-start | bytes 2322440 | tf_op jit(solution)/shard_map/ppermute | solution.py:57
  132.1 12.2 %collective-permute-start.8 = (bf16[608,256]{1,0:T(8,128)(2,1)S(1)}, bf16[608,256]{1,0:T(8,128)(2,1)S(1)}, u32[]{:S(2)}, u32[]{:S(2)}) collective-permute-start(bf16[608,256]{1,0:T(8,128)(2,1)S(1)} %get-tuple-element.66), channel_id=1, source_target_pairs={{0,1},{1,2},{2,3},{3,0},{4,5},{5,6},{6,7},{7,4},{8,9},{9,10},{10,1... | collective-permute-start | bytes 933896 | tf_op jit(solution)/shard_map/ppermute | solution.py:57
  133.4 10.9 %collective-permute-start.9 = (bf16[592,256]{1,0:T(8,128)(2,1)S(1)}, bf16[592,256]{1,0:T(8,128)(2,1)S(1)}, u32[]{:S(2)}, u32[]{:S(2)}) collective-permute-start(bf16[592,256]{1,0:T(8,128)(2,1)S(1)} %get-tuple-element.67), channel_id=1, source_target_pairs={{0,3},{1,0},{2,1},{3,2},{4,7},{5,4},{6,5},{7,6},{8,11},{9,8},{10,9... | collective-permute-start | bytes 909320 | tf_op jit(solution)/shard_map/ppermute | solution.py:57
  134.9 9.4 %collective-permute-start.10 = (bf16[592,256]{1,0:T(8,128)(2,1)S(1)}, bf16[592,256]{1,0:T(8,128)(2,1)S(1)}, u32[]{:S(2)}, u32[]{:S(2)}) collective-permute-start(bf16[592,256]{1,0:T(8,128)(2,1)S(1)} %get-tuple-element.68), channel_id=1, source_target_pairs={{0,4},{1,5},{2,6},{3,7},{4,0},{5,1},{6,2},{7,3},{8,12},{9,13},{10,... | collective-permute-start | bytes 909320 | tf_op jit(solution)/shard_map/ppermute | solution.py:57
  144.6 21.2 %collective-permute-start.12 = (bf16[1792,256]{1,0:T(8,128)(2,1)S(1)}, bf16[1792,256]{1,0:T(8,128)(2,1)S(1)}, u32[]{:S(2)}, u32[]{:S(2)}) collective-permute-start(bf16[1792,256]{1,0:T(8,128)(2,1)S(1)} %get-tuple-element.81), channel_id=1, source_target_pairs={{0,3},{1,0},{2,1},{3,2},{4,7},{5,4},{6,5},{7,6},{8,11},{9,8},{10,9... | collective-permute-start | bytes 2752520 | tf_op jit(solution)/shard_map/ppermute | solution.py:57
  146.1 21.8 %collective-permute-start.13 = (bf16[1792,256]{1,0:T(8,128)(2,1)S(1)}, bf16[1792,256]{1,0:T(8,128)(2,1)S(1)}, u32[]{:S(2)}, u32[]{:S(2)}) collective-permute-start(bf16[1792,256]{1,0:T(8,128)(2,1)S(1)} %get-tuple-element.82), channel_id=1, source_target_pairs={{0,1},{1,2},{2,3},{3,0},{4,5},{5,6},{6,7},{7,4},{8,9},{9,10},{10,1... | collective-permute-start | bytes 2752520 | tf_op jit(solution)/shard_map/ppermute | solution.py:57
  146.2 21.7 %collective-permute-start.11 = (bf16[1792,256]{1,0:T(8,128)(2,1)S(1)}, bf16[1792,256]{1,0:T(8,128)(2,1)S(1)}, u32[]{:S(2)}, u32[]{:S(2)}) collective-permute-start(bf16[1792,256]{1,0:T(8,128)(2,1)S(1)} %get-tuple-element.69), channel_id=1, source_target_pairs={{0,4},{1,5},{2,6},{3,7},{4,0},{5,1},{6,2},{7,3},{8,12},{9,13},{10,... | collective-permute-start | bytes 2752520 | tf_op jit(solution)/shard_map/ppermute | solution.py:57
  156.3 29.2 %collective-permute-start.16 = (bf16[1792,256]{1,0:T(8,128)(2,1)S(1)}, bf16[1792,256]{1,0:T(8,128)(2,1)S(1)}, u32[]{:S(2)}, u32[]{:S(2)}) collective-permute-start(bf16[1792,256]{1,0:T(8,128)(2,1)S(1)} %get-tuple-element.85), channel_id=1, source_target_pairs={{0,3},{1,0},{2,1},{3,2},{4,7},{5,4},{6,5},{7,6},{8,11},{9,8},{10,9... | collective-permute-start | bytes 2752520 | tf_op jit(solution)/shard_map/ppermute | solution.py:57
  168.4 19.8 %collective-permute-start.15 = (bf16[1792,256]{1,0:T(8,128)(2,1)S(1)}, bf16[1792,256]{1,0:T(8,128)(2,1)S(1)}, u32[]{:S(2)}, u32[]{:S(2)}) collective-permute-start(bf16[1792,256]{1,0:T(8,128)(2,1)S(1)} %get-tuple-element.84), channel_id=1, source_target_pairs={{0,4},{1,5},{2,6},{3,7},{4,0},{5,1},{6,2},{7,3},{8,12},{9,13},{10,... | collective-permute-start | bytes 2752520 | tf_op jit(solution)/shard_map/ppermute | solution.py:57
  168.8 20.6 %collective-permute-start.14 = (bf16[1792,256]{1,0:T(8,128)(2,1)S(1)}, bf16[1792,256]{1,0:T(8,128)(2,1)S(1)}, u32[]{:S(2)}, u32[]{:S(2)}) collective-permute-start(bf16[1792,256]{1,0:T(8,128)(2,1)S(1)} %get-tuple-element.83), channel_id=1, source_target_pairs={{0,1},{1,2},{2,3},{3,0},{4,5},{5,6},{6,7},{7,4},{8,9},{9,10},{10,1... | collective-permute-start | bytes 2752520 | tf_op jit(solution)/shard_map/ppermute | solution.py:57
  189.8 18.6 %collective-permute-start.19 = (bf16[1792,256]{1,0:T(8,128)(2,1)S(1)}, bf16[1792,256]{1,0:T(8,128)(2,1)S(1)}, u32[]{:S(2)}, u32[]{:S(2)}) collective-permute-start(bf16[1792,256]{1,0:T(8,128)(2,1)S(1)} %shard_map.59.refs_0_), channel_id=1, source_target_pairs={{0,4},{1,5},{2,6},{3,7},{4,0},{5,1},{6,2},{7,3},{8,12},{9,13},{10,... | collective-permute-start | bytes 2752520 | tf_op jit(solution)/shard_map/ppermute | solution.py:57
  191.0 18.2 %collective-permute-start.18 = (bf16[1792,256]{1,0:T(8,128)(2,1)S(1)}, bf16[1792,256]{1,0:T(8,128)(2,1)S(1)}, u32[]{:S(2)}, u32[]{:S(2)}) collective-permute-start(bf16[1792,256]{1,0:T(8,128)(2,1)S(1)} %shard_map.59.refs_0_), channel_id=1, source_target_pairs={{0,3},{1,0},{2,1},{3,2},{4,7},{5,4},{6,5},{7,6},{8,11},{9,8},{10,9... | collective-permute-start | bytes 2752520 | tf_op jit(solution)/shard_map/ppermute | solution.py:57
  191.0 19.2 %collective-permute-start.17 = (bf16[1792,256]{1,0:T(8,128)(2,1)S(1)}, bf16[1792,256]{1,0:T(8,128)(2,1)S(1)}, u32[]{:S(2)}, u32[]{:S(2)}) collective-permute-start(bf16[1792,256]{1,0:T(8,128)(2,1)S(1)} %shard_map.59.refs_0_), channel_id=1, source_target_pairs={{0,1},{1,2},{2,3},{3,0},{4,5},{5,6},{6,7},{7,4},{8,9},{9,10},{10,1... | collective-permute-start | bytes 2752520 | tf_op jit(solution)/shard_map/ppermute | solution.py:57
  211.1 41.7 %collective-permute-start.26 = (bf16[7168,256]{1,0:T(8,128)(2,1)S(1)}, bf16[7168,256]{1,0:T(8,128)(2,1)S(1)}, u32[]{:S(2)}, u32[]{:S(2)}) collective-permute-start(bf16[7168,256]{1,0:T(8,128)(2,1)S(1)} %pad_maximum_fusion), channel_id=1, source_target_pairs={{0,16},{1,17},{2,18},{3,19},{4,20},{5,21},{6,22},{7,23},{8,24},{9,... | collective-permute-start | bytes 11010056 | tf_op jit(solution)/shard_map/ppermute | solution.py:57
  216.0 23.2 %collective-permute-start.21 = (bf16[1792,256]{1,0:T(8,128)(2,1)S(1)}, bf16[1792,256]{1,0:T(8,128)(2,1)S(1)}, u32[]{:S(2)}, u32[]{:S(2)}) collective-permute-start(bf16[1792,256]{1,0:T(8,128)(2,1)S(1)} %collective-permute-done.19.refs_3_), channel_id=1, source_target_pairs={{0,1},{1,2},{2,3},{3,0},{4,5},{5,6},{6,7},{7,4},{8,9},{9,10},{10,1... | collective-permute-start | bytes 2752520 | tf_op jit(solution)/shard_map/ppermute | solution.py:57
  216.2 22.9 %collective-permute-start.22 = (bf16[1792,256]{1,0:T(8,128)(2,1)S(1)}, bf16[1792,256]{1,0:T(8,128)(2,1)S(1)}, u32[]{:S(2)}, u32[]{:S(2)}) collective-permute-start(bf16[1792,256]{1,0:T(8,128)(2,1)S(1)} %collective-permute-done.18.refs_2_), channel_id=1, source_target_pairs={{0,3},{1,0},{2,1},{3,2},{4,7},{5,4},{6,5},{7,6},{8,11},{9,8},{10,9... | collective-permute-start | bytes 2752520 | tf_op jit(solution)/shard_map/ppermute | solution.py:57
  218.7 21.3 %collective-permute-start.20 = (bf16[1792,256]{1,0:T(8,128)(2,1)S(1)}, bf16[1792,256]{1,0:T(8,128)(2,1)S(1)}, u32[]{:S(2)}, u32[]{:S(2)}) collective-permute-start(bf16[1792,256]{1,0:T(8,128)(2,1)S(1)} %collective-permute-done.18.refs_2_), channel_id=1, source_target_pairs={{0,4},{1,5},{2,6},{3,7},{4,0},{5,1},{6,2},{7,3},{8,12},{9,13},{10,... | collective-permute-start | bytes 2752520 | tf_op jit(solution)/shard_map/ppermute | solution.py:57
  240.2 13.9 %collective-permute-start.27 = (bf16[5376,256]{1,0:T(8,128)(2,1)S(1)}, bf16[5376,256]{1,0:T(8,128)(2,1)S(1)}, u32[]{:S(2)}, u32[]{:S(2)}) collective-permute-start(bf16[5376,256]{1,0:T(8,128)(2,1)S(1)} %pad_maximum_fusion.1), channel_id=1, source_target_pairs={{0,16},{1,17},{2,18},{3,19},{4,20},{5,21},{6,22},{7,23},{8,24},{9,... | collective-permute-start | bytes 8257544 | tf_op jit(solution)/shard_map/ppermute | solution.py:57
  241.7 11.1 %collective-permute-start.23 = (bf16[608,256]{1,0:T(8,128)(2,1)S(1)}, bf16[608,256]{1,0:T(8,128)(2,1)S(1)}, u32[]{:S(2)}, u32[]{:S(2)}) collective-permute-start(bf16[608,256]{1,0:T(8,128)(2,1)S(1)} %slice.17), channel_id=1, source_target_pairs={{0,3},{1,0},{2,1},{3,2},{4,7},{5,4},{6,5},{7,6},{8,11},{9,8},{10,9... | collective-permute-start | bytes 933896 | tf_op jit(solution)/shard_map/ppermute | solution.py:57
  243.0 9.8 %collective-permute-start.24 = (bf16[592,256]{1,0:T(8,128)(2,1)S(1)}, bf16[592,256]{1,0:T(8,128)(2,1)S(1)}, u32[]{:S(2)}, u32[]{:S(2)}) collective-permute-start(bf16[592,256]{1,0:T(8,128)(2,1)S(1)} %slice.18), channel_id=1, source_target_pairs={{0,1},{1,2},{2,3},{3,0},{4,5},{5,6},{6,7},{7,4},{8,9},{9,10},{10,1... | collective-permute-start | bytes 909320 | tf_op jit(solution)/shard_map/ppermute | solution.py:57
  243.4 9.4 %collective-permute-start.25 = (bf16[592,256]{1,0:T(8,128)(2,1)S(1)}, bf16[592,256]{1,0:T(8,128)(2,1)S(1)}, u32[]{:S(2)}, u32[]{:S(2)}) collective-permute-start(bf16[592,256]{1,0:T(8,128)(2,1)S(1)} %slice.19), channel_id=1, source_target_pairs={{0,4},{1,5},{2,6},{3,7},{4,0},{5,1},{6,2},{7,3},{8,12},{9,13},{10,... | collective-permute-start | bytes 909320 | tf_op jit(solution)/shard_map/ppermute | solution.py:57
  294.9 28.9 %collective-permute-start.29 = (bf16[4032,128]{1,0:T(8,128)(2,1)}, bf16[4032,128]{1,0:T(8,128)(2,1)S(1)}, u32[]{:S(2)}, u32[]{:S(2)}) collective-permute-start(bf16[4032,128]{1,0:T(8,128)(2,1)} %get-tuple-element.98), channel_id=1, source_target_pairs={{0,0},{1,1},{2,2},{3,3},{4,4},{5,5},{6,6},{7,7},{8,16},{9,17},{10,... | collective-permute-start | bytes 3096584 | tf_op jit(solution)/shard_map/ppermute | solution.py:57
  299.4 35.1 %collective-permute-start.30 = (bf16[4032,128]{1,0:T(8,128)(2,1)}, bf16[4032,128]{1,0:T(8,128)(2,1)}, u32[]{:S(2)}, u32[]{:S(2)}) collective-permute-start(bf16[4032,128]{1,0:T(8,128)(2,1)} %get-tuple-element.99), channel_id=1, source_target_pairs={{0,4},{1,5},{2,6},{3,7},{4,0},{5,1},{6,2},{7,3},{8,20},{9,21},{10,... | collective-permute-start | bytes 3096584 | tf_op jit(solution)/shard_map/ppermute | solution.py:57
  316.4 26.5 %collective-permute-start.31 = (bf16[4032,128]{1,0:T(8,128)(2,1)}, bf16[4032,128]{1,0:T(8,128)(2,1)S(1)}, u32[]{:S(2)}, u32[]{:S(2)}) collective-permute-start(bf16[4032,128]{1,0:T(8,128)(2,1)} %get-tuple-element.104), channel_id=1, source_target_pairs={{0,8},{1,9},{2,10},{3,11},{4,12},{5,13},{6,14},{7,15},{8,24},{9,25... | collective-permute-start | bytes 3096584 | tf_op jit(solution)/shard_map/ppermute | solution.py:57
  316.5 30.5 %collective-permute-start.32 = (bf16[4032,128]{1,0:T(8,128)(2,1)}, bf16[4032,128]{1,0:T(8,128)(2,1)S(1)}, u32[]{:S(2)}, u32[]{:S(2)}) collective-permute-start(bf16[4032,128]{1,0:T(8,128)(2,1)} %get-tuple-element.105), channel_id=1, source_target_pairs={{0,12},{1,13},{2,14},{3,15},{4,8},{5,9},{6,10},{7,11},{8,28},{9,29... | collective-permute-start | bytes 3096584 | tf_op jit(solution)/shard_map/ppermute | solution.py:57
  (23 other events, 270.5 us)
